TPU v7x, 32 devices: a whole 2x2x4 slice. The times are simulated.
32 devices in a mesh: row: 4 (over y, x), col: 8 (over z, core).
Axes of the slice: x: 2, y: 2, z: 4, core: 2. Of those that a mesh axis runs over, the one named last changes fastest.
Arguments:
- node_features: bfloat16 [3072, 1024], P('row'), may hold values from -28 to 28
- edge_weight: bfloat16 [3072, 3072], P('row', 'col'), may hold values from -0.109375 to 0.109375
- pattern: int32 [24, 24], P('row', 'col'), may hold values from 0 to 1, as said below
- w_qkv: bfloat16 [1024, 3072], replicated, may hold values from -0.1875 to 0.1875
- w_out: bfloat16 [1024, 1024], P(None, 'col'), may hold values from -0.1875 to 0.1875
- bias_gain: float32 [16], replicated, may hold values from -2 to 2
- bias_rate: float32 [16], replicated, may hold values from 2 to 12
Outputs:
- mixed: bfloat16 [3072, 1024], P('row', 'col')
Inputs may be any that keep to these rules, and one draw needn't show every extreme that they name: pattern[i][i] is 1 for every i; the share of ones differs from block-row to block-row.
All inputs are finite; a program needn't handle non-finite values.
Results may differ from a plain program's by a relative error of at most 0.02.
Values may be sent and summed in bfloat16 or wider, within the bound.
No kernel may reach another device: no remote copies, remote signals or barrier semaphores. Data moves between devices by JAX's collectives and lax.ppermute only.
A program may use at most 128 MiB of HBM per device.

v0:
```python
import math

import jax
import jax.numpy as jnp
from jax import lax
from jax.sharding import PartitionSpec as P

D = 1024
HEADS = 16
BLK = 128
SWEEPS = 3
HDIM = 64


def spread(value, axis, source):
    kept = jnp.where(lax.axis_index(axis) == source, value, 0).astype(value.dtype)
    return lax.psum(kept, axis)


def expand_blocks(pattern):
    block_rows, block_cols = pattern.shape
    grid = jnp.broadcast_to(pattern[:, None, :, None] > 0, (block_rows, BLK, block_cols, BLK))
    return grid.reshape(block_rows * BLK, block_cols * BLK)


def sweep(operator_panel, ranks, keep_mask, identity):
    product = jnp.dot(
        operator_panel,
        lax.all_gather(ranks.astype(jnp.bfloat16), "row", axis=0, tiled=True),
        preferred_element_type=jnp.float32,
    )
    return jnp.where(keep_mask, 0.15 * identity + 0.85 * product, jnp.zeros((), jnp.float32))


def shards(node_features, edge_weight, pattern, w_qkv, w_out, bias_gain, bias_rate):
    rows_here, cols_here = edge_weight.shape
    col_count = lax.axis_size("col")
    nodes_all = cols_here * col_count
    col_pos = lax.axis_index("col")
    keep_mask = expand_blocks(pattern)
    adjacency = jnp.where(keep_mask, edge_weight, jnp.zeros_like(edge_weight))
    row_ids = lax.axis_index("row") * rows_here + lax.iota(jnp.int32, rows_here)
    col_ids = col_pos * cols_here + lax.iota(jnp.int32, cols_here)
    identity = (row_ids[:, None] == col_ids[None, :]).astype(jnp.float32)
    ranks = jnp.where(
        keep_mask,
        0.15 * identity + 0.1275 * adjacency.astype(jnp.float32),
        jnp.zeros((), jnp.float32),
    )
    for sweep_index in range(SWEEPS - 1):
        operator_panel = lax.all_gather(adjacency, "col", axis=1, tiled=True)
        ranks = sweep(operator_panel, ranks, keep_mask, identity)
    w_query = w_qkv[:, :D]
    queries = jnp.dot(node_features, w_query, preferred_element_type=jnp.float32).astype(
        jnp.bfloat16
    )
    key_half = lax.dynamic_slice_in_dim(node_features, col_pos % 2 * cols_here, cols_here, 0)
    key_rows = spread(key_half, "row", col_pos // 2)
    keys_values = jnp.dot(key_rows, w_qkv[:, D:], preferred_element_type=jnp.float32).astype(
        jnp.bfloat16
    )
    query_heads = queries.reshape(rows_here, HEADS, HDIM)
    key_heads = keys_values[:, :D].reshape(cols_here, HEADS, HDIM)
    value_heads = keys_values[:, D:].reshape(cols_here, HEADS, HDIM)
    score_scale = 1.0 / math.sqrt(HDIM)
    root_nodes = math.sqrt(nodes_all)
    scores = (
        jnp.einsum("rhd,chd->hrc", query_heads, key_heads, preferred_element_type=jnp.float32)
        * score_scale
    )
    scores = scores + bias_gain[:, None, None] * jnp.tanh(
        bias_rate[:, None, None] * root_nodes * ranks[None]
    )
    masked = jnp.where(keep_mask[None], scores, -1e30)
    local_peak = jnp.max(masked, axis=2)
    row_peak = lax.pmax(local_peak.astype(jnp.bfloat16), "col").astype(local_peak.dtype)
    expo = jnp.where(
        keep_mask[None], jnp.exp(masked - row_peak[:, :, None]), jnp.zeros((), jnp.float32)
    )
    totals = jnp.sum(expo, axis=2).T
    numer = jnp.einsum(
        "hrc,chd->rhd", expo.astype(jnp.bfloat16), value_heads, preferred_element_type=jnp.float32
    )
    numer = numer.reshape(rows_here, D)
    numer_all, totals_all = (
        lax.psum(numer.astype(jnp.bfloat16), "col").astype(jnp.float32),
        lax.psum(totals.astype(jnp.bfloat16), "col").astype(jnp.float32),
    )
    attended = numer_all.reshape(rows_here, HEADS, HDIM) / totals_all[:, :, None]
    attended = attended.reshape(rows_here, D).astype(jnp.bfloat16)
    return jnp.dot(attended, w_out, preferred_element_type=jnp.float32).astype(jnp.bfloat16)


def solution(mesh):
    in_specs = (P("row", None), P("row", "col"), P("row", "col"), P(), P(None, "col"), P(), P())
    out_specs = P("row", "col")
    return jax.shard_map(shards, mesh=mesh, in_specs=in_specs, out_specs=out_specs, check_vma=False)
```

profile of v0, /device:TPU:0, one launch (start us, length us, event | category | flops | bytes accessed | tf_op | source)
XLA Modules:
  0.0 324.0 jit_solution(12695955652672199298)
XLA Ops:
  6.5 0.8 broadcast_compare_fusion
  7.7 0.4 copy.21
  8.0 2.4 fusion.25
  10.5 1.0 broadcast_select_fusion
  11.6 1.0 dynamic-slice_select_fusion
  12.7 38.1 %all-gather.6.cloned.1.call-done = bf16[3072,384]{1,0:T(8,128)(2,1)} async-done(((bf16[768,384]{1,0:T(8,128)(2,1)}), bf16[3072,384]{1,0:T(8,128)(2,1)}) %all-gather.6.cloned.1.call-update) | async-done | bytes 2359312 | tf_op jit(solution)/shard_map/all_gather | solution.py:29
  50.8 53.1 %all-gather.4.cloned.1.call-done = bf16[768,3072]{1,0:T(8,128)(2,1)} async-done(((bf16[768,384]{1,0:T(8,128)(2,1)}), bf16[768,3072]{1,0:T(8,128)(2,1)}) %all-gather.4.cloned.1.call-update) | async-done | bytes 4718608 | tf_op jit(solution)/shard_map/all_gather | solution.py:51
  103.9 6.6 %fusion.23 = bf16[768,384]{1,0:T(8,128)(2,1)} fusion(pred[768,384]{1,0:T(32,128)(4,1)S(1)} %copy.21, bf16[768,3072]{1,0:T(8,128)(2,1)} %all-gather.4.cloned.1.call-done, bf16[3072,384]{1,0:T(8,128)(2,1)} %all-gather.6.cloned.1.call-done, s32[384]{0:T(512)S(1)} %iota_add_fusion.1, s32[768]{0:T(1024)S(1)} %iota_add_fusion), kind=kOutput, calls=%fused_computation.24 | convolution fusion | flops 1813708800 | bytes 7967232 | tf_op jit(solution)/shard_map/dot_general | solution.py:27
  110.8 3.9 %fusion.15 = bf16[768,1024]{1,0:T(8,128)(2,1)S(1)} fusion(bf16[768,1024]{1,0:T(8,128)(2,1)} %param.7, bf16[1024,3072]{1,0:T(8,128)(2,1)} %param.10), kind=kOutput, calls=%fused_computation.18 | convolution fusion | flops 1611399168 | bytes 5242880 | tf_op jit(solution)/shard_map/dot_general | solution.py:54
  114.7 1.7 copy.16
  116.4 38.1 %all-reduce.3.cloned.1.call-done = bf16[384,1024]{1,0:T(8,128)(2,1)} async-done(((bf16[384,1024]{1,0:T(8,128)(2,1)}), bf16[384,1024]{1,0:T(8,128)(2,1)}) %all-reduce.3.cloned.1.call-update) | async-done | bytes 786448 | tf_op jit(solution)/shard_map/psum | solution.py:17
  154.5 4.2 %fusion.10 = bf16[384,2048]{1,0:T(8,128)(2,1)S(1)} fusion(bf16[384,1024]{1,0:T(8,128)(2,1)} %all-reduce.3.cloned.1.call-done, bf16[1024,3072]{1,0:T(8,128)(2,1)} %param.10), kind=kOutput, calls=%fused_computation.12 | convolution fusion | flops 1611399168 | bytes 6553600 | tf_op jit(solution)/shard_map/dot_general | solution.py:59
  158.8 1.2 copy.17
  160.4 33.4 %all-gather.8.cloned.1.call-done = bf16[3072,384]{1,0:T(8,128)(2,1)} async-done(((bf16[768,384]{1,0:T(8,128)(2,1)}), bf16[3072,384]{1,0:T(8,128)(2,1)}) %all-gather.8.cloned.1.call-update) | async-done | bytes 2359312 | tf_op jit(solution)/shard_map/all_gather | solution.py:29
  193.8 6.9 %fusion.22 = f32[768,384]{1,0:T(8,128)} fusion(pred[768,384]{1,0:T(32,128)(4,1)S(1)} %copy.21, bf16[768,3072]{1,0:T(8,128)(2,1)} %all-gather.4.cloned.1.call-done, bf16[3072,384]{1,0:T(8,128)(2,1)} %all-gather.8.cloned.1.call-done, s32[384]{0:T(512)S(1)} %iota_add_fusion.1, s32[768]{0:T(1024)S(1)} %iota_add_fusion), kind=kOutput, calls=%fused_computation.23 | convolution fusion | flops 1813413888 | bytes 8557056 | tf_op jit(solution)/shard_map/dot_general | solution.py:27
  200.7 2.8 copy.22
  203.5 12.0 %fusion.28 = (bf16[16,768]{1,0:T(8,128)(2,1)S(1)}, f32[16,768,384]{1,2,0:T(8,128)}) fusion(f32[768,384]{0,1:T(8,128)} %copy.22, f32[16]{0:T(128)S(1)} %broadcast_multiply_fusion, f32[16]{0:T(128)S(1)} %copy-done.5, bf16[768,16,64]{0,2,1:T(8,128)(2,1)S(1)} %bitcast.37, bf16[384,16,64]{0,2,1:T(8,128)(2,1)} %bitcast.39, pred[768,384]{0,1:T(8,128)(4,1)S(1)} %bitcast.33), kind=kOutput, calls=%fused_computation.38 | convolution fusion | flops 632279040 | bytes 22732928 | tf_op jit(solution)/shard_map/rhd,chd->hrc/dot_general | solution.py:68
  215.5 28.5 %pmax.7 = bf16[16,768]{1,0:T(8,128)(2,1)S(1)} all-reduce(bf16[16,768]{1,0:T(8,128)(2,1)S(1)} %get-tuple-element.7), channel_id=1, replica_groups=mesh['row'=4,'col'=8] {'col'}, use_global_device_ids=true, to_apply=%region_2.3 | all-reduce | flops 12288 | bytes 49152 | tf_op jit(solution)/shard_map/pmax | solution.py:76
  244.1 10.7 %fusion.18 = bf16[16,64,768]{2,1,0:T(8,128)(2,1)} fusion(bf16[384,16,64]{0,2,1:T(8,128)(2,1)S(1)} %bitcast.36, f32[16,768,384]{1,2,0:T(8,128)} %get-tuple-element.8, f32[16,768]{1,0:T(8,128)S(1)} %convert_element_type.60, pred[768,384]{0,1:T(8,128)(4,1)S(1)} %bitcast.34), kind=kOutput, calls=%fused_computation.19 | convolution fusion | flops 618921984 | bytes 21577728 | tf_op jit(solution)/shard_map/hrc,chd->rhd/dot_general | solution.py:81
  254.8 9.7 %fusion = bf16[16,768]{1,0:T(8,128)(2,1)S(1)} fusion(f32[16,768,384]{1,2,0:T(8,128)} %get-tuple-element.8, f32[16,768]{1,0:T(8,128)S(1)} %convert_element_type.60, pred[768,384]{0,1:T(8,128)(4,1)S(1)} %bitcast.35), kind=kLoop, calls=%fused_computation.2 | loop fusion | flops 14143488 | bytes 19243008 | tf_op jit(solution)/shard_map/reduce_sum | solution.py:80
  264.6 26.3 %psum.23 = bf16[768,16]{0,1:T(8,128)(2,1)S(1)} all-reduce(bf16[768,16]{0,1:T(8,128)(2,1)S(1)} %bitcast.40), channel_id=1, replica_groups=mesh['row'=4,'col'=8] {'col'}, use_global_device_ids=true, to_apply=%region_5.6 | all-reduce | flops 12288 | bytes 49152 | tf_op jit(solution)/shard_map/psum | solution.py:87
  290.9 23.5 %all-reduce.5.cloned.1.call-done = bf16[768,1024]{0,1:T(8,128)(2,1)} async-done(((bf16[768,1024]{0,1:T(8,128)(2,1)}), bf16[768,1024]{0,1:T(8,128)(2,1)}) %all-reduce.5.cloned.1.call-update) | async-done | bytes 1572880 | tf_op jit(solution)/shard_map/psum | solution.py:86
  314.4 1.7 fusion.9
  316.1 1.3 convolution_convert_fusion
  (31 shorter events, 1.3 us)
Async XLA Ops:
  6.5 309.6 %copy-start = (bf16[1024,128]{1,0:T(8,128)(2,1)S(1)}, bf16[1024,128]{1,0:T(8,128)(2,1)}, u32[]{:S(2)}) copy-start(bf16[1024,128]{1,0:T(8,128)(2,1)} %param.11) | copy-start | bytes 786436
  6.5 4.0 %copy-start.1 = (bf16[768,384]{1,0:T(8,128)(2,1)S(1)}, bf16[768,384]{1,0:T(8,128)(2,1)}, u32[]{:S(2)}) copy-start(bf16[768,384]{1,0:T(8,128)(2,1)} %param.8) | copy-start | bytes 1769476
  6.5 44.2 %all-gather.6.cloned.1.call-start = ((), (), s32[]{:S(2)}) async-start(), calls=%async_computation.2 | async-start | bytes 2949120 | tf_op jit(solution)/shard_map/all_gather | solution.py:29
  7.6 3.9 %copy-start.3 = (bf16[768,1024]{1,0:T(8,128)(2,1)S(1)}, bf16[768,1024]{1,0:T(8,128)(2,1)}, u32[]{:S(2)}) copy-start(bf16[768,1024]{1,0:T(8,128)(2,1)} %param.7) | copy-start | bytes 4718596
  10.4 93.5 %all-gather.4.cloned.1.call-start = ((), (), s32[]{:S(2)}) async-start(), calls=%async_computation.1 | async-start | bytes 5308416 | tf_op jit(solution)/shard_map/all_gather | solution.py:51
  11.5 143.0 %all-reduce.3.cloned.1.call-start = ((), (), s32[]{:S(2)}) async-start(), calls=%async_computation | async-start | bytes 1572864 | tf_op jit(solution)/shard_map/psum | solution.py:17
  12.7 181.2 %all-gather.8.cloned.1.call-start = ((), (), s32[]{:S(2)}) async-start(), calls=%async_computation.3 | async-start | bytes 2949120 | tf_op jit(solution)/shard_map/all_gather | solution.py:29
  110.6 203.9 %all-reduce.5.cloned.1.call-start = ((), (), s32[]{:S(2)}) async-start(), calls=%async_computation.4 | async-start | bytes 3145728 | tf_op jit(solution)/shard_map/psum | solution.py:86
  114.7 1.7 copy-start.4
  200.7 2.8 copy-start.2
  200.7 2.8 copy-start.5
Sparse Core Ops, SparseCore 0:
  10.6 40.1 all-gather.5
  52.4 51.4 all-gather.3
  107.0 47.4 all-reduce.2
  156.3 37.4 all-gather.7
  255.0 59.3 all-reduce.4
where the time goes:
time: 324 us
  waiting for transfers between devices  186 us (57%)
  blocking collectives  54.8 us (17%)
  matrix products  45.7 us (14%)
  other arithmetic  16.6 us (5%)
  between operations  13.3 us (4%)
  local copies, waits for them, and re-layouts  6.84 us (2%)
    all_gather x2, waiting for transfers between devices, sweep(): lax.all_gather(ranks.astype(jnp.bfloat16), 'row', axis=0, tiled=True)  71.5 us
    all_gather x1, waiting for transfers between devices, shards(): operator_panel = lax.all_gather(adjacency, 'col', axis=1, tiled=True)  53.1 us
    psum x1, waiting for transfers between devices, spread(): return lax.psum(kept, axis)  38.1 us
    pmax x1, blocking collectives, shards(): lax.pmax(local_peak.astype(jnp.bfloat16), 'col').astype(local_peak.dtype)  28.5 us
    psum x1, blocking collectives, shards(): lax.psum(totals.astype(jnp.bfloat16), 'col').astype(jnp.float32)  26.3 us
    psum x1, waiting for transfers between devices, shards(): lax.psum(numer.astype(jnp.bfloat16), 'col').astype(jnp.float32)  23.5 us
    dot_general x2, matrix products, sweep(): jnp.dot(operator_panel, lax.all_gather(ranks.astype(jnp.bfloat16), 'row',...  13.5 us
    dot_general x1, matrix products, shards(): jnp.einsum('rhd,chd->hrc', query_heads, key_heads, preferred_element_type...  12 us
  transfers between devices with their start and end apart: 5, of which 5 were waited for; matrix products, arithmetic and copies ran while one was open for 9% of the time, Pallas kernels for 0%

commit v1 on v0

v1 whole, which is shorter than its diff:
```python
import functools
import math

import jax
import jax.numpy as jnp
from jax import lax
from jax.experimental import pallas as pl
from jax.experimental.pallas import tpu as pltpu
from jax.sharding import PartitionSpec as P

D = 1024
HEADS = 16
BLK = 128
HDIM = 64
PAIRS = HEADS // 2
LANES = 128
VMEM_LIMIT = 56 * 2**20

VMEM = pl.BlockSpec(memory_space=pltpu.VMEM)
SMEM = pl.BlockSpec(memory_space=pltpu.SMEM)
BF16 = jnp.bfloat16
F32 = jnp.float32


def params():
    return pltpu.CompilerParams(vmem_limit_bytes=VMEM_LIMIT)


def cost(flops, nbytes, trans=0):
    return pl.CostEstimate(flops=int(flops), bytes_accessed=int(nbytes), transcendentals=int(trans))


def xor_pairs(n, j):
    return [(i, i ^ j) for i in range(n)]


def keep_rows(pattern_ref, block_row, block_cols):
    parts = [
        jnp.full((1, BLK), jnp.where(pattern_ref[block_row, b] > 0, 1.0, 0.0), F32)
        for b in range(block_cols)
    ]
    return jnp.concatenate(parts, axis=1)


def sweep_kernel(first, ratio, place_ref, pattern_ref, own_ref, panel_ref, *rest):
    blocks, out_ref = rest[:-1], rest[-1]
    rows, cols = own_ref.shape
    row_pos, col_pos = place_ref[0], place_ref[1]
    block_cols = cols // BLK
    tile = 256

    def step(t, carry):
        start = pl.multiple_of(t * tile, tile)
        acc = jnp.zeros((tile, cols), F32)
        for j, block in enumerate(blocks):
            source = lax.bitwise_xor(row_pos, j) * ratio
            left = jnp.concatenate(
                [panel_ref[source + i, pl.ds(start, tile), :] for i in range(ratio)], axis=1
            )
            acc += jnp.dot(left, block[...], preferred_element_type=F32)
        own = own_ref[pl.ds(start, tile), :].astype(F32)
        total = 0.1275 * own + (0.85 * 0.1275 if first else 0.85) * acc
        keep = jnp.concatenate(
            [
                jnp.broadcast_to(
                    keep_rows(pattern_ref, t * (tile // BLK) + b, block_cols), (BLK, cols)
                )
                for b in range(tile // BLK)
            ],
            axis=0,
        )
        if not first:
            row_ids = row_pos * rows + start + lax.broadcasted_iota(jnp.int32, (tile, cols), 0)
            col_ids = col_pos * cols + lax.broadcasted_iota(jnp.int32, (tile, cols), 1)
            total = jnp.where(row_ids == col_ids, total + 0.15, total)
        out_ref[pl.ds(start, tile), :] = jnp.where(keep > 0, total, 0.0).astype(out_ref.dtype)
        return carry

    lax.fori_loop(0, rows // tile, step, 0)


def sweep(first, place, pattern, own, panel, blocks, dtype):
    rows, cols = own.shape
    flops = 2 * rows * panel.shape[0] * cols * cols
    return pl.pallas_call(
        functools.partial(sweep_kernel, first, rows // cols),
        out_shape=jax.ShapeDtypeStruct((rows, cols), dtype),
        in_specs=[SMEM, SMEM] + [VMEM] * (2 + len(blocks)),
        out_specs=VMEM,
        compiler_params=params(),
        cost_estimate=cost(flops, 2 * panel.size + 4 * rows * cols * len(blocks)),
        name="rank_sweep",
    )(place, pattern, own, panel, *blocks)


def split_heads(keys):
    lane = lax.broadcasted_iota(jnp.int32, keys.shape, 1)
    zero = jnp.zeros_like(keys)
    return jnp.concatenate(
        [jnp.where(lane < HDIM, keys, zero), jnp.where(lane >= HDIM, keys, zero)], axis=0
    )


def peak_kernel(pattern_ref, q_ref, k_ref, out_ref):
    rows, cols = q_ref.shape[0], k_ref.shape[0]
    block_rows, block_cols = rows // BLK, cols // BLK
    masks = []
    for b in range(block_cols):
        masks.append(
            jnp.concatenate(
                [
                    jnp.full((1, BLK), jnp.where(pattern_ref[i, b] > 0, 0.0, -1e30), F32)
                    for i in range(block_rows)
                ],
                axis=1,
            )
        )
    for p in range(PAIRS):
        lanes = slice(p * LANES, (p + 1) * LANES)
        both = split_heads(k_ref[:, lanes])
        for side in range(2):
            peak = jnp.full((1, rows), -1e30, F32)
            for b in range(block_cols):
                start = side * cols + b * BLK
                s = lax.dot_general(
                    both[start : start + BLK, :],
                    q_ref[:, lanes],
                    (((1,), (1,)), ((), ())),
                    preferred_element_type=F32,
                )
                peak = jnp.maximum(peak, jnp.max(s, axis=0, keepdims=True) + masks[b])
            out_ref[2 * p + side : 2 * p + side + 1, :] = peak


def local_peak(pattern, queries, keys):
    rows, cols = queries.shape[0], keys.shape[0]
    return pl.pallas_call(
        peak_kernel,
        out_shape=jax.ShapeDtypeStruct((HEADS, rows), F32),
        in_specs=[SMEM, VMEM, VMEM],
        out_specs=VMEM,
        compiler_params=params(),
        cost_estimate=cost(4 * rows * cols * D, 2 * rows * D + 2 * cols * D),
        name="local_peak",
    )(pattern, queries, keys)


def expo_kernel(pattern_ref, q_ref, k_ref, peak_ref, out_ref):
    rows, cols = q_ref.shape[0], k_ref.shape[0]
    block_rows, block_cols = rows // BLK, cols // BLK
    extra = [peak_ref[...].astype(F32)]
    for b in range(block_cols):
        extra.append(
            jnp.concatenate(
                [
                    jnp.full((1, BLK), jnp.where(pattern_ref[i, b] > 0, 0.0, -1e30), F32)
                    for i in range(block_rows)
                ],
                axis=1,
            )
        )
    extra.append(jnp.zeros((LANES - HEADS - block_cols, rows), F32))
    extra = jnp.concatenate(extra, axis=0).T.astype(BF16)
    lane = lax.broadcasted_iota(jnp.int32, (2 * cols, LANES), 1)
    key = lax.broadcasted_iota(jnp.int32, (2 * cols, LANES), 0)
    block_of = jnp.where(key >= cols, key - cols, key) // BLK
    in_block = jnp.where(lane - HEADS == block_of, 1.0, 0.0)
    side = jnp.where(key >= cols, 1, 0)
    for p in range(PAIRS):
        lanes = slice(p * LANES, (p + 1) * LANES)
        head_lane = jnp.where(lane == 2 * p + side, -1.0, in_block).astype(BF16)
        right = jnp.concatenate([split_heads(k_ref[:, lanes]), head_lane], axis=1)

        for t in range(block_rows):
            left = jnp.concatenate(
                [q_ref[t * BLK : (t + 1) * BLK, lanes], extra[t * BLK : (t + 1) * BLK, :]], axis=1
            )
            s = lax.dot_general(
                left, right, (((1,), (1,)), ((), ())), preferred_element_type=F32
            )
            out_ref[p, t * BLK : (t + 1) * BLK, :] = jnp.exp(s).astype(BF16)


def exponentials(pattern, queries, keys, peak):
    rows, cols = queries.shape[0], keys.shape[0]
    return pl.pallas_call(
        expo_kernel,
        out_shape=jax.ShapeDtypeStruct((PAIRS, rows, 2 * cols), BF16),
        in_specs=[SMEM, VMEM, VMEM, VMEM],
        out_specs=VMEM,
        compiler_params=params(),
        cost_estimate=cost(
            8 * rows * cols * D, 2 * HEADS * rows * cols, HEADS * rows * cols
        ),
        name="expo",
    )(pattern, queries, keys, peak)


def weigh_kernel(root, place_ref, gain_ref, rate_ref, ranks_ref, expo_ref, v_ref, out_ref, p_ref):
    rows, cols = ranks_ref.shape
    chip, side = place_ref[0], place_ref[1]
    chips = place_ref.shape[0] - 2
    seg = out_ref.shape[0] // chips
    lane = lax.broadcasted_iota(jnp.int32, (cols, LANES), 1)
    zero = jnp.zeros((cols, LANES), BF16)
    low = jnp.where(lane < HDIM, 1.0, 0.0).astype(BF16)
    high = jnp.where(lane < HDIM, 0.0, 1.0).astype(BF16)
    out_lane = lax.broadcasted_iota(jnp.int32, (out_ref.shape[0], LANES), 1)
    totals = jnp.zeros((out_ref.shape[0], LANES), F32)
    for p in range(PAIRS):
        lanes = slice(p * LANES, (p + 1) * LANES)
        values = v_ref[:, lanes]
        right = jnp.concatenate(
            [
                jnp.concatenate([jnp.where(lane < HDIM, values, zero), low], axis=1),
                jnp.concatenate([jnp.where(lane < HDIM, zero, values), high], axis=1),
            ],
            axis=0,
        )
        for k in range(chips):
            start = pl.multiple_of((2 * lax.bitwise_xor(chip, k) + side) * seg, seg)
            ranks = ranks_ref[pl.ds(start, seg), :]
            for head_side in range(2):
                head = 2 * p + head_side
                rate = jnp.full((1, cols), rate_ref[head] * root, F32).astype(BF16)
                gain = jnp.full((1, cols), gain_ref[head] * math.log2(math.e), F32).astype(BF16)
                bias = gain * jnp.tanh(rate * ranks)
                at = slice(head_side * cols, (head_side + 1) * cols)
                p_ref[k * seg : (k + 1) * seg, at] = (
                    expo_ref[p, pl.ds(start, seg), at] * jnp.exp2(bias)
                )
        sums = jnp.dot(p_ref[...], right, preferred_element_type=F32)
        out_ref[:, lanes] = sums[:, :LANES].astype(BF16)
        totals = jnp.where(out_lane % HDIM == p, sums[:, LANES:], totals)
    out_ref[:, D:] = totals.astype(BF16)


def weigh(root, place, chips, gain, rate, ranks, expo, values):
    rows, cols = ranks.shape
    return pl.pallas_call(
        functools.partial(weigh_kernel, root),
        out_shape=jax.ShapeDtypeStruct((rows // 2, D + LANES), BF16),
        in_specs=[SMEM, SMEM, SMEM, VMEM, VMEM, VMEM],
        out_specs=VMEM,
        scratch_shapes=[pltpu.VMEM((rows // 2, 2 * cols), BF16)],
        compiler_params=params(),
        cost_estimate=cost(
            4 * rows * cols * D, HEADS * rows * cols, HEADS * rows * cols
        ),
        name="weigh",
    )(place, gain, rate, ranks, expo, values)


def project_kernel(*refs):
    parts, w_ref, out_ref = refs[:-2], refs[-2], refs[-1]
    total = parts[0][...].astype(F32)
    for part in parts[1:]:
        total += part[...].astype(F32)
    seg = total.shape[0]
    inverse = 1.0 / total[:, D:]
    lane = lax.broadcasted_iota(jnp.int32, (seg, LANES), 1)
    attended = []
    for p in range(PAIRS):
        scale = jnp.where(
            lane < HDIM,
            jnp.broadcast_to(inverse[:, p : p + 1], (seg, LANES)),
            jnp.broadcast_to(inverse[:, HDIM + p : HDIM + p + 1], (seg, LANES)),
        )
        attended.append((total[:, p * LANES : (p + 1) * LANES] * scale).astype(BF16))
    attended = jnp.concatenate(attended, axis=1)
    for c in range(w_ref.shape[0]):
        out_ref[c] = jnp.dot(attended, w_ref[c], preferred_element_type=F32).astype(BF16)


def project(parts, w_all):
    seg = parts[0].shape[0]
    return pl.pallas_call(
        project_kernel,
        out_shape=jax.ShapeDtypeStruct((w_all.shape[0], seg, w_all.shape[2]), BF16),
        in_specs=[VMEM] * (len(parts) + 1),
        out_specs=VMEM,
        compiler_params=params(),
        cost_estimate=cost(2 * seg * w_all.size, 2 * w_all.size),
        name="project",
    )(*parts, w_all)


def gather_rows(block, count):
    return [block] + [lax.ppermute(block, "row", xor_pairs(count, j)) for j in range(1, count)]


def fetch_key_rows(features, cols, row_count, col_count):
    ratio = features.shape[0] // cols
    col_pos, row_pos = lax.axis_index("col"), lax.axis_index("row")
    half = lax.dynamic_slice_in_dim(features, col_pos % ratio * cols, cols, 0)
    away = lax.bitwise_xor(row_pos, col_pos // ratio)

    def pairs(sends):
        found = []
        for c in range(col_count):
            source = c // ratio
            for a, b in sends:
                found.append(((source ^ a) * col_count + c, (source ^ b) * col_count + c))
        return found

    axes = ("row", "col")
    if row_count != 4:
        got = half
        for j in range(1, row_count):
            got = jnp.where(away == j, lax.ppermute(half, axes, pairs([(0, j)])), got)
        return got
    near = lax.ppermute(half, axes, pairs([(0, 1)]))
    side = lax.ppermute(half, axes, pairs([(0, 2)]))
    mid = cols // 2
    first = lax.ppermute(near[:mid], axes, pairs([(1, 3)]))
    second = lax.ppermute(side[mid:], axes, pairs([(2, 3)]))
    return jnp.where(
        away == 0,
        half,
        jnp.where(
            away == 1,
            near,
            jnp.where(away == 2, side, jnp.concatenate([first, second], axis=0)),
        ),
    )


def expand_blocks(pattern):
    block_rows, block_cols = pattern.shape
    grid = jnp.broadcast_to(pattern[:, None, :, None] > 0, (block_rows, BLK, block_cols, BLK))
    return grid.reshape(block_rows * BLK, block_cols * BLK)


def shards(node_features, edge_weight, pattern, w_qkv, w_out, bias_gain, bias_rate):
    rows, cols = edge_weight.shape
    row_count, col_count = lax.axis_size("row"), lax.axis_size("col")
    row_pos, col_pos = lax.axis_index("row"), lax.axis_index("col")
    chips = col_count // 2
    chip, core = col_pos // 2, col_pos % 2
    root = math.sqrt(rows * row_count)
    place = jnp.stack([row_pos, col_pos]).astype(jnp.int32)

    adjacency = jnp.where(expand_blocks(pattern), edge_weight, jnp.zeros_like(edge_weight))
    panel = lax.all_gather(adjacency, "col", axis=0, tiled=False)
    w_all = lax.all_gather(w_out, "col", axis=0, tiled=False)
    columns = gather_rows(adjacency, row_count)
    key_rows = fetch_key_rows(node_features, cols, row_count, col_count)

    queries = jnp.dot(node_features, w_qkv[:, :D], preferred_element_type=F32).astype(BF16)
    queries = queries * jnp.asarray(1.0 / math.sqrt(HDIM), BF16)
    keys = jnp.dot(key_rows, w_qkv[:, D : 2 * D], preferred_element_type=F32).astype(BF16)
    values = jnp.dot(key_rows, w_qkv[:, 2 * D :], preferred_element_type=F32).astype(BF16)

    peak = local_peak(pattern, queries, keys).astype(BF16)
    step = 1
    while step < col_count:
        peak = jnp.maximum(peak, lax.ppermute(peak, "col", xor_pairs(col_count, step)))
        step *= 2
    expo = exponentials(pattern, queries, keys, peak)

    ranks = sweep(True, place, pattern, adjacency, panel, columns, BF16)
    columns = gather_rows(ranks, row_count)
    ranks = sweep(False, place, pattern, adjacency, panel, columns, BF16)

    def part(side):
        where = jnp.concatenate(
            [jnp.stack([chip, side]).astype(jnp.int32), jnp.zeros((chips,), jnp.int32)]
        )
        return weigh(root, where, chips, bias_gain, bias_rate, ranks, expo, values)

    other = lax.ppermute(part(1 - core), "col", xor_pairs(col_count, 1))
    mine = part(core)
    seg = rows // col_count
    parts = []
    for k in range(chips):
        at = slice(k * seg, (k + 1) * seg)
        both = (mine[at].astype(F32) + other[at].astype(F32)).astype(BF16)
        parts.append(both if k == 0 else lax.ppermute(both, "col", xor_pairs(col_count, 2 * k)))
    mixed = project(parts, w_all)
    mixed = lax.all_to_all(mixed, "col", split_axis=0, concat_axis=0, tiled=True)
    return mixed.reshape(rows, w_out.shape[1])


def solution(mesh):
    in_specs = (P("row", None), P("row", "col"), P("row", "col"), P(), P(None, "col"), P(), P())
    out_specs = P("row", "col")
    return jax.shard_map(shards, mesh=mesh, in_specs=in_specs, out_specs=out_specs, check_vma=False)
```

time: 324 us -> 183 us (0.56)
  waiting for transfers between devices: 186 us -> 47.2 us
  Pallas kernels: 0 us -> 52 us
  blocking collectives: 54.8 us -> 16 us
  matrix products: 45.7 us -> 12.1 us
  starting transfers between devices: 0.35 us -> 28.1 us
  other arithmetic: 16.6 us -> 9.14 us
    all_gather x3 -> x2, waiting for transfers between devices: 125 us -> 0.38 us  [the longest x1 0.38 us: shards(): panel = lax.all_gather(adjacency, 'col', axis=0, tiled=False)]
    psum x2 -> x0, waiting for transfers between devices: 61.6 us -> none  [the longest x1 38.1 us: spread(): return lax.psum(kept, axis)]
    pallas_call x0 -> x7, Pallas kernels: none -> 52 us  [the longest x2 17.5 us: weigh(): pl.pallas_call(functools.partial(weigh_kernel, root), out_shape=jax.Shape...]
    ppermute x0 -> x17, waiting for transfers between devices: none -> 46.8 us  [the longest x1 24.9 us: fetch_key_rows(): side = lax.ppermute(half, axes, pairs([(0, 2)]))]
    dot_general x7 -> x3, matrix products: 45.7 us -> 12.1 us  [the longest x1 5.1 us: shards(): jnp.dot(node_features, w_qkv[:, :D], preferred_element_type=F32)]
    pmax x1 -> x0, blocking collectives: 28.5 us -> none  [shards(): lax.pmax(local_peak.astype(jnp.bfloat16), 'col').astype(local_peak.dtype)]
    ppermute x0 -> x17, starting transfers between devices: none -> 28 us  [the longest x6 12.7 us: gather_rows(): lax.ppermute(block, 'row', xor_pairs(count, j))]
    psum x1 -> x0, blocking collectives: 26.3 us -> none  [shards(): lax.psum(totals.astype(jnp.bfloat16), 'col').astype(jnp.float32)]
  transfers between devices with their start and end apart: 5 -> 19, of which waited for: 5 -> 7; matrix products, arithmetic and copies ran while one was open for 9% -> 11% of each run, Pallas kernels for 0% -> 27%
where the time goes in v1:
time: 183 us; the launch traced here: 182 us
  Pallas kernels  52 us (28%)
  waiting for transfers between devices  47.2 us (26%)
  starting transfers between devices  28.1 us (15%)
  blocking collectives  16 us (9%)
  between operations  13.6 us (7%)
  matrix products  12.1 us (7%)
  other arithmetic  9.14 us (5%)
  local copies, waits for them, and re-layouts  4.19 us (2%)
    ppermute x1, waiting for transfers between devices, fetch_key_rows(): side = lax.ppermute(half, axes, pairs([(0, 2)]))  24.9 us
    pallas_call x2, Pallas kernels, weigh(): pl.pallas_call(functools.partial(weigh_kernel, root), out_shape=jax.Shape...  17.5 us
    all_to_all x1, blocking collectives, shards(): lax.all_to_all(mixed, 'col', split_axis=0, concat_axis=0, tiled=True)  16 us
    ppermute x3, waiting for transfers between devices, shards(): lax.ppermute(both, 'col', xor_pairs(col_count, 2 * k))  15.1 us
    pallas_call x2, Pallas kernels, sweep(): pl.pallas_call(functools.partial(sweep_kernel, first, rows // cols), out_...  14.4 us
    ppermute x6, starting transfers between devices, gather_rows(): lax.ppermute(block, 'row', xor_pairs(count, j))  12.7 us
    pallas_call x1, Pallas kernels, exponentials(): pl.pallas_call(expo_kernel, out_shape=jax.ShapeDtypeStruct((PAIRS, rows,...  11.6 us
    ppermute x6, waiting for transfers between devices, gather_rows(): lax.ppermute(block, 'row', xor_pairs(count, j))  6.3 us
  transfers between devices with their start and end apart: 19, of which 7 were waited for; matrix products, arithmetic and copies ran while one was open for 11% of the time, Pallas kernels for 27%

profile of v1, /device:TPU:0, one launch (start us, length us, event | category | flops | bytes accessed | tf_op | source)
XLA Modules:
  0.0 182.3 jit_solution(4806024077890217745)
XLA Ops:
  8.2 2.0 %broadcast_select_fusion.own_ref.rest_0_ = bf16[768,384]{1,0:T(8,128)(2,1)} fusion(pred[768,384]{1,0:T(8,128)(4,1)S(1)} %copy.13, bf16[768,384]{1,0:T(8,128)(2,1)} %param.8), kind=kLoop, calls=%fused_computation.18 | loop fusion | flops 294912 | bytes 1474560 | tf_op jit(solution)/shard_map/jit(_where)/select_n | solution.py:343
  10.3 4.9 %collective-permute-start.7 = (bf16[384,1024]{1,0:T(8,128)(2,1)S(1)}, bf16[384,1024]{1,0:T(8,128)(2,1)S(1)}, u32[]{:S(2)}, u32[]{:S(2)}) collective-permute-start(bf16[384,1024]{1,0:T(8,128)(2,1)S(1)} %constant_dynamic-slice_fusion), channel_id=1, source_target_pairs={{0,16},{1,17},{10,26},{11,27},{20,4},{21,5},{30,14},{31,15}} | collective-permute-start | bytes 2359304 | tf_op jit(solution)/shard_map/ppermute | solution.py:313
  16.7 3.4 %collective-permute-start.2 = (bf16[768,384]{1,0:T(8,128)(2,1)S(1)}, bf16[768,384]{1,0:T(8,128)(2,1)}, u32[]{:S(2)}, u32[]{:S(2)}) collective-permute-start(bf16[768,384]{1,0:T(8,128)(2,1)S(1)} %copy-done), channel_id=1, source_target_pairs={{0,24},{8,16},{16,8},{24,0},{1,25},{9,17},{17,9},{25,1},{2,26},{10... | collective-permute-start | bytes 1769480 | tf_op jit(solution)/shard_map/ppermute | solution.py:289
  20.8 24.9 %collective-permute-done.7 = bf16[384,1024]{1,0:T(8,128)(2,1)S(1)} collective-permute-done((bf16[384,1024]{1,0:T(8,128)(2,1)S(1)}, bf16[384,1024]{1,0:T(8,128)(2,1)S(1)}, u32[]{:S(2)}, u32[]{:S(2)}) %collective-permute-start.7) | collective-permute-done | bytes 786464 | tf_op jit(solution)/shard_map/ppermute | solution.py:313
  47.3 5.1 %fusion.9.q_ref = bf16[768,1024]{1,0:T(8,128)(2,1)} fusion(bf16[768,1024]{1,0:T(8,128)(2,1)} %param.7, bf16[1024,3072]{1,0:T(8,128)(2,1)} %param.10), kind=kOutput, calls=%fused_computation.7 | convolution fusion | flops 1612185600 | bytes 5242880 | tf_op jit(solution)/shard_map/dot_general | solution.py:349
  53.1 3.5 %fusion.12.k_ref = bf16[384,1024]{1,0:T(8,128)(2,1)} fusion(bf16[384,1024]{1,0:T(8,128)(2,1)S(1)} %fusion.19, bf16[1024,3072]{1,0:T(8,128)(2,1)} %param.10), kind=kOutput, calls=%fused_computation.8 | convolution fusion | flops 805699584 | bytes 3670016 | tf_op jit(solution)/shard_map/dot_general | solution.py:351
  56.6 4.9 %local_peak.1 = f32[16,768]{1,0:T(8,128)} custom-call(s32[6,3]{1,0:T(8,128)} %copy.15.pattern_ref, bf16[768,1024]{1,0:T(8,128)(2,1)} %fusion.9.q_ref, bf16[384,1024]{1,0:T(8,128)(2,1)} %fusion.12.k_ref), custom_call_target="tpu_custom_call" | custom-call | flops 1207959552 | bytes 2359296 | tf_op jit(solution)/shard_map/local_peak/pallas_call | solution.py:137
  65.1 7.2 %rank_sweep.2.rest_0_ = bf16[768,384]{1,0:T(8,128)(2,1)} custom-call(s32[2]{0:T(128)} %pad_add_fusion.2.place_ref, s32[6,3]{1,0:T(8,128)} %copy.15.pattern_ref, bf16[768,384]{1,0:T(8,128)(2,1)} %broadcast_select_fusion.own_ref.rest_0_, bf16[8,768,384]{2,1,0:T(8,128)(2,1)} %bitcast.18, bf16[768,384]{1,0:T(8,128)(2,1)} %broadcast_select_fusion.own_ref.rest_0_, ...), custom_call_target="tpu_custom_call" | custom-call | flops 1811939328 | bytes 9437184 | tf_op jit(solution)/shard_map/rank_sweep/pallas_call | solution.py:85
  72.3 3.0 %collective-permute-start.3 = (bf16[768,384]{1,0:T(8,128)(2,1)}, bf16[768,384]{1,0:T(8,128)(2,1)S(1)}, u32[]{:S(2)}, u32[]{:S(2)}) collective-permute-start(bf16[768,384]{1,0:T(8,128)(2,1)} %rank_sweep.2.rest_0_), channel_id=1, source_target_pairs={{0,8},{8,0},{16,24},{24,16},{1,9},{9,1},{17,25},{25,17},{2,10},{10... | collective-permute-start | bytes 1769480 | tf_op jit(solution)/shard_map/ppermute | solution.py:289
  75.3 4.7 %collective-permute-start.4 = (bf16[768,384]{1,0:T(8,128)(2,1)}, bf16[768,384]{1,0:T(8,128)(2,1)S(1)}, u32[]{:S(2)}, u32[]{:S(2)}) collective-permute-start(bf16[768,384]{1,0:T(8,128)(2,1)} %rank_sweep.2.rest_0_), channel_id=1, source_target_pairs={{0,16},{8,24},{16,0},{24,8},{1,17},{9,25},{17,1},{25,9},{2,18},{10... | collective-permute-start | bytes 1769480 | tf_op jit(solution)/shard_map/ppermute | solution.py:289
  82.1 3.2 %collective-permute-start.12 = (bf16[16,768]{1,0:T(8,128)(2,1)S(1)}, bf16[16,768]{1,0:T(8,128)(2,1)S(1)}, u32[]{:S(2)}, u32[]{:S(2)}) collective-permute-start(bf16[16,768]{1,0:T(8,128)(2,1)S(1)} %max.10), channel_id=1, source_target_pairs={{0,4},{1,5},{2,6},{3,7},{4,0},{5,1},{6,2},{7,3},{8,12},{9,13},{10,... | collective-permute-start | bytes 73736 | tf_op jit(solution)/shard_map/ppermute | solution.py:357
  85.3 3.6 %fusion.15.v_ref = bf16[384,1024]{1,0:T(8,128)(2,1)} fusion(bf16[384,1024]{1,0:T(8,128)(2,1)S(1)} %fusion.19, bf16[1024,3072]{1,0:T(8,128)(2,1)} %param.10), kind=kOutput, calls=%fused_computation.9 | convolution fusion | flops 805699584 | bytes 3670016 | tf_op jit(solution)/shard_map/dot_general | solution.py:352
  89.5 11.6 %expo.1.expo_ref = bf16[8,768,768]{2,1,0:T(8,128)(2,1)} custom-call(s32[6,3]{1,0:T(8,128)} %copy.15.pattern_ref, bf16[768,1024]{1,0:T(8,128)(2,1)} %fusion.9.q_ref, bf16[384,1024]{1,0:T(8,128)(2,1)} %fusion.12.k_ref, bf16[16,768]{1,0:T(8,128)(2,1)} %max.11.peak_ref), custom_call_target="tpu_custom_call" | custom-call | flops 2415919104 | bytes 9437184 | tf_op jit(solution)/shard_map/expo/pallas_call | solution.py:186
  101.1 4.5 %collective-permute-done.4.rest_2_ = bf16[768,384]{1,0:T(8,128)(2,1)S(1)} collective-permute-done((bf16[768,384]{1,0:T(8,128)(2,1)}, bf16[768,384]{1,0:T(8,128)(2,1)S(1)}, u32[]{:S(2)}, u32[]{:S(2)}) %collective-permute-start.4) | collective-permute-done | bytes 589856 | tf_op jit(solution)/shard_map/ppermute | solution.py:289
  105.6 1.8 collective-permute-done.5.rest_3_
  108.2 7.2 %rank_sweep.3.ranks_ref = bf16[768,384]{1,0:T(8,128)(2,1)} custom-call(s32[2]{0:T(128)} %pad_add_fusion.2.place_ref, s32[6,3]{1,0:T(8,128)} %copy.15.pattern_ref, bf16[768,384]{1,0:T(8,128)(2,1)} %broadcast_select_fusion.own_ref.rest_0_, bf16[8,768,384]{2,1,0:T(8,128)(2,1)} %bitcast.19, bf16[768,384]{1,0:T(8,128)(2,1)} %rank_sweep.2.rest_0_, ...), custom_call_target="tpu_custom_call" | custom-call | flops 1811939328 | bytes 9437184 | tf_op jit(solution)/shard_map/rank_sweep/pallas_call | solution.py:85
  115.4 8.8 %weigh.3 = bf16[384,1152]{1,0:T(8,128)(2,1)} custom-call(s32[6]{0:T(128)} %get-tuple-element.10.place_ref, f32[16]{0:T(128)} %gain_ref.3, f32[16]{0:T(128)} %rate_ref.3, bf16[768,384]{1,0:T(8,128)(2,1)} %rank_sweep.3.ranks_ref, bf16[8,768,768]{2,1,0:T(8,128)(2,1)} %expo.1.expo_ref, bf16[384,1024]{1,0:T(8,128)(2,1)} %fusion.15.v_ref), custom_call_target="tpu_custom_call" | custom-call | flops 1207959552 | bytes 4718592 | tf_op jit(solution)/shard_map/weigh/pallas_call | solution.py:240
  124.2 8.7 %weigh.2 = bf16[384,1152]{1,0:T(8,128)(2,1)} custom-call(s32[6]{0:T(128)} %get-tuple-element.9.place_ref, f32[16]{0:T(128)} %gain_ref.3, f32[16]{0:T(128)} %rate_ref.3, bf16[768,384]{1,0:T(8,128)(2,1)} %rank_sweep.3.ranks_ref, bf16[8,768,768]{2,1,0:T(8,128)(2,1)} %expo.1.expo_ref, bf16[384,1024]{1,0:T(8,128)(2,1)} %fusion.15.v_ref), custom_call_target="tpu_custom_call" | custom-call | flops 1207959552 | bytes 4718592 | tf_op jit(solution)/shard_map/weigh/pallas_call | solution.py:240
  132.9 2.2 %add_convert_fusion = (bf16[96,1152]{1,0:T(8,128)(2,1)S(1)}, bf16[96,1152]{1,0:T(8,128)(2,1)S(1)}, bf16[96,1152]{1,0:T(8,128)(2,1)S(1)}, bf16[96,1152]{1,0:T(8,128)(2,1)}) fusion(bf16[384,1152]{1,0:T(8,128)(2,1)S(1)} %collective-permute-done.13, bf16[384,1152]{1,0:T(8,128)(2,1)} %weigh.2), kind=kLoop, calls=%fused_computation.14 | loop fusion | flops 1769472 | bytes 2654208 | tf_op jit(solution)/shard_map/convert_element_type | solution.py:377
  135.1 2.5 %collective-permute-start.15 = (bf16[96,1152]{1,0:T(8,128)(2,1)S(1)}, bf16[96,1152]{1,0:T(8,128)(2,1)S(1)}, u32[]{:S(2)}, u32[]{:S(2)}) collective-permute-start(bf16[96,1152]{1,0:T(8,128)(2,1)S(1)} %get-tuple-element.6), channel_id=1, source_target_pairs={{0,4},{1,5},{2,6},{3,7},{4,0},{5,1},{6,2},{7,3},{8,12},{9,13},{10,... | collective-permute-start | bytes 663560 | tf_op jit(solution)/shard_map/ppermute | solution.py:378
  139.5 8.2 %collective-permute-done.14.refs_1_ = bf16[96,1152]{1,0:T(8,128)(2,1)S(1)} collective-permute-done((bf16[96,1152]{1,0:T(8,128)(2,1)S(1)}, bf16[96,1152]{1,0:T(8,128)(2,1)S(1)}, u32[]{:S(2)}, u32[]{:S(2)}) %collective-permute-start.14) | collective-permute-done | bytes 221216 | tf_op jit(solution)/shard_map/ppermute | solution.py:378
  147.7 6.8 %collective-permute-done.16.refs_3_ = bf16[96,1152]{1,0:T(8,128)(2,1)S(1)} collective-permute-done((bf16[96,1152]{1,0:T(8,128)(2,1)S(1)}, bf16[96,1152]{1,0:T(8,128)(2,1)S(1)}, u32[]{:S(2)}, u32[]{:S(2)}) %collective-permute-start.16) | collective-permute-done | bytes 221216 | tf_op jit(solution)/shard_map/ppermute | solution.py:378
  155.2 3.6 %project.1 = bf16[8,96,128]{2,1,0:T(8,128)(2,1)} custom-call(bf16[96,1152]{1,0:T(8,128)(2,1)} %get-tuple-element.8.refs_0_, bf16[96,1152]{1,0:T(8,128)(2,1)} %copy-done.7, bf16[96,1152]{1,0:T(8,128)(2,1)} %copy-done.8, bf16[96,1152]{1,0:T(8,128)(2,1)} %copy-done.9, bf16[8,1024,128]{2,1,0:T(8,128)(2,1)} %bitcast.20), custom_call_target="tpu_custom_call" | custom-call | flops 201326592 | bytes 2097152 | tf_op jit(solution)/shard_map/project/pallas_call | solution.py:277
  158.8 16.0 %all_to_all.5 = bf16[8,96,128]{2,1,0:T(8,128)(2,1)S(1)} all-to-all(bf16[8,96,128]{2,1,0:T(8,128)(2,1)} %project.1), channel_id=1, replica_groups=mesh['row'=4,'col'=8] {'col'}, dimensions={0} | all-to-all | bytes 393216 | tf_op jit(solution)/shard_map/all_to_all | solution.py:380
  (68 shorter events, 16.5 us)
Async XLA Ops:
  6.5 58.2 %all-gather.5.cloned.1.call-start = ((), (), s32[]{:S(2)}) async-start(), calls=%async_computation.1 | async-start | bytes 5308416 | tf_op jit(solution)/shard_map/all_gather | solution.py:344
  8.1 12.0 %copy-start.10 = (s32[6,3]{0,1:T(4,128)S(1)}, s32[6,3]{0,1:T(4,128)}, u32[]{:S(2)}) copy-start(s32[6,3]{0,1:T(4,128)} %param.9) | copy-start | bytes 220
  10.1 6.4 %copy-start = (bf16[768,384]{1,0:T(8,128)(2,1)S(1)}, bf16[768,384]{1,0:T(8,128)(2,1)}, u32[]{:S(2)}) copy-start(bf16[768,384]{1,0:T(8,128)(2,1)} %broadcast_select_fusion.own_ref.rest_0_) | copy-start | bytes 1769476
  10.1 129.3 %all-gather.7.cloned.1.call-start = ((), (), s32[]{:S(2)}) async-start(), calls=%async_computation.2 | async-start | bytes 2359296 | tf_op jit(solution)/shard_map/all_gather | solution.py:345
  10.3 35.4 %collective-permute-start.7 = (bf16[384,1024]{1,0:T(8,128)(2,1)S(1)}, bf16[384,1024]{1,0:T(8,128)(2,1)S(1)}, u32[]{:S(2)}, u32[]{:S(2)}) collective-permute-start(bf16[384,1024]{1,0:T(8,128)(2,1)S(1)} %constant_dynamic-slice_fusion), channel_id=1, source_target_pairs={{0,16},{1,17},{10,26},{11,27},{20,4},{21,5},{30,14},{31,15}} | collective-permute-start | bytes 2359304 | tf_op jit(solution)/shard_map/ppermute | solution.py:313
  15.2 31.2 %collective-permute-start.6 = (bf16[384,1024]{1,0:T(8,128)(2,1)S(1)}, bf16[384,1024]{1,0:T(8,128)(2,1)S(1)}, u32[]{:S(2)}, u32[]{:S(2)}) collective-permute-start(bf16[384,1024]{1,0:T(8,128)(2,1)S(1)} %constant_dynamic-slice_fusion), channel_id=1, source_target_pairs={{0,8},{1,9},{10,2},{11,3},{20,28},{21,29},{30,22},{31,23}} | collective-permute-start | bytes 2359304 | tf_op jit(solution)/shard_map/ppermute | solution.py:312
  16.6 47.7 %collective-permute-start = (bf16[768,384]{1,0:T(8,128)(2,1)S(1)}, bf16[768,384]{1,0:T(8,128)(2,1)S(1)}, u32[]{:S(2)}, u32[]{:S(2)}) collective-permute-start(bf16[768,384]{1,0:T(8,128)(2,1)S(1)} %copy-done), channel_id=1, source_target_pairs={{0,8},{8,0},{16,24},{24,16},{1,9},{9,1},{17,25},{25,17},{2,10},{10... | collective-permute-start | bytes 1769480 | tf_op jit(solution)/shard_map/ppermute | solution.py:289
  16.6 47.7 %collective-permute-start.1 = (bf16[768,384]{1,0:T(8,128)(2,1)S(1)}, bf16[768,384]{1,0:T(8,128)(2,1)}, u32[]{:S(2)}, u32[]{:S(2)}) collective-permute-start(bf16[768,384]{1,0:T(8,128)(2,1)S(1)} %copy-done), channel_id=1, source_target_pairs={{0,16},{8,24},{16,0},{24,8},{1,17},{9,25},{17,1},{25,9},{2,18},{10... | collective-permute-start | bytes 1769480 | tf_op jit(solution)/shard_map/ppermute | solution.py:289
  16.7 47.6 %collective-permute-start.2 = (bf16[768,384]{1,0:T(8,128)(2,1)S(1)}, bf16[768,384]{1,0:T(8,128)(2,1)}, u32[]{:S(2)}, u32[]{:S(2)}) collective-permute-start(bf16[768,384]{1,0:T(8,128)(2,1)S(1)} %copy-done), channel_id=1, source_target_pairs={{0,24},{8,16},{16,8},{24,0},{1,25},{9,17},{17,9},{25,1},{2,26},{10... | collective-permute-start | bytes 1769480 | tf_op jit(solution)/shard_map/ppermute | solution.py:289
  45.8 6.7 %collective-permute-start.9 = (bf16[192,1024]{1,0:T(8,128)(2,1)S(1)}, bf16[192,1024]{1,0:T(8,128)(2,1)S(1)}, u32[]{:S(2)}, u32[]{:S(2)}) collective-permute-start(bf16[192,1024]{1,0:T(8,128)(2,1)S(1)} %slice.53), channel_id=1, source_target_pairs={{16,24},{17,25},{26,18},{27,19},{4,12},{5,13},{14,6},{15,7}} | collective-permute-start | bytes 1179656 | tf_op jit(solution)/shard_map/ppermute | solution.py:316
  46.5 5.9 %collective-permute-start.8 = (bf16[192,1024]{1,0:T(8,128)(2,1)S(1)}, bf16[192,1024]{1,0:T(8,128)(2,1)S(1)}, u32[]{:S(2)}, u32[]{:S(2)}) collective-permute-start(bf16[192,1024]{1,0:T(8,128)(2,1)S(1)} %slice.52), channel_id=1, source_target_pairs={{8,24},{9,25},{2,18},{3,19},{28,12},{29,13},{22,6},{23,7}} | collective-permute-start | bytes 1179656 | tf_op jit(solution)/shard_map/ppermute | solution.py:315
  62.3 1.2 collective-permute-start.10
  64.3 17.8 %collective-permute-start.11 = (bf16[16,768]{1,0:T(8,128)(2,1)S(1)}, bf16[16,768]{1,0:T(8,128)(2,1)S(1)}, u32[]{:S(2)}, u32[]{:S(2)}) collective-permute-start(bf16[16,768]{1,0:T(8,128)(2,1)S(1)} %convert_maximum_fusion), channel_id=1, source_target_pairs={{0,2},{1,3},{2,0},{3,1},{4,6},{5,7},{6,4},{7,5},{8,10},{9,11},{10,... | collective-permute-start | bytes 73736 | tf_op jit(solution)/shard_map/ppermute | solution.py:357
  72.3 28.8 %collective-permute-start.3 = (bf16[768,384]{1,0:T(8,128)(2,1)}, bf16[768,384]{1,0:T(8,128)(2,1)S(1)}, u32[]{:S(2)}, u32[]{:S(2)}) collective-permute-start(bf16[768,384]{1,0:T(8,128)(2,1)} %rank_sweep.2.rest_0_), channel_id=1, source_target_pairs={{0,8},{8,0},{16,24},{24,16},{1,9},{9,1},{17,25},{25,17},{2,10},{10... | collective-permute-start | bytes 1769480 | tf_op jit(solution)/shard_map/ppermute | solution.py:289
  75.3 30.3 %collective-permute-start.4 = (bf16[768,384]{1,0:T(8,128)(2,1)}, bf16[768,384]{1,0:T(8,128)(2,1)S(1)}, u32[]{:S(2)}, u32[]{:S(2)}) collective-permute-start(bf16[768,384]{1,0:T(8,128)(2,1)} %rank_sweep.2.rest_0_), channel_id=1, source_target_pairs={{0,16},{8,24},{16,0},{24,8},{1,17},{9,25},{17,1},{25,9},{2,18},{10... | collective-permute-start | bytes 1769480 | tf_op jit(solution)/shard_map/ppermute | solution.py:289
  80.0 27.4 %collective-permute-start.5 = (bf16[768,384]{1,0:T(8,128)(2,1)}, bf16[768,384]{1,0:T(8,128)(2,1)S(1)}, u32[]{:S(2)}, u32[]{:S(2)}) collective-permute-start(bf16[768,384]{1,0:T(8,128)(2,1)} %rank_sweep.2.rest_0_), channel_id=1, source_target_pairs={{0,24},{8,16},{16,8},{24,0},{1,25},{9,17},{17,9},{25,1},{2,26},{10... | collective-permute-start | bytes 1769480 | tf_op jit(solution)/shard_map/ppermute | solution.py:289
  82.1 6.7 %collective-permute-start.12 = (bf16[16,768]{1,0:T(8,128)(2,1)S(1)}, bf16[16,768]{1,0:T(8,128)(2,1)S(1)}, u32[]{:S(2)}, u32[]{:S(2)}) collective-permute-start(bf16[16,768]{1,0:T(8,128)(2,1)S(1)} %max.10), channel_id=1, source_target_pairs={{0,4},{1,5},{2,6},{3,7},{4,0},{5,1},{6,2},{7,3},{8,12},{9,13},{10,... | collective-permute-start | bytes 73736 | tf_op jit(solution)/shard_map/ppermute | solution.py:357
  101.1 6.3 %copy-start.4 = (bf16[768,384]{1,0:T(8,128)(2,1)}, bf16[768,384]{1,0:T(8,128)(2,1)S(1)}, u32[]{:S(2)}) copy-start(bf16[768,384]{1,0:T(8,128)(2,1)S(1)} %collective-permute-done.3.rest_1_) | copy-start | bytes 1769476
  124.2 8.7 %collective-permute-start.13 = (bf16[384,1152]{1,0:T(8,128)(2,1)}, bf16[384,1152]{1,0:T(8,128)(2,1)S(1)}, u32[]{:S(2)}, u32[]{:S(2)}) collective-permute-start(bf16[384,1152]{1,0:T(8,128)(2,1)} %weigh.3), channel_id=1, source_target_pairs={{0,1},{1,0},{2,3},{3,2},{4,5},{5,4},{6,7},{7,6},{8,9},{9,8},{10,11... | collective-permute-start | bytes 2654216 | tf_op jit(solution)/shard_map/ppermute | solution.py:371
  135.1 12.6 %collective-permute-start.14 = (bf16[96,1152]{1,0:T(8,128)(2,1)S(1)}, bf16[96,1152]{1,0:T(8,128)(2,1)S(1)}, u32[]{:S(2)}, u32[]{:S(2)}) collective-permute-start(bf16[96,1152]{1,0:T(8,128)(2,1)S(1)} %get-tuple-element.7), channel_id=1, source_target_pairs={{0,2},{1,3},{2,0},{3,1},{4,6},{5,7},{6,4},{7,5},{8,10},{9,11},{10,... | collective-permute-start | bytes 663560 | tf_op jit(solution)/shard_map/ppermute | solution.py:378
  135.1 12.6 %collective-permute-start.15 = (bf16[96,1152]{1,0:T(8,128)(2,1)S(1)}, bf16[96,1152]{1,0:T(8,128)(2,1)S(1)}, u32[]{:S(2)}, u32[]{:S(2)}) collective-permute-start(bf16[96,1152]{1,0:T(8,128)(2,1)S(1)} %get-tuple-element.6), channel_id=1, source_target_pairs={{0,4},{1,5},{2,6},{3,7},{4,0},{5,1},{6,2},{7,3},{8,12},{9,13},{10,... | collective-permute-start | bytes 663560 | tf_op jit(solution)/shard_map/ppermute | solution.py:378
  137.6 16.9 %collective-permute-start.16 = (bf16[96,1152]{1,0:T(8,128)(2,1)S(1)}, bf16[96,1152]{1,0:T(8,128)(2,1)S(1)}, u32[]{:S(2)}, u32[]{:S(2)}) collective-permute-start(bf16[96,1152]{1,0:T(8,128)(2,1)S(1)} %get-tuple-element.5), channel_id=1, source_target_pairs={{0,6},{1,7},{2,4},{3,5},{4,2},{5,3},{6,0},{7,1},{8,14},{9,15},{10,... | collective-permute-start | bytes 663560 | tf_op jit(solution)/shard_map/ppermute | solution.py:378
  147.7 6.8 %copy-start.7 = (bf16[96,1152]{1,0:T(8,128)(2,1)}, bf16[96,1152]{1,0:T(8,128)(2,1)S(1)}, u32[]{:S(2)}) copy-start(bf16[96,1152]{1,0:T(8,128)(2,1)S(1)} %collective-permute-done.14.refs_1_) | copy-start | bytes 663556
  147.7 6.8 %copy-start.8 = (bf16[96,1152]{1,0:T(8,128)(2,1)}, bf16[96,1152]{1,0:T(8,128)(2,1)S(1)}, u32[]{:S(2)}) copy-start(bf16[96,1152]{1,0:T(8,128)(2,1)S(1)} %collective-permute-done.15.refs_2_) | copy-start | bytes 663556
  (6 other events, 13.8 us)
Sparse Core Ops, SparseCore 0:
  10.3 54.3 all-gather.4
  66.3 29.5 all-gather.6

commit v2 on v0

v2 whole, which is shorter than its diff:
```python
import functools
import math

import jax
import jax.numpy as jnp
from jax import lax
from jax.experimental import pallas as pl
from jax.experimental.pallas import tpu as pltpu
from jax.sharding import PartitionSpec as P

D = 1024
HEADS = 16
BLK = 128
HDIM = 64
CORES = 2
PAIRS = HEADS // 2 // CORES
WIDTH = D // CORES
STEP = 8
LANES = 128
VMEM_LIMIT = 58 * 2**20
SMALL_LIMIT = 16 * 2**20

VMEM = pl.BlockSpec(memory_space=pltpu.VMEM)
SMEM = pl.BlockSpec(memory_space=pltpu.SMEM)
HBM = pl.BlockSpec(memory_space=pltpu.HBM)
BF16 = jnp.bfloat16
F32 = jnp.float32


def params(limit=VMEM_LIMIT):
    return pltpu.CompilerParams(vmem_limit_bytes=limit)


def cost(flops, nbytes, trans=0):
    return pl.CostEstimate(flops=int(flops), bytes_accessed=int(nbytes), transcendentals=int(trans))


def xor_pairs(n, j):
    return [(i, i ^ j) for i in range(n)]


def keep_tile(pattern_ref, first_row, block_rows):
    block_cols = pattern_ref.shape[0]
    tiles = []
    for i in range(block_rows):
        parts = [
            jnp.full((1, BLK), jnp.where(pattern_ref[b, first_row + i] > 0, 1.0, 0.0), F32)
            for b in range(block_cols)
        ]
        tiles.append(
            jnp.broadcast_to(jnp.concatenate(parts, axis=1), (BLK, block_cols * BLK))
        )
    return jnp.concatenate(tiles, axis=0)


def mask_kernel(pattern_ref, weight_ref, out_ref):
    for i in range(out_ref.shape[0] // BLK):
        at = slice(i * BLK, (i + 1) * BLK)
        keep = keep_tile(pattern_ref, i, 1)
        out_ref[at, :] = jnp.where(keep > 0, weight_ref[at, :].astype(F32), 0.0).astype(BF16)


def mask(pattern, weight):
    rows, cols = weight.shape
    return pl.pallas_call(
        mask_kernel,
        out_shape=jax.ShapeDtypeStruct((rows, cols), BF16),
        in_specs=[SMEM, VMEM],
        out_specs=VMEM,
        compiler_params=params(SMALL_LIMIT),
        cost_estimate=cost(rows * cols, 4 * rows * cols),
        name="mask",
    )(pattern, weight)


def project_in_kernel(scale, place_ref, *refs):
    xs, (w_ref, out_ref) = refs[:-2], refs[-2:]
    rows = xs[0].shape[0]
    for i, x_ref in enumerate(xs):
        out = jnp.dot(x_ref[...], w_ref[...], preferred_element_type=F32).astype(BF16)
        if scale is not None:
            out = out * jnp.asarray(scale, BF16)
        out_ref[i * rows : (i + 1) * rows, :] = out


def project_in(core, xs, w, firsts, scale=None, tile=256):
    rows, depth = xs[0].shape
    steps = WIDTH // tile

    def column(i, core_ref):
        first = firsts[0] // tile
        for n, start in enumerate(firsts[1:], 1):
            first = jnp.where(i >= n * steps, start // tile, first)
        return 0, first + core_ref[0] * steps + lax.rem(i, steps)

    return pl.pallas_call(
        functools.partial(project_in_kernel, scale),
        out_shape=jax.ShapeDtypeStruct((rows * len(xs), WIDTH * len(firsts)), BF16),
        grid_spec=pltpu.PrefetchScalarGridSpec(
            num_scalar_prefetch=1,
            grid=(steps * len(firsts),),
            in_specs=[pl.BlockSpec((rows, depth), lambda i, c: (0, 0))] * len(xs)
            + [pl.BlockSpec((depth, tile), column)],
            out_specs=pl.BlockSpec((rows * len(xs), tile), lambda i, c: (0, i)),
        ),
        compiler_params=params(),
        cost_estimate=cost(
            2 * rows * len(xs) * depth * WIDTH * len(firsts),
            2 * depth * (rows * len(xs) + WIDTH * len(firsts)),
        ),
        name="project_in",
    )(core, *xs, w)


def sweep_kernel(first, ks, n_right, place_ref, pattern_ref, panel_ref, *refs):
    rights, (out_ref, left_ref, right_ref, acc_ref, sem) = refs[:n_right], refs[-5:]
    count, rows, cols = panel_ref.shape
    ratio = count // n_right
    seg = out_ref.shape[0] // len(ks)
    row_pos, col_pos = place_ref[0], place_ref[1]
    starts = [
        pl.multiple_of(lax.bitwise_xor(lax.div(col_pos, CORES), k) * seg, seg) for k in ks
    ]
    if len(ks) == count // CORES:
        starts = [n * seg for n in range(len(ks))]

    def left_copies(j):
        for i in range(ratio):
            c = lax.bitwise_xor(row_pos, j) * ratio + i
            for n, start in enumerate(starts):
                yield pltpu.make_async_copy(
                    panel_ref.at[c, pl.ds(start, seg), :],
                    left_ref.at[j, pl.ds(n * seg, seg), i * cols : (i + 1) * cols],
                    sem.at[j, i * len(ks) + n],
                )

    def right_copy(j):
        return pltpu.make_async_copy(rights[j], right_ref.at[j], sem.at[j, ratio * len(ks)])

    for j in range(n_right):
        right_copy(j).start()
        for copy in left_copies(j):
            copy.start()
    for j in range(n_right):
        right_copy(j).wait()
        for copy in left_copies(j):
            copy.wait()
        product = jnp.dot(left_ref[j], right_ref[j], preferred_element_type=F32)
        if j == 0:
            acc_ref[...] = product
        elif j < n_right - 1:
            acc_ref[...] += product
    product = product + acc_ref[...]
    home = lax.bitwise_xor(row_pos, lax.div(col_pos, ratio))
    at = pl.multiple_of(lax.rem(col_pos, ratio) * cols, cols)
    own = left_ref[home, :, pl.ds(at, cols)].astype(F32)
    total = 0.1275 * own + (0.85 * 0.1275 if first else 0.85) * product
    diagonal = lax.broadcasted_iota(jnp.int32, (seg, cols), 1) - lax.broadcasted_iota(
        jnp.int32, (seg, cols), 0
    )
    lane_block = lax.broadcasted_iota(jnp.int32, (1, cols), 1) // BLK
    for n, start in enumerate(starts):
        at = slice(n * seg, (n + 1) * seg)
        part = total[at, :]
        if not first:
            here = diagonal == row_pos * rows + start - col_pos * cols
            part = jnp.where(here, part + 0.15, part)
        size = math.gcd(seg, BLK)
        for i in range(seg // size):
            keep = jnp.zeros((1, cols), F32)
            for b in range(cols // BLK):
                kept = pattern_ref[b, lax.div(start + i * size, BLK)] > 0
                keep = jnp.where(lane_block == b, jnp.where(kept, 1.0, 0.0), keep)
            piece = part[i * size : (i + 1) * size, :]
            out_ref[n * seg + i * size : n * seg + (i + 1) * size, :] = jnp.where(
                keep > 0, piece, 0.0
            ).astype(BF16)


def sweep(first, ks, place, pattern, panel, blocks, follows, limit=VMEM_LIMIT):
    count, rows, cols = panel.shape
    ratio = count // len(blocks)
    n_rows = rows * CORES // count * len(ks)
    return pl.pallas_call(
        functools.partial(sweep_kernel, first, ks, len(blocks)),
        out_shape=jax.ShapeDtypeStruct((n_rows, cols), BF16),
        in_specs=[SMEM, SMEM] + [HBM] * (2 + len(blocks)),
        out_specs=VMEM,
        scratch_shapes=[
            pltpu.VMEM((len(blocks), n_rows, ratio * cols), BF16),
            pltpu.VMEM((len(blocks), rows, cols), BF16),
            pltpu.VMEM((n_rows, cols), F32),
            pltpu.SemaphoreType.DMA((len(blocks), ratio * len(ks) + 1)),
        ],
        compiler_params=params(limit),
        cost_estimate=cost(2 * n_rows * count * cols * cols, 2 * (n_rows + rows) * count * cols),
        name="rank_sweep",
    )(place, pattern, panel, *blocks, follows)


def split_heads(keys):
    lane = lax.broadcasted_iota(jnp.int32, keys.shape, 1)
    zero = jnp.zeros_like(keys)
    return jnp.concatenate(
        [jnp.where(lane < HDIM, keys, zero), jnp.where(lane >= HDIM, keys, zero)], axis=0
    )


def expo_kernel(own_ref, other_ref, q_ref, k_ref, out_ref, peak_ref, mask_ref):
    p = pl.program_id(0)
    rows, keys = q_ref.shape[0], k_ref.shape[0]
    block_rows, block_cols = rows // BLK, keys // BLK
    tile = BLK

    @pl.when(p == 0)
    def _():
        lane = lax.broadcasted_iota(jnp.int32, (BLK, LANES), 1)
        for i in range(block_rows):
            excluded = jnp.zeros((BLK, LANES), F32)
            for b in range(block_cols):
                ref, at = (own_ref, b) if b < block_cols // 2 else (other_ref, b - block_cols // 2)
                excluded = jnp.where(lane == b, jnp.where(ref[at, i] > 0, 0.0, -1e30), excluded)
            mask_ref[i * BLK : (i + 1) * BLK, :] = excluded.astype(BF16)
        peak_ref[...] = jnp.zeros_like(peak_ref)

    lane = lax.broadcasted_iota(jnp.int32, (2 * keys, LANES), 1)
    key = lax.broadcasted_iota(jnp.int32, (2 * keys, LANES), 0)
    block_of = jnp.where(key >= keys, key - keys, key) // BLK
    in_block = jnp.where(lane == block_of, 1.0, 0.0).astype(BF16)
    right = jnp.concatenate([split_heads(k_ref[...]), in_block], axis=1)
    peak_lane = lax.broadcasted_iota(jnp.int32, (tile, LANES), 1)
    for t in range(rows // tile):
        at = slice(t * tile, (t + 1) * tile)
        left = jnp.concatenate([q_ref[at, :], mask_ref[at, :]], axis=1)
        s = lax.dot_general(left, right, (((1,), (1,)), ((), ())), preferred_element_type=F32)
        peaks = peak_ref[at, :]
        for side in range(2):
            part = s[:, side * keys : (side + 1) * keys]
            peak = jnp.max(part, axis=1, keepdims=True)
            peaks = jnp.where(peak_lane == HDIM * side + p, peak, peaks)
            out_ref[0, at, side * keys : (side + 1) * keys] = jnp.exp(part - peak).astype(BF16)
        peak_ref[at, :] = peaks


def exponentials(own, other, queries, keys_values):
    rows, keys = queries.shape[0], keys_values.shape[0]
    work = rows * keys * 2 * PAIRS
    return pl.pallas_call(
        expo_kernel,
        out_shape=(
            jax.ShapeDtypeStruct((PAIRS, rows, 2 * keys), BF16),
            jax.ShapeDtypeStruct((rows, LANES), F32),
        ),
        grid=(PAIRS,),
        in_specs=[
            SMEM,
            SMEM,
            pl.BlockSpec((rows, LANES), lambda p: (0, p)),
            pl.BlockSpec((keys, LANES), lambda p: (0, p)),
        ],
        out_specs=(
            pl.BlockSpec((1, rows, 2 * keys), lambda p: (p, 0, 0)),
            pl.BlockSpec((rows, LANES), lambda p: (0, 0)),
        ),
        scratch_shapes=[pltpu.VMEM((rows, LANES), BF16)],
        compiler_params=params(),
        cost_estimate=cost(512 * work, 2 * work, work),
        name="expo",
    )(own, other, queries, keys_values)


def weigh_kernel(
    root, ks, seg, place_ref, gain_ref, rate_ref, own_ref, other_ref, expo_ref, v_ref, peak_ref,
    *refs,
):
    out_refs, (e_ref, p_ref, ranks_ref, right_ref, sem) = refs[: len(ks)], refs[len(ks) :]
    cols = own_ref.shape[1]
    keys = 2 * cols
    chip = lax.div(place_ref[1], CORES)
    first_head = lax.rem(place_ref[1], CORES) * 2 * PAIRS
    starts = [pl.multiple_of(lax.bitwise_xor(chip, k) * seg, seg) for k in ks]

    def copy(p, i):
        return pltpu.make_async_copy(
            expo_ref.at[p, pl.ds(starts[i], seg), :],
            e_ref.at[p, pl.ds(i * seg, seg), :],
            sem.at[p, i],
        )

    for p in range(PAIRS):
        for i in range(len(ks)):
            copy(p, i).start()
    for i in range(len(ks)):
        at = slice(i * seg, (i + 1) * seg)
        ranks_ref[at, :cols] = own_ref[at, :].astype(F32)
        ranks_ref[at, cols:] = other_ref[at, :].astype(F32)
    lane = lax.broadcasted_iota(jnp.int32, (keys, LANES), 1)
    zero = jnp.zeros((keys, LANES), BF16)
    right_ref[:keys, LANES:] = jnp.where(lane < HDIM, 1.0, 0.0).astype(BF16)
    right_ref[keys:, LANES:] = jnp.where(lane < HDIM, 0.0, 1.0).astype(BF16)
    out_lane = lax.broadcasted_iota(jnp.int32, (seg, LANES), 1)

    def pair(p, totals):
        lanes = pl.ds(pl.multiple_of(p * LANES, LANES), LANES)
        values = v_ref[:, lanes]
        right_ref[:keys, :LANES] = jnp.where(lane < HDIM, values, zero)
        right_ref[keys:, :LANES] = jnp.where(lane < HDIM, zero, values)
        for i in range(len(ks)):
            copy(p, i).wait()
        for i in range(len(ks)):
            rows_at = slice(i * seg, (i + 1) * seg)
            for half in range(2):
                ranks = ranks_ref[rows_at, half * cols : (half + 1) * cols]
                for side in range(2):
                    rate = rate_ref[first_head + 2 * p + side] * root
                    gain = gain_ref[first_head + 2 * p + side] * math.log2(math.e)
                    at = slice(side * keys + half * cols, side * keys + (half + 1) * cols)
                    weight = e_ref[p, rows_at, at].astype(F32) * jnp.exp2(
                        gain * jnp.tanh(rate * ranks)
                    )
                    p_ref[rows_at, at] = weight.astype(BF16)
        sums = jnp.dot(p_ref[...], right_ref[...], preferred_element_type=F32)
        now = []
        for i, out_ref in enumerate(out_refs):
            part = sums[i * seg : (i + 1) * seg, :]
            out_ref[:, lanes] = part[:, :LANES].astype(BF16)
            now.append(jnp.where(out_lane % HDIM == p, part[:, LANES:], totals[i]))
        return tuple(now)

    totals = lax.fori_loop(
        0, PAIRS, pair, tuple(jnp.zeros((seg, LANES), F32) for _ in ks)
    )
    for i, out_ref in enumerate(out_refs):
        extra = totals[i]
        rest = peak_ref[pl.ds(starts[i], seg), :]
        for n in range(1, 4):
            piece = rest.astype(BF16).astype(F32)
            rest = rest - piece
            here = (out_lane % HDIM >= n * STEP) & (out_lane % HDIM < n * STEP + PAIRS)
            extra = jnp.where(here, pltpu.roll(piece, n * STEP, 1), extra)
        out_ref[:, WIDTH:] = extra.astype(BF16)


def weigh(root, chips, ks, place, gain, rate, own, other, expo, values, peak):
    n_rows, cols = own.shape
    seg = n_rows // len(ks)
    rows, keys = seg * chips, 2 * cols
    work = n_rows * keys * 2 * PAIRS
    return pl.pallas_call(
        functools.partial(weigh_kernel, root, ks, seg),
        out_shape=(jax.ShapeDtypeStruct((seg, WIDTH + LANES), BF16),) * len(ks),
        grid=(1,),
        in_specs=[
            SMEM,
            SMEM,
            SMEM,
            pl.BlockSpec((n_rows, cols), lambda i: (0, 0)),
            pl.BlockSpec((n_rows, cols), lambda i: (0, 0)),
            HBM,
            pl.BlockSpec((keys, WIDTH), lambda i: (0, 1)),
            pl.BlockSpec((rows, LANES), lambda i: (0, 0)),
        ],
        out_specs=(pl.BlockSpec((seg, WIDTH + LANES), lambda i: (0, 0)),) * len(ks),
        scratch_shapes=[
            pltpu.VMEM((PAIRS, n_rows, 2 * keys), BF16),
            pltpu.VMEM((n_rows, 2 * keys), BF16),
            pltpu.VMEM((n_rows, keys), F32),
            pltpu.VMEM((2 * keys, 2 * LANES), BF16),
            pltpu.SemaphoreType.DMA((PAIRS, len(ks))),
        ],
        compiler_params=params(),
        cost_estimate=cost(512 * work, 2 * work, 2 * work),
        name="weigh",
    )(place, gain, rate, own, other, expo, values, peak)


def divide_kernel(*refs):
    parts, out_ref = refs[:-1], refs[-1]
    extras = [part[:, WIDTH:].astype(F32) for part in parts]
    seg = extras[0].shape[0]
    peaks = [sum(pltpu.roll(x, LANES - n * STEP, 1) for n in range(1, 4)) for x in extras]
    largest = functools.reduce(jnp.maximum, peaks)
    weights = [jnp.exp(peak - largest) for peak in peaks]
    inverse = 1.0 / sum(w * x for w, x in zip(weights, extras, strict=True))
    scales = [w * inverse for w in weights]
    lane = lax.broadcasted_iota(jnp.int32, (seg, LANES), 1)
    for p in range(PAIRS):
        lanes = slice(p * LANES, (p + 1) * LANES)
        total = jnp.zeros((seg, LANES), F32)
        for part, scale in zip(parts, scales, strict=True):
            both = jnp.where(lane < HDIM, scale[:, p : p + 1], scale[:, HDIM + p : HDIM + p + 1])
            total += part[:, lanes].astype(F32) * both
        out_ref[:, lanes] = total.astype(BF16)


def divide(parts):
    seg = parts[0].shape[0]
    return pl.pallas_call(
        divide_kernel,
        out_shape=jax.ShapeDtypeStruct((seg, WIDTH), BF16),
        in_specs=[VMEM] * len(parts),
        out_specs=VMEM,
        compiler_params=params(SMALL_LIMIT),
        cost_estimate=cost(8 * seg * D, 8 * seg * D),
        name="divide",
    )(*parts)


def project_out_kernel(place_ref, own_ref, other_ref, w_ref, *out_refs):
    chip, core = lax.div(place_ref[1], CORES), lax.rem(place_ref[1], CORES)
    for k, out_ref in enumerate(out_refs):
        slot = CORES * lax.bitwise_xor(chip, k) + core
        total = jnp.dot(
            own_ref[...],
            w_ref[slot, pl.ds(pl.multiple_of(core * WIDTH, WIDTH), WIDTH), :],
            preferred_element_type=F32,
        ) + jnp.dot(
            other_ref[...],
            w_ref[slot, pl.ds(pl.multiple_of((1 - core) * WIDTH, WIDTH), WIDTH), :],
            preferred_element_type=F32,
        )
        out_ref[...] = total.astype(BF16)


def project_out(place, own, other, w_all, chips):
    seg = own.shape[0]
    return pl.pallas_call(
        project_out_kernel,
        out_shape=(jax.ShapeDtypeStruct((seg, w_all.shape[2]), BF16),) * chips,
        in_specs=[SMEM] + [VMEM] * 3,
        out_specs=(VMEM,) * chips,
        compiler_params=params(SMALL_LIMIT),
        cost_estimate=cost(seg * w_all.size, 2 * w_all.size),
        name="project_out",
    )(place, own, other, w_all)


def assemble_kernel(place_ref, *refs):
    parts, out_ref = refs[:-1], refs[-1]
    chip = lax.div(place_ref[1], CORES)
    seg = parts[0].shape[0]
    for k, part in enumerate(parts):
        at = pl.multiple_of(lax.bitwise_xor(chip, k) * seg, seg)
        out_ref[pl.ds(at, seg), :] = part[...]


def assemble(place, parts):
    seg, width = parts[0].shape
    return pl.pallas_call(
        assemble_kernel,
        out_shape=jax.ShapeDtypeStruct((seg * len(parts), width), BF16),
        in_specs=[SMEM] + [VMEM] * len(parts),
        out_specs=VMEM,
        compiler_params=params(SMALL_LIMIT),
        name="assemble",
    )(place, *parts)


def from_rows(value, row_count):
    return [value] + [
        lax.ppermute(value, "row", xor_pairs(row_count, j)) for j in range(1, row_count)
    ]


def key_features(features, cols, row_count, col_count, beside):
    ratio = features.shape[0] // cols
    col_pos, row_pos = lax.axis_index("col"), lax.axis_index("row")
    own = lax.dynamic_slice_in_dim(features, col_pos % ratio * cols, cols, 0)
    away = lax.bitwise_xor(row_pos, col_pos // ratio)

    def send(value, a, b):
        pairs = [
            (((c // ratio) ^ a) * col_count + c, ((c // ratio) ^ b) * col_count + c)
            for c in range(col_count)
        ]
        return lax.ppermute(value, ("row", "col"), pairs)

    if row_count != 4:
        got = own
        for j in range(1, row_count):
            got = jnp.where(away == j, send(own, 0, j), got)
        return got, beside
    near, side = send(own, 0, 1), send(own, 0, 2)
    near, side, beside = lax.optimization_barrier((near, side, beside))
    mid = cols // 2
    low, high = send(near[:mid], 1, 3), send(side[mid:], 2, 3)
    got = jnp.where(away == 1, near, jnp.where(away == 2, side, own))
    return jnp.where(away == 3, jnp.concatenate([low, high], axis=0), got), beside


def shards(node_features, edge_weight, pattern, w_qkv, w_out, bias_gain, bias_rate):
    rows, cols = edge_weight.shape
    row_count, col_count = lax.axis_size("row"), lax.axis_size("col")
    row_pos, col_pos = lax.axis_index("row"), lax.axis_index("col")
    chips = col_count // CORES
    root = math.sqrt(rows * row_count)
    place = jnp.stack([row_pos, col_pos]).astype(jnp.int32)
    core = (col_pos % CORES).astype(jnp.int32).reshape(1)
    pattern = pattern.T

    def along_col(value, j):
        return lax.ppermute(value, "col", xor_pairs(col_count, j))

    adjacency = mask(pattern, edge_weight)
    panel = lax.all_gather(adjacency, "col", axis=0, tiled=False)
    w_all = lax.all_gather(w_out, "col", axis=0, tiled=False)
    columns = from_rows(adjacency, row_count)
    queries = project_in(core, [node_features], w_qkv, [0], 1.0 / math.sqrt(HDIM))
    key_rows, queries = key_features(node_features, cols, row_count, col_count, queries)

    other_rows = along_col(key_rows, 1)
    other_pattern = along_col(pattern.astype(F32), 1).astype(jnp.int32)
    keys_values = project_in(core, [key_rows, other_rows], w_qkv, [D, 2 * D])
    expo, peak = exponentials(pattern, other_pattern, queries, keys_values)

    ranks = sweep(True, range(chips), place, pattern, panel, columns, node_features)
    columns = from_rows(ranks, row_count)

    parts = [None] * chips
    for ks in (list(range(chips // 2, chips)), list(range(chips // 2))):
        ranks = sweep(False, ks, place, pattern, panel, columns, peak)
        sums = weigh(
            root, chips, ks, place, bias_gain, bias_rate, ranks, along_col(ranks, 1), expo,
            keys_values, peak,
        )
        for k, part in zip(ks, sums, strict=True):
            parts[k] = part if k == 0 else along_col(part, CORES * k)
    attended = divide(parts)
    mixed = project_out(place, attended, along_col(attended, 1), w_all, chips)
    mixed = [x if k == 0 else along_col(x, CORES * k) for k, x in enumerate(mixed)]
    return assemble(place, mixed)


def solution(mesh):
    in_specs = (P("row", None), P("row", "col"), P("row", "col"), P(), P(None, "col"), P(), P())
    out_specs = P("row", "col")
    return jax.shard_map(shards, mesh=mesh, in_specs=in_specs, out_specs=out_specs, check_vma=False)
```

time: 324 us -> 175 us (0.54)
  waiting for transfers between devices: 186 us -> 63.6 us
  blocking collectives: 54.8 us -> 0 us
  Pallas kernels: 0 us -> 54 us
  matrix products: 45.7 us -> 0 us
  starting transfers between devices: 0.35 us -> 30 us
  other arithmetic: 16.6 us -> 2.94 us
  local copies, waits for them, and re-layouts: 6.84 us -> 10.2 us
    all_gather x3 -> x2, waiting for transfers between devices: 125 us -> 0.02 us  [the longest x1 0.02 us: shards(): w_all = lax.all_gather(w_out, 'col', axis=0, tiled=False)]
    ppermute x0 -> x21, waiting for transfers between devices: none -> 63.6 us  [the longest x6 29.5 us: from_rows(): lax.ppermute(value, 'row', xor_pairs(row_count, j))]
    psum x2 -> x0, waiting for transfers between devices: 61.6 us -> none  [the longest x1 38.1 us: spread(): return lax.psum(kept, axis)]
    pallas_call x0 -> x12, Pallas kernels: none -> 54 us  [the longest x3 15.1 us: sweep(): pl.pallas_call(functools.partial(sweep_kernel, first, ks, len(blocks)), o...]
    dot_general x7 -> x0, matrix products: 45.7 us -> none  [the longest x2 13.5 us: sweep(): jnp.dot(operator_panel, lax.all_gather(ranks.astype(jnp.bfloat16), 'row',...]
    ppermute x0 -> x21, starting transfers between devices: none -> 29.9 us  [the longest x6 12.5 us: from_rows(): lax.ppermute(value, 'row', xor_pairs(row_count, j))]
    pmax x1 -> x0, blocking collectives: 28.5 us -> none  [shards(): lax.pmax(local_peak.astype(jnp.bfloat16), 'col').astype(local_peak.dtype)]
    psum x1 -> x0, blocking collectives: 26.3 us -> none  [shards(): lax.psum(totals.astype(jnp.bfloat16), 'col').astype(jnp.float32)]
  transfers between devices with their start and end apart: 5 -> 23, of which waited for: 5 -> 12; matrix products, arithmetic and copies ran while one was open for 9% -> 3% of each run, Pallas kernels for 0% -> 29%
where the time goes in v2:
time: 175 us; the launch traced here: 174 us
  waiting for transfers between devices  63.6 us (36%)
  Pallas kernels  54 us (31%)
  starting transfers between devices  30 us (17%)
  between operations  13.6 us (8%)
  local copies, waits for them, and re-layouts  10.2 us (6%)
  other arithmetic  2.94 us (2%)
    ppermute x6, waiting for transfers between devices, from_rows(): lax.ppermute(value, 'row', xor_pairs(row_count, j))  29.5 us
    ppermute x11, waiting for transfers between devices, along_col(): return lax.ppermute(value, 'col', xor_pairs(col_count, j))  20.6 us
    pallas_call x3, Pallas kernels, sweep(): pl.pallas_call(functools.partial(sweep_kernel, first, ks, len(blocks)), o...  15.1 us
    pallas_call x2, Pallas kernels, weigh(): pl.pallas_call(functools.partial(weigh_kernel, root, ks, seg), out_shape=...  14.8 us
    ppermute x4, waiting for transfers between devices, send(): return lax.ppermute(value, ('row', 'col'), pairs)  13.5 us
    ppermute x6, starting transfers between devices, from_rows(): lax.ppermute(value, 'row', xor_pairs(row_count, j))  12.5 us
    pallas_call x1, Pallas kernels, exponentials(): pl.pallas_call(expo_kernel, out_shape=(jax.ShapeDtypeStruct((PAIRS, rows,...  10.1 us
    ppermute x11, starting transfers between devices, along_col(): return lax.ppermute(value, 'col', xor_pairs(col_count, j))  9.06 us
  transfers between devices with their start and end apart: 23, of which 12 were waited for; matrix products, arithmetic and copies ran while one was open for 3% of the time, Pallas kernels for 29%

profile of v2, /device:TPU:0, one launch (start us, length us, event | category | flops | bytes accessed | tf_op | source)
XLA Modules:
  0.0 174.3 jit_solution(8307799911080013137)
XLA Ops:
  10.9 4.9 %collective-permute-start.7 = (bf16[384,1024]{1,0:T(8,128)(2,1)}, bf16[384,1024]{1,0:T(8,128)(2,1)S(1)}, u32[]{:S(2)}, u32[]{:S(2)}) collective-permute-start(bf16[384,1024]{1,0:T(8,128)(2,1)} %constant_dynamic-slice_fusion), channel_id=1, source_target_pairs={{0,8},{1,9},{10,2},{11,3},{20,28},{21,29},{30,22},{31,23}} | collective-permute-start | bytes 2359304 | tf_op jit(solution)/shard_map/ppermute | solution.py:476
  17.1 3.6 %project_in.2.q_ref = bf16[768,512]{1,0:T(8,128)(2,1)} custom-call(s32[1]{0:T(128)} %bitcast.4.place_ref, bf16[768,1024]{1,0:T(8,128)(2,1)} %refs_0_.1, bf16[1024,3072]{1,0:T(8,128)(2,1)} %refs_2_.1), custom_call_target="tpu_custom_call" | custom-call | flops 805306368 | bytes 2621440 | tf_op jit(solution)/shard_map/project_in/pallas_call | solution.py:96
  20.7 12.1 %collective-permute-done.7 = bf16[384,1024]{1,0:T(8,128)(2,1)S(1)} collective-permute-done((bf16[384,1024]{1,0:T(8,128)(2,1)}, bf16[384,1024]{1,0:T(8,128)(2,1)S(1)}, u32[]{:S(2)}, u32[]{:S(2)}) %collective-permute-start.7) | collective-permute-done | bytes 786464 | tf_op jit(solution)/shard_map/ppermute | solution.py:476
  37.8 1.7 collective-permute-start
  42.3 1.6 maximum_select_fusion.refs_0_
  44.8 9.6 %collective-permute-done.refs_1_ = bf16[768,384]{1,0:T(8,128)(2,1)} collective-permute-done((bf16[768,384]{1,0:T(8,128)(2,1)}, bf16[768,384]{1,0:T(8,128)(2,1)}, u32[]{:S(2)}, u32[]{:S(2)}) %collective-permute-start) | collective-permute-done | bytes 589856 | tf_op jit(solution)/shard_map/ppermute | solution.py:461
  54.4 11.2 %collective-permute-done.1.refs_2_ = bf16[768,384]{1,0:T(8,128)(2,1)} collective-permute-done((bf16[768,384]{1,0:T(8,128)(2,1)}, bf16[768,384]{1,0:T(8,128)(2,1)}, u32[]{:S(2)}, u32[]{:S(2)}) %collective-permute-start.1) | collective-permute-done | bytes 589856 | tf_op jit(solution)/shard_map/ppermute | solution.py:461
  65.6 1.9 %collective-permute-done.2.refs_3_ = bf16[768,384]{1,0:T(8,128)(2,1)} collective-permute-done((bf16[768,384]{1,0:T(8,128)(2,1)}, bf16[768,384]{1,0:T(8,128)(2,1)}, u32[]{:S(2)}, u32[]{:S(2)}) %collective-permute-start.2) | collective-permute-done | bytes 589856 | tf_op jit(solution)/shard_map/ppermute | solution.py:461
  67.6 6.2 %rank_sweep.3.refs_0_ = bf16[768,384]{1,0:T(8,128)(2,1)} custom-call(s32[2]{0:T(128)} %pad_add_fusion.place_ref, s32[3,6]{1,0:T(4,128)} %bitcast.8, bf16[8,768,384]{2,1,0:T(8,128)(2,1)} %bitcast.13, bf16[768,384]{1,0:T(8,128)(2,1)} %mask.1.refs_0_, bf16[768,384]{1,0:T(8,128)(2,1)} %collective-permute-done.refs_1_, ...), custom_call_target="tpu_custom_call" | custom-call | flops 1811939328 | bytes 9437184 | tf_op jit(solution)/shard_map/rank_sweep/pallas_call | solution.py:184
  73.8 6.5 %collective-permute-start.3 = (bf16[768,384]{1,0:T(8,128)(2,1)}, bf16[768,384]{1,0:T(8,128)(2,1)S(1)}, u32[]{:S(2)}, u32[]{:S(2)}) collective-permute-start(bf16[768,384]{1,0:T(8,128)(2,1)} %rank_sweep.3.refs_0_), channel_id=1, source_target_pairs={{0,8},{8,0},{16,24},{24,16},{1,9},{9,1},{17,25},{25,17},{2,10},{10... | collective-permute-start | bytes 1769480 | tf_op jit(solution)/shard_map/ppermute | solution.py:461
  84.5 5.3 %project_in.3.k_ref.v_ref = bf16[768,1024]{1,0:T(8,128)(2,1)} custom-call(s32[1]{0:T(128)} %bitcast.4.place_ref, bf16[384,1024]{1,0:T(8,128)(2,1)} %copy-done.8, bf16[384,1024]{1,0:T(8,128)(2,1)} %copy-done.13, bf16[1024,3072]{1,0:T(8,128)(2,1)} %refs_2_.1), custom_call_target="tpu_custom_call" | custom-call | flops 1610612736 | bytes 3670016 | tf_op jit(solution)/shard_map/project_in/pallas_call | solution.py:96
  89.8 10.1 %expo.1 = (bf16[4,768,1536]{2,1,0:T(8,128)(2,1)}, f32[768,128]{1,0:T(8,128)}) custom-call(s32[3,6]{1,0:T(4,128)} %bitcast.9, s32[3,6]{1,0:T(4,128)} %convert_element_type.7.other_ref, bf16[768,512]{1,0:T(8,128)(2,1)} %project_in.2.q_ref, bf16[768,1024]{1,0:T(8,128)(2,1)} %project_in.3.k_ref.v_ref), custom_call_target="tpu_custom_call" | custom-call | flops 2415919104 | bytes 9437184 | tf_op jit(solution)/shard_map/expo/pallas_call | solution.py:248
  99.9 6.8 %collective-permute-done.4.refs_2_ = bf16[768,384]{1,0:T(8,128)(2,1)S(1)} collective-permute-done((bf16[768,384]{1,0:T(8,128)(2,1)}, bf16[768,384]{1,0:T(8,128)(2,1)S(1)}, u32[]{:S(2)}, u32[]{:S(2)}) %collective-permute-start.4) | collective-permute-done | bytes 589856 | tf_op jit(solution)/shard_map/ppermute | solution.py:461
  107.7 4.4 %rank_sweep.5.own_ref = bf16[384,384]{1,0:T(8,128)(2,1)} custom-call(s32[2]{0:T(128)} %pad_add_fusion.place_ref, s32[3,6]{1,0:T(4,128)} %bitcast.10, bf16[8,768,384]{2,1,0:T(8,128)(2,1)} %bitcast.14, bf16[768,384]{1,0:T(8,128)(2,1)} %rank_sweep.3.refs_0_, bf16[768,384]{1,0:T(8,128)(2,1)} %copy-done.9, bf16[768,384]{1,0:T(8,128)(2,1)} %copy-done.10, ...), custom_call_target="tpu_custom_call" | custom-call | flops 905969664 | bytes 7077888 | tf_op jit(solution)/shard_map/rank_sweep/pallas_call | solution.py:184
  112.2 4.5 %rank_sweep.4.own_ref = bf16[384,384]{1,0:T(8,128)(2,1)} custom-call(s32[2]{0:T(128)} %pad_add_fusion.place_ref, s32[3,6]{1,0:T(4,128)} %bitcast.11, bf16[8,768,384]{2,1,0:T(8,128)(2,1)} %bitcast.15, bf16[768,384]{1,0:T(8,128)(2,1)} %rank_sweep.3.refs_0_, bf16[768,384]{1,0:T(8,128)(2,1)} %copy-done.9, bf16[768,384]{1,0:T(8,128)(2,1)} %copy-done.10, ...), custom_call_target="tpu_custom_call" | custom-call | flops 905969664 | bytes 7077888 | tf_op jit(solution)/shard_map/rank_sweep/pallas_call | solution.py:184
  117.9 7.4 %weigh.3 = (bf16[192,640]{1,0:T(8,128)(2,1)}, bf16[192,640]{1,0:T(8,128)(2,1)}) custom-call(s32[2]{0:T(128)} %pad_add_fusion.place_ref, f32[16]{0:T(128)} %gain_ref.3, f32[16]{0:T(128)} %rate_ref.3, bf16[384,384]{1,0:T(8,128)(2,1)} %rank_sweep.5.own_ref, bf16[384,384]{1,0:T(8,128)(2,1)} %copy-done.15, bf16[4,768,1536]{2,1,0:T(8,128)(2,1)} %get-tuple-element.22.expo_ref, ...), custom_call_target="tpu_custom_call" | custom-call | flops 1207959552 | bytes 4718592 | tf_op jit(solution)/shard_map/weigh/pallas_call | solution.py:349
  125.3 2.8 %collective-permute-start.15 = (bf16[192,640]{1,0:T(8,128)(2,1)}, bf16[192,640]{1,0:T(8,128)(2,1)S(1)}, u32[]{:S(2)}, u32[]{:S(2)}) collective-permute-start(bf16[192,640]{1,0:T(8,128)(2,1)} %get-tuple-element.25), channel_id=1, source_target_pairs={{0,4},{1,5},{2,6},{3,7},{4,0},{5,1},{6,2},{7,3},{8,12},{9,13},{10,... | collective-permute-start | bytes 737288 | tf_op jit(solution)/shard_map/ppermute | solution.py:502
  129.3 7.4 %weigh.2 = (bf16[192,640]{1,0:T(8,128)(2,1)}, bf16[192,640]{1,0:T(8,128)(2,1)}) custom-call(s32[2]{0:T(128)} %pad_add_fusion.place_ref, f32[16]{0:T(128)} %gain_ref.3, f32[16]{0:T(128)} %rate_ref.3, bf16[384,384]{1,0:T(8,128)(2,1)} %rank_sweep.4.own_ref, bf16[384,384]{1,0:T(8,128)(2,1)} %copy-done.14, bf16[4,768,1536]{2,1,0:T(8,128)(2,1)} %get-tuple-element.22.expo_ref, ...), custom_call_target="tpu_custom_call" | custom-call | flops 1207959552 | bytes 4718592 | tf_op jit(solution)/shard_map/weigh/pallas_call | solution.py:349
  137.3 8.2 %collective-permute-done.15.refs_2_ = bf16[192,640]{1,0:T(8,128)(2,1)S(1)} collective-permute-done((bf16[192,640]{1,0:T(8,128)(2,1)}, bf16[192,640]{1,0:T(8,128)(2,1)S(1)}, u32[]{:S(2)}, u32[]{:S(2)}) %collective-permute-start.15) | collective-permute-done | bytes 245792 | tf_op jit(solution)/shard_map/ppermute | solution.py:502
  145.5 4.8 %collective-permute-done.13.refs_1_ = bf16[192,640]{1,0:T(8,128)(2,1)S(1)} collective-permute-done((bf16[192,640]{1,0:T(8,128)(2,1)}, bf16[192,640]{1,0:T(8,128)(2,1)S(1)}, u32[]{:S(2)}, u32[]{:S(2)}) %collective-permute-start.13) | collective-permute-done | bytes 245792 | tf_op jit(solution)/shard_map/ppermute | solution.py:502
  154.0 1.6 copy-done
  157.4 3.0 %collective-permute-start.19 = (bf16[192,128]{1,0:T(8,128)(2,1)S(1)}, bf16[192,128]{1,0:T(8,128)(2,1)S(1)}, u32[]{:S(2)}, u32[]{:S(2)}) collective-permute-start(bf16[192,128]{1,0:T(8,128)(2,1)S(1)} %get-tuple-element.29), channel_id=1, source_target_pairs={{0,4},{1,5},{2,6},{3,7},{4,0},{5,1},{6,2},{7,3},{8,12},{9,13},{10,... | collective-permute-start | bytes 147464 | tf_op jit(solution)/shard_map/ppermute | solution.py:502
  161.2 2.2 %collective-permute-done.19.refs_2_ = bf16[192,128]{1,0:T(8,128)(2,1)S(1)} collective-permute-done((bf16[192,128]{1,0:T(8,128)(2,1)S(1)}, bf16[192,128]{1,0:T(8,128)(2,1)S(1)}, u32[]{:S(2)}, u32[]{:S(2)}) %collective-permute-start.19) | collective-permute-done | bytes 49184 | tf_op jit(solution)/shard_map/ppermute | solution.py:502
  163.4 2.9 %collective-permute-done.20.refs_3_ = bf16[192,128]{1,0:T(8,128)(2,1)S(1)} collective-permute-done((bf16[192,128]{1,0:T(8,128)(2,1)S(1)}, bf16[192,128]{1,0:T(8,128)(2,1)S(1)}, u32[]{:S(2)}, u32[]{:S(2)}) %collective-permute-start.20) | collective-permute-done | bytes 49184 | tf_op jit(solution)/shard_map/ppermute | solution.py:502
  (75 shorter events, 30.1 us)
Async XLA Ops:
  6.5 61.0 %all-gather.5.cloned.1.call-start = ((), (), s32[]{:S(2)}) async-start(), calls=%async_computation | async-start | bytes 5308416 | tf_op jit(solution)/shard_map/all_gather | solution.py:505
  9.8 142.8 %all-gather.7.cloned.1.call-start = ((), (), s32[]{:S(2)}) async-start(), calls=%async_computation.1 | async-start | bytes 2359296 | tf_op jit(solution)/shard_map/all_gather | solution.py:506
  10.9 21.9 %collective-permute-start.7 = (bf16[384,1024]{1,0:T(8,128)(2,1)}, bf16[384,1024]{1,0:T(8,128)(2,1)S(1)}, u32[]{:S(2)}, u32[]{:S(2)}) collective-permute-start(bf16[384,1024]{1,0:T(8,128)(2,1)} %constant_dynamic-slice_fusion), channel_id=1, source_target_pairs={{0,8},{1,9},{10,2},{11,3},{20,28},{21,29},{30,22},{31,23}} | collective-permute-start | bytes 2359304 | tf_op jit(solution)/shard_map/ppermute | solution.py:476
  15.7 18.4 %collective-permute-start.8 = (bf16[384,1024]{1,0:T(8,128)(2,1)}, bf16[384,1024]{1,0:T(8,128)(2,1)S(1)}, u32[]{:S(2)}, u32[]{:S(2)}) collective-permute-start(bf16[384,1024]{1,0:T(8,128)(2,1)} %constant_dynamic-slice_fusion), channel_id=1, source_target_pairs={{0,16},{1,17},{10,26},{11,27},{20,4},{21,5},{30,14},{31,15}} | collective-permute-start | bytes 2359304 | tf_op jit(solution)/shard_map/ppermute | solution.py:476
  35.0 7.3 %collective-permute-start.10 = (bf16[192,1024]{1,0:T(8,128)(2,1)}, bf16[192,1024]{1,0:T(8,128)(2,1)S(1)}, u32[]{:S(2)}, u32[]{:S(2)}) collective-permute-start(bf16[192,1024]{1,0:T(8,128)(2,1)} %slice.7), channel_id=1, source_target_pairs={{16,24},{17,25},{26,18},{27,19},{4,12},{5,13},{14,6},{15,7}} | collective-permute-start | bytes 1179656 | tf_op jit(solution)/shard_map/ppermute | solution.py:476
  36.4 5.9 %collective-permute-start.9 = (bf16[192,1024]{1,0:T(8,128)(2,1)}, bf16[192,1024]{1,0:T(8,128)(2,1)}, u32[]{:S(2)}, u32[]{:S(2)}) collective-permute-start(bf16[192,1024]{1,0:T(8,128)(2,1)} %slice.6), channel_id=1, source_target_pairs={{8,24},{9,25},{2,18},{3,19},{28,12},{29,13},{22,6},{23,7}} | collective-permute-start | bytes 1179656 | tf_op jit(solution)/shard_map/ppermute | solution.py:476
  37.8 16.6 %collective-permute-start = (bf16[768,384]{1,0:T(8,128)(2,1)}, bf16[768,384]{1,0:T(8,128)(2,1)}, u32[]{:S(2)}, u32[]{:S(2)}) collective-permute-start(bf16[768,384]{1,0:T(8,128)(2,1)} %mask.1.refs_0_), channel_id=1, source_target_pairs={{0,8},{8,0},{16,24},{24,16},{1,9},{9,1},{17,25},{25,17},{2,10},{10... | collective-permute-start | bytes 1769480 | tf_op jit(solution)/shard_map/ppermute | solution.py:461
  39.5 26.1 %collective-permute-start.1 = (bf16[768,384]{1,0:T(8,128)(2,1)}, bf16[768,384]{1,0:T(8,128)(2,1)}, u32[]{:S(2)}, u32[]{:S(2)}) collective-permute-start(bf16[768,384]{1,0:T(8,128)(2,1)} %mask.1.refs_0_), channel_id=1, source_target_pairs={{0,16},{8,24},{16,0},{24,8},{1,17},{9,25},{17,1},{25,9},{2,18},{10... | collective-permute-start | bytes 1769480 | tf_op jit(solution)/shard_map/ppermute | solution.py:461
  40.9 26.7 %collective-permute-start.2 = (bf16[768,384]{1,0:T(8,128)(2,1)}, bf16[768,384]{1,0:T(8,128)(2,1)}, u32[]{:S(2)}, u32[]{:S(2)}) collective-permute-start(bf16[768,384]{1,0:T(8,128)(2,1)} %mask.1.refs_0_), channel_id=1, source_target_pairs={{0,24},{8,16},{16,8},{24,0},{1,25},{9,17},{17,9},{25,1},{2,26},{10... | collective-permute-start | bytes 1769480 | tf_op jit(solution)/shard_map/ppermute | solution.py:461
  44.0 29.8 %copy-start.8 = (bf16[384,1024]{1,0:T(8,128)(2,1)}, bf16[384,1024]{1,0:T(8,128)(2,1)S(1)}, u32[]{:S(2)}) copy-start(bf16[384,1024]{1,0:T(8,128)(2,1)S(1)} %maximum_select_fusion.refs_0_) | copy-start | bytes 2359300
  44.0 39.6 %collective-permute-start.11 = (bf16[384,1024]{1,0:T(8,128)(2,1)S(1)}, bf16[384,1024]{1,0:T(8,128)(2,1)S(1)}, u32[]{:S(2)}, u32[]{:S(2)}) collective-permute-start(bf16[384,1024]{1,0:T(8,128)(2,1)S(1)} %maximum_select_fusion.refs_0_), channel_id=1, source_target_pairs={{0,1},{1,0},{2,3},{3,2},{4,5},{5,4},{6,7},{7,6},{8,9},{9,8},{10,11... | collective-permute-start | bytes 2359304 | tf_op jit(solution)/shard_map/ppermute | solution.py:502
  73.8 26.1 %collective-permute-start.3 = (bf16[768,384]{1,0:T(8,128)(2,1)}, bf16[768,384]{1,0:T(8,128)(2,1)S(1)}, u32[]{:S(2)}, u32[]{:S(2)}) collective-permute-start(bf16[768,384]{1,0:T(8,128)(2,1)} %rank_sweep.3.refs_0_), channel_id=1, source_target_pairs={{0,8},{8,0},{16,24},{24,16},{1,9},{9,1},{17,25},{25,17},{2,10},{10... | collective-permute-start | bytes 1769480 | tf_op jit(solution)/shard_map/ppermute | solution.py:461
  80.3 26.3 %collective-permute-start.4 = (bf16[768,384]{1,0:T(8,128)(2,1)}, bf16[768,384]{1,0:T(8,128)(2,1)S(1)}, u32[]{:S(2)}, u32[]{:S(2)}) collective-permute-start(bf16[768,384]{1,0:T(8,128)(2,1)} %rank_sweep.3.refs_0_), channel_id=1, source_target_pairs={{0,16},{8,24},{16,0},{24,8},{1,17},{9,25},{17,1},{25,9},{2,18},{10... | collective-permute-start | bytes 1769480 | tf_op jit(solution)/shard_map/ppermute | solution.py:461
  81.2 25.5 %collective-permute-start.5 = (bf16[768,384]{1,0:T(8,128)(2,1)}, bf16[768,384]{1,0:T(8,128)(2,1)S(1)}, u32[]{:S(2)}, u32[]{:S(2)}) collective-permute-start(bf16[768,384]{1,0:T(8,128)(2,1)} %rank_sweep.3.refs_0_), channel_id=1, source_target_pairs={{0,24},{8,16},{16,8},{24,0},{1,25},{9,17},{17,9},{25,1},{2,26},{10... | collective-permute-start | bytes 1769480 | tf_op jit(solution)/shard_map/ppermute | solution.py:461
  81.9 1.2 collective-permute-start.6
  112.1 5.1 %collective-permute-start.14 = (bf16[384,384]{1,0:T(8,128)(2,1)}, bf16[384,384]{1,0:T(8,128)(2,1)S(1)}, u32[]{:S(2)}, u32[]{:S(2)}) collective-permute-start(bf16[384,384]{1,0:T(8,128)(2,1)} %rank_sweep.5.own_ref), channel_id=1, source_target_pairs={{0,1},{1,0},{2,3},{3,2},{4,5},{5,4},{6,7},{7,6},{8,9},{9,8},{10,11... | collective-permute-start | bytes 884744 | tf_op jit(solution)/shard_map/ppermute | solution.py:502
  116.7 12.0 %collective-permute-start.12 = (bf16[384,384]{1,0:T(8,128)(2,1)}, bf16[384,384]{1,0:T(8,128)(2,1)S(1)}, u32[]{:S(2)}, u32[]{:S(2)}) collective-permute-start(bf16[384,384]{1,0:T(8,128)(2,1)} %rank_sweep.4.own_ref), channel_id=1, source_target_pairs={{0,1},{1,0},{2,3},{3,2},{4,5},{5,4},{6,7},{7,6},{8,9},{9,8},{10,11... | collective-permute-start | bytes 884744 | tf_op jit(solution)/shard_map/ppermute | solution.py:502
  125.3 20.2 %collective-permute-start.15 = (bf16[192,640]{1,0:T(8,128)(2,1)}, bf16[192,640]{1,0:T(8,128)(2,1)S(1)}, u32[]{:S(2)}, u32[]{:S(2)}) collective-permute-start(bf16[192,640]{1,0:T(8,128)(2,1)} %get-tuple-element.25), channel_id=1, source_target_pairs={{0,4},{1,5},{2,6},{3,7},{4,0},{5,1},{6,2},{7,3},{8,12},{9,13},{10,... | collective-permute-start | bytes 737288 | tf_op jit(solution)/shard_map/ppermute | solution.py:502
  128.2 17.4 %collective-permute-start.16 = (bf16[192,640]{1,0:T(8,128)(2,1)}, bf16[192,640]{1,0:T(8,128)(2,1)S(1)}, u32[]{:S(2)}, u32[]{:S(2)}) collective-permute-start(bf16[192,640]{1,0:T(8,128)(2,1)} %get-tuple-element.26), channel_id=1, source_target_pairs={{0,6},{1,7},{2,4},{3,5},{4,2},{5,3},{6,0},{7,1},{8,14},{9,15},{10,... | collective-permute-start | bytes 737288 | tf_op jit(solution)/shard_map/ppermute | solution.py:502
  136.8 13.5 %collective-permute-start.13 = (bf16[192,640]{1,0:T(8,128)(2,1)}, bf16[192,640]{1,0:T(8,128)(2,1)S(1)}, u32[]{:S(2)}, u32[]{:S(2)}) collective-permute-start(bf16[192,640]{1,0:T(8,128)(2,1)} %get-tuple-element.24), channel_id=1, source_target_pairs={{0,2},{1,3},{2,0},{3,1},{4,6},{5,7},{6,4},{7,5},{8,10},{9,11},{10,... | collective-permute-start | bytes 737288 | tf_op jit(solution)/shard_map/ppermute | solution.py:502
  152.5 1.5 collective-permute-start.17
  156.7 4.5 %collective-permute-start.18 = (bf16[192,128]{1,0:T(8,128)(2,1)S(1)}, bf16[192,128]{1,0:T(8,128)(2,1)S(1)}, u32[]{:S(2)}, u32[]{:S(2)}) collective-permute-start(bf16[192,128]{1,0:T(8,128)(2,1)S(1)} %get-tuple-element.28), channel_id=1, source_target_pairs={{0,2},{1,3},{2,0},{3,1},{4,6},{5,7},{6,4},{7,5},{8,10},{9,11},{10,... | collective-permute-start | bytes 147464 | tf_op jit(solution)/shard_map/ppermute | solution.py:502
  157.4 6.0 %collective-permute-start.19 = (bf16[192,128]{1,0:T(8,128)(2,1)S(1)}, bf16[192,128]{1,0:T(8,128)(2,1)S(1)}, u32[]{:S(2)}, u32[]{:S(2)}) collective-permute-start(bf16[192,128]{1,0:T(8,128)(2,1)S(1)} %get-tuple-element.29), channel_id=1, source_target_pairs={{0,4},{1,5},{2,6},{3,7},{4,0},{5,1},{6,2},{7,3},{8,12},{9,13},{10,... | collective-permute-start | bytes 147464 | tf_op jit(solution)/shard_map/ppermute | solution.py:502
  160.3 5.9 %collective-permute-start.20 = (bf16[192,128]{1,0:T(8,128)(2,1)S(1)}, bf16[192,128]{1,0:T(8,128)(2,1)S(1)}, u32[]{:S(2)}, u32[]{:S(2)}) collective-permute-start(bf16[192,128]{1,0:T(8,128)(2,1)S(1)} %get-tuple-element.30), channel_id=1, source_target_pairs={{0,6},{1,7},{2,4},{3,5},{4,2},{5,3},{6,0},{7,1},{8,14},{9,15},{10,... | collective-permute-start | bytes 147464 | tf_op jit(solution)/shard_map/ppermute | solution.py:502
  (15 other events, 86.8 us)
Sparse Core Ops, SparseCore 0:
  9.9 54.3 all-gather.4
  66.0 27.9 all-gather.6

commit v3 on v2

--- a/solution.py
+++ b/solution.py
@@ -83,7 +83,7 @@
         out_ref[i * rows : (i + 1) * rows, :] = out
 
 
-def project_in(core, xs, w, firsts, scale=None, tile=256):
+def project_in(core, xs, w, firsts, scale=None, tile=256, limit=VMEM_LIMIT):
     rows, depth = xs[0].shape
     steps = WIDTH // tile
 
@@ -103,7 +103,7 @@
             + [pl.BlockSpec((depth, tile), column)],
             out_specs=pl.BlockSpec((rows * len(xs), tile), lambda i, c: (0, i)),
         ),
-        compiler_params=params(),
+        compiler_params=params(limit),
         cost_estimate=cost(
             2 * rows * len(xs) * depth * WIDTH * len(firsts),
             2 * depth * (rows * len(xs) + WIDTH * len(firsts)),
@@ -112,48 +112,56 @@
     )(core, *xs, w)
 
 
-def sweep_kernel(first, ks, n_right, place_ref, pattern_ref, panel_ref, *refs):
-    rights, (out_ref, left_ref, right_ref, acc_ref, sem) = refs[:n_right], refs[-5:]
-    count, rows, cols = panel_ref.shape
-    ratio = count // n_right
-    seg = out_ref.shape[0] // len(ks)
+def sweep_kernel(first, ks, chips, left_at, right_at, place_ref, pattern_ref, *refs):
+    n_right = len(right_at)
+    panel, rights = refs[: len(left_at)], refs[len(left_at) : len(left_at) + n_right]
+    out_ref, left_ref, right_ref, acc_ref, left_sem, right_sem = refs[-6:]
+    rows, cols = panel[0].shape[-2:]
+    seg = rows // chips
     row_pos, col_pos = place_ref[0], place_ref[1]
-    starts = [
-        pl.multiple_of(lax.bitwise_xor(lax.div(col_pos, CORES), k) * seg, seg) for k in ks
-    ]
-    if len(ks) == count // CORES:
-        starts = [n * seg for n in range(len(ks))]
-
-    def left_copies(j):
-        for i in range(ratio):
-            c = lax.bitwise_xor(row_pos, j) * ratio + i
+    chip, core = lax.div(col_pos, CORES), lax.rem(col_pos, CORES)
+    starts = [pl.multiple_of(lax.bitwise_xor(chip, k) * seg, seg) for k in ks]
+    if len(ks) == chips:
+        starts = [n * seg for n in range(chips)]
+
+    def right_copy(i):
+        xor, offset = right_at[i]
+        slot = lax.bitwise_xor(lax.bitwise_xor(row_pos, chip), xor)
+        target = right_ref.at[slot, pl.ds(offset, rights[i].shape[0]), :]
+        return pltpu.make_async_copy(rights[i], target, right_sem.at[i])
+
+    def left_copies(k):
+        for ref, (j, index) in zip(panel, left_at, strict=True):
+            if j // CORES != k:
+                continue
+            block = ref if index is None else ref.at[index]
+            at = pl.multiple_of(lax.bitwise_xor(core, j % CORES) * cols, cols)
             for n, start in enumerate(starts):
                 yield pltpu.make_async_copy(
-                    panel_ref.at[c, pl.ds(start, seg), :],
-                    left_ref.at[j, pl.ds(n * seg, seg), i * cols : (i + 1) * cols],
-                    sem.at[j, i * len(ks) + n],
+                    block.at[pl.ds(start, seg), :],
+                    left_ref.at[k, pl.ds(n * seg, seg), pl.ds(at, cols)],
+                    left_sem.at[k, j % CORES * len(ks) + n],
                 )
-
-    def right_copy(j):
-        return pltpu.make_async_copy(rights[j], right_ref.at[j], sem.at[j, ratio * len(ks)])
 
     for j in range(n_right):
         right_copy(j).start()
-        for copy in left_copies(j):
+    for k in range(chips):
+        for copy in left_copies(k):
             copy.start()
     for j in range(n_right):
         right_copy(j).wait()
-        for copy in left_copies(j):
+    for k in range(chips):
+        for copy in left_copies(k):
             copy.wait()
-        product = jnp.dot(left_ref[j], right_ref[j], preferred_element_type=F32)
-        if j == 0:
+        product = jnp.dot(
+            left_ref[k], right_ref[k], preferred_element_type=F32
+        )
+        if k == 0:
             acc_ref[...] = product
-        elif j < n_right - 1:
+        elif k < chips - 1:
             acc_ref[...] += product
     product = product + acc_ref[...]
-    home = lax.bitwise_xor(row_pos, lax.div(col_pos, ratio))
-    at = pl.multiple_of(lax.rem(col_pos, ratio) * cols, cols)
-    own = left_ref[home, :, pl.ds(at, cols)].astype(F32)
+    own = left_ref[0, :, pl.ds(pl.multiple_of(core * cols, cols), cols)].astype(F32)
     total = 0.1275 * own + (0.85 * 0.1275 if first else 0.85) * product
     diagonal = lax.broadcasted_iota(jnp.int32, (seg, cols), 1) - lax.broadcasted_iota(
         jnp.int32, (seg, cols), 0
@@ -178,24 +186,33 @@
 
 
 def sweep(first, ks, place, pattern, panel, blocks, follows, limit=VMEM_LIMIT):
-    count, rows, cols = panel.shape
-    ratio = count // len(blocks)
-    n_rows = rows * CORES // count * len(ks)
-    return pl.pallas_call(
-        functools.partial(sweep_kernel, first, ks, len(blocks)),
+    rows, cols = panel[0][0].shape[-2:]
+    chips = len(panel) // CORES
+    n_rows = rows // chips * len(ks)
+    depth = len(panel) * cols
+    return pl.pallas_call(
+        functools.partial(
+            sweep_kernel,
+            first,
+            ks,
+            chips,
+            [at for _, *at in panel],
+            [(j, at) for j, at, _ in blocks],
+        ),
         out_shape=jax.ShapeDtypeStruct((n_rows, cols), BF16),
-        in_specs=[SMEM, SMEM] + [HBM] * (2 + len(blocks)),
+        in_specs=[SMEM, SMEM] + [HBM] * (len(panel) + len(blocks) + len(follows)),
         out_specs=VMEM,
         scratch_shapes=[
-            pltpu.VMEM((len(blocks), n_rows, ratio * cols), BF16),
-            pltpu.VMEM((len(blocks), rows, cols), BF16),
+            pltpu.VMEM((chips, n_rows, CORES * cols), BF16),
+            pltpu.VMEM((depth // rows, rows, cols), BF16),
             pltpu.VMEM((n_rows, cols), F32),
-            pltpu.SemaphoreType.DMA((len(blocks), ratio * len(ks) + 1)),
+            pltpu.SemaphoreType.DMA((chips, CORES * len(ks))),
+            pltpu.SemaphoreType.DMA((len(blocks),)),
         ],
         compiler_params=params(limit),
-        cost_estimate=cost(2 * n_rows * count * cols * cols, 2 * (n_rows + rows) * count * cols),
+        cost_estimate=cost(2 * n_rows * depth * cols, 2 * (n_rows + rows) * depth),
         name="rank_sweep",
-    )(place, pattern, panel, *blocks, follows)
+    )(place, pattern, *[x for x, *_ in panel], *[x for *_, x in blocks], *follows)
 
 
 def split_heads(keys):
@@ -263,7 +280,7 @@
             pl.BlockSpec((rows, LANES), lambda p: (0, 0)),
         ),
         scratch_shapes=[pltpu.VMEM((rows, LANES), BF16)],
-        compiler_params=params(),
+        compiler_params=params(28 * 2**20),
         cost_estimate=cost(512 * work, 2 * work, work),
         name="expo",
     )(own, other, queries, keys_values)
@@ -273,7 +290,7 @@
     root, ks, seg, place_ref, gain_ref, rate_ref, own_ref, other_ref, expo_ref, v_ref, peak_ref,
     *refs,
 ):
-    out_refs, (e_ref, p_ref, ranks_ref, right_ref, sem) = refs[: len(ks)], refs[len(ks) :]
+    out_refs, (e_ref, p_ref, ranks_ref, right_ref, sem) = refs[-5 - len(ks) : -5], refs[-5:]
     cols = own_ref.shape[1]
     keys = 2 * cols
     chip = lax.div(place_ref[1], CORES)
@@ -341,7 +358,7 @@
         out_ref[:, WIDTH:] = extra.astype(BF16)
 
 
-def weigh(root, chips, ks, place, gain, rate, own, other, expo, values, peak):
+def weigh(root, chips, ks, place, gain, rate, own, other, expo, values, peak, follows):
     n_rows, cols = own.shape
     seg = n_rows // len(ks)
     rows, keys = seg * chips, 2 * cols
@@ -359,6 +376,7 @@
             HBM,
             pl.BlockSpec((keys, WIDTH), lambda i: (0, 1)),
             pl.BlockSpec((rows, LANES), lambda i: (0, 0)),
+            HBM,
         ],
         out_specs=(pl.BlockSpec((seg, WIDTH + LANES), lambda i: (0, 0)),) * len(ks),
         scratch_shapes=[
@@ -368,10 +386,10 @@
             pltpu.VMEM((2 * keys, 2 * LANES), BF16),
             pltpu.SemaphoreType.DMA((PAIRS, len(ks))),
         ],
-        compiler_params=params(),
+        compiler_params=params(28 * 2**20),
         cost_estimate=cost(512 * work, 2 * work, 2 * work),
         name="weigh",
-    )(place, gain, rate, own, other, expo, values, peak)
+    )(place, gain, rate, own, other, expo, values, peak, follows)
 
 
 def divide_kernel(*refs):
@@ -406,33 +424,29 @@
     )(*parts)
 
 
-def project_out_kernel(place_ref, own_ref, other_ref, w_ref, *out_refs):
-    chip, core = lax.div(place_ref[1], CORES), lax.rem(place_ref[1], CORES)
-    for k, out_ref in enumerate(out_refs):
-        slot = CORES * lax.bitwise_xor(chip, k) + core
-        total = jnp.dot(
-            own_ref[...],
-            w_ref[slot, pl.ds(pl.multiple_of(core * WIDTH, WIDTH), WIDTH), :],
-            preferred_element_type=F32,
-        ) + jnp.dot(
-            other_ref[...],
-            w_ref[slot, pl.ds(pl.multiple_of((1 - core) * WIDTH, WIDTH), WIDTH), :],
-            preferred_element_type=F32,
-        )
+def project_out_kernel(place_ref, own_ref, other_ref, *refs):
+    n = len(refs) // 2
+    core = lax.rem(place_ref[1], CORES)
+    mine = pl.ds(pl.multiple_of(core * WIDTH, WIDTH), WIDTH)
+    others = pl.ds(pl.multiple_of((1 - core) * WIDTH, WIDTH), WIDTH)
+    for w_ref, out_ref in zip(refs[:n], refs[n:], strict=True):
+        total = jnp.dot(own_ref[...], w_ref[mine, :], preferred_element_type=F32)
+        total += jnp.dot(other_ref[...], w_ref[others, :], preferred_element_type=F32)
         out_ref[...] = total.astype(BF16)
 
 
-def project_out(place, own, other, w_all, chips):
-    seg = own.shape[0]
+def project_out(place, own, other, w_all):
+    seg, (depth, width) = own.shape[0], w_all[0].shape
+    chips = len(w_all)
     return pl.pallas_call(
         project_out_kernel,
-        out_shape=(jax.ShapeDtypeStruct((seg, w_all.shape[2]), BF16),) * chips,
-        in_specs=[SMEM] + [VMEM] * 3,
+        out_shape=(jax.ShapeDtypeStruct((seg, width), BF16),) * chips,
+        in_specs=[SMEM] + [VMEM] * (2 + chips),
         out_specs=(VMEM,) * chips,
         compiler_params=params(SMALL_LIMIT),
-        cost_estimate=cost(seg * w_all.size, 2 * w_all.size),
+        cost_estimate=cost(2 * seg * depth * width * chips, 2 * depth * width * chips),
         name="project_out",
-    )(place, own, other, w_all)
+    )(place, own, other, *w_all)
 
 
 def assemble_kernel(place_ref, *refs):
@@ -456,77 +470,112 @@
     )(place, *parts)
 
 
-def from_rows(value, row_count):
-    return [value] + [
-        lax.ppermute(value, "row", xor_pairs(row_count, j)) for j in range(1, row_count)
-    ]
-
-
-def key_features(features, cols, row_count, col_count, beside):
-    ratio = features.shape[0] // cols
-    col_pos, row_pos = lax.axis_index("col"), lax.axis_index("row")
-    own = lax.dynamic_slice_in_dim(features, col_pos % ratio * cols, cols, 0)
-    away = lax.bitwise_xor(row_pos, col_pos // ratio)
-
-    def send(value, a, b):
-        pairs = [
-            (((c // ratio) ^ a) * col_count + c, ((c // ratio) ^ b) * col_count + c)
-            for c in range(col_count)
-        ]
-        return lax.ppermute(value, ("row", "col"), pairs)
-
-    if row_count != 4:
-        got = own
-        for j in range(1, row_count):
-            got = jnp.where(away == j, send(own, 0, j), got)
-        return got, beside
-    near, side = send(own, 0, 1), send(own, 0, 2)
-    near, side, beside = lax.optimization_barrier((near, side, beside))
-    mid = cols // 2
-    low, high = send(near[:mid], 1, 3), send(side[mid:], 2, 3)
-    got = jnp.where(away == 1, near, jnp.where(away == 2, side, own))
-    return jnp.where(away == 3, jnp.concatenate([low, high], axis=0), got), beside
-
-
 def shards(node_features, edge_weight, pattern, w_qkv, w_out, bias_gain, bias_rate):
     rows, cols = edge_weight.shape
     row_count, col_count = lax.axis_size("row"), lax.axis_size("col")
     row_pos, col_pos = lax.axis_index("row"), lax.axis_index("col")
+    ratio = rows // cols
     chips = col_count // CORES
     root = math.sqrt(rows * row_count)
     place = jnp.stack([row_pos, col_pos]).astype(jnp.int32)
     core = (col_pos % CORES).astype(jnp.int32).reshape(1)
     pattern = pattern.T
+    together = lax.optimization_barrier
 
     def along_col(value, j):
         return lax.ppermute(value, "col", xor_pairs(col_count, j))
 
+    def along_row(value, j):
+        return lax.ppermute(value, "row", xor_pairs(row_count, j))
+
+    def from_rows(value):
+        return [value] + [along_row(value, j) for j in range(1, row_count)]
+
+    def spread(blocks, bits):
+        new = dict(blocks)
+        for k in range(chips - 1, 0, -1):
+            if k.bit_count() == bits:
+                low = k & -k
+                new[k] = along_col(blocks[k ^ low], CORES * low)
+        return new
+
+    ring = [0, 1, 3, 2] if row_count == 4 else list(range(row_count))
+    def place_of(r):
+        return r ^ (r >> 1) if row_count == 4 else r
+
+    steps_away = (
+        (place_of(row_pos) - place_of(col_pos // ratio)) * (1 - 2 * (col_pos % CORES))
+    ) % row_count
+
+    def feature_step(value, s):
+        pairs = []
+        for c in range(col_count):
+            way = 1 - 2 * (c % CORES)
+            i = ring.index(c // ratio) + way * (s - 1)
+            here, there = ring[i % row_count], ring[(i + way) % row_count]
+            pairs.append((here * col_count + c, there * col_count + c))
+        return lax.ppermute(value, ("row", "col"), pairs)
+
     adjacency = mask(pattern, edge_weight)
-    panel = lax.all_gather(adjacency, "col", axis=0, tiled=False)
-    w_all = lax.all_gather(w_out, "col", axis=0, tiled=False)
-    columns = from_rows(adjacency, row_count)
+    adjacency, node_features = together((adjacency, node_features))
+    blocks = spread({0: adjacency}, 1)
+    other_pattern = along_col(pattern, 1)
+    other_pattern, node_features = together((other_pattern, node_features))
+    near = [1, 2] if row_count == 4 else list(range(1, row_count))
+    columns = {j: along_row(adjacency, j) for j in near}
     queries = project_in(core, [node_features], w_qkv, [0], 1.0 / math.sqrt(HDIM))
-    key_rows, queries = key_features(node_features, cols, row_count, col_count, queries)
-
-    other_rows = along_col(key_rows, 1)
-    other_pattern = along_col(pattern.astype(F32), 1).astype(jnp.int32)
-    keys_values = project_in(core, [key_rows, other_rows], w_qkv, [D, 2 * D])
+    queries, node_features = together((queries, node_features))
+    features = lax.dynamic_slice_in_dim(node_features, col_pos % ratio * cols, cols, 0)
+    moved = [features, feature_step(features, 1)]
+    queries, moved, columns, blocks = together((queries, moved, columns, blocks))
+
+    order = sorted(blocks)
+    swapped = along_col(jnp.stack([blocks[k] for k in order]), 1)
+    far = []
+    if row_count == 4:
+        half = rows // 2
+        far = [along_row(columns[2][:half], 1), along_row(columns[1][half:], 2)]
+    moved.append(feature_step(moved[-1], 2))
+    for bits in range(2, chips.bit_length()):
+        blocks = spread(blocks, bits)
+    moved, far, swapped, blocks = together((moved, far, swapped, blocks))
+    for s in range(3, row_count):
+        moved.append(feature_step(moved[-1], s))
+    panel = [(x, CORES * k, None) for k, x in blocks.items()]
+    panel += [(swapped, CORES * k + 1, i) for i, k in enumerate(order)]
+    panel += [(along_col(x, 1), CORES * k + 1, None) for k, x in blocks.items() if k not in order]
+    columns = [(0, 0, adjacency)] + [(j, 0, x) for j, x in columns.items()]
+    columns += [(3, i * x.shape[0], x) for i, x in enumerate(far)]
+    ranks = sweep(True, range(chips), place, pattern, panel, columns, [], 24 * 2**20)
+    columns = [(j, 0, x) for j, x in enumerate(from_rows(ranks))]
+
+    ranks, moved = together((ranks, moved))
+    key_rows = features
+    for s in range(1, row_count):
+        key_rows = jnp.where(steps_away == s, moved[s], key_rows)
+    keys_values = project_in(core, [key_rows, along_col(key_rows, 1)], w_qkv, [D, 2 * D], limit=28 * 2**20)
+    keys_values, w_out = together((keys_values, w_out))
+    w_all = spread({0: w_out}, 1)
     expo, peak = exponentials(pattern, other_pattern, queries, keys_values)
-
-    ranks = sweep(True, range(chips), place, pattern, panel, columns, node_features)
-    columns = from_rows(ranks, row_count)
-
-    parts = [None] * chips
-    for ks in (list(range(chips // 2, chips)), list(range(chips // 2))):
-        ranks = sweep(False, ks, place, pattern, panel, columns, peak)
+    w_all, peak = together((w_all, peak))
+    for bits in range(2, chips.bit_length()):
+        w_all = spread(w_all, bits)
+    w_all = [w_all[k] for k in range(chips)]
+
+    groups = [list(range(chips // 2, chips)), list(range(chips // 2))]
+    ranks = [sweep(False, ks, place, pattern, panel, columns, [peak], 24 * 2**20) for ks in groups]
+    others = [along_col(x, 1) for x in ranks]
+    parts, follows = [None] * chips, ranks[1]
+    for ks, own, other in zip(groups, ranks, others, strict=True):
         sums = weigh(
-            root, chips, ks, place, bias_gain, bias_rate, ranks, along_col(ranks, 1), expo,
-            keys_values, peak,
+            root, chips, ks, place, bias_gain, bias_rate, own, other, expo, keys_values, peak,
+            follows,
         )
         for k, part in zip(ks, sums, strict=True):
             parts[k] = part if k == 0 else along_col(part, CORES * k)
+        follows = sums[0]
     attended = divide(parts)
-    mixed = project_out(place, attended, along_col(attended, 1), w_all, chips)
+    mixed = project_out(place, attended, along_col(attended, 1), w_all)
     mixed = [x if k == 0 else along_col(x, CORES * k) for k, x in enumerate(mixed)]
     return assemble(place, mixed)
 

time: 175 us -> 157 us (0.90)
  starting transfers between devices: 30 us -> 45.4 us
  between operations: 13.6 us -> 0.32 us
  Pallas kernels: 54 us -> 41.4 us
  waiting for transfers between devices: 63.6 us -> 60.2 us
  local copies, waits for them, and re-layouts: 10.2 us -> 7.98 us
  other arithmetic: 2.94 us -> 0.95 us
    ppermute x10, waiting for transfers between devices: 43 us -> 14.4 us  [the longest x7 14.4 us: along_row(): return lax.ppermute(value, 'row', xor_pairs(row_count, j))]
    ppermute x11 -> x19, waiting for transfers between devices: 20.6 us -> 45.8 us  [along_col(): return lax.ppermute(value, 'col', xor_pairs(col_count, j))]
    ppermute x11 -> x19, starting transfers between devices: 9.06 us -> 18.4 us  [along_col(): return lax.ppermute(value, 'col', xor_pairs(col_count, j))]
    ppermute x10, starting transfers between devices: 20.8 us -> 27 us  [the longest x7 19.5 us: along_row(): return lax.ppermute(value, 'row', xor_pairs(row_count, j))]
    pallas_call x3, Pallas kernels: 15.1 us -> 10.9 us  [sweep(): pl.pallas_call(functools.partial(sweep_kernel, first, ks, chips, [at for...]
    pallas_call x2, Pallas kernels: 14.8 us -> 11.5 us  [weigh(): pl.pallas_call(functools.partial(weigh_kernel, root, ks, seg), out_shape=...]
    pallas_call x2, Pallas kernels: 8.9 us -> 6.48 us  [project_in(): pl.pallas_call(functools.partial(project_in_kernel, scale), out_shape=jax...]
    unnamed x32 -> x42, local copies, waits for them, and re-layouts: 7.63 us -> 7.87 us
  transfers between devices with their start and end apart: 23 -> 29, of which waited for: 12 -> 14; matrix products, arithmetic and copies ran while one was open for 3% -> 0% of each run, Pallas kernels for 29% -> 21%
where the time goes in v3:
time: 157 us; the launch traced here: 156 us
  waiting for transfers between devices  60.2 us (38%)
  starting transfers between devices  45.4 us (29%)
  Pallas kernels  41.4 us (26%)
  local copies, waits for them, and re-layouts  7.98 us (5%)
    ppermute x19, waiting for transfers between devices, along_col(): return lax.ppermute(value, 'col', xor_pairs(col_count, j))  45.8 us
    ppermute x7, starting transfers between devices, along_row(): return lax.ppermute(value, 'row', xor_pairs(row_count, j))  19.5 us
    ppermute x19, starting transfers between devices, along_col(): return lax.ppermute(value, 'col', xor_pairs(col_count, j))  18.4 us
    ppermute x7, waiting for transfers between devices, along_row(): return lax.ppermute(value, 'row', xor_pairs(row_count, j))  14.4 us
    pallas_call x2, Pallas kernels, weigh(): pl.pallas_call(functools.partial(weigh_kernel, root, ks, seg), out_shape=...  11.5 us
    pallas_call x3, Pallas kernels, sweep(): pl.pallas_call(functools.partial(sweep_kernel, first, ks, chips, [at for...  10.9 us
    pallas_call x1, Pallas kernels, exponentials(): pl.pallas_call(expo_kernel, out_shape=(jax.ShapeDtypeStruct((PAIRS, rows,...  8.34 us
    unnamed x42, local copies, waits for them, and re-layouts  7.87 us
  transfers between devices with their start and end apart: 29, of which 14 were waited for; matrix products, arithmetic and copies ran while one was open for 0% of the time, Pallas kernels for 21%

profile of v3, /device:TPU:0, one launch (start us, length us, event | category | flops | bytes accessed | tf_op | source)
XLA Modules:
  0.0 156.3 jit_solution(15217831115814779531)
XLA Ops:
  2.9 3.6 %project_in.2.q_ref = bf16[768,512]{1,0:T(8,128)(2,1)} custom-call(s32[1]{0:T(128)} %bitcast.3.place_ref, bf16[768,1024]{1,0:T(8,128)(2,1)} %refs_0_, bf16[1024,3072]{1,0:T(8,128)(2,1)} %refs_2_.1), custom_call_target="tpu_custom_call" | custom-call | flops 805306368 | bytes 2621440 | tf_op jit(solution)/shard_map/project_in/pallas_call | solution.py:96
  6.6 4.4 %collective-permute-start.1 = (bf16[384,1024]{1,0:T(8,128)(2,1)S(1)}, bf16[384,1024]{1,0:T(8,128)(2,1)S(1)}, u32[]{:S(2)}, u32[]{:S(2)}) collective-permute-start(bf16[384,1024]{1,0:T(8,128)(2,1)S(1)} %constant_dynamic-slice_fusion), channel_id=1, source_target_pairs={{0,8},{1,17},{10,26},{11,3},{20,4},{21,29},{30,22},{31,15}} | collective-permute-start | bytes 2359304 | tf_op jit(solution)/shard_map/ppermute | solution.py:517
  12.6 2.1 %collective-permute-start.3 = (bf16[768,384]{1,0:T(8,128)(2,1)S(1)}, bf16[768,384]{1,0:T(8,128)(2,1)S(1)}, u32[]{:S(2)}, u32[]{:S(2)}) collective-permute-start(bf16[768,384]{1,0:T(8,128)(2,1)S(1)} %mask.1.refs_0_.refs_8_), channel_id=1, source_target_pairs={{0,16},{8,24},{16,0},{24,8},{1,17},{9,25},{17,1},{25,9},{2,18},{10... | collective-permute-start | bytes 1769480 | tf_op jit(solution)/shard_map/ppermute | solution.py:489
  14.7 2.7 %collective-permute-start.2 = (bf16[768,384]{1,0:T(8,128)(2,1)S(1)}, bf16[768,384]{1,0:T(8,128)(2,1)S(1)}, u32[]{:S(2)}, u32[]{:S(2)}) collective-permute-start(bf16[768,384]{1,0:T(8,128)(2,1)S(1)} %mask.1.refs_0_.refs_8_), channel_id=1, source_target_pairs={{0,8},{8,0},{16,24},{24,16},{1,9},{9,1},{17,25},{25,17},{2,10},{10... | collective-permute-start | bytes 1769480 | tf_op jit(solution)/shard_map/ppermute | solution.py:489
  17.4 21.9 %collective-permute-done.5.refs_2_ = bf16[768,384]{1,0:T(8,128)(2,1)S(1)} collective-permute-done((bf16[768,384]{1,0:T(8,128)(2,1)S(1)}, bf16[768,384]{1,0:T(8,128)(2,1)S(1)}, u32[]{:S(2)}, u32[]{:S(2)}) %collective-permute-start.5) | collective-permute-done | bytes 589856 | tf_op jit(solution)/shard_map/ppermute | solution.py:486
  42.2 3.4 %collective-permute-start.8 = (bf16[384,384]{1,0:T(8,128)(2,1)S(1)}, bf16[384,384]{1,0:T(8,128)(2,1)S(1)}, u32[]{:S(2)}, u32[]{:S(2)}) collective-permute-start(bf16[384,384]{1,0:T(8,128)(2,1)S(1)} %slice.7), channel_id=1, source_target_pairs={{0,16},{8,24},{16,0},{24,8},{1,17},{9,25},{17,1},{25,9},{2,18},{10... | collective-permute-start | bytes 884744 | tf_op jit(solution)/shard_map/ppermute | solution.py:489
  45.6 3.2 %collective-permute-start.7 = (bf16[384,384]{1,0:T(8,128)(2,1)S(1)}, bf16[384,384]{1,0:T(8,128)(2,1)S(1)}, u32[]{:S(2)}, u32[]{:S(2)}) collective-permute-start(bf16[384,384]{1,0:T(8,128)(2,1)S(1)} %slice.6), channel_id=1, source_target_pairs={{0,8},{8,0},{16,24},{24,16},{1,9},{9,1},{17,25},{25,17},{2,10},{10... | collective-permute-start | bytes 884744 | tf_op jit(solution)/shard_map/ppermute | solution.py:489
  48.8 4.2 %collective-permute-done.8.refs_12_ = bf16[384,384]{1,0:T(8,128)(2,1)S(1)} collective-permute-done((bf16[384,384]{1,0:T(8,128)(2,1)S(1)}, bf16[384,384]{1,0:T(8,128)(2,1)S(1)}, u32[]{:S(2)}, u32[]{:S(2)}) %collective-permute-start.8) | collective-permute-done | bytes 294944 | tf_op jit(solution)/shard_map/ppermute | solution.py:489
  57.7 1.8 %collective-permute-start.11 = (bf16[768,384]{1,0:T(8,128)(2,1)}, bf16[768,384]{1,0:T(8,128)(2,1)}, u32[]{:S(2)}, u32[]{:S(2)}) collective-permute-start(bf16[768,384]{1,0:T(8,128)(2,1)} %collective-permute-done.10.refs_3_), channel_id=1, source_target_pairs={{0,1},{1,0},{2,3},{3,2},{4,5},{5,4},{6,7},{7,6},{8,9},{9,8},{10,11... | collective-permute-start | bytes 1769480 | tf_op jit(solution)/shard_map/ppermute | solution.py:486
  59.6 1.9 %collective-permute-done.11.refs_7_ = bf16[768,384]{1,0:T(8,128)(2,1)} collective-permute-done((bf16[768,384]{1,0:T(8,128)(2,1)}, bf16[768,384]{1,0:T(8,128)(2,1)}, u32[]{:S(2)}, u32[]{:S(2)}) %collective-permute-start.11) | collective-permute-done | bytes 589856 | tf_op jit(solution)/shard_map/ppermute | solution.py:486
  65.6 4.6 %rank_sweep.3.refs_8_ = bf16[768,384]{1,0:T(8,128)(2,1)S(1)} custom-call(s32[2]{0:T(128)S(1)} %pad_add_fusion.place_ref, s32[3,6]{1,0:T(4,128)S(1)} %bitcast.14, bf16[768,384]{1,0:T(8,128)(2,1)S(1)} %mask.1.refs_0_.refs_8_, bf16[768,384]{1,0:T(8,128)(2,1)S(1)} %collective-permute-done.4.refs_1_, bf16[768,384]{1,0:T(8,128)(2,1)S(1)} %collective-permute-done.5.refs_2_, ...), custom_call_target="tpu_custom_call" | custom-call | flops 1811939328 | bytes 9437184 | tf_op jit(solution)/shard_map/rank_sweep/pallas_call | solution.py:193
  71.3 7.5 %collective-permute-start.14 = (bf16[768,384]{1,0:T(8,128)(2,1)S(1)}, bf16[768,384]{1,0:T(8,128)(2,1)S(1)}, u32[]{:S(2)}, u32[]{:S(2)}) collective-permute-start(bf16[768,384]{1,0:T(8,128)(2,1)S(1)} %rank_sweep.3.refs_8_), channel_id=1, source_target_pairs={{0,24},{8,16},{16,8},{24,0},{1,25},{9,17},{17,9},{25,1},{2,26},{10... | collective-permute-start | bytes 1769480 | tf_op jit(solution)/shard_map/ppermute | solution.py:489
  79.4 2.8 %project_in.3.k_ref.v_ref = bf16[768,1024]{1,0:T(8,128)(2,1)S(1)} custom-call(s32[1]{0:T(128)} %bitcast.3.place_ref, bf16[384,1024]{1,0:T(8,128)(2,1)S(1)} %select_select_fusion.refs_0_, bf16[384,1024]{1,0:T(8,128)(2,1)S(1)} %collective-permute-done.16.refs_1_, bf16[1024,3072]{1,0:T(8,128)(2,1)S(1)} %bitcast.8), custom_call_target="tpu_custom_call" | custom-call | flops 1610612736 | bytes 3670016 | tf_op jit(solution)/shard_map/project_in/pallas_call | solution.py:96
  85.1 8.3 %expo.1 = (bf16[4,768,1536]{2,1,0:T(8,128)(2,1)S(1)}, f32[768,128]{1,0:T(8,128)S(1)}) custom-call(s32[3,6]{1,0:T(4,128)S(1)} %bitcast.15, s32[3,6]{1,0:T(4,128)S(1)} %collective-permute-done.other_ref, bf16[768,512]{1,0:T(8,128)(2,1)S(1)} %copy-done.4, bf16[768,1024]{1,0:T(8,128)(2,1)S(1)} %project_in.3.k_ref.v_ref), custom_call_target="tpu_custom_call" | custom-call | flops 2415919104 | bytes 9437184 | tf_op jit(solution)/shard_map/expo/pallas_call | solution.py:265
  93.4 3.5 %collective-permute-done.18.refs_2_ = bf16[1024,128]{1,0:T(8,128)(2,1)S(1)} collective-permute-done((bf16[1024,128]{1,0:T(8,128)(2,1)S(1)}, bf16[1024,128]{1,0:T(8,128)(2,1)S(1)}, u32[]{:S(2)}, u32[]{:S(2)}) %collective-permute-start.18) | collective-permute-done | bytes 262176 | tf_op jit(solution)/shard_map/ppermute | solution.py:486
  96.9 8.5 %collective-permute-done.13.refs_10_ = bf16[768,384]{1,0:T(8,128)(2,1)S(1)} collective-permute-done((bf16[768,384]{1,0:T(8,128)(2,1)S(1)}, bf16[768,384]{1,0:T(8,128)(2,1)S(1)}, u32[]{:S(2)}, u32[]{:S(2)}) %collective-permute-start.13) | collective-permute-done | bytes 589856 | tf_op jit(solution)/shard_map/ppermute | solution.py:489
  105.4 3.1 %rank_sweep.5.own_ref = bf16[384,384]{1,0:T(8,128)(2,1)S(1)} custom-call(s32[2]{0:T(128)S(1)} %pad_add_fusion.place_ref, s32[3,6]{1,0:T(4,128)S(1)} %bitcast.16, bf16[768,384]{1,0:T(8,128)(2,1)S(1)} %mask.1.refs_0_.refs_8_, bf16[768,384]{1,0:T(8,128)(2,1)S(1)} %collective-permute-done.4.refs_1_, bf16[768,384]{1,0:T(8,128)(2,1)S(1)} %collective-permute-done.5.refs_2_, ...), custom_call_target="tpu_custom_call" | custom-call | flops 905969664 | bytes 7077888 | tf_op jit(solution)/shard_map/rank_sweep/pallas_call | solution.py:193
  108.7 3.1 %rank_sweep.4.refs_0_.own_ref = bf16[384,384]{1,0:T(8,128)(2,1)S(1)} custom-call(s32[2]{0:T(128)S(1)} %pad_add_fusion.place_ref, s32[3,6]{1,0:T(4,128)S(1)} %bitcast.17, bf16[768,384]{1,0:T(8,128)(2,1)S(1)} %mask.1.refs_0_.refs_8_, bf16[768,384]{1,0:T(8,128)(2,1)S(1)} %collective-permute-done.4.refs_1_, bf16[768,384]{1,0:T(8,128)(2,1)S(1)} %collective-permute-done.5.refs_2_, ...), custom_call_target="tpu_custom_call" | custom-call | flops 905969664 | bytes 7077888 | tf_op jit(solution)/shard_map/rank_sweep/pallas_call | solution.py:193
  112.4 5.7 %weigh.2 = (bf16[192,640]{1,0:T(8,128)(2,1)S(1)}, bf16[192,640]{1,0:T(8,128)(2,1)S(1)}) custom-call(s32[2]{0:T(128)S(1)} %pad_add_fusion.place_ref, f32[16]{0:T(128)S(1)} %copy-done.13, f32[16]{0:T(128)S(1)} %copy-done.14, bf16[384,384]{1,0:T(8,128)(2,1)S(1)} %rank_sweep.5.own_ref, bf16[384,384]{1,0:T(8,128)(2,1)S(1)} %collective-permute-done.20.other_ref, ...), custom_call_target="tpu_custom_call" | custom-call | flops 1207959552 | bytes 4718592 | tf_op jit(solution)/shard_map/weigh/pallas_call | solution.py:366
  119.0 2.9 %collective-permute-start.22 = (bf16[192,640]{1,0:T(8,128)(2,1)S(1)}, bf16[192,640]{1,0:T(8,128)(2,1)S(1)}, u32[]{:S(2)}, u32[]{:S(2)}) collective-permute-start(bf16[192,640]{1,0:T(8,128)(2,1)S(1)} %get-tuple-element.76.refs_0_), channel_id=1, source_target_pairs={{0,4},{1,5},{2,6},{3,7},{4,0},{5,1},{6,2},{7,3},{8,12},{9,13},{10,... | collective-permute-start | bytes 737288 | tf_op jit(solution)/shard_map/ppermute | solution.py:486
  121.9 5.7 %weigh.3 = (bf16[192,640]{1,0:T(8,128)(2,1)S(1)}, bf16[192,640]{1,0:T(8,128)(2,1)S(1)}) custom-call(s32[2]{0:T(128)S(1)} %pad_add_fusion.place_ref, f32[16]{0:T(128)S(1)} %copy-done.13, f32[16]{0:T(128)S(1)} %copy-done.14, bf16[384,384]{1,0:T(8,128)(2,1)S(1)} %rank_sweep.4.refs_0_.own_ref, bf16[384,384]{1,0:T(8,128)(2,1)S(1)} %collective-permute-done.19.other_ref, ...), custom_call_target="tpu_custom_call" | custom-call | flops 1207959552 | bytes 4718592 | tf_op jit(solution)/shard_map/weigh/pallas_call | solution.py:366
  129.8 13.9 %collective-permute-done.22.refs_2_ = bf16[192,640]{1,0:T(8,128)(2,1)S(1)} collective-permute-done((bf16[192,640]{1,0:T(8,128)(2,1)S(1)}, bf16[192,640]{1,0:T(8,128)(2,1)S(1)}, u32[]{:S(2)}, u32[]{:S(2)}) %collective-permute-start.22) | collective-permute-done | bytes 245792 | tf_op jit(solution)/shard_map/ppermute | solution.py:486
  149.2 2.9 %collective-permute-start.28 = (bf16[192,128]{1,0:T(8,128)(2,1)S(1)}, bf16[192,128]{1,0:T(8,128)(2,1)S(1)}, u32[]{:S(2)}, u32[]{:S(2)}) collective-permute-start(bf16[192,128]{1,0:T(8,128)(2,1)S(1)} %get-tuple-element.86), channel_id=1, source_target_pairs={{0,6},{1,7},{2,4},{3,5},{4,2},{5,3},{6,0},{7,1},{8,14},{9,15},{10,... | collective-permute-start | bytes 147464 | tf_op jit(solution)/shard_map/ppermute | solution.py:486
  152.4 2.7 %collective-permute-done.27.refs_2_ = bf16[192,128]{1,0:T(8,128)(2,1)S(1)} collective-permute-done((bf16[192,128]{1,0:T(8,128)(2,1)S(1)}, bf16[192,128]{1,0:T(8,128)(2,1)S(1)}, u32[]{:S(2)}, u32[]{:S(2)}) %collective-permute-start.27) | collective-permute-done | bytes 49184 | tf_op jit(solution)/shard_map/ppermute | solution.py:486
  (95 shorter events, 31.4 us)
Async XLA Ops:
  6.6 32.7 %collective-permute-start.1 = (bf16[384,1024]{1,0:T(8,128)(2,1)S(1)}, bf16[384,1024]{1,0:T(8,128)(2,1)S(1)}, u32[]{:S(2)}, u32[]{:S(2)}) collective-permute-start(bf16[384,1024]{1,0:T(8,128)(2,1)S(1)} %constant_dynamic-slice_fusion), channel_id=1, source_target_pairs={{0,8},{1,17},{10,26},{11,3},{20,4},{21,29},{30,22},{31,15}} | collective-permute-start | bytes 2359304 | tf_op jit(solution)/shard_map/ppermute | solution.py:517
  11.1 28.2 %collective-permute-start.5 = (bf16[768,384]{1,0:T(8,128)(2,1)S(1)}, bf16[768,384]{1,0:T(8,128)(2,1)S(1)}, u32[]{:S(2)}, u32[]{:S(2)}) collective-permute-start(bf16[768,384]{1,0:T(8,128)(2,1)S(1)} %mask.1.refs_0_.refs_8_), channel_id=1, source_target_pairs={{0,4},{1,5},{2,6},{3,7},{4,0},{5,1},{6,2},{7,3},{8,12},{9,13},{10,... | collective-permute-start | bytes 1769480 | tf_op jit(solution)/shard_map/ppermute | solution.py:486
  11.6 27.8 %collective-permute-start.4 = (bf16[768,384]{1,0:T(8,128)(2,1)S(1)}, bf16[768,384]{1,0:T(8,128)(2,1)S(1)}, u32[]{:S(2)}, u32[]{:S(2)}) collective-permute-start(bf16[768,384]{1,0:T(8,128)(2,1)S(1)} %mask.1.refs_0_.refs_8_), channel_id=1, source_target_pairs={{0,2},{1,3},{2,0},{3,1},{4,6},{5,7},{6,4},{7,5},{8,10},{9,11},{10,... | collective-permute-start | bytes 1769480 | tf_op jit(solution)/shard_map/ppermute | solution.py:486
  12.6 26.8 %collective-permute-start.3 = (bf16[768,384]{1,0:T(8,128)(2,1)S(1)}, bf16[768,384]{1,0:T(8,128)(2,1)S(1)}, u32[]{:S(2)}, u32[]{:S(2)}) collective-permute-start(bf16[768,384]{1,0:T(8,128)(2,1)S(1)} %mask.1.refs_0_.refs_8_), channel_id=1, source_target_pairs={{0,16},{8,24},{16,0},{24,8},{1,17},{9,25},{17,1},{25,9},{2,18},{10... | collective-permute-start | bytes 1769480 | tf_op jit(solution)/shard_map/ppermute | solution.py:489
  14.7 24.7 %collective-permute-start.2 = (bf16[768,384]{1,0:T(8,128)(2,1)S(1)}, bf16[768,384]{1,0:T(8,128)(2,1)S(1)}, u32[]{:S(2)}, u32[]{:S(2)}) collective-permute-start(bf16[768,384]{1,0:T(8,128)(2,1)S(1)} %mask.1.refs_0_.refs_8_), channel_id=1, source_target_pairs={{0,8},{8,0},{16,24},{24,16},{1,9},{9,1},{17,25},{25,17},{2,10},{10... | collective-permute-start | bytes 1769480 | tf_op jit(solution)/shard_map/ppermute | solution.py:489
  39.6 16.5 %collective-permute-start.9 = (bf16[3,768,384]{2,1,0:T(8,128)(2,1)S(1)}, bf16[3,768,384]{2,1,0:T(8,128)(2,1)S(1)}, u32[]{:S(2)}, u32[]{:S(2)}) collective-permute-start(bf16[3,768,384]{2,1,0:T(8,128)(2,1)S(1)} %pad_maximum_fusion), channel_id=1, source_target_pairs={{0,1},{1,0},{2,3},{3,2},{4,5},{5,4},{6,7},{7,6},{8,9},{9,8},{10,11... | collective-permute-start | bytes 5308424 | tf_op jit(solution)/shard_map/ppermute | solution.py:486
  40.3 15.9 %collective-permute-start.6 = (bf16[384,1024]{1,0:T(8,128)(2,1)S(1)}, bf16[384,1024]{1,0:T(8,128)(2,1)}, u32[]{:S(2)}, u32[]{:S(2)}) collective-permute-start(bf16[384,1024]{1,0:T(8,128)(2,1)S(1)} %collective-permute-done.1), channel_id=1, source_target_pairs={{8,24},{17,25},{26,18},{3,19},{4,12},{29,13},{22,6},{15,7}} | collective-permute-start | bytes 2359304 | tf_op jit(solution)/shard_map/ppermute | solution.py:517
  41.9 14.3 %collective-permute-start.10 = (bf16[768,384]{1,0:T(8,128)(2,1)S(1)}, bf16[768,384]{1,0:T(8,128)(2,1)}, u32[]{:S(2)}, u32[]{:S(2)}) collective-permute-start(bf16[768,384]{1,0:T(8,128)(2,1)S(1)} %collective-permute-done.5.refs_2_), channel_id=1, source_target_pairs={{0,2},{1,3},{2,0},{3,1},{4,6},{5,7},{6,4},{7,5},{8,10},{9,11},{10,... | collective-permute-start | bytes 1769480 | tf_op jit(solution)/shard_map/ppermute | solution.py:486
  42.2 10.8 %collective-permute-start.8 = (bf16[384,384]{1,0:T(8,128)(2,1)S(1)}, bf16[384,384]{1,0:T(8,128)(2,1)S(1)}, u32[]{:S(2)}, u32[]{:S(2)}) collective-permute-start(bf16[384,384]{1,0:T(8,128)(2,1)S(1)} %slice.7), channel_id=1, source_target_pairs={{0,16},{8,24},{16,0},{24,8},{1,17},{9,25},{17,1},{25,9},{2,18},{10... | collective-permute-start | bytes 884744 | tf_op jit(solution)/shard_map/ppermute | solution.py:489
  45.6 9.7 %collective-permute-start.7 = (bf16[384,384]{1,0:T(8,128)(2,1)S(1)}, bf16[384,384]{1,0:T(8,128)(2,1)S(1)}, u32[]{:S(2)}, u32[]{:S(2)}) collective-permute-start(bf16[384,384]{1,0:T(8,128)(2,1)S(1)} %slice.6), channel_id=1, source_target_pairs={{0,8},{8,0},{16,24},{24,16},{1,9},{9,1},{17,25},{25,17},{2,10},{10... | collective-permute-start | bytes 884744 | tf_op jit(solution)/shard_map/ppermute | solution.py:489
  56.2 14.0 %collective-permute-start.15 = (bf16[384,1024]{1,0:T(8,128)(2,1)}, bf16[384,1024]{1,0:T(8,128)(2,1)}, u32[]{:S(2)}, u32[]{:S(2)}) collective-permute-start(bf16[384,1024]{1,0:T(8,128)(2,1)} %collective-permute-done.6), channel_id=1, source_target_pairs={{24,16},{25,9},{18,2},{19,27},{12,28},{13,5},{6,14},{7,23}} | collective-permute-start | bytes 2359304 | tf_op jit(solution)/shard_map/ppermute | solution.py:517
  70.9 8.5 %collective-permute-start.16 = (bf16[384,1024]{1,0:T(8,128)(2,1)S(1)}, bf16[384,1024]{1,0:T(8,128)(2,1)S(1)}, u32[]{:S(2)}, u32[]{:S(2)}) collective-permute-start(bf16[384,1024]{1,0:T(8,128)(2,1)S(1)} %select_select_fusion.refs_0_), channel_id=1, source_target_pairs={{0,1},{1,0},{2,3},{3,2},{4,5},{5,4},{6,7},{7,6},{8,9},{9,8},{10,11... | collective-permute-start | bytes 2359304 | tf_op jit(solution)/shard_map/ppermute | solution.py:486
  71.3 25.6 %collective-permute-start.14 = (bf16[768,384]{1,0:T(8,128)(2,1)S(1)}, bf16[768,384]{1,0:T(8,128)(2,1)S(1)}, u32[]{:S(2)}, u32[]{:S(2)}) collective-permute-start(bf16[768,384]{1,0:T(8,128)(2,1)S(1)} %rank_sweep.3.refs_8_), channel_id=1, source_target_pairs={{0,24},{8,16},{16,8},{24,0},{1,25},{9,17},{17,9},{25,1},{2,26},{10... | collective-permute-start | bytes 1769480 | tf_op jit(solution)/shard_map/ppermute | solution.py:489
  78.9 26.5 %collective-permute-start.13 = (bf16[768,384]{1,0:T(8,128)(2,1)S(1)}, bf16[768,384]{1,0:T(8,128)(2,1)S(1)}, u32[]{:S(2)}, u32[]{:S(2)}) collective-permute-start(bf16[768,384]{1,0:T(8,128)(2,1)S(1)} %rank_sweep.3.refs_8_), channel_id=1, source_target_pairs={{0,16},{8,24},{16,0},{24,8},{1,17},{9,25},{17,1},{25,9},{2,18},{10... | collective-permute-start | bytes 1769480 | tf_op jit(solution)/shard_map/ppermute | solution.py:489
  78.9 26.6 %collective-permute-start.12 = (bf16[768,384]{1,0:T(8,128)(2,1)S(1)}, bf16[768,384]{1,0:T(8,128)(2,1)S(1)}, u32[]{:S(2)}, u32[]{:S(2)}) collective-permute-start(bf16[768,384]{1,0:T(8,128)(2,1)S(1)} %rank_sweep.3.refs_8_), channel_id=1, source_target_pairs={{0,8},{8,0},{16,24},{24,16},{1,9},{9,1},{17,25},{25,17},{2,10},{10... | collective-permute-start | bytes 1769480 | tf_op jit(solution)/shard_map/ppermute | solution.py:489
  82.3 14.6 %collective-permute-start.18 = (bf16[1024,128]{1,0:T(8,128)(2,1)S(1)}, bf16[1024,128]{1,0:T(8,128)(2,1)S(1)}, u32[]{:S(2)}, u32[]{:S(2)}) collective-permute-start(bf16[1024,128]{1,0:T(8,128)(2,1)S(1)} %copy-done.10), channel_id=1, source_target_pairs={{0,4},{1,5},{2,6},{3,7},{4,0},{5,1},{6,2},{7,3},{8,12},{9,13},{10,... | collective-permute-start | bytes 786440 | tf_op jit(solution)/shard_map/ppermute | solution.py:486
  83.8 13.0 %collective-permute-start.17 = (bf16[1024,128]{1,0:T(8,128)(2,1)S(1)}, bf16[1024,128]{1,0:T(8,128)(2,1)S(1)}, u32[]{:S(2)}, u32[]{:S(2)}) collective-permute-start(bf16[1024,128]{1,0:T(8,128)(2,1)S(1)} %copy-done.10), channel_id=1, source_target_pairs={{0,2},{1,3},{2,0},{3,1},{4,6},{5,7},{6,4},{7,5},{8,10},{9,11},{10,... | collective-permute-start | bytes 786440 | tf_op jit(solution)/shard_map/ppermute | solution.py:486
  111.8 10.2 %collective-permute-start.19 = (bf16[384,384]{1,0:T(8,128)(2,1)S(1)}, bf16[384,384]{1,0:T(8,128)(2,1)S(1)}, u32[]{:S(2)}, u32[]{:S(2)}) collective-permute-start(bf16[384,384]{1,0:T(8,128)(2,1)S(1)} %rank_sweep.4.refs_0_.own_ref), channel_id=1, source_target_pairs={{0,1},{1,0},{2,3},{3,2},{4,5},{5,4},{6,7},{7,6},{8,9},{9,8},{10,11... | collective-permute-start | bytes 884744 | tf_op jit(solution)/shard_map/ppermute | solution.py:486
  118.1 11.7 %collective-permute-start.23 = (bf16[192,640]{1,0:T(8,128)(2,1)S(1)}, bf16[192,640]{1,0:T(8,128)(2,1)S(1)}, u32[]{:S(2)}, u32[]{:S(2)}) collective-permute-start(bf16[192,640]{1,0:T(8,128)(2,1)S(1)} %get-tuple-element.79), channel_id=1, source_target_pairs={{0,6},{1,7},{2,4},{3,5},{4,2},{5,3},{6,0},{7,1},{8,14},{9,15},{10,... | collective-permute-start | bytes 737288 | tf_op jit(solution)/shard_map/ppermute | solution.py:486
  119.0 24.7 %collective-permute-start.22 = (bf16[192,640]{1,0:T(8,128)(2,1)S(1)}, bf16[192,640]{1,0:T(8,128)(2,1)S(1)}, u32[]{:S(2)}, u32[]{:S(2)}) collective-permute-start(bf16[192,640]{1,0:T(8,128)(2,1)S(1)} %get-tuple-element.76.refs_0_), channel_id=1, source_target_pairs={{0,4},{1,5},{2,6},{3,7},{4,0},{5,1},{6,2},{7,3},{8,12},{9,13},{10,... | collective-permute-start | bytes 737288 | tf_op jit(solution)/shard_map/ppermute | solution.py:486
  127.7 16.0 %collective-permute-start.21 = (bf16[192,640]{1,0:T(8,128)(2,1)S(1)}, bf16[192,640]{1,0:T(8,128)(2,1)S(1)}, u32[]{:S(2)}, u32[]{:S(2)}) collective-permute-start(bf16[192,640]{1,0:T(8,128)(2,1)S(1)} %get-tuple-element.78), channel_id=1, source_target_pairs={{0,2},{1,3},{2,0},{3,1},{4,6},{5,7},{6,4},{7,5},{8,10},{9,11},{10,... | collective-permute-start | bytes 737288 | tf_op jit(solution)/shard_map/ppermute | solution.py:486
  128.4 17.6 %collective-permute-start.25 = (bf16[1024,128]{1,0:T(8,128)(2,1)S(1)}, bf16[1024,128]{1,0:T(8,128)(2,1)S(1)}, u32[]{:S(2)}, u32[]{:S(2)}) collective-permute-start(bf16[1024,128]{1,0:T(8,128)(2,1)S(1)} %collective-permute-done.18.refs_2_), channel_id=1, source_target_pairs={{0,2},{1,3},{2,0},{3,1},{4,6},{5,7},{6,4},{7,5},{8,10},{9,11},{10,... | collective-permute-start | bytes 786440 | tf_op jit(solution)/shard_map/ppermute | solution.py:486
  147.7 7.4 %collective-permute-start.27 = (bf16[192,128]{1,0:T(8,128)(2,1)S(1)}, bf16[192,128]{1,0:T(8,128)(2,1)S(1)}, u32[]{:S(2)}, u32[]{:S(2)}) collective-permute-start(bf16[192,128]{1,0:T(8,128)(2,1)S(1)} %get-tuple-element.85), channel_id=1, source_target_pairs={{0,4},{1,5},{2,6},{3,7},{4,0},{5,1},{6,2},{7,3},{8,12},{9,13},{10,... | collective-permute-start | bytes 147464 | tf_op jit(solution)/shard_map/ppermute | solution.py:486
  149.2 5.9 %collective-permute-start.28 = (bf16[192,128]{1,0:T(8,128)(2,1)S(1)}, bf16[192,128]{1,0:T(8,128)(2,1)S(1)}, u32[]{:S(2)}, u32[]{:S(2)}) collective-permute-start(bf16[192,128]{1,0:T(8,128)(2,1)S(1)} %get-tuple-element.86), channel_id=1, source_target_pairs={{0,6},{1,7},{2,4},{3,5},{4,2},{5,3},{6,0},{7,1},{8,14},{9,15},{10,... | collective-permute-start | bytes 147464 | tf_op jit(solution)/shard_map/ppermute | solution.py:486
  (26 other events, 138.5 us)

commit v4 on v3

--- a/solution.py
+++ b/solution.py
@@ -15,7 +15,7 @@
 CORES = 2
 PAIRS = HEADS // 2 // CORES
 WIDTH = D // CORES
-STEP = 8
+EXTRA = 4 * PAIRS
 LANES = 128
 VMEM_LIMIT = 58 * 2**20
 SMALL_LIMIT = 16 * 2**20
@@ -53,24 +53,34 @@
     return jnp.concatenate(tiles, axis=0)
 
 
-def mask_kernel(pattern_ref, weight_ref, out_ref):
+def start_kernel(place_ref, pattern_ref, weight_ref, features_ref, out_ref, cut_ref, sem):
+    cols = cut_ref.shape[0]
+    ratio = features_ref.shape[0] // cols
+    at = pl.multiple_of(lax.rem(place_ref[1], ratio) * cols, cols)
+    copy = pltpu.make_async_copy(features_ref.at[pl.ds(at, cols), :], cut_ref, sem)
+    copy.start()
     for i in range(out_ref.shape[0] // BLK):
         at = slice(i * BLK, (i + 1) * BLK)
         keep = keep_tile(pattern_ref, i, 1)
         out_ref[at, :] = jnp.where(keep > 0, weight_ref[at, :].astype(F32), 0.0).astype(BF16)
-
-
-def mask(pattern, weight):
+    copy.wait()
+
+
+def start(place, pattern, weight, features):
     rows, cols = weight.shape
     return pl.pallas_call(
-        mask_kernel,
-        out_shape=jax.ShapeDtypeStruct((rows, cols), BF16),
-        in_specs=[SMEM, VMEM],
-        out_specs=VMEM,
-        compiler_params=params(SMALL_LIMIT),
+        start_kernel,
+        out_shape=(
+            jax.ShapeDtypeStruct((rows, cols), BF16),
+            jax.ShapeDtypeStruct((cols, features.shape[1]), BF16),
+        ),
+        in_specs=[SMEM, SMEM, VMEM, HBM],
+        out_specs=(VMEM, VMEM),
+        scratch_shapes=[pltpu.SemaphoreType.DMA],
+        compiler_params=params(),
         cost_estimate=cost(rows * cols, 4 * rows * cols),
-        name="mask",
-    )(pattern, weight)
+        name="start",
+    )(place, pattern, weight, features)
 
 
 def project_in_kernel(scale, place_ref, *refs):
@@ -122,7 +132,7 @@
     chip, core = lax.div(col_pos, CORES), lax.rem(col_pos, CORES)
     starts = [pl.multiple_of(lax.bitwise_xor(chip, k) * seg, seg) for k in ks]
     if len(ks) == chips:
-        starts = [n * seg for n in range(chips)]
+        starts, seg = [0], rows
 
     def right_copy(i):
         xor, offset = right_at[i]
@@ -140,7 +150,7 @@
                 yield pltpu.make_async_copy(
                     block.at[pl.ds(start, seg), :],
                     left_ref.at[k, pl.ds(n * seg, seg), pl.ds(at, cols)],
-                    left_sem.at[k, j % CORES * len(ks) + n],
+                    left_sem.at[k, j % CORES * len(starts) + n],
                 )
 
     for j in range(n_right):
@@ -153,9 +163,7 @@
     for k in range(chips):
         for copy in left_copies(k):
             copy.wait()
-        product = jnp.dot(
-            left_ref[k], right_ref[k], preferred_element_type=F32
-        )
+        product = jnp.dot(left_ref[k], right_ref[k], preferred_element_type=F32)
         if k == 0:
             acc_ref[...] = product
         elif k < chips - 1:
@@ -340,22 +348,27 @@
         now = []
         for i, out_ref in enumerate(out_refs):
             part = sums[i * seg : (i + 1) * seg, :]
-            out_ref[:, lanes] = part[:, :LANES].astype(BF16)
+            out_ref[:seg, lanes] = part[:, :LANES].astype(BF16)
             now.append(jnp.where(out_lane % HDIM == p, part[:, LANES:], totals[i]))
         return tuple(now)
 
     totals = lax.fori_loop(
         0, PAIRS, pair, tuple(jnp.zeros((seg, LANES), F32) for _ in ks)
     )
+    half = WIDTH // 2
     for i, out_ref in enumerate(out_refs):
         extra = totals[i]
         rest = peak_ref[pl.ds(starts[i], seg), :]
         for n in range(1, 4):
             piece = rest.astype(BF16).astype(F32)
             rest = rest - piece
-            here = (out_lane % HDIM >= n * STEP) & (out_lane % HDIM < n * STEP + PAIRS)
-            extra = jnp.where(here, pltpu.roll(piece, n * STEP, 1), extra)
-        out_ref[:, WIDTH:] = extra.astype(BF16)
+            here = (out_lane % HDIM >= n * PAIRS) & (out_lane % HDIM < (n + 1) * PAIRS)
+            extra = jnp.where(here, pltpu.roll(piece, n * PAIRS, 1), extra)
+        extra = jnp.concatenate([extra, jnp.zeros((half - seg, LANES), F32)], axis=0).T
+        for side in range(2):
+            out_ref[seg:, side * half : (side + 1) * half] = extra[
+                side * HDIM : side * HDIM + EXTRA
+            ].astype(BF16)
 
 
 def weigh(root, chips, ks, place, gain, rate, own, other, expo, values, peak, follows):
@@ -365,7 +378,7 @@
     work = n_rows * keys * 2 * PAIRS
     return pl.pallas_call(
         functools.partial(weigh_kernel, root, ks, seg),
-        out_shape=(jax.ShapeDtypeStruct((seg, WIDTH + LANES), BF16),) * len(ks),
+        out_shape=(jax.ShapeDtypeStruct((seg + EXTRA, WIDTH), BF16),) * len(ks),
         grid=(1,),
         in_specs=[
             SMEM,
@@ -378,7 +391,7 @@
             pl.BlockSpec((rows, LANES), lambda i: (0, 0)),
             HBM,
         ],
-        out_specs=(pl.BlockSpec((seg, WIDTH + LANES), lambda i: (0, 0)),) * len(ks),
+        out_specs=(pl.BlockSpec((seg + EXTRA, WIDTH), lambda i: (0, 0)),) * len(ks),
         scratch_shapes=[
             pltpu.VMEM((PAIRS, n_rows, 2 * keys), BF16),
             pltpu.VMEM((n_rows, 2 * keys), BF16),
@@ -394,25 +407,56 @@
 
 def divide_kernel(*refs):
     parts, out_ref = refs[:-1], refs[-1]
-    extras = [part[:, WIDTH:].astype(F32) for part in parts]
-    seg = extras[0].shape[0]
-    peaks = [sum(pltpu.roll(x, LANES - n * STEP, 1) for n in range(1, 4)) for x in extras]
-    largest = functools.reduce(jnp.maximum, peaks)
+    seg, half = out_ref.shape[0], WIDTH // 2
+    lane = lax.broadcasted_iota(jnp.int32, (seg, LANES), 1)
+    fit = LANES // (2 * EXTRA)
+    totals, peaks, largest = [], [], None
+    for first in range(0, len(parts), fit):
+        group = parts[first : first + fit]
+        extra = [
+            part[seg:, side * half : (side + 1) * half].astype(F32)
+            for part in group
+            for side in range(2)
+        ]
+        spare = LANES - EXTRA * len(extra)
+        if spare:
+            extra.append(jnp.zeros((spare, half), F32))
+        extra = jnp.concatenate(extra, axis=0).T[:seg]
+        totals.append(extra)
+        peak = sum(pltpu.roll(extra, LANES - n * PAIRS, 1) for n in range(1, 4))
+        if spare:
+            peak = jnp.where(lane < LANES - spare, peak, -jnp.inf)
+        peaks.append(peak)
+        largest = peak if largest is None else jnp.maximum(largest, peak)
+
+    def over_parts(value, combine):
+        step = 2 * EXTRA
+        while step < LANES:
+            value = combine(value, pltpu.roll(value, step, 1))
+            step *= 2
+        return value
+
+    largest = over_parts(largest, jnp.maximum)
     weights = [jnp.exp(peak - largest) for peak in peaks]
-    inverse = 1.0 / sum(w * x for w, x in zip(weights, extras, strict=True))
+    inverse = 1.0 / over_parts(
+        sum(w * x for w, x in zip(weights, totals, strict=True)), lambda x, y: x + y
+    )
     scales = [w * inverse for w in weights]
-    lane = lax.broadcasted_iota(jnp.int32, (seg, LANES), 1)
     for p in range(PAIRS):
         lanes = slice(p * LANES, (p + 1) * LANES)
         total = jnp.zeros((seg, LANES), F32)
-        for part, scale in zip(parts, scales, strict=True):
-            both = jnp.where(lane < HDIM, scale[:, p : p + 1], scale[:, HDIM + p : HDIM + p + 1])
-            total += part[:, lanes].astype(F32) * both
+        for i, part in enumerate(parts):
+            at = i % fit * 2 * EXTRA + p
+            scale = scales[i // fit]
+            both = jnp.where(
+                lane < HDIM, scale[:, at : at + 1], scale[:, at + EXTRA : at + EXTRA + 1]
+            )
+            total += part[:seg, lanes].astype(F32) * both
         out_ref[:, lanes] = total.astype(BF16)
 
 
 def divide(parts):
-    seg = parts[0].shape[0]
+    seg = parts[0].shape[0] - EXTRA
     return pl.pallas_call(
         divide_kernel,
         out_shape=jax.ShapeDtypeStruct((seg, WIDTH), BF16),
@@ -516,17 +560,14 @@
             pairs.append((here * col_count + c, there * col_count + c))
         return lax.ppermute(value, ("row", "col"), pairs)
 
-    adjacency = mask(pattern, edge_weight)
-    adjacency, node_features = together((adjacency, node_features))
+    adjacency, features = start(place, pattern, edge_weight, node_features)
     blocks = spread({0: adjacency}, 1)
-    other_pattern = along_col(pattern, 1)
-    other_pattern, node_features = together((other_pattern, node_features))
     near = [1, 2] if row_count == 4 else list(range(1, row_count))
     columns = {j: along_row(adjacency, j) for j in near}
+    other_pattern = along_col(pattern, 1)
     queries = project_in(core, [node_features], w_qkv, [0], 1.0 / math.sqrt(HDIM))
-    queries, node_features = together((queries, node_features))
-    features = lax.dynamic_slice_in_dim(node_features, col_pos % ratio * cols, cols, 0)
     moved = [features, feature_step(features, 1)]
+    raw_columns = columns
     queries, moved, columns, blocks = together((queries, moved, columns, blocks))
 
     order = sorted(blocks)
@@ -538,14 +579,15 @@
     moved.append(feature_step(moved[-1], 2))
     for bits in range(2, chips.bit_length()):
         blocks = spread(blocks, bits)
-    moved, far, swapped, blocks = together((moved, far, swapped, blocks))
+    raw_far = far
+    far, swapped, blocks = together((far, swapped, blocks))
     for s in range(3, row_count):
         moved.append(feature_step(moved[-1], s))
     panel = [(x, CORES * k, None) for k, x in blocks.items()]
     panel += [(swapped, CORES * k + 1, i) for i, k in enumerate(order)]
     panel += [(along_col(x, 1), CORES * k + 1, None) for k, x in blocks.items() if k not in order]
-    columns = [(0, 0, adjacency)] + [(j, 0, x) for j, x in columns.items()]
-    columns += [(3, i * x.shape[0], x) for i, x in enumerate(far)]
+    columns = [(0, 0, adjacency)] + [(j, 0, x) for j, x in raw_columns.items()]
+    columns += [(3, i * x.shape[0], x) for i, x in enumerate(raw_far)]
     ranks = sweep(True, range(chips), place, pattern, panel, columns, [], 24 * 2**20)
     columns = [(j, 0, x) for j, x in enumerate(from_rows(ranks))]
 

time: 157 us -> 152 us (0.968)
  waiting for transfers between devices: 60.2 us -> 48.7 us
  local copies, waits for them, and re-layouts: 7.98 us -> 11.3 us
  Pallas kernels: 41.4 us -> 44.1 us
    ppermute x19, waiting for transfers between devices: 45.8 us -> 39.3 us  [along_col(): return lax.ppermute(value, 'col', xor_pairs(col_count, j))]
    ppermute x7, waiting for transfers between devices: 14.4 us -> 9.43 us  [along_row(): return lax.ppermute(value, 'row', xor_pairs(row_count, j))]
    pallas_call x1, Pallas kernels: 0.68 us -> 3.29 us  [start(): pl.pallas_call(start_kernel, out_shape=(jax.ShapeDtypeStruct((rows, cols)...]
    slice x2, local copies, waits for them, and re-layouts: 0.06 us -> 1.98 us  [shards(): far = [along_row(columns[2][:half], 1), along_row(columns[1][half:], 2)]]
    unnamed x42 -> x34, local copies, waits for them, and re-layouts: 7.87 us -> 9.32 us
  transfers between devices with their start and end apart: 29 -> 29, of which waited for: 14 -> 12; matrix products, arithmetic and copies ran while one was open for 0% -> 1% of each run, Pallas kernels for 21% -> 23%
where the time goes in v4:
time: 152 us; the launch traced here: 151 us
  waiting for transfers between devices  48.7 us (32%)
  starting transfers between devices  45.9 us (30%)
  Pallas kernels  44.1 us (29%)
  local copies, waits for them, and re-layouts  11.3 us (7%)
    ppermute x19, waiting for transfers between devices, along_col(): return lax.ppermute(value, 'col', xor_pairs(col_count, j))  39.3 us
    ppermute x19, starting transfers between devices, along_col(): return lax.ppermute(value, 'col', xor_pairs(col_count, j))  18.9 us
    ppermute x7, starting transfers between devices, along_row(): return lax.ppermute(value, 'row', xor_pairs(row_count, j))  18.2 us
    pallas_call x2, Pallas kernels, weigh(): pl.pallas_call(functools.partial(weigh_kernel, root, ks, seg), out_shape=...  11.6 us
    pallas_call x3, Pallas kernels, sweep(): pl.pallas_call(functools.partial(sweep_kernel, first, ks, chips, [at for...  10.8 us
    ppermute x7, waiting for transfers between devices, along_row(): return lax.ppermute(value, 'row', xor_pairs(row_count, j))  9.43 us
    unnamed x34, local copies, waits for them, and re-layouts  9.32 us
    ppermute x3, starting transfers between devices, feature_step(): return lax.ppermute(value, ('row', 'col'), pairs)  8.84 us
  transfers between devices with their start and end apart: 29, of which 12 were waited for; matrix products, arithmetic and copies ran while one was open for 1% of the time, Pallas kernels for 23%

profile of v4, /device:TPU:0, one launch (start us, length us, event | category | flops | bytes accessed | tf_op | source)
XLA Modules:
  0.0 151.4 jit_solution(2478942805054115650)
XLA Ops:
  0.6 3.3 %start.1 = (bf16[768,384]{1,0:T(8,128)(2,1)}, bf16[384,1024]{1,0:T(8,128)(2,1)}) custom-call(s32[2]{0:T(128)} %pad_add_fusion.place_ref, s32[3,6]{1,0:T(4,128)} %bitcast.10, bf16[768,384]{1,0:T(8,128)(2,1)} %weight_ref.1, bf16[768,1024]{1,0:T(8,128)(2,1)} %features_ref.1), custom_call_target="tpu_custom_call" | custom-call | flops 294912 | bytes 1179648 | tf_op jit(solution)/shard_map/start/pallas_call | solution.py:71
  3.9 5.7 %collective-permute-start = (bf16[384,1024]{1,0:T(8,128)(2,1)}, bf16[384,1024]{1,0:T(8,128)(2,1)}, u32[]{:S(2)}, u32[]{:S(2)}) collective-permute-start(bf16[384,1024]{1,0:T(8,128)(2,1)} %get-tuple-element.38), channel_id=1, source_target_pairs={{0,8},{1,17},{10,26},{11,3},{20,4},{21,29},{30,22},{31,15}} | collective-permute-start | bytes 2359304 | tf_op jit(solution)/shard_map/ppermute | solution.py:561
  12.8 3.1 %collective-permute-start.1 = (bf16[768,384]{1,0:T(8,128)(2,1)}, bf16[768,384]{1,0:T(8,128)(2,1)S(1)}, u32[]{:S(2)}, u32[]{:S(2)}) collective-permute-start(bf16[768,384]{1,0:T(8,128)(2,1)} %get-tuple-element.45.refs_0_.refs_8_), channel_id=1, source_target_pairs={{0,8},{8,0},{16,24},{24,16},{1,9},{9,1},{17,25},{25,17},{2,10},{10... | collective-permute-start | bytes 1769480 | tf_op jit(solution)/shard_map/ppermute | solution.py:533
  15.9 3.6 %project_in.2.q_ref = bf16[768,512]{1,0:T(8,128)(2,1)} custom-call(s32[1]{0:T(128)} %bitcast.3.place_ref, bf16[768,1024]{1,0:T(8,128)(2,1)} %features_ref.1, bf16[1024,3072]{1,0:T(8,128)(2,1)} %refs_2_.1), custom_call_target="tpu_custom_call" | custom-call | flops 805306368 | bytes 2621440 | tf_op jit(solution)/shard_map/project_in/pallas_call | solution.py:106
  19.5 17.3 %collective-permute-done.4.refs_2_ = bf16[768,384]{1,0:T(8,128)(2,1)S(1)} collective-permute-done((bf16[768,384]{1,0:T(8,128)(2,1)}, bf16[768,384]{1,0:T(8,128)(2,1)S(1)}, u32[]{:S(2)}, u32[]{:S(2)}) %collective-permute-start.4) | collective-permute-done | bytes 589856 | tf_op jit(solution)/shard_map/ppermute | solution.py:530
  42.6 3.7 %collective-permute-start.6 = (bf16[384,384]{1,0:T(8,128)(2,1)S(1)}, bf16[384,384]{1,0:T(8,128)(2,1)S(1)}, u32[]{:S(2)}, u32[]{:S(2)}) collective-permute-start(bf16[384,384]{1,0:T(8,128)(2,1)S(1)} %slice.7), channel_id=1, source_target_pairs={{0,16},{8,24},{16,0},{24,8},{1,17},{9,25},{17,1},{25,9},{2,18},{10... | collective-permute-start | bytes 884744 | tf_op jit(solution)/shard_map/ppermute | solution.py:533
  46.2 3.4 %collective-permute-start.5 = (bf16[384,384]{1,0:T(8,128)(2,1)S(1)}, bf16[384,384]{1,0:T(8,128)(2,1)S(1)}, u32[]{:S(2)}, u32[]{:S(2)}) collective-permute-start(bf16[384,384]{1,0:T(8,128)(2,1)S(1)} %slice.6), channel_id=1, source_target_pairs={{0,8},{8,0},{16,24},{24,16},{1,9},{9,1},{17,25},{25,17},{2,10},{10... | collective-permute-start | bytes 884744 | tf_op jit(solution)/shard_map/ppermute | solution.py:533
  53.7 2.8 %collective-permute-done.5.refs_11_ = bf16[384,384]{1,0:T(8,128)(2,1)S(1)} collective-permute-done((bf16[384,384]{1,0:T(8,128)(2,1)S(1)}, bf16[384,384]{1,0:T(8,128)(2,1)S(1)}, u32[]{:S(2)}, u32[]{:S(2)}) %collective-permute-start.5) | collective-permute-done | bytes 294944 | tf_op jit(solution)/shard_map/ppermute | solution.py:533
  63.7 4.6 %rank_sweep.3.refs_8_ = bf16[768,384]{1,0:T(8,128)(2,1)S(1)} custom-call(s32[2]{0:T(128)S(1)} %copy-done.13, s32[3,6]{1,0:T(4,128)S(1)} %bitcast.11, bf16[768,384]{1,0:T(8,128)(2,1)S(1)} %copy-done.1, bf16[768,384]{1,0:T(8,128)(2,1)S(1)} %collective-permute-done.3.refs_1_, bf16[768,384]{1,0:T(8,128)(2,1)S(1)} %collective-permute-done.4.refs_2_, ...), custom_call_target="tpu_custom_call" | custom-call | flops 1811939328 | bytes 9437184 | tf_op jit(solution)/shard_map/rank_sweep/pallas_call | solution.py:201
  68.7 5.7 %collective-permute-start.12 = (bf16[768,384]{1,0:T(8,128)(2,1)S(1)}, bf16[768,384]{1,0:T(8,128)(2,1)S(1)}, u32[]{:S(2)}, u32[]{:S(2)}) collective-permute-start(bf16[768,384]{1,0:T(8,128)(2,1)S(1)} %rank_sweep.3.refs_8_), channel_id=1, source_target_pairs={{0,24},{8,16},{16,8},{24,0},{1,25},{9,17},{17,9},{25,1},{2,26},{10... | collective-permute-start | bytes 1769480 | tf_op jit(solution)/shard_map/ppermute | solution.py:533
  75.0 2.8 %copy-done = bf16[1024,3072]{1,0:T(8,128)(2,1)S(1)} copy-done((bf16[1024,3072]{1,0:T(8,128)(2,1)S(1)}, bf16[1024,3072]{1,0:T(8,128)(2,1)}, u32[]{:S(2)}) %copy-start) | copy-done | bytes 6291480
  77.8 2.8 %project_in.3.k_ref.v_ref = bf16[768,1024]{1,0:T(8,128)(2,1)S(1)} custom-call(s32[1]{0:T(128)} %bitcast.3.place_ref, bf16[384,1024]{1,0:T(8,128)(2,1)S(1)} %select_select_fusion.refs_0_, bf16[384,1024]{1,0:T(8,128)(2,1)S(1)} %collective-permute-done.15.refs_1_, bf16[1024,3072]{1,0:T(8,128)(2,1)S(1)} %copy-done), custom_call_target="tpu_custom_call" | custom-call | flops 1610612736 | bytes 3670016 | tf_op jit(solution)/shard_map/project_in/pallas_call | solution.py:106
  82.8 2.3 %collective-permute-start.16 = (bf16[1024,128]{1,0:T(8,128)(2,1)S(1)}, bf16[1024,128]{1,0:T(8,128)(2,1)S(1)}, u32[]{:S(2)}, u32[]{:S(2)}) collective-permute-start(bf16[1024,128]{1,0:T(8,128)(2,1)S(1)} %copy-done.11), channel_id=1, source_target_pairs={{0,2},{1,3},{2,0},{3,1},{4,6},{5,7},{6,4},{7,5},{8,10},{9,11},{10,... | collective-permute-start | bytes 786440 | tf_op jit(solution)/shard_map/ppermute | solution.py:530
  85.1 8.3 %expo.1 = (bf16[4,768,1536]{2,1,0:T(8,128)(2,1)S(1)}, f32[768,128]{1,0:T(8,128)S(1)}) custom-call(s32[3,6]{1,0:T(4,128)S(1)} %bitcast.13, s32[3,6]{1,0:T(4,128)S(1)} %collective-permute-done.18.other_ref, bf16[768,512]{1,0:T(8,128)(2,1)S(1)} %copy-done.6, bf16[768,1024]{1,0:T(8,128)(2,1)S(1)} %project_in.3.k_ref.v_ref), custom_call_target="tpu_custom_call" | custom-call | flops 2415919104 | bytes 9437184 | tf_op jit(solution)/shard_map/expo/pallas_call | solution.py:273
  93.4 2.5 %collective-permute-done.17.refs_2_ = bf16[1024,128]{1,0:T(8,128)(2,1)S(1)} collective-permute-done((bf16[1024,128]{1,0:T(8,128)(2,1)S(1)}, bf16[1024,128]{1,0:T(8,128)(2,1)S(1)}, u32[]{:S(2)}, u32[]{:S(2)}) %collective-permute-start.17) | collective-permute-done | bytes 262176 | tf_op jit(solution)/shard_map/ppermute | solution.py:530
  95.9 4.8 %collective-permute-done.11.refs_10_ = bf16[768,384]{1,0:T(8,128)(2,1)S(1)} collective-permute-done((bf16[768,384]{1,0:T(8,128)(2,1)S(1)}, bf16[768,384]{1,0:T(8,128)(2,1)S(1)}, u32[]{:S(2)}, u32[]{:S(2)}) %collective-permute-start.11) | collective-permute-done | bytes 589856 | tf_op jit(solution)/shard_map/ppermute | solution.py:533
  100.7 3.1 %rank_sweep.5.own_ref = bf16[384,384]{1,0:T(8,128)(2,1)S(1)} custom-call(s32[2]{0:T(128)S(1)} %copy-done.13, s32[3,6]{1,0:T(4,128)S(1)} %bitcast.14, bf16[768,384]{1,0:T(8,128)(2,1)S(1)} %copy-done.1, bf16[768,384]{1,0:T(8,128)(2,1)S(1)} %collective-permute-done.3.refs_1_, bf16[768,384]{1,0:T(8,128)(2,1)S(1)} %collective-permute-done.4.refs_2_, ...), custom_call_target="tpu_custom_call" | custom-call | flops 905969664 | bytes 7077888 | tf_op jit(solution)/shard_map/rank_sweep/pallas_call | solution.py:201
  104.0 3.1 %rank_sweep.4.refs_0_.own_ref = bf16[384,384]{1,0:T(8,128)(2,1)S(1)} custom-call(s32[2]{0:T(128)S(1)} %copy-done.13, s32[3,6]{1,0:T(4,128)S(1)} %bitcast.15, bf16[768,384]{1,0:T(8,128)(2,1)S(1)} %copy-done.1, bf16[768,384]{1,0:T(8,128)(2,1)S(1)} %collective-permute-done.3.refs_1_, bf16[768,384]{1,0:T(8,128)(2,1)S(1)} %collective-permute-done.4.refs_2_, ...), custom_call_target="tpu_custom_call" | custom-call | flops 905969664 | bytes 7077888 | tf_op jit(solution)/shard_map/rank_sweep/pallas_call | solution.py:201
  107.7 5.8 %weigh.2 = (bf16[208,512]{1,0:T(8,128)(2,1)S(1)}, bf16[208,512]{1,0:T(8,128)(2,1)S(1)}) custom-call(s32[2]{0:T(128)S(1)} %copy-done.13, f32[16]{0:T(128)S(1)} %copy-done.14, f32[16]{0:T(128)S(1)} %copy-done.15, bf16[384,384]{1,0:T(8,128)(2,1)S(1)} %rank_sweep.5.own_ref, bf16[384,384]{1,0:T(8,128)(2,1)S(1)} %collective-permute-done.20.other_ref, ...), custom_call_target="tpu_custom_call" | custom-call | flops 1207959552 | bytes 4718592 | tf_op jit(solution)/shard_map/weigh/pallas_call | solution.py:379
  113.5 3.0 %collective-permute-start.23 = (bf16[208,512]{1,0:T(8,128)(2,1)S(1)}, bf16[208,512]{1,0:T(8,128)(2,1)S(1)}, u32[]{:S(2)}, u32[]{:S(2)}) collective-permute-start(bf16[208,512]{1,0:T(8,128)(2,1)S(1)} %get-tuple-element.63), channel_id=1, source_target_pairs={{0,6},{1,7},{2,4},{3,5},{4,2},{5,3},{6,0},{7,1},{8,14},{9,15},{10,... | collective-permute-start | bytes 638984 | tf_op jit(solution)/shard_map/ppermute | solution.py:530
  118.5 5.8 %weigh.3 = (bf16[208,512]{1,0:T(8,128)(2,1)S(1)}, bf16[208,512]{1,0:T(8,128)(2,1)S(1)}) custom-call(s32[2]{0:T(128)S(1)} %copy-done.13, f32[16]{0:T(128)S(1)} %copy-done.14, f32[16]{0:T(128)S(1)} %copy-done.15, bf16[384,384]{1,0:T(8,128)(2,1)S(1)} %rank_sweep.4.refs_0_.own_ref, bf16[384,384]{1,0:T(8,128)(2,1)S(1)} %collective-permute-done.19.other_ref, ...), custom_call_target="tpu_custom_call" | custom-call | flops 1207959552 | bytes 4718592 | tf_op jit(solution)/shard_map/weigh/pallas_call | solution.py:379
  126.5 9.9 %collective-permute-done.22.refs_2_ = bf16[208,512]{1,0:T(8,128)(2,1)S(1)} collective-permute-done((bf16[208,512]{1,0:T(8,128)(2,1)S(1)}, bf16[208,512]{1,0:T(8,128)(2,1)S(1)}, u32[]{:S(2)}, u32[]{:S(2)}) %collective-permute-start.22) | collective-permute-done | bytes 213024 | tf_op jit(solution)/shard_map/ppermute | solution.py:530
  138.7 2.5 %collective-permute-done.25.refs_3_ = bf16[1024,128]{1,0:T(8,128)(2,1)S(1)} collective-permute-done((bf16[1024,128]{1,0:T(8,128)(2,1)S(1)}, bf16[1024,128]{1,0:T(8,128)(2,1)S(1)}, u32[]{:S(2)}, u32[]{:S(2)}) %collective-permute-start.25) | collective-permute-done | bytes 262176 | tf_op jit(solution)/shard_map/ppermute | solution.py:530
  144.2 2.6 %collective-permute-start.28 = (bf16[192,128]{1,0:T(8,128)(2,1)S(1)}, bf16[192,128]{1,0:T(8,128)(2,1)S(1)}, u32[]{:S(2)}, u32[]{:S(2)}) collective-permute-start(bf16[192,128]{1,0:T(8,128)(2,1)S(1)} %get-tuple-element.70), channel_id=1, source_target_pairs={{0,6},{1,7},{2,4},{3,5},{4,2},{5,3},{6,0},{7,1},{8,14},{9,15},{10,... | collective-permute-start | bytes 147464 | tf_op jit(solution)/shard_map/ppermute | solution.py:530
  (85 shorter events, 38.5 us)
Async XLA Ops:
  3.9 33.4 %collective-permute-start = (bf16[384,1024]{1,0:T(8,128)(2,1)}, bf16[384,1024]{1,0:T(8,128)(2,1)}, u32[]{:S(2)}, u32[]{:S(2)}) collective-permute-start(bf16[384,1024]{1,0:T(8,128)(2,1)} %get-tuple-element.38), channel_id=1, source_target_pairs={{0,8},{1,17},{10,26},{11,3},{20,4},{21,29},{30,22},{31,15}} | collective-permute-start | bytes 2359304 | tf_op jit(solution)/shard_map/ppermute | solution.py:561
  9.7 27.1 %collective-permute-start.4 = (bf16[768,384]{1,0:T(8,128)(2,1)}, bf16[768,384]{1,0:T(8,128)(2,1)S(1)}, u32[]{:S(2)}, u32[]{:S(2)}) collective-permute-start(bf16[768,384]{1,0:T(8,128)(2,1)} %get-tuple-element.45.refs_0_.refs_8_), channel_id=1, source_target_pairs={{0,4},{1,5},{2,6},{3,7},{4,0},{5,1},{6,2},{7,3},{8,12},{9,13},{10,... | collective-permute-start | bytes 1769480 | tf_op jit(solution)/shard_map/ppermute | solution.py:530
  9.7 27.7 %collective-permute-start.3 = (bf16[768,384]{1,0:T(8,128)(2,1)}, bf16[768,384]{1,0:T(8,128)(2,1)S(1)}, u32[]{:S(2)}, u32[]{:S(2)}) collective-permute-start(bf16[768,384]{1,0:T(8,128)(2,1)} %get-tuple-element.45.refs_0_.refs_8_), channel_id=1, source_target_pairs={{0,2},{1,3},{2,0},{3,1},{4,6},{5,7},{6,4},{7,5},{8,10},{9,11},{10,... | collective-permute-start | bytes 1769480 | tf_op jit(solution)/shard_map/ppermute | solution.py:530
  11.1 26.2 %collective-permute-start.2 = (bf16[768,384]{1,0:T(8,128)(2,1)}, bf16[768,384]{1,0:T(8,128)(2,1)S(1)}, u32[]{:S(2)}, u32[]{:S(2)}) collective-permute-start(bf16[768,384]{1,0:T(8,128)(2,1)} %get-tuple-element.45.refs_0_.refs_8_), channel_id=1, source_target_pairs={{0,16},{8,24},{16,0},{24,8},{1,17},{9,25},{17,1},{25,9},{2,18},{10... | collective-permute-start | bytes 1769480 | tf_op jit(solution)/shard_map/ppermute | solution.py:533
  12.8 24.6 %collective-permute-start.1 = (bf16[768,384]{1,0:T(8,128)(2,1)}, bf16[768,384]{1,0:T(8,128)(2,1)S(1)}, u32[]{:S(2)}, u32[]{:S(2)}) collective-permute-start(bf16[768,384]{1,0:T(8,128)(2,1)} %get-tuple-element.45.refs_0_.refs_8_), channel_id=1, source_target_pairs={{0,8},{8,0},{16,24},{24,16},{1,9},{9,1},{17,25},{25,17},{2,10},{10... | collective-permute-start | bytes 1769480 | tf_op jit(solution)/shard_map/ppermute | solution.py:533
  38.6 18.7 %collective-permute-start.7 = (bf16[3,768,384]{2,1,0:T(8,128)(2,1)S(1)}, bf16[3,768,384]{2,1,0:T(8,128)(2,1)S(1)}, u32[]{:S(2)}, u32[]{:S(2)}) collective-permute-start(bf16[3,768,384]{2,1,0:T(8,128)(2,1)S(1)} %pad_maximum_fusion), channel_id=1, source_target_pairs={{0,1},{1,0},{2,3},{3,2},{4,5},{5,4},{6,7},{7,6},{8,9},{9,8},{10,11... | collective-permute-start | bytes 5308424 | tf_op jit(solution)/shard_map/ppermute | solution.py:530
  38.7 11.0 %collective-permute-start.13 = (bf16[384,1024]{1,0:T(8,128)(2,1)}, bf16[384,1024]{1,0:T(8,128)(2,1)}, u32[]{:S(2)}, u32[]{:S(2)}) collective-permute-start(bf16[384,1024]{1,0:T(8,128)(2,1)} %collective-permute-done), channel_id=1, source_target_pairs={{8,24},{17,25},{26,18},{3,19},{4,12},{29,13},{22,6},{15,7}} | collective-permute-start | bytes 2359304 | tf_op jit(solution)/shard_map/ppermute | solution.py:561
  40.2 17.1 %collective-permute-start.8 = (bf16[768,384]{1,0:T(8,128)(2,1)S(1)}, bf16[768,384]{1,0:T(8,128)(2,1)}, u32[]{:S(2)}, u32[]{:S(2)}) collective-permute-start(bf16[768,384]{1,0:T(8,128)(2,1)S(1)} %collective-permute-done.4.refs_2_), channel_id=1, source_target_pairs={{0,2},{1,3},{2,0},{3,1},{4,6},{5,7},{6,4},{7,5},{8,10},{9,11},{10,... | collective-permute-start | bytes 1769480 | tf_op jit(solution)/shard_map/ppermute | solution.py:530
  42.6 10.5 %collective-permute-start.6 = (bf16[384,384]{1,0:T(8,128)(2,1)S(1)}, bf16[384,384]{1,0:T(8,128)(2,1)S(1)}, u32[]{:S(2)}, u32[]{:S(2)}) collective-permute-start(bf16[384,384]{1,0:T(8,128)(2,1)S(1)} %slice.7), channel_id=1, source_target_pairs={{0,16},{8,24},{16,0},{24,8},{1,17},{9,25},{17,1},{25,9},{2,18},{10... | collective-permute-start | bytes 884744 | tf_op jit(solution)/shard_map/ppermute | solution.py:533
  46.2 10.3 %collective-permute-start.5 = (bf16[384,384]{1,0:T(8,128)(2,1)S(1)}, bf16[384,384]{1,0:T(8,128)(2,1)S(1)}, u32[]{:S(2)}, u32[]{:S(2)}) collective-permute-start(bf16[384,384]{1,0:T(8,128)(2,1)S(1)} %slice.6), channel_id=1, source_target_pairs={{0,8},{8,0},{16,24},{24,16},{1,9},{9,1},{17,25},{25,17},{2,10},{10... | collective-permute-start | bytes 884744 | tf_op jit(solution)/shard_map/ppermute | solution.py:533
  49.7 18.6 %collective-permute-start.14 = (bf16[384,1024]{1,0:T(8,128)(2,1)}, bf16[384,1024]{1,0:T(8,128)(2,1)}, u32[]{:S(2)}, u32[]{:S(2)}) collective-permute-start(bf16[384,1024]{1,0:T(8,128)(2,1)} %collective-permute-done.13), channel_id=1, source_target_pairs={{24,16},{25,9},{18,2},{19,27},{12,28},{13,5},{6,14},{7,23}} | collective-permute-start | bytes 2359304 | tf_op jit(solution)/shard_map/ppermute | solution.py:561
  68.5 6.5 %collective-permute-start.15 = (bf16[384,1024]{1,0:T(8,128)(2,1)S(1)}, bf16[384,1024]{1,0:T(8,128)(2,1)S(1)}, u32[]{:S(2)}, u32[]{:S(2)}) collective-permute-start(bf16[384,1024]{1,0:T(8,128)(2,1)S(1)} %select_select_fusion.refs_0_), channel_id=1, source_target_pairs={{0,1},{1,0},{2,3},{3,2},{4,5},{5,4},{6,7},{7,6},{8,9},{9,8},{10,11... | collective-permute-start | bytes 2359304 | tf_op jit(solution)/shard_map/ppermute | solution.py:530
  68.7 27.2 %collective-permute-start.12 = (bf16[768,384]{1,0:T(8,128)(2,1)S(1)}, bf16[768,384]{1,0:T(8,128)(2,1)S(1)}, u32[]{:S(2)}, u32[]{:S(2)}) collective-permute-start(bf16[768,384]{1,0:T(8,128)(2,1)S(1)} %rank_sweep.3.refs_8_), channel_id=1, source_target_pairs={{0,24},{8,16},{16,8},{24,0},{1,25},{9,17},{17,9},{25,1},{2,26},{10... | collective-permute-start | bytes 1769480 | tf_op jit(solution)/shard_map/ppermute | solution.py:533
  74.4 26.3 %collective-permute-start.11 = (bf16[768,384]{1,0:T(8,128)(2,1)S(1)}, bf16[768,384]{1,0:T(8,128)(2,1)S(1)}, u32[]{:S(2)}, u32[]{:S(2)}) collective-permute-start(bf16[768,384]{1,0:T(8,128)(2,1)S(1)} %rank_sweep.3.refs_8_), channel_id=1, source_target_pairs={{0,16},{8,24},{16,0},{24,8},{1,17},{9,25},{17,1},{25,9},{2,18},{10... | collective-permute-start | bytes 1769480 | tf_op jit(solution)/shard_map/ppermute | solution.py:533
  74.5 26.3 %collective-permute-start.10 = (bf16[768,384]{1,0:T(8,128)(2,1)S(1)}, bf16[768,384]{1,0:T(8,128)(2,1)S(1)}, u32[]{:S(2)}, u32[]{:S(2)}) collective-permute-start(bf16[768,384]{1,0:T(8,128)(2,1)S(1)} %rank_sweep.3.refs_8_), channel_id=1, source_target_pairs={{0,8},{8,0},{16,24},{24,16},{1,9},{9,1},{17,25},{25,17},{2,10},{10... | collective-permute-start | bytes 1769480 | tf_op jit(solution)/shard_map/ppermute | solution.py:533
  75.0 7.8 %collective-permute-start.18 = (s32[3,6]{1,0:T(4,128)S(1)}, s32[3,6]{1,0:T(4,128)S(1)}, u32[]{:S(2)}, u32[]{:S(2)}) collective-permute-start(s32[3,6]{1,0:T(4,128)S(1)} %bitcast.12), channel_id=1, source_target_pairs={{0,1},{1,0},{2,3},{3,2},{4,5},{5,4},{6,7},{7,6},{8,9},{9,8},{10,11... | collective-permute-start | bytes 224 | tf_op jit(solution)/shard_map/ppermute | solution.py:530
  80.6 15.3 %collective-permute-start.17 = (bf16[1024,128]{1,0:T(8,128)(2,1)S(1)}, bf16[1024,128]{1,0:T(8,128)(2,1)S(1)}, u32[]{:S(2)}, u32[]{:S(2)}) collective-permute-start(bf16[1024,128]{1,0:T(8,128)(2,1)S(1)} %copy-done.11), channel_id=1, source_target_pairs={{0,4},{1,5},{2,6},{3,7},{4,0},{5,1},{6,2},{7,3},{8,12},{9,13},{10,... | collective-permute-start | bytes 786440 | tf_op jit(solution)/shard_map/ppermute | solution.py:530
  82.8 13.1 %collective-permute-start.16 = (bf16[1024,128]{1,0:T(8,128)(2,1)S(1)}, bf16[1024,128]{1,0:T(8,128)(2,1)S(1)}, u32[]{:S(2)}, u32[]{:S(2)}) collective-permute-start(bf16[1024,128]{1,0:T(8,128)(2,1)S(1)} %copy-done.11), channel_id=1, source_target_pairs={{0,2},{1,3},{2,0},{3,1},{4,6},{5,7},{6,4},{7,5},{8,10},{9,11},{10,... | collective-permute-start | bytes 786440 | tf_op jit(solution)/shard_map/ppermute | solution.py:530
  107.1 11.5 %collective-permute-start.19 = (bf16[384,384]{1,0:T(8,128)(2,1)S(1)}, bf16[384,384]{1,0:T(8,128)(2,1)S(1)}, u32[]{:S(2)}, u32[]{:S(2)}) collective-permute-start(bf16[384,384]{1,0:T(8,128)(2,1)S(1)} %rank_sweep.4.refs_0_.own_ref), channel_id=1, source_target_pairs={{0,1},{1,0},{2,3},{3,2},{4,5},{5,4},{6,7},{7,6},{8,9},{9,8},{10,11... | collective-permute-start | bytes 884744 | tf_op jit(solution)/shard_map/ppermute | solution.py:530
  113.5 13.0 %collective-permute-start.23 = (bf16[208,512]{1,0:T(8,128)(2,1)S(1)}, bf16[208,512]{1,0:T(8,128)(2,1)S(1)}, u32[]{:S(2)}, u32[]{:S(2)}) collective-permute-start(bf16[208,512]{1,0:T(8,128)(2,1)S(1)} %get-tuple-element.63), channel_id=1, source_target_pairs={{0,6},{1,7},{2,4},{3,5},{4,2},{5,3},{6,0},{7,1},{8,14},{9,15},{10,... | collective-permute-start | bytes 638984 | tf_op jit(solution)/shard_map/ppermute | solution.py:530
  116.4 19.9 %collective-permute-start.22 = (bf16[208,512]{1,0:T(8,128)(2,1)S(1)}, bf16[208,512]{1,0:T(8,128)(2,1)S(1)}, u32[]{:S(2)}, u32[]{:S(2)}) collective-permute-start(bf16[208,512]{1,0:T(8,128)(2,1)S(1)} %get-tuple-element.60.refs_0_), channel_id=1, source_target_pairs={{0,4},{1,5},{2,6},{3,7},{4,0},{5,1},{6,2},{7,3},{8,12},{9,13},{10,... | collective-permute-start | bytes 638984 | tf_op jit(solution)/shard_map/ppermute | solution.py:530
  124.4 12.8 %collective-permute-start.21 = (bf16[208,512]{1,0:T(8,128)(2,1)S(1)}, bf16[208,512]{1,0:T(8,128)(2,1)S(1)}, u32[]{:S(2)}, u32[]{:S(2)}) collective-permute-start(bf16[208,512]{1,0:T(8,128)(2,1)S(1)} %get-tuple-element.62), channel_id=1, source_target_pairs={{0,2},{1,3},{2,0},{3,1},{4,6},{5,7},{6,4},{7,5},{8,10},{9,11},{10,... | collective-permute-start | bytes 638984 | tf_op jit(solution)/shard_map/ppermute | solution.py:530
  124.4 16.8 %collective-permute-start.25 = (bf16[1024,128]{1,0:T(8,128)(2,1)S(1)}, bf16[1024,128]{1,0:T(8,128)(2,1)S(1)}, u32[]{:S(2)}, u32[]{:S(2)}) collective-permute-start(bf16[1024,128]{1,0:T(8,128)(2,1)S(1)} %collective-permute-done.17.refs_2_), channel_id=1, source_target_pairs={{0,2},{1,3},{2,0},{3,1},{4,6},{5,7},{6,4},{7,5},{8,10},{9,11},{10,... | collective-permute-start | bytes 786440 | tf_op jit(solution)/shard_map/ppermute | solution.py:530
  144.2 5.9 %collective-permute-start.28 = (bf16[192,128]{1,0:T(8,128)(2,1)S(1)}, bf16[192,128]{1,0:T(8,128)(2,1)S(1)}, u32[]{:S(2)}, u32[]{:S(2)}) collective-permute-start(bf16[192,128]{1,0:T(8,128)(2,1)S(1)} %get-tuple-element.70), channel_id=1, source_target_pairs={{0,6},{1,7},{2,4},{3,5},{4,2},{5,3},{6,0},{7,1},{8,14},{9,15},{10,... | collective-permute-start | bytes 147464 | tf_op jit(solution)/shard_map/ppermute | solution.py:530
  (22 other events, 135.3 us)

commit v5 on v4

--- a/solution.py
+++ b/solution.py
@@ -134,11 +134,14 @@
     if len(ks) == chips:
         starts, seg = [0], rows
 
-    def right_copy(i):
+    part = min(ref.shape[0] for ref in rights)
+
+    def right_copies(i, slot):
         xor, offset = right_at[i]
-        slot = lax.bitwise_xor(lax.bitwise_xor(row_pos, chip), xor)
-        target = right_ref.at[slot, pl.ds(offset, rights[i].shape[0]), :]
-        return pltpu.make_async_copy(rights[i], target, right_sem.at[i])
+        for at in range(0, rights[i].shape[0], part):
+            target = right_ref.at[slot, pl.ds(offset + at, part), :]
+            source = rights[i].at[pl.ds(at, part), :]
+            yield pltpu.make_async_copy(source, target, right_sem.at[slot, (offset + at) // part])
 
     def left_copies(k):
         for ref, (j, index) in zip(panel, left_at, strict=True):
@@ -153,14 +156,22 @@
                     left_sem.at[k, j % CORES * len(starts) + n],
                 )
 
-    for j in range(n_right):
-        right_copy(j).start()
     for k in range(chips):
         for copy in left_copies(k):
             copy.start()
-    for j in range(n_right):
-        right_copy(j).wait()
+        for xor in sorted({at[0] for at in right_at}):
+
+            @pl.when(lax.bitwise_xor(row_pos, chip) == xor ^ k)
+            def _():
+                for i in range(n_right):
+                    if right_at[i][0] == xor:
+                        for copy in right_copies(i, k):
+                            copy.start()
+
     for k in range(chips):
+        for at in range(0, rows, part):
+            half = right_ref.at[k, pl.ds(at, part), :]
+            pltpu.make_async_copy(half, half, right_sem.at[k, at // part]).wait()
         for copy in left_copies(k):
             copy.wait()
         product = jnp.dot(left_ref[k], right_ref[k], preferred_element_type=F32)
@@ -215,7 +226,7 @@
             pltpu.VMEM((depth // rows, rows, cols), BF16),
             pltpu.VMEM((n_rows, cols), F32),
             pltpu.SemaphoreType.DMA((chips, CORES * len(ks))),
-            pltpu.SemaphoreType.DMA((len(blocks),)),
+            pltpu.SemaphoreType.DMA((chips, rows // min(x.shape[0] for *_, x in blocks))),
         ],
         compiler_params=params(limit),
         cost_estimate=cost(2 * n_rows * depth * cols, 2 * (n_rows + rows) * depth),
@@ -298,23 +309,13 @@
     root, ks, seg, place_ref, gain_ref, rate_ref, own_ref, other_ref, expo_ref, v_ref, peak_ref,
     *refs,
 ):
-    out_refs, (e_ref, p_ref, ranks_ref, right_ref, sem) = refs[-5 - len(ks) : -5], refs[-5:]
+    out_refs, (p_ref, ranks_ref, right_ref) = refs[-3 - len(ks) : -3], refs[-3:]
     cols = own_ref.shape[1]
     keys = 2 * cols
     chip = lax.div(place_ref[1], CORES)
     first_head = lax.rem(place_ref[1], CORES) * 2 * PAIRS
     starts = [pl.multiple_of(lax.bitwise_xor(chip, k) * seg, seg) for k in ks]
 
-    def copy(p, i):
-        return pltpu.make_async_copy(
-            expo_ref.at[p, pl.ds(starts[i], seg), :],
-            e_ref.at[p, pl.ds(i * seg, seg), :],
-            sem.at[p, i],
-        )
-
-    for p in range(PAIRS):
-        for i in range(len(ks)):
-            copy(p, i).start()
     for i in range(len(ks)):
         at = slice(i * seg, (i + 1) * seg)
         ranks_ref[at, :cols] = own_ref[at, :].astype(F32)
@@ -331,8 +332,6 @@
         right_ref[:keys, :LANES] = jnp.where(lane < HDIM, values, zero)
         right_ref[keys:, :LANES] = jnp.where(lane < HDIM, zero, values)
         for i in range(len(ks)):
-            copy(p, i).wait()
-        for i in range(len(ks)):
             rows_at = slice(i * seg, (i + 1) * seg)
             for half in range(2):
                 ranks = ranks_ref[rows_at, half * cols : (half + 1) * cols]
@@ -340,7 +339,7 @@
                     rate = rate_ref[first_head + 2 * p + side] * root
                     gain = gain_ref[first_head + 2 * p + side] * math.log2(math.e)
                     at = slice(side * keys + half * cols, side * keys + (half + 1) * cols)
-                    weight = e_ref[p, rows_at, at].astype(F32) * jnp.exp2(
+                    weight = expo_ref[p, pl.ds(starts[i], seg), at].astype(F32) * jnp.exp2(
                         gain * jnp.tanh(rate * ranks)
                     )
                     p_ref[rows_at, at] = weight.astype(BF16)
@@ -386,23 +385,21 @@
             SMEM,
             pl.BlockSpec((n_rows, cols), lambda i: (0, 0)),
             pl.BlockSpec((n_rows, cols), lambda i: (0, 0)),
-            HBM,
+            VMEM,
             pl.BlockSpec((keys, WIDTH), lambda i: (0, 1)),
             pl.BlockSpec((rows, LANES), lambda i: (0, 0)),
-            HBM,
+            *[HBM] * len(follows),
         ],
         out_specs=(pl.BlockSpec((seg + EXTRA, WIDTH), lambda i: (0, 0)),) * len(ks),
         scratch_shapes=[
-            pltpu.VMEM((PAIRS, n_rows, 2 * keys), BF16),
             pltpu.VMEM((n_rows, 2 * keys), BF16),
             pltpu.VMEM((n_rows, keys), F32),
             pltpu.VMEM((2 * keys, 2 * LANES), BF16),
-            pltpu.SemaphoreType.DMA((PAIRS, len(ks))),
         ],
         compiler_params=params(28 * 2**20),
         cost_estimate=cost(512 * work, 2 * work, 2 * work),
         name="weigh",
-    )(place, gain, rate, own, other, expo, values, peak, follows)
+    )(place, gain, rate, own, other, expo, values, peak, *follows)
 
 
 def divide_kernel(*refs):
@@ -588,7 +585,7 @@
     panel += [(along_col(x, 1), CORES * k + 1, None) for k, x in blocks.items() if k not in order]
     columns = [(0, 0, adjacency)] + [(j, 0, x) for j, x in raw_columns.items()]
     columns += [(3, i * x.shape[0], x) for i, x in enumerate(raw_far)]
-    ranks = sweep(True, range(chips), place, pattern, panel, columns, [], 24 * 2**20)
+    ranks = sweep(True, range(chips), place, pattern, panel, columns, [], 58 * 2**20)
     columns = [(j, 0, x) for j, x in enumerate(from_rows(ranks))]
 
     ranks, moved = together((ranks, moved))
@@ -605,9 +602,12 @@
     w_all = [w_all[k] for k in range(chips)]
 
     groups = [list(range(chips // 2, chips)), list(range(chips // 2))]
-    ranks = [sweep(False, ks, place, pattern, panel, columns, [peak], 24 * 2**20) for ks in groups]
+    ranks = [
+        sweep(False, ks, place, pattern, panel, columns, follow, 24 * 2**20)
+        for ks, follow in zip(groups, [[peak], [peak, *w_all[1:]]], strict=True)
+    ]
     others = [along_col(x, 1) for x in ranks]
-    parts, follows = [None] * chips, ranks[1]
+    parts, follows = [None] * chips, [ranks[1]]
     for ks, own, other in zip(groups, ranks, others, strict=True):
         sums = weigh(
             root, chips, ks, place, bias_gain, bias_rate, own, other, expo, keys_values, peak,
@@ -615,7 +615,7 @@
         )
         for k, part in zip(ks, sums, strict=True):
             parts[k] = part if k == 0 else along_col(part, CORES * k)
-        follows = sums[0]
+        follows = [sums[0]]
     attended = divide(parts)
     mixed = project_out(place, attended, along_col(attended, 1), w_all)
     mixed = [x if k == 0 else along_col(x, CORES * k) for k, x in enumerate(mixed)]

time: 152 us -> 149 us (0.980)
  local copies, waits for them, and re-layouts: 11.3 us -> 6.9 us
  waiting for transfers between devices: 48.7 us -> 50.7 us
    unnamed x34 -> x50, local copies, waits for them, and re-layouts: 9.32 us -> 5.88 us
    pallas_call x3, Pallas kernels: 10.8 us -> 13.5 us  [sweep(): pl.pallas_call(functools.partial(sweep_kernel, first, ks, chips, [at for...]
    ppermute x19, waiting for transfers between devices: 39.3 us -> 41.7 us  [along_col(): return lax.ppermute(value, 'col', xor_pairs(col_count, j))]
    pallas_call x2, Pallas kernels: 11.6 us -> 9.33 us  [weigh(): pl.pallas_call(functools.partial(weigh_kernel, root, ks, seg), out_shape=...]
    ppermute x19, starting transfers between devices: 18.9 us -> 17.3 us  [along_col(): return lax.ppermute(value, 'col', xor_pairs(col_count, j))]
  transfers between devices with their start and end apart: 29 -> 29, of which waited for: 12 -> 13; matrix products, arithmetic and copies ran while one was open for 1% -> 1% of each run, Pallas kernels for 23% -> 25%
where the time goes in v5:
time: 149 us; the launch traced here: 148 us
  waiting for transfers between devices  50.7 us (34%)
  Pallas kernels  44.7 us (30%)
  starting transfers between devices  44.5 us (30%)
  local copies, waits for them, and re-layouts  6.9 us (5%)
    ppermute x19, waiting for transfers between devices, along_col(): return lax.ppermute(value, 'col', xor_pairs(col_count, j))  41.7 us
    ppermute x7, starting transfers between devices, along_row(): return lax.ppermute(value, 'row', xor_pairs(row_count, j))  18.4 us
    ppermute x19, starting transfers between devices, along_col(): return lax.ppermute(value, 'col', xor_pairs(col_count, j))  17.3 us
    pallas_call x3, Pallas kernels, sweep(): pl.pallas_call(functools.partial(sweep_kernel, first, ks, chips, [at for...  13.5 us
    pallas_call x2, Pallas kernels, weigh(): pl.pallas_call(functools.partial(weigh_kernel, root, ks, seg), out_shape=...  9.33 us
    ppermute x7, waiting for transfers between devices, along_row(): return lax.ppermute(value, 'row', xor_pairs(row_count, j))  9 us
    ppermute x3, starting transfers between devices, feature_step(): return lax.ppermute(value, ('row', 'col'), pairs)  8.85 us
    pallas_call x1, Pallas kernels, exponentials(): pl.pallas_call(expo_kernel, out_shape=(jax.ShapeDtypeStruct((PAIRS, rows,...  8.34 us
  transfers between devices with their start and end apart: 29, of which 13 were waited for; matrix products, arithmetic and copies ran while one was open for 1% of the time, Pallas kernels for 25%

profile of v5, /device:TPU:0, one launch (start us, length us, event | category | flops | bytes accessed | tf_op | source)
XLA Modules:
  0.0 148.2 jit_solution(6716663000234581106)
XLA Ops:
  0.7 3.3 %start.1 = (bf16[768,384]{1,0:T(8,128)(2,1)}, bf16[384,1024]{1,0:T(8,128)(2,1)}) custom-call(s32[2]{0:T(128)} %pad_add_fusion.place_ref, s32[3,6]{1,0:T(4,128)} %bitcast.10, bf16[768,384]{1,0:T(8,128)(2,1)} %weight_ref.1, bf16[768,1024]{1,0:T(8,128)(2,1)} %features_ref.1), custom_call_target="tpu_custom_call" | custom-call | flops 294912 | bytes 1179648 | tf_op jit(solution)/shard_map/start/pallas_call | solution.py:71
  4.0 5.7 %collective-permute-start = (bf16[384,1024]{1,0:T(8,128)(2,1)}, bf16[384,1024]{1,0:T(8,128)(2,1)}, u32[]{:S(2)}, u32[]{:S(2)}) collective-permute-start(bf16[384,1024]{1,0:T(8,128)(2,1)} %get-tuple-element.38), channel_id=1, source_target_pairs={{0,8},{1,17},{10,26},{11,3},{20,4},{21,29},{30,22},{31,15}} | collective-permute-start | bytes 2359304 | tf_op jit(solution)/shard_map/ppermute | solution.py:558
  12.9 3.1 %collective-permute-start.1 = (bf16[768,384]{1,0:T(8,128)(2,1)}, bf16[768,384]{1,0:T(8,128)(2,1)S(1)}, u32[]{:S(2)}, u32[]{:S(2)}) collective-permute-start(bf16[768,384]{1,0:T(8,128)(2,1)} %get-tuple-element.45.refs_0_.refs_8_), channel_id=1, source_target_pairs={{0,8},{8,0},{16,24},{24,16},{1,9},{9,1},{17,25},{25,17},{2,10},{10... | collective-permute-start | bytes 1769480 | tf_op jit(solution)/shard_map/ppermute | solution.py:530
  16.0 3.6 %project_in.2.q_ref = bf16[768,512]{1,0:T(8,128)(2,1)} custom-call(s32[1]{0:T(128)} %bitcast.3.place_ref, bf16[768,1024]{1,0:T(8,128)(2,1)} %features_ref.1, bf16[1024,3072]{1,0:T(8,128)(2,1)} %refs_2_.1), custom_call_target="tpu_custom_call" | custom-call | flops 805306368 | bytes 2621440 | tf_op jit(solution)/shard_map/project_in/pallas_call | solution.py:106
  19.6 17.3 %collective-permute-done.4.refs_2_ = bf16[768,384]{1,0:T(8,128)(2,1)S(1)} collective-permute-done((bf16[768,384]{1,0:T(8,128)(2,1)}, bf16[768,384]{1,0:T(8,128)(2,1)S(1)}, u32[]{:S(2)}, u32[]{:S(2)}) %collective-permute-start.4) | collective-permute-done | bytes 589856 | tf_op jit(solution)/shard_map/ppermute | solution.py:527
  41.5 3.7 %collective-permute-start.6 = (bf16[384,384]{1,0:T(8,128)(2,1)S(1)}, bf16[384,384]{1,0:T(8,128)(2,1)S(1)}, u32[]{:S(2)}, u32[]{:S(2)}) collective-permute-start(bf16[384,384]{1,0:T(8,128)(2,1)S(1)} %slice.7), channel_id=1, source_target_pairs={{0,16},{8,24},{16,0},{24,8},{1,17},{9,25},{17,1},{25,9},{2,18},{10... | collective-permute-start | bytes 884744 | tf_op jit(solution)/shard_map/ppermute | solution.py:530
  45.2 3.5 %collective-permute-start.5 = (bf16[384,384]{1,0:T(8,128)(2,1)S(1)}, bf16[384,384]{1,0:T(8,128)(2,1)S(1)}, u32[]{:S(2)}, u32[]{:S(2)}) collective-permute-start(bf16[384,384]{1,0:T(8,128)(2,1)S(1)} %slice.6), channel_id=1, source_target_pairs={{0,8},{8,0},{16,24},{24,16},{1,9},{9,1},{17,25},{25,17},{2,10},{10... | collective-permute-start | bytes 884744 | tf_op jit(solution)/shard_map/ppermute | solution.py:530
  52.0 3.6 %collective-permute-done.5.refs_11_ = bf16[384,384]{1,0:T(8,128)(2,1)S(1)} collective-permute-done((bf16[384,384]{1,0:T(8,128)(2,1)S(1)}, bf16[384,384]{1,0:T(8,128)(2,1)S(1)}, u32[]{:S(2)}, u32[]{:S(2)}) %collective-permute-start.5) | collective-permute-done | bytes 294944 | tf_op jit(solution)/shard_map/ppermute | solution.py:530
  59.2 6.9 %rank_sweep.3.refs_8_ = bf16[768,384]{1,0:T(8,128)(2,1)} custom-call(s32[2]{0:T(128)} %pad_add_fusion.place_ref, s32[3,6]{1,0:T(4,128)} %bitcast.11, bf16[768,384]{1,0:T(8,128)(2,1)} %get-tuple-element.45.refs_0_.refs_8_, bf16[768,384]{1,0:T(8,128)(2,1)} %copy-done.7, bf16[768,384]{1,0:T(8,128)(2,1)} %copy-done.5, bf16[768,384]{1,0:T(8,128)(2,1)} %copy-done.9, ...), custom_call_target="tpu_custom_call" | custom-call | flops 1811939328 | bytes 9437184 | tf_op jit(solution)/shard_map/rank_sweep/pallas_call | solution.py:212
  67.1 5.9 %collective-permute-start.12 = (bf16[768,384]{1,0:T(8,128)(2,1)S(1)}, bf16[768,384]{1,0:T(8,128)(2,1)S(1)}, u32[]{:S(2)}, u32[]{:S(2)}) collective-permute-start(bf16[768,384]{1,0:T(8,128)(2,1)S(1)} %copy-done.13), channel_id=1, source_target_pairs={{0,24},{8,16},{16,8},{24,0},{1,25},{9,17},{17,9},{25,1},{2,26},{10... | collective-permute-start | bytes 1769480 | tf_op jit(solution)/shard_map/ppermute | solution.py:530
  73.6 2.8 %copy-done.2 = bf16[1024,3072]{1,0:T(8,128)(2,1)S(1)} copy-done((bf16[1024,3072]{1,0:T(8,128)(2,1)S(1)}, bf16[1024,3072]{1,0:T(8,128)(2,1)}, u32[]{:S(2)}) %copy-start.2) | copy-done | bytes 6291480
  76.4 2.8 %project_in.3.k_ref.v_ref = bf16[768,1024]{1,0:T(8,128)(2,1)S(1)} custom-call(s32[1]{0:T(128)} %bitcast.3.place_ref, bf16[384,1024]{1,0:T(8,128)(2,1)S(1)} %select_select_fusion.refs_0_, bf16[384,1024]{1,0:T(8,128)(2,1)S(1)} %collective-permute-done.15.refs_1_, bf16[1024,3072]{1,0:T(8,128)(2,1)S(1)} %copy-done.2), custom_call_target="tpu_custom_call" | custom-call | flops 1610612736 | bytes 3670016 | tf_op jit(solution)/shard_map/project_in/pallas_call | solution.py:106
  79.3 2.0 %collective-permute-start.17 = (bf16[1024,128]{1,0:T(8,128)(2,1)S(1)}, bf16[1024,128]{1,0:T(8,128)(2,1)S(1)}, u32[]{:S(2)}, u32[]{:S(2)}) collective-permute-start(bf16[1024,128]{1,0:T(8,128)(2,1)S(1)} %copy-done.15), channel_id=1, source_target_pairs={{0,4},{1,5},{2,6},{3,7},{4,0},{5,1},{6,2},{7,3},{8,12},{9,13},{10,... | collective-permute-start | bytes 786440 | tf_op jit(solution)/shard_map/ppermute | solution.py:527
  83.1 8.3 %expo.1 = (bf16[4,768,1536]{2,1,0:T(8,128)(2,1)S(1)}, f32[768,128]{1,0:T(8,128)S(1)}) custom-call(s32[3,6]{1,0:T(4,128)S(1)} %bitcast.13, s32[3,6]{1,0:T(4,128)S(1)} %collective-permute-done.18.other_ref, bf16[768,512]{1,0:T(8,128)(2,1)S(1)} %copy-done.14, bf16[768,1024]{1,0:T(8,128)(2,1)S(1)} %project_in.3.k_ref.v_ref), custom_call_target="tpu_custom_call" | custom-call | flops 2415919104 | bytes 9437184 | tf_op jit(solution)/shard_map/expo/pallas_call | solution.py:284
  91.5 3.1 %collective-permute-done.17.refs_14_.refs_2_ = bf16[1024,128]{1,0:T(8,128)(2,1)S(1)} collective-permute-done((bf16[1024,128]{1,0:T(8,128)(2,1)S(1)}, bf16[1024,128]{1,0:T(8,128)(2,1)S(1)}, u32[]{:S(2)}, u32[]{:S(2)}) %collective-permute-start.17) | collective-permute-done | bytes 262176 | tf_op jit(solution)/shard_map/ppermute | solution.py:527
  95.6 3.6 %collective-permute-done.11.refs_10_ = bf16[768,384]{1,0:T(8,128)(2,1)S(1)} collective-permute-done((bf16[768,384]{1,0:T(8,128)(2,1)S(1)}, bf16[768,384]{1,0:T(8,128)(2,1)S(1)}, u32[]{:S(2)}, u32[]{:S(2)}) %collective-permute-start.11) | collective-permute-done | bytes 589856 | tf_op jit(solution)/shard_map/ppermute | solution.py:530
  99.3 3.2 %rank_sweep.5.own_ref = bf16[384,384]{1,0:T(8,128)(2,1)S(1)} custom-call(s32[2]{0:T(128)S(1)} %copy-done.17, s32[3,6]{1,0:T(4,128)S(1)} %bitcast.14, bf16[768,384]{1,0:T(8,128)(2,1)S(1)} %copy-done.4, bf16[768,384]{1,0:T(8,128)(2,1)S(1)} %copy-done.8, bf16[768,384]{1,0:T(8,128)(2,1)S(1)} %copy-done.6, bf16[768,384]{1,0:T(8,128)(2,1)S(1)} %copy-done.10, ...), custom_call_target="tpu_custom_call" | custom-call | flops 905969664 | bytes 7077888 | tf_op jit(solution)/shard_map/rank_sweep/pallas_call | solution.py:212
  102.7 3.4 %rank_sweep.4.refs_0_.own_ref = bf16[384,384]{1,0:T(8,128)(2,1)S(1)} custom-call(s32[2]{0:T(128)S(1)} %copy-done.17, s32[3,6]{1,0:T(4,128)S(1)} %bitcast.15, bf16[768,384]{1,0:T(8,128)(2,1)S(1)} %copy-done.4, bf16[768,384]{1,0:T(8,128)(2,1)S(1)} %copy-done.8, bf16[768,384]{1,0:T(8,128)(2,1)S(1)} %copy-done.6, bf16[768,384]{1,0:T(8,128)(2,1)S(1)} %copy-done.10, ...), custom_call_target="tpu_custom_call" | custom-call | flops 905969664 | bytes 7077888 | tf_op jit(solution)/shard_map/rank_sweep/pallas_call | solution.py:212
  106.6 4.7 %weigh.2 = (bf16[208,512]{1,0:T(8,128)(2,1)S(1)}, bf16[208,512]{1,0:T(8,128)(2,1)S(1)}) custom-call(s32[2]{0:T(128)S(1)} %copy-done.17, f32[16]{0:T(128)S(1)} %copy-done.18, f32[16]{0:T(128)S(1)} %copy-done.19, bf16[384,384]{1,0:T(8,128)(2,1)S(1)} %rank_sweep.5.own_ref, bf16[384,384]{1,0:T(8,128)(2,1)S(1)} %collective-permute-done.21.other_ref, ...), custom_call_target="tpu_custom_call" | custom-call | flops 1207959552 | bytes 4718592 | tf_op jit(solution)/shard_map/weigh/pallas_call | solution.py:378
  111.3 3.3 %collective-permute-start.24 = (bf16[208,512]{1,0:T(8,128)(2,1)S(1)}, bf16[208,512]{1,0:T(8,128)(2,1)S(1)}, u32[]{:S(2)}, u32[]{:S(2)}) collective-permute-start(bf16[208,512]{1,0:T(8,128)(2,1)S(1)} %get-tuple-element.65), channel_id=1, source_target_pairs={{0,6},{1,7},{2,4},{3,5},{4,2},{5,3},{6,0},{7,1},{8,14},{9,15},{10,... | collective-permute-start | bytes 638984 | tf_op jit(solution)/shard_map/ppermute | solution.py:527
  116.4 4.7 %weigh.3 = (bf16[208,512]{1,0:T(8,128)(2,1)S(1)}, bf16[208,512]{1,0:T(8,128)(2,1)S(1)}) custom-call(s32[2]{0:T(128)S(1)} %copy-done.17, f32[16]{0:T(128)S(1)} %copy-done.18, f32[16]{0:T(128)S(1)} %copy-done.19, bf16[384,384]{1,0:T(8,128)(2,1)S(1)} %rank_sweep.4.refs_0_.own_ref, bf16[384,384]{1,0:T(8,128)(2,1)S(1)} %collective-permute-done.20.other_ref, ...), custom_call_target="tpu_custom_call" | custom-call | flops 1207959552 | bytes 4718592 | tf_op jit(solution)/shard_map/weigh/pallas_call | solution.py:378
  121.3 12.8 %collective-permute-done.23.refs_2_ = bf16[208,512]{1,0:T(8,128)(2,1)S(1)} collective-permute-done((bf16[208,512]{1,0:T(8,128)(2,1)S(1)}, bf16[208,512]{1,0:T(8,128)(2,1)S(1)}, u32[]{:S(2)}, u32[]{:S(2)}) %collective-permute-start.23) | collective-permute-done | bytes 213024 | tf_op jit(solution)/shard_map/ppermute | solution.py:527
  138.3 2.8 %collective-permute-start.27 = (bf16[192,128]{1,0:T(8,128)(2,1)S(1)}, bf16[192,128]{1,0:T(8,128)(2,1)S(1)}, u32[]{:S(2)}, u32[]{:S(2)}) collective-permute-start(bf16[192,128]{1,0:T(8,128)(2,1)S(1)} %get-tuple-element.69), channel_id=1, source_target_pairs={{0,4},{1,5},{2,6},{3,7},{4,0},{5,1},{6,2},{7,3},{8,12},{9,13},{10,... | collective-permute-start | bytes 147464 | tf_op jit(solution)/shard_map/ppermute | solution.py:527
  144.2 2.8 %collective-permute-done.28.refs_3_ = bf16[192,128]{1,0:T(8,128)(2,1)S(1)} collective-permute-done((bf16[192,128]{1,0:T(8,128)(2,1)S(1)}, bf16[192,128]{1,0:T(8,128)(2,1)S(1)}, u32[]{:S(2)}, u32[]{:S(2)}) %collective-permute-start.28) | collective-permute-done | bytes 49184 | tf_op jit(solution)/shard_map/ppermute | solution.py:527
  (101 shorter events, 31.1 us)
Async XLA Ops:
  4.0 33.4 %collective-permute-start = (bf16[384,1024]{1,0:T(8,128)(2,1)}, bf16[384,1024]{1,0:T(8,128)(2,1)}, u32[]{:S(2)}, u32[]{:S(2)}) collective-permute-start(bf16[384,1024]{1,0:T(8,128)(2,1)} %get-tuple-element.38), channel_id=1, source_target_pairs={{0,8},{1,17},{10,26},{11,3},{20,4},{21,29},{30,22},{31,15}} | collective-permute-start | bytes 2359304 | tf_op jit(solution)/shard_map/ppermute | solution.py:558
  9.7 27.1 %collective-permute-start.4 = (bf16[768,384]{1,0:T(8,128)(2,1)}, bf16[768,384]{1,0:T(8,128)(2,1)S(1)}, u32[]{:S(2)}, u32[]{:S(2)}) collective-permute-start(bf16[768,384]{1,0:T(8,128)(2,1)} %get-tuple-element.45.refs_0_.refs_8_), channel_id=1, source_target_pairs={{0,4},{1,5},{2,6},{3,7},{4,0},{5,1},{6,2},{7,3},{8,12},{9,13},{10,... | collective-permute-start | bytes 1769480 | tf_op jit(solution)/shard_map/ppermute | solution.py:527
  9.7 27.7 %collective-permute-start.3 = (bf16[768,384]{1,0:T(8,128)(2,1)}, bf16[768,384]{1,0:T(8,128)(2,1)S(1)}, u32[]{:S(2)}, u32[]{:S(2)}) collective-permute-start(bf16[768,384]{1,0:T(8,128)(2,1)} %get-tuple-element.45.refs_0_.refs_8_), channel_id=1, source_target_pairs={{0,2},{1,3},{2,0},{3,1},{4,6},{5,7},{6,4},{7,5},{8,10},{9,11},{10,... | collective-permute-start | bytes 1769480 | tf_op jit(solution)/shard_map/ppermute | solution.py:527
  11.2 26.2 %collective-permute-start.2 = (bf16[768,384]{1,0:T(8,128)(2,1)}, bf16[768,384]{1,0:T(8,128)(2,1)S(1)}, u32[]{:S(2)}, u32[]{:S(2)}) collective-permute-start(bf16[768,384]{1,0:T(8,128)(2,1)} %get-tuple-element.45.refs_0_.refs_8_), channel_id=1, source_target_pairs={{0,16},{8,24},{16,0},{24,8},{1,17},{9,25},{17,1},{25,9},{2,18},{10... | collective-permute-start | bytes 1769480 | tf_op jit(solution)/shard_map/ppermute | solution.py:530
  12.9 24.6 %collective-permute-start.1 = (bf16[768,384]{1,0:T(8,128)(2,1)}, bf16[768,384]{1,0:T(8,128)(2,1)S(1)}, u32[]{:S(2)}, u32[]{:S(2)}) collective-permute-start(bf16[768,384]{1,0:T(8,128)(2,1)} %get-tuple-element.45.refs_0_.refs_8_), channel_id=1, source_target_pairs={{0,8},{8,0},{16,24},{24,16},{1,9},{9,1},{17,25},{25,17},{2,10},{10... | collective-permute-start | bytes 1769480 | tf_op jit(solution)/shard_map/ppermute | solution.py:530
  38.5 17.0 %collective-permute-start.7 = (bf16[3,768,384]{2,1,0:T(8,128)(2,1)S(1)}, bf16[3,768,384]{2,1,0:T(8,128)(2,1)S(1)}, u32[]{:S(2)}, u32[]{:S(2)}) collective-permute-start(bf16[3,768,384]{2,1,0:T(8,128)(2,1)S(1)} %pad_maximum_fusion), channel_id=1, source_target_pairs={{0,1},{1,0},{2,3},{3,2},{4,5},{5,4},{6,7},{7,6},{8,9},{9,8},{10,11... | collective-permute-start | bytes 5308424 | tf_op jit(solution)/shard_map/ppermute | solution.py:527
  38.6 10.1 %collective-permute-start.13 = (bf16[384,1024]{1,0:T(8,128)(2,1)}, bf16[384,1024]{1,0:T(8,128)(2,1)}, u32[]{:S(2)}, u32[]{:S(2)}) collective-permute-start(bf16[384,1024]{1,0:T(8,128)(2,1)} %collective-permute-done), channel_id=1, source_target_pairs={{8,24},{17,25},{26,18},{3,19},{4,12},{29,13},{22,6},{15,7}} | collective-permute-start | bytes 2359304 | tf_op jit(solution)/shard_map/ppermute | solution.py:558
  40.2 15.4 %collective-permute-start.8 = (bf16[768,384]{1,0:T(8,128)(2,1)S(1)}, bf16[768,384]{1,0:T(8,128)(2,1)S(1)}, u32[]{:S(2)}, u32[]{:S(2)}) collective-permute-start(bf16[768,384]{1,0:T(8,128)(2,1)S(1)} %collective-permute-done.4.refs_2_), channel_id=1, source_target_pairs={{0,2},{1,3},{2,0},{3,1},{4,6},{5,7},{6,4},{7,5},{8,10},{9,11},{10,... | collective-permute-start | bytes 1769480 | tf_op jit(solution)/shard_map/ppermute | solution.py:527
  41.5 10.4 %collective-permute-start.6 = (bf16[384,384]{1,0:T(8,128)(2,1)S(1)}, bf16[384,384]{1,0:T(8,128)(2,1)S(1)}, u32[]{:S(2)}, u32[]{:S(2)}) collective-permute-start(bf16[384,384]{1,0:T(8,128)(2,1)S(1)} %slice.7), channel_id=1, source_target_pairs={{0,16},{8,24},{16,0},{24,8},{1,17},{9,25},{17,1},{25,9},{2,18},{10... | collective-permute-start | bytes 884744 | tf_op jit(solution)/shard_map/ppermute | solution.py:530
  45.2 10.4 %collective-permute-start.5 = (bf16[384,384]{1,0:T(8,128)(2,1)S(1)}, bf16[384,384]{1,0:T(8,128)(2,1)S(1)}, u32[]{:S(2)}, u32[]{:S(2)}) collective-permute-start(bf16[384,384]{1,0:T(8,128)(2,1)S(1)} %slice.6), channel_id=1, source_target_pairs={{0,8},{8,0},{16,24},{24,16},{1,9},{9,1},{17,25},{25,17},{2,10},{10... | collective-permute-start | bytes 884744 | tf_op jit(solution)/shard_map/ppermute | solution.py:530
  48.7 17.4 %collective-permute-start.14 = (bf16[384,1024]{1,0:T(8,128)(2,1)}, bf16[384,1024]{1,0:T(8,128)(2,1)}, u32[]{:S(2)}, u32[]{:S(2)}) collective-permute-start(bf16[384,1024]{1,0:T(8,128)(2,1)} %collective-permute-done.13), channel_id=1, source_target_pairs={{24,16},{25,9},{18,2},{19,27},{12,28},{13,5},{6,14},{7,23}} | collective-permute-start | bytes 2359304 | tf_op jit(solution)/shard_map/ppermute | solution.py:558
  66.3 7.3 %collective-permute-start.15 = (bf16[384,1024]{1,0:T(8,128)(2,1)S(1)}, bf16[384,1024]{1,0:T(8,128)(2,1)S(1)}, u32[]{:S(2)}, u32[]{:S(2)}) collective-permute-start(bf16[384,1024]{1,0:T(8,128)(2,1)S(1)} %select_select_fusion.refs_0_), channel_id=1, source_target_pairs={{0,1},{1,0},{2,3},{3,2},{4,5},{5,4},{6,7},{7,6},{8,9},{9,8},{10,11... | collective-permute-start | bytes 2359304 | tf_op jit(solution)/shard_map/ppermute | solution.py:527
  67.1 28.5 %collective-permute-start.12 = (bf16[768,384]{1,0:T(8,128)(2,1)S(1)}, bf16[768,384]{1,0:T(8,128)(2,1)S(1)}, u32[]{:S(2)}, u32[]{:S(2)}) collective-permute-start(bf16[768,384]{1,0:T(8,128)(2,1)S(1)} %copy-done.13), channel_id=1, source_target_pairs={{0,24},{8,16},{16,8},{24,0},{1,25},{9,17},{17,9},{25,1},{2,26},{10... | collective-permute-start | bytes 1769480 | tf_op jit(solution)/shard_map/ppermute | solution.py:530
  73.0 26.3 %collective-permute-start.11 = (bf16[768,384]{1,0:T(8,128)(2,1)S(1)}, bf16[768,384]{1,0:T(8,128)(2,1)S(1)}, u32[]{:S(2)}, u32[]{:S(2)}) collective-permute-start(bf16[768,384]{1,0:T(8,128)(2,1)S(1)} %copy-done.13), channel_id=1, source_target_pairs={{0,16},{8,24},{16,0},{24,8},{1,17},{9,25},{17,1},{25,9},{2,18},{10... | collective-permute-start | bytes 1769480 | tf_op jit(solution)/shard_map/ppermute | solution.py:530
  73.0 26.3 %collective-permute-start.10 = (bf16[768,384]{1,0:T(8,128)(2,1)S(1)}, bf16[768,384]{1,0:T(8,128)(2,1)S(1)}, u32[]{:S(2)}, u32[]{:S(2)}) collective-permute-start(bf16[768,384]{1,0:T(8,128)(2,1)S(1)} %copy-done.13), channel_id=1, source_target_pairs={{0,8},{8,0},{16,24},{24,16},{1,9},{9,1},{17,25},{25,17},{2,10},{10... | collective-permute-start | bytes 1769480 | tf_op jit(solution)/shard_map/ppermute | solution.py:530
  73.6 7.7 %collective-permute-start.18 = (s32[3,6]{1,0:T(4,128)S(1)}, s32[3,6]{1,0:T(4,128)S(1)}, u32[]{:S(2)}, u32[]{:S(2)}) collective-permute-start(s32[3,6]{1,0:T(4,128)S(1)} %bitcast.12), channel_id=1, source_target_pairs={{0,1},{1,0},{2,3},{3,2},{4,5},{5,4},{6,7},{7,6},{8,9},{9,8},{10,11... | collective-permute-start | bytes 224 | tf_op jit(solution)/shard_map/ppermute | solution.py:527
  79.3 15.3 %collective-permute-start.17 = (bf16[1024,128]{1,0:T(8,128)(2,1)S(1)}, bf16[1024,128]{1,0:T(8,128)(2,1)S(1)}, u32[]{:S(2)}, u32[]{:S(2)}) collective-permute-start(bf16[1024,128]{1,0:T(8,128)(2,1)S(1)} %copy-done.15), channel_id=1, source_target_pairs={{0,4},{1,5},{2,6},{3,7},{4,0},{5,1},{6,2},{7,3},{8,12},{9,13},{10,... | collective-permute-start | bytes 786440 | tf_op jit(solution)/shard_map/ppermute | solution.py:527
  81.3 13.3 %collective-permute-start.16 = (bf16[1024,128]{1,0:T(8,128)(2,1)S(1)}, bf16[1024,128]{1,0:T(8,128)(2,1)S(1)}, u32[]{:S(2)}, u32[]{:S(2)}) collective-permute-start(bf16[1024,128]{1,0:T(8,128)(2,1)S(1)} %copy-done.15), channel_id=1, source_target_pairs={{0,2},{1,3},{2,0},{3,1},{4,6},{5,7},{6,4},{7,5},{8,10},{9,11},{10,... | collective-permute-start | bytes 786440 | tf_op jit(solution)/shard_map/ppermute | solution.py:527
  94.6 8.1 %collective-permute-start.19 = (bf16[1024,128]{1,0:T(8,128)(2,1)S(1)}, bf16[1024,128]{1,0:T(8,128)(2,1)S(1)}, u32[]{:S(2)}, u32[]{:S(2)}) collective-permute-start(bf16[1024,128]{1,0:T(8,128)(2,1)S(1)} %collective-permute-done.17.refs_14_.refs_2_), channel_id=1, source_target_pairs={{0,2},{1,3},{2,0},{3,1},{4,6},{5,7},{6,4},{7,5},{8,10},{9,11},{10,... | collective-permute-start | bytes 786440 | tf_op jit(solution)/shard_map/ppermute | solution.py:527
  106.1 10.3 %collective-permute-start.20 = (bf16[384,384]{1,0:T(8,128)(2,1)S(1)}, bf16[384,384]{1,0:T(8,128)(2,1)S(1)}, u32[]{:S(2)}, u32[]{:S(2)}) collective-permute-start(bf16[384,384]{1,0:T(8,128)(2,1)S(1)} %rank_sweep.4.refs_0_.own_ref), channel_id=1, source_target_pairs={{0,1},{1,0},{2,3},{3,2},{4,5},{5,4},{6,7},{7,6},{8,9},{9,8},{10,11... | collective-permute-start | bytes 884744 | tf_op jit(solution)/shard_map/ppermute | solution.py:527
  111.3 10.1 %collective-permute-start.24 = (bf16[208,512]{1,0:T(8,128)(2,1)S(1)}, bf16[208,512]{1,0:T(8,128)(2,1)S(1)}, u32[]{:S(2)}, u32[]{:S(2)}) collective-permute-start(bf16[208,512]{1,0:T(8,128)(2,1)S(1)} %get-tuple-element.65), channel_id=1, source_target_pairs={{0,6},{1,7},{2,4},{3,5},{4,2},{5,3},{6,0},{7,1},{8,14},{9,15},{10,... | collective-permute-start | bytes 638984 | tf_op jit(solution)/shard_map/ppermute | solution.py:527
  114.6 19.6 %collective-permute-start.23 = (bf16[208,512]{1,0:T(8,128)(2,1)S(1)}, bf16[208,512]{1,0:T(8,128)(2,1)S(1)}, u32[]{:S(2)}, u32[]{:S(2)}) collective-permute-start(bf16[208,512]{1,0:T(8,128)(2,1)S(1)} %get-tuple-element.62.refs_0_), channel_id=1, source_target_pairs={{0,4},{1,5},{2,6},{3,7},{4,0},{5,1},{6,2},{7,3},{8,12},{9,13},{10,... | collective-permute-start | bytes 638984 | tf_op jit(solution)/shard_map/ppermute | solution.py:527
  121.0 13.2 %collective-permute-start.22 = (bf16[208,512]{1,0:T(8,128)(2,1)S(1)}, bf16[208,512]{1,0:T(8,128)(2,1)S(1)}, u32[]{:S(2)}, u32[]{:S(2)}) collective-permute-start(bf16[208,512]{1,0:T(8,128)(2,1)S(1)} %get-tuple-element.64), channel_id=1, source_target_pairs={{0,2},{1,3},{2,0},{3,1},{4,6},{5,7},{6,4},{7,5},{8,10},{9,11},{10,... | collective-permute-start | bytes 638984 | tf_op jit(solution)/shard_map/ppermute | solution.py:527
  138.3 5.9 %collective-permute-start.27 = (bf16[192,128]{1,0:T(8,128)(2,1)S(1)}, bf16[192,128]{1,0:T(8,128)(2,1)S(1)}, u32[]{:S(2)}, u32[]{:S(2)}) collective-permute-start(bf16[192,128]{1,0:T(8,128)(2,1)S(1)} %get-tuple-element.69), channel_id=1, source_target_pairs={{0,4},{1,5},{2,6},{3,7},{4,0},{5,1},{6,2},{7,3},{8,12},{9,13},{10,... | collective-permute-start | bytes 147464 | tf_op jit(solution)/shard_map/ppermute | solution.py:527
  (30 other events, 276.7 us)

commit v6 on v5

--- a/solution.py
+++ b/solution.py
@@ -370,10 +370,11 @@
             ].astype(BF16)
 
 
-def weigh(root, chips, ks, place, gain, rate, own, other, expo, values, peak, follows):
-    n_rows, cols = own.shape
-    seg = n_rows // len(ks)
-    rows, keys = seg * chips, 2 * cols
+def weigh(root, chips, ks, first, place, gain, rate, own, other, expo, values, peak, follows):
+    (_, rows, _), cols = expo.shape, own.shape[1]
+    seg = rows // chips
+    n_rows, keys = seg * len(ks), 2 * cols
+    part = pl.BlockSpec((n_rows, cols), lambda i: (first // len(ks), 0))
     work = n_rows * keys * 2 * PAIRS
     return pl.pallas_call(
         functools.partial(weigh_kernel, root, ks, seg),
@@ -383,8 +384,8 @@
             SMEM,
             SMEM,
             SMEM,
-            pl.BlockSpec((n_rows, cols), lambda i: (0, 0)),
-            pl.BlockSpec((n_rows, cols), lambda i: (0, 0)),
+            part,
+            part,
             VMEM,
             pl.BlockSpec((keys, WIDTH), lambda i: (0, 1)),
             pl.BlockSpec((rows, LANES), lambda i: (0, 0)),
@@ -490,33 +491,13 @@
     )(place, own, other, *w_all)
 
 
-def assemble_kernel(place_ref, *refs):
-    parts, out_ref = refs[:-1], refs[-1]
-    chip = lax.div(place_ref[1], CORES)
-    seg = parts[0].shape[0]
-    for k, part in enumerate(parts):
-        at = pl.multiple_of(lax.bitwise_xor(chip, k) * seg, seg)
-        out_ref[pl.ds(at, seg), :] = part[...]
-
-
-def assemble(place, parts):
-    seg, width = parts[0].shape
-    return pl.pallas_call(
-        assemble_kernel,
-        out_shape=jax.ShapeDtypeStruct((seg * len(parts), width), BF16),
-        in_specs=[SMEM] + [VMEM] * len(parts),
-        out_specs=VMEM,
-        compiler_params=params(SMALL_LIMIT),
-        name="assemble",
-    )(place, *parts)
-
-
 def shards(node_features, edge_weight, pattern, w_qkv, w_out, bias_gain, bias_rate):
     rows, cols = edge_weight.shape
     row_count, col_count = lax.axis_size("row"), lax.axis_size("col")
     row_pos, col_pos = lax.axis_index("row"), lax.axis_index("col")
     ratio = rows // cols
     chips = col_count // CORES
+    chip = col_pos // CORES
     root = math.sqrt(rows * row_count)
     place = jnp.stack([row_pos, col_pos]).astype(jnp.int32)
     core = (col_pos % CORES).astype(jnp.int32).reshape(1)
@@ -585,13 +566,14 @@
     panel += [(along_col(x, 1), CORES * k + 1, None) for k, x in blocks.items() if k not in order]
     columns = [(0, 0, adjacency)] + [(j, 0, x) for j, x in raw_columns.items()]
     columns += [(3, i * x.shape[0], x) for i, x in enumerate(raw_far)]
-    ranks = sweep(True, range(chips), place, pattern, panel, columns, [], 58 * 2**20)
+    key_rows = features
+    for s in range(1, row_count - 1):
+        key_rows = jnp.where(steps_away == s, moved[s], key_rows)
+    ranks = sweep(True, range(chips), place, pattern, panel, columns, [key_rows], 50 * 2**20)
     columns = [(j, 0, x) for j, x in enumerate(from_rows(ranks))]
 
-    ranks, moved = together((ranks, moved))
-    key_rows = features
-    for s in range(1, row_count):
-        key_rows = jnp.where(steps_away == s, moved[s], key_rows)
+    ranks, last = together((ranks, moved[-1]))
+    key_rows = jnp.where(steps_away == row_count - 1, last, key_rows)
     keys_values = project_in(core, [key_rows, along_col(key_rows, 1)], w_qkv, [D, 2 * D], limit=28 * 2**20)
     keys_values, w_out = together((keys_values, w_out))
     w_all = spread({0: w_out}, 1)
@@ -608,18 +590,23 @@
     ]
     others = [along_col(x, 1) for x in ranks]
     parts, follows = [None] * chips, [ranks[1]]
-    for ks, own, other in zip(groups, ranks, others, strict=True):
+    cuts = [(0, n, n + 1) for n in reversed(range(len(groups[0])))] + [(1, 0, len(groups[1]))]
+    for g, begin, end in cuts:
+        ks = groups[g][begin:end]
         sums = weigh(
-            root, chips, ks, place, bias_gain, bias_rate, own, other, expo, keys_values, peak,
-            follows,
+            root, chips, ks, begin, place, bias_gain, bias_rate, ranks[g], others[g], expo,
+            keys_values, peak, follows,
         )
-        for k, part in zip(ks, sums, strict=True):
+        for k, part in zip(ks, sums, strict=False):
             parts[k] = part if k == 0 else along_col(part, CORES * k)
         follows = [sums[0]]
     attended = divide(parts)
     mixed = project_out(place, attended, along_col(attended, 1), w_all)
     mixed = [x if k == 0 else along_col(x, CORES * k) for k, x in enumerate(mixed)]
-    return assemble(place, mixed)
+    for bit in range(chips.bit_length() - 1):
+        turned = chip >> bit & 1 == 1
+        mixed = [jnp.where(turned, mixed[k ^ 1 << bit], mixed[k]) for k in range(chips)]
+    return jnp.concatenate(mixed, axis=0)
 
 
 def solution(mesh):

time: 149 us -> 146 us (0.980)
  other arithmetic: 1.05 us -> 4.4 us
  waiting for transfers between devices: 50.7 us -> 47.7 us
  Pallas kernels: 44.7 us -> 42.8 us
    ppermute x19, waiting for transfers between devices: 41.7 us -> 36.3 us  [along_col(): return lax.ppermute(value, 'col', xor_pairs(col_count, j))]
    select_n x1, other arithmetic: 0.16 us -> 2.7 us  [shards(): key_rows = jnp.where(steps_away == s, moved[s], key_rows)]
    ppermute x7, waiting for transfers between devices: 9 us -> 11.4 us  [along_row(): return lax.ppermute(value, 'row', xor_pairs(row_count, j))]
    pallas_call x3, Pallas kernels: 13.5 us -> 11.3 us  [sweep(): pl.pallas_call(functools.partial(sweep_kernel, first, ks, chips, [at for...]
    pallas_call x2 -> x3, Pallas kernels: 9.33 us -> 10.8 us  [weigh(): pl.pallas_call(functools.partial(weigh_kernel, root, ks, seg), out_shape=...]
    unnamed x50 -> x36, local copies, waits for them, and re-layouts: 5.88 us -> 4.57 us
  transfers between devices with their start and end apart: 29 -> 29, of which waited for: 13 -> 12; matrix products, arithmetic and copies ran while one was open for 1% -> 3% of each run, Pallas kernels for 25% -> 25%
where the time goes in v6:
time: 146 us
  waiting for transfers between devices  47.7 us (33%)
  starting transfers between devices  43.7 us (30%)
  Pallas kernels  42.8 us (29%)
  local copies, waits for them, and re-layouts  6.56 us (4%)
  other arithmetic  4.4 us (3%)
    ppermute x19, waiting for transfers between devices, along_col(): return lax.ppermute(value, 'col', xor_pairs(col_count, j))  36.3 us
    ppermute x7, starting transfers between devices, along_row(): return lax.ppermute(value, 'row', xor_pairs(row_count, j))  17.5 us
    ppermute x19, starting transfers between devices, along_col(): return lax.ppermute(value, 'col', xor_pairs(col_count, j))  17.3 us
    ppermute x7, waiting for transfers between devices, along_row(): return lax.ppermute(value, 'row', xor_pairs(row_count, j))  11.4 us
    pallas_call x3, Pallas kernels, sweep(): pl.pallas_call(functools.partial(sweep_kernel, first, ks, chips, [at for...  11.3 us
    pallas_call x3, Pallas kernels, weigh(): pl.pallas_call(functools.partial(weigh_kernel, root, ks, seg), out_shape=...  10.8 us
    ppermute x3, starting transfers between devices, feature_step(): return lax.ppermute(value, ('row', 'col'), pairs)  8.86 us
    pallas_call x1, Pallas kernels, exponentials(): pl.pallas_call(expo_kernel, out_shape=(jax.ShapeDtypeStruct((PAIRS, rows,...  8.34 us
  transfers between devices with their start and end apart: 29, of which 12 were waited for; matrix products, arithmetic and copies ran while one was open for 3% of the time, Pallas kernels for 25%

profile of v6, /device:TPU:0, one launch (start us, length us, event | category | flops | bytes accessed | tf_op | source)
XLA Modules:
  0.0 145.5 jit_solution(1619489924259807845)
XLA Ops:
  0.6 3.3 %start.1 = (bf16[768,384]{1,0:T(8,128)(2,1)}, bf16[384,1024]{1,0:T(8,128)(2,1)}) custom-call(s32[2]{0:T(128)} %pad_add_fusion.place_ref, s32[3,6]{1,0:T(4,128)} %bitcast.12, bf16[768,384]{1,0:T(8,128)(2,1)} %weight_ref.1, bf16[768,1024]{1,0:T(8,128)(2,1)} %features_ref.1), custom_call_target="tpu_custom_call" | custom-call | flops 294912 | bytes 1179648 | tf_op jit(solution)/shard_map/start/pallas_call | solution.py:71
  3.9 5.7 %collective-permute-start = (bf16[384,1024]{1,0:T(8,128)(2,1)}, bf16[384,1024]{1,0:T(8,128)(2,1)}, u32[]{:S(2)}, u32[]{:S(2)}) collective-permute-start(bf16[384,1024]{1,0:T(8,128)(2,1)} %get-tuple-element.34), channel_id=1, source_target_pairs={{0,8},{1,17},{10,26},{11,3},{20,4},{21,29},{30,22},{31,15}} | collective-permute-start | bytes 2359304 | tf_op jit(solution)/shard_map/ppermute | solution.py:539
  12.8 3.1 %collective-permute-start.1 = (bf16[768,384]{1,0:T(8,128)(2,1)}, bf16[768,384]{1,0:T(8,128)(2,1)S(1)}, u32[]{:S(2)}, u32[]{:S(2)}) collective-permute-start(bf16[768,384]{1,0:T(8,128)(2,1)} %get-tuple-element.41.refs_0_.refs_8_), channel_id=1, source_target_pairs={{0,8},{8,0},{16,24},{24,16},{1,9},{9,1},{17,25},{25,17},{2,10},{10... | collective-permute-start | bytes 1769480 | tf_op jit(solution)/shard_map/ppermute | solution.py:511
  15.9 3.6 %project_in.2.q_ref = bf16[768,512]{1,0:T(8,128)(2,1)} custom-call(s32[1]{0:T(128)} %bitcast.3.place_ref, bf16[768,1024]{1,0:T(8,128)(2,1)} %features_ref.1, bf16[1024,3072]{1,0:T(8,128)(2,1)} %refs_2_.1), custom_call_target="tpu_custom_call" | custom-call | flops 805306368 | bytes 2621440 | tf_op jit(solution)/shard_map/project_in/pallas_call | solution.py:106
  19.5 17.3 %collective-permute-done.4.refs_2_ = bf16[768,384]{1,0:T(8,128)(2,1)S(1)} collective-permute-done((bf16[768,384]{1,0:T(8,128)(2,1)}, bf16[768,384]{1,0:T(8,128)(2,1)S(1)}, u32[]{:S(2)}, u32[]{:S(2)}) %collective-permute-start.4) | collective-permute-done | bytes 589856 | tf_op jit(solution)/shard_map/ppermute | solution.py:508
  42.6 3.6 %collective-permute-start.6 = (bf16[384,384]{1,0:T(8,128)(2,1)S(1)}, bf16[384,384]{1,0:T(8,128)(2,1)S(1)}, u32[]{:S(2)}, u32[]{:S(2)}) collective-permute-start(bf16[384,384]{1,0:T(8,128)(2,1)S(1)} %slice.7), channel_id=1, source_target_pairs={{0,16},{8,24},{16,0},{24,8},{1,17},{9,25},{17,1},{25,9},{2,18},{10... | collective-permute-start | bytes 884744 | tf_op jit(solution)/shard_map/ppermute | solution.py:511
  46.3 3.5 %collective-permute-start.5 = (bf16[384,384]{1,0:T(8,128)(2,1)S(1)}, bf16[384,384]{1,0:T(8,128)(2,1)S(1)}, u32[]{:S(2)}, u32[]{:S(2)}) collective-permute-start(bf16[384,384]{1,0:T(8,128)(2,1)S(1)} %slice.6), channel_id=1, source_target_pairs={{0,8},{8,0},{16,24},{24,16},{1,9},{9,1},{17,25},{25,17},{2,10},{10... | collective-permute-start | bytes 884744 | tf_op jit(solution)/shard_map/ppermute | solution.py:511
  53.7 2.9 %collective-permute-done.5.refs_11_ = bf16[384,384]{1,0:T(8,128)(2,1)S(1)} collective-permute-done((bf16[384,384]{1,0:T(8,128)(2,1)S(1)}, bf16[384,384]{1,0:T(8,128)(2,1)S(1)}, u32[]{:S(2)}, u32[]{:S(2)}) %collective-permute-start.5) | collective-permute-done | bytes 294944 | tf_op jit(solution)/shard_map/ppermute | solution.py:511
  57.5 2.7 %select_select_fusion.refs_13_ = bf16[384,1024]{1,0:T(8,128)(2,1)} fusion(bf16[384,1024]{1,0:T(8,128)(2,1)} %collective-permute-done.10, bf16[384,1024]{1,0:T(8,128)(2,1)} %collective-permute-done, bf16[384,1024]{1,0:T(8,128)(2,1)} %get-tuple-element.34, pred[]{:T(512)S(6)} %eq.22, pred[]{:T(512)S(6)} %eq.21), kind=kLoop, calls=%fused_computation.1 | loop fusion | flops 786432 | bytes 3145730 | tf_op jit(solution)/shard_map/jit(_where)/select_n | solution.py:571
  62.3 4.9 %rank_sweep.3.refs_8_ = bf16[768,384]{1,0:T(8,128)(2,1)S(1)} custom-call(s32[2]{0:T(128)S(1)} %copy-done.10, s32[3,6]{1,0:T(4,128)S(1)} %bitcast.13, bf16[768,384]{1,0:T(8,128)(2,1)S(1)} %copy-done.2, bf16[768,384]{1,0:T(8,128)(2,1)S(1)} %collective-permute-done.3.refs_1_, bf16[768,384]{1,0:T(8,128)(2,1)S(1)} %collective-permute-done.4.refs_2_, ...), custom_call_target="tpu_custom_call" | custom-call | flops 1811939328 | bytes 9437184 | tf_op jit(solution)/shard_map/rank_sweep/pallas_call | solution.py:212
  67.5 4.8 %collective-permute-start.13 = (bf16[768,384]{1,0:T(8,128)(2,1)S(1)}, bf16[768,384]{1,0:T(8,128)(2,1)S(1)}, u32[]{:S(2)}, u32[]{:S(2)}) collective-permute-start(bf16[768,384]{1,0:T(8,128)(2,1)S(1)} %rank_sweep.3.refs_8_), channel_id=1, source_target_pairs={{0,24},{8,16},{16,8},{24,0},{1,25},{9,17},{17,9},{25,1},{2,26},{10... | collective-permute-start | bytes 1769480 | tf_op jit(solution)/shard_map/ppermute | solution.py:511
  73.1 2.9 %project_in.3.k_ref.v_ref = bf16[768,1024]{1,0:T(8,128)(2,1)S(1)} custom-call(s32[1]{0:T(128)} %bitcast.3.place_ref, bf16[384,1024]{1,0:T(8,128)(2,1)S(1)} %broadcast_select_fusion.refs_0_, bf16[384,1024]{1,0:T(8,128)(2,1)S(1)} %collective-permute-done.15.refs_1_, bf16[1024,3072]{1,0:T(8,128)(2,1)S(1)} %bitcast.8), custom_call_target="tpu_custom_call" | custom-call | flops 1610612736 | bytes 3670016 | tf_op jit(solution)/shard_map/project_in/pallas_call | solution.py:106
  76.0 2.3 %collective-permute-start.17 = (bf16[1024,128]{1,0:T(8,128)(2,1)S(1)}, bf16[1024,128]{1,0:T(8,128)(2,1)S(1)}, u32[]{:S(2)}, u32[]{:S(2)}) collective-permute-start(bf16[1024,128]{1,0:T(8,128)(2,1)S(1)} %copy-done.8), channel_id=1, source_target_pairs={{0,4},{1,5},{2,6},{3,7},{4,0},{5,1},{6,2},{7,3},{8,12},{9,13},{10,... | collective-permute-start | bytes 786440 | tf_op jit(solution)/shard_map/ppermute | solution.py:508
  80.2 8.3 %expo.1 = (bf16[4,768,1536]{2,1,0:T(8,128)(2,1)S(1)}, f32[768,128]{1,0:T(8,128)S(1)}) custom-call(s32[3,6]{1,0:T(4,128)S(1)} %bitcast.15, s32[3,6]{1,0:T(4,128)S(1)} %collective-permute-done.18.other_ref, bf16[768,512]{1,0:T(8,128)(2,1)S(1)} %copy-done.3, bf16[768,1024]{1,0:T(8,128)(2,1)S(1)} %project_in.3.k_ref.v_ref), custom_call_target="tpu_custom_call" | custom-call | flops 2415919104 | bytes 9437184 | tf_op jit(solution)/shard_map/expo/pallas_call | solution.py:284
  88.6 2.7 %collective-permute-done.17.refs_14_.refs_2_ = bf16[1024,128]{1,0:T(8,128)(2,1)S(1)} collective-permute-done((bf16[1024,128]{1,0:T(8,128)(2,1)S(1)}, bf16[1024,128]{1,0:T(8,128)(2,1)S(1)}, u32[]{:S(2)}, u32[]{:S(2)}) %collective-permute-start.17) | collective-permute-done | bytes 262176 | tf_op jit(solution)/shard_map/ppermute | solution.py:508
  92.6 5.9 %collective-permute-done.12.refs_10_ = bf16[768,384]{1,0:T(8,128)(2,1)S(1)} collective-permute-done((bf16[768,384]{1,0:T(8,128)(2,1)S(1)}, bf16[768,384]{1,0:T(8,128)(2,1)S(1)}, u32[]{:S(2)}, u32[]{:S(2)}) %collective-permute-start.12) | collective-permute-done | bytes 589856 | tf_op jit(solution)/shard_map/ppermute | solution.py:511
  99.4 3.1 %rank_sweep.5.own_ref = bf16[384,384]{1,0:T(8,128)(2,1)S(1)} custom-call(s32[2]{0:T(128)S(1)} %copy-done.10, s32[3,6]{1,0:T(4,128)S(1)} %bitcast.16, bf16[768,384]{1,0:T(8,128)(2,1)S(1)} %copy-done.2, bf16[768,384]{1,0:T(8,128)(2,1)S(1)} %collective-permute-done.3.refs_1_, bf16[768,384]{1,0:T(8,128)(2,1)S(1)} %collective-permute-done.4.refs_2_, ...), custom_call_target="tpu_custom_call" | custom-call | flops 905969664 | bytes 7077888 | tf_op jit(solution)/shard_map/rank_sweep/pallas_call | solution.py:212
  102.7 3.3 %rank_sweep.4.refs_0_.own_ref = bf16[384,384]{1,0:T(8,128)(2,1)S(1)} custom-call(s32[2]{0:T(128)S(1)} %copy-done.10, s32[3,6]{1,0:T(4,128)S(1)} %bitcast.17, bf16[768,384]{1,0:T(8,128)(2,1)S(1)} %copy-done.2, bf16[768,384]{1,0:T(8,128)(2,1)S(1)} %collective-permute-done.3.refs_1_, bf16[768,384]{1,0:T(8,128)(2,1)S(1)} %collective-permute-done.4.refs_2_, ...), custom_call_target="tpu_custom_call" | custom-call | flops 905969664 | bytes 7077888 | tf_op jit(solution)/shard_map/rank_sweep/pallas_call | solution.py:212
  106.5 3.1 %weigh.3.refs_0_ = bf16[208,512]{1,0:T(8,128)(2,1)S(1)} custom-call(s32[2]{0:T(128)S(1)} %copy-done.10, f32[16]{0:T(128)S(1)} %copy-done.11, f32[16]{0:T(128)S(1)} %copy-done.12, bf16[384,384]{1,0:T(8,128)(2,1)S(1)} %rank_sweep.5.own_ref, bf16[384,384]{1,0:T(8,128)(2,1)S(1)} %collective-permute-done.21.other_ref, ...), custom_call_target="tpu_custom_call" | custom-call | flops 603979776 | bytes 2359296 | tf_op jit(solution)/shard_map/weigh/pallas_call | solution.py:379
  109.6 2.2 %collective-permute-start.24 = (bf16[208,512]{1,0:T(8,128)(2,1)S(1)}, bf16[208,512]{1,0:T(8,128)(2,1)S(1)}, u32[]{:S(2)}, u32[]{:S(2)}) collective-permute-start(bf16[208,512]{1,0:T(8,128)(2,1)S(1)} %weigh.3.refs_0_), channel_id=1, source_target_pairs={{0,6},{1,7},{2,4},{3,5},{4,2},{5,3},{6,0},{7,1},{8,14},{9,15},{10,... | collective-permute-start | bytes 638984 | tf_op jit(solution)/shard_map/ppermute | solution.py:508
  111.8 3.1 %weigh.4.refs_0_ = bf16[208,512]{1,0:T(8,128)(2,1)S(1)} custom-call(s32[2]{0:T(128)S(1)} %copy-done.10, f32[16]{0:T(128)S(1)} %copy-done.11, f32[16]{0:T(128)S(1)} %copy-done.12, bf16[384,384]{1,0:T(8,128)(2,1)S(1)} %rank_sweep.5.own_ref, bf16[384,384]{1,0:T(8,128)(2,1)S(1)} %collective-permute-done.21.other_ref, ...), custom_call_target="tpu_custom_call" | custom-call | flops 603979776 | bytes 2359296 | tf_op jit(solution)/shard_map/weigh/pallas_call | solution.py:379
  117.0 4.7 %weigh.5 = (bf16[208,512]{1,0:T(8,128)(2,1)S(1)}, bf16[208,512]{1,0:T(8,128)(2,1)S(1)}) custom-call(s32[2]{0:T(128)S(1)} %copy-done.10, f32[16]{0:T(128)S(1)} %copy-done.11, f32[16]{0:T(128)S(1)} %copy-done.12, bf16[384,384]{1,0:T(8,128)(2,1)S(1)} %rank_sweep.4.refs_0_.own_ref, bf16[384,384]{1,0:T(8,128)(2,1)S(1)} %collective-permute-done.20.other_ref, ...), custom_call_target="tpu_custom_call" | custom-call | flops 1207959552 | bytes 4718592 | tf_op jit(solution)/shard_map/weigh/pallas_call | solution.py:379
  122.0 10.5 %collective-permute-done.23.refs_2_ = bf16[208,512]{1,0:T(8,128)(2,1)S(1)} collective-permute-done((bf16[208,512]{1,0:T(8,128)(2,1)S(1)}, bf16[208,512]{1,0:T(8,128)(2,1)S(1)}, u32[]{:S(2)}, u32[]{:S(2)}) %collective-permute-start.23) | collective-permute-done | bytes 213024 | tf_op jit(solution)/shard_map/ppermute | solution.py:508
  138.3 3.2 %collective-permute-start.28 = (bf16[192,128]{1,0:T(8,128)(2,1)S(1)}, bf16[192,128]{1,0:T(8,128)(2,1)S(1)}, u32[]{:S(2)}, u32[]{:S(2)}) collective-permute-start(bf16[192,128]{1,0:T(8,128)(2,1)S(1)} %get-tuple-element.61), channel_id=1, source_target_pairs={{0,2},{1,3},{2,0},{3,1},{4,6},{5,7},{6,4},{7,5},{8,10},{9,11},{10,... | collective-permute-start | bytes 147464 | tf_op jit(solution)/shard_map/ppermute | solution.py:508
  (91 shorter events, 34.4 us)
Async XLA Ops:
  3.9 33.4 %collective-permute-start = (bf16[384,1024]{1,0:T(8,128)(2,1)}, bf16[384,1024]{1,0:T(8,128)(2,1)}, u32[]{:S(2)}, u32[]{:S(2)}) collective-permute-start(bf16[384,1024]{1,0:T(8,128)(2,1)} %get-tuple-element.34), channel_id=1, source_target_pairs={{0,8},{1,17},{10,26},{11,3},{20,4},{21,29},{30,22},{31,15}} | collective-permute-start | bytes 2359304 | tf_op jit(solution)/shard_map/ppermute | solution.py:539
  9.7 27.1 %collective-permute-start.4 = (bf16[768,384]{1,0:T(8,128)(2,1)}, bf16[768,384]{1,0:T(8,128)(2,1)S(1)}, u32[]{:S(2)}, u32[]{:S(2)}) collective-permute-start(bf16[768,384]{1,0:T(8,128)(2,1)} %get-tuple-element.41.refs_0_.refs_8_), channel_id=1, source_target_pairs={{0,4},{1,5},{2,6},{3,7},{4,0},{5,1},{6,2},{7,3},{8,12},{9,13},{10,... | collective-permute-start | bytes 1769480 | tf_op jit(solution)/shard_map/ppermute | solution.py:508
  9.7 27.7 %collective-permute-start.3 = (bf16[768,384]{1,0:T(8,128)(2,1)}, bf16[768,384]{1,0:T(8,128)(2,1)S(1)}, u32[]{:S(2)}, u32[]{:S(2)}) collective-permute-start(bf16[768,384]{1,0:T(8,128)(2,1)} %get-tuple-element.41.refs_0_.refs_8_), channel_id=1, source_target_pairs={{0,2},{1,3},{2,0},{3,1},{4,6},{5,7},{6,4},{7,5},{8,10},{9,11},{10,... | collective-permute-start | bytes 1769480 | tf_op jit(solution)/shard_map/ppermute | solution.py:508
  11.1 26.2 %collective-permute-start.2 = (bf16[768,384]{1,0:T(8,128)(2,1)}, bf16[768,384]{1,0:T(8,128)(2,1)S(1)}, u32[]{:S(2)}, u32[]{:S(2)}) collective-permute-start(bf16[768,384]{1,0:T(8,128)(2,1)} %get-tuple-element.41.refs_0_.refs_8_), channel_id=1, source_target_pairs={{0,16},{8,24},{16,0},{24,8},{1,17},{9,25},{17,1},{25,9},{2,18},{10... | collective-permute-start | bytes 1769480 | tf_op jit(solution)/shard_map/ppermute | solution.py:511
  12.8 24.6 %collective-permute-start.1 = (bf16[768,384]{1,0:T(8,128)(2,1)}, bf16[768,384]{1,0:T(8,128)(2,1)S(1)}, u32[]{:S(2)}, u32[]{:S(2)}) collective-permute-start(bf16[768,384]{1,0:T(8,128)(2,1)} %get-tuple-element.41.refs_0_.refs_8_), channel_id=1, source_target_pairs={{0,8},{8,0},{16,24},{24,16},{1,9},{9,1},{17,25},{25,17},{2,10},{10... | collective-permute-start | bytes 1769480 | tf_op jit(solution)/shard_map/ppermute | solution.py:511
  38.6 18.7 %collective-permute-start.7 = (bf16[3,768,384]{2,1,0:T(8,128)(2,1)S(1)}, bf16[3,768,384]{2,1,0:T(8,128)(2,1)S(1)}, u32[]{:S(2)}, u32[]{:S(2)}) collective-permute-start(bf16[3,768,384]{2,1,0:T(8,128)(2,1)S(1)} %pad_maximum_fusion), channel_id=1, source_target_pairs={{0,1},{1,0},{2,3},{3,2},{4,5},{5,4},{6,7},{7,6},{8,9},{9,8},{10,11... | collective-permute-start | bytes 5308424 | tf_op jit(solution)/shard_map/ppermute | solution.py:508
  38.7 11.0 %collective-permute-start.10 = (bf16[384,1024]{1,0:T(8,128)(2,1)}, bf16[384,1024]{1,0:T(8,128)(2,1)}, u32[]{:S(2)}, u32[]{:S(2)}) collective-permute-start(bf16[384,1024]{1,0:T(8,128)(2,1)} %collective-permute-done), channel_id=1, source_target_pairs={{8,24},{17,25},{26,18},{3,19},{4,12},{29,13},{22,6},{15,7}} | collective-permute-start | bytes 2359304 | tf_op jit(solution)/shard_map/ppermute | solution.py:539
  40.3 17.1 %collective-permute-start.8 = (bf16[768,384]{1,0:T(8,128)(2,1)S(1)}, bf16[768,384]{1,0:T(8,128)(2,1)}, u32[]{:S(2)}, u32[]{:S(2)}) collective-permute-start(bf16[768,384]{1,0:T(8,128)(2,1)S(1)} %collective-permute-done.4.refs_2_), channel_id=1, source_target_pairs={{0,2},{1,3},{2,0},{3,1},{4,6},{5,7},{6,4},{7,5},{8,10},{9,11},{10,... | collective-permute-start | bytes 1769480 | tf_op jit(solution)/shard_map/ppermute | solution.py:508
  42.6 10.4 %collective-permute-start.6 = (bf16[384,384]{1,0:T(8,128)(2,1)S(1)}, bf16[384,384]{1,0:T(8,128)(2,1)S(1)}, u32[]{:S(2)}, u32[]{:S(2)}) collective-permute-start(bf16[384,384]{1,0:T(8,128)(2,1)S(1)} %slice.7), channel_id=1, source_target_pairs={{0,16},{8,24},{16,0},{24,8},{1,17},{9,25},{17,1},{25,9},{2,18},{10... | collective-permute-start | bytes 884744 | tf_op jit(solution)/shard_map/ppermute | solution.py:511
  46.3 10.4 %collective-permute-start.5 = (bf16[384,384]{1,0:T(8,128)(2,1)S(1)}, bf16[384,384]{1,0:T(8,128)(2,1)S(1)}, u32[]{:S(2)}, u32[]{:S(2)}) collective-permute-start(bf16[384,384]{1,0:T(8,128)(2,1)S(1)} %slice.6), channel_id=1, source_target_pairs={{0,8},{8,0},{16,24},{24,16},{1,9},{9,1},{17,25},{25,17},{2,10},{10... | collective-permute-start | bytes 884744 | tf_op jit(solution)/shard_map/ppermute | solution.py:511
  49.8 17.4 %collective-permute-start.14 = (bf16[384,1024]{1,0:T(8,128)(2,1)}, bf16[384,1024]{1,0:T(8,128)(2,1)}, u32[]{:S(2)}, u32[]{:S(2)}) collective-permute-start(bf16[384,1024]{1,0:T(8,128)(2,1)} %collective-permute-done.10), channel_id=1, source_target_pairs={{24,16},{25,9},{18,2},{19,27},{12,28},{13,5},{6,14},{7,23}} | collective-permute-start | bytes 2359304 | tf_op jit(solution)/shard_map/ppermute | solution.py:539
  67.5 25.2 %collective-permute-start.13 = (bf16[768,384]{1,0:T(8,128)(2,1)S(1)}, bf16[768,384]{1,0:T(8,128)(2,1)S(1)}, u32[]{:S(2)}, u32[]{:S(2)}) collective-permute-start(bf16[768,384]{1,0:T(8,128)(2,1)S(1)} %rank_sweep.3.refs_8_), channel_id=1, source_target_pairs={{0,24},{8,16},{16,8},{24,0},{1,25},{9,17},{17,9},{25,1},{2,26},{10... | collective-permute-start | bytes 1769480 | tf_op jit(solution)/shard_map/ppermute | solution.py:511
  72.3 26.3 %collective-permute-start.12 = (bf16[768,384]{1,0:T(8,128)(2,1)S(1)}, bf16[768,384]{1,0:T(8,128)(2,1)S(1)}, u32[]{:S(2)}, u32[]{:S(2)}) collective-permute-start(bf16[768,384]{1,0:T(8,128)(2,1)S(1)} %rank_sweep.3.refs_8_), channel_id=1, source_target_pairs={{0,16},{8,24},{16,0},{24,8},{1,17},{9,25},{17,1},{25,9},{2,18},{10... | collective-permute-start | bytes 1769480 | tf_op jit(solution)/shard_map/ppermute | solution.py:511
  72.6 26.8 %collective-permute-start.11 = (bf16[768,384]{1,0:T(8,128)(2,1)S(1)}, bf16[768,384]{1,0:T(8,128)(2,1)S(1)}, u32[]{:S(2)}, u32[]{:S(2)}) collective-permute-start(bf16[768,384]{1,0:T(8,128)(2,1)S(1)} %rank_sweep.3.refs_8_), channel_id=1, source_target_pairs={{0,8},{8,0},{16,24},{24,16},{1,9},{9,1},{17,25},{25,17},{2,10},{10... | collective-permute-start | bytes 1769480 | tf_op jit(solution)/shard_map/ppermute | solution.py:511
  76.0 15.3 %collective-permute-start.17 = (bf16[1024,128]{1,0:T(8,128)(2,1)S(1)}, bf16[1024,128]{1,0:T(8,128)(2,1)S(1)}, u32[]{:S(2)}, u32[]{:S(2)}) collective-permute-start(bf16[1024,128]{1,0:T(8,128)(2,1)S(1)} %copy-done.8), channel_id=1, source_target_pairs={{0,4},{1,5},{2,6},{3,7},{4,0},{5,1},{6,2},{7,3},{8,12},{9,13},{10,... | collective-permute-start | bytes 786440 | tf_op jit(solution)/shard_map/ppermute | solution.py:508
  78.3 13.0 %collective-permute-start.16 = (bf16[1024,128]{1,0:T(8,128)(2,1)S(1)}, bf16[1024,128]{1,0:T(8,128)(2,1)S(1)}, u32[]{:S(2)}, u32[]{:S(2)}) collective-permute-start(bf16[1024,128]{1,0:T(8,128)(2,1)S(1)} %copy-done.8), channel_id=1, source_target_pairs={{0,2},{1,3},{2,0},{3,1},{4,6},{5,7},{6,4},{7,5},{8,10},{9,11},{10,... | collective-permute-start | bytes 786440 | tf_op jit(solution)/shard_map/ppermute | solution.py:508
  91.3 11.3 %collective-permute-start.19 = (bf16[1024,128]{1,0:T(8,128)(2,1)S(1)}, bf16[1024,128]{1,0:T(8,128)(2,1)S(1)}, u32[]{:S(2)}, u32[]{:S(2)}) collective-permute-start(bf16[1024,128]{1,0:T(8,128)(2,1)S(1)} %collective-permute-done.17.refs_14_.refs_2_), channel_id=1, source_target_pairs={{0,2},{1,3},{2,0},{3,1},{4,6},{5,7},{6,4},{7,5},{8,10},{9,11},{10,... | collective-permute-start | bytes 786440 | tf_op jit(solution)/shard_map/ppermute | solution.py:508
  106.0 11.0 %collective-permute-start.20 = (bf16[384,384]{1,0:T(8,128)(2,1)S(1)}, bf16[384,384]{1,0:T(8,128)(2,1)S(1)}, u32[]{:S(2)}, u32[]{:S(2)}) collective-permute-start(bf16[384,384]{1,0:T(8,128)(2,1)S(1)} %rank_sweep.4.refs_0_.own_ref), channel_id=1, source_target_pairs={{0,1},{1,0},{2,3},{3,2},{4,5},{5,4},{6,7},{7,6},{8,9},{9,8},{10,11... | collective-permute-start | bytes 884744 | tf_op jit(solution)/shard_map/ppermute | solution.py:508
  109.6 22.9 %collective-permute-start.24 = (bf16[208,512]{1,0:T(8,128)(2,1)S(1)}, bf16[208,512]{1,0:T(8,128)(2,1)S(1)}, u32[]{:S(2)}, u32[]{:S(2)}) collective-permute-start(bf16[208,512]{1,0:T(8,128)(2,1)S(1)} %weigh.3.refs_0_), channel_id=1, source_target_pairs={{0,6},{1,7},{2,4},{3,5},{4,2},{5,3},{6,0},{7,1},{8,14},{9,15},{10,... | collective-permute-start | bytes 638984 | tf_op jit(solution)/shard_map/ppermute | solution.py:508
  114.9 17.6 %collective-permute-start.23 = (bf16[208,512]{1,0:T(8,128)(2,1)S(1)}, bf16[208,512]{1,0:T(8,128)(2,1)S(1)}, u32[]{:S(2)}, u32[]{:S(2)}) collective-permute-start(bf16[208,512]{1,0:T(8,128)(2,1)S(1)} %weigh.4.refs_0_), channel_id=1, source_target_pairs={{0,4},{1,5},{2,6},{3,7},{4,0},{5,1},{6,2},{7,3},{8,12},{9,13},{10,... | collective-permute-start | bytes 638984 | tf_op jit(solution)/shard_map/ppermute | solution.py:508
  121.7 11.3 %collective-permute-start.22 = (bf16[208,512]{1,0:T(8,128)(2,1)S(1)}, bf16[208,512]{1,0:T(8,128)(2,1)S(1)}, u32[]{:S(2)}, u32[]{:S(2)}) collective-permute-start(bf16[208,512]{1,0:T(8,128)(2,1)S(1)} %get-tuple-element.57), channel_id=1, source_target_pairs={{0,2},{1,3},{2,0},{3,1},{4,6},{5,7},{6,4},{7,5},{8,10},{9,11},{10,... | collective-permute-start | bytes 638984 | tf_op jit(solution)/shard_map/ppermute | solution.py:508
  137.0 6.5 %collective-permute-start.26 = (bf16[192,128]{1,0:T(8,128)(2,1)S(1)}, bf16[192,128]{1,0:T(8,128)(2,1)S(1)}, u32[]{:S(2)}, u32[]{:S(2)}) collective-permute-start(bf16[192,128]{1,0:T(8,128)(2,1)S(1)} %get-tuple-element.59), channel_id=1, source_target_pairs={{0,6},{1,7},{2,4},{3,5},{4,2},{5,3},{6,0},{7,1},{8,14},{9,15},{10,... | collective-permute-start | bytes 147464 | tf_op jit(solution)/shard_map/ppermute | solution.py:508
  138.3 6.5 %collective-permute-start.27 = (bf16[192,128]{1,0:T(8,128)(2,1)S(1)}, bf16[192,128]{1,0:T(8,128)(2,1)S(1)}, u32[]{:S(2)}, u32[]{:S(2)}) collective-permute-start(bf16[192,128]{1,0:T(8,128)(2,1)S(1)} %get-tuple-element.60), channel_id=1, source_target_pairs={{0,4},{1,5},{2,6},{3,7},{4,0},{5,1},{6,2},{7,3},{8,12},{9,13},{10,... | collective-permute-start | bytes 147464 | tf_op jit(solution)/shard_map/ppermute | solution.py:508
  138.3 6.5 %collective-permute-start.28 = (bf16[192,128]{1,0:T(8,128)(2,1)S(1)}, bf16[192,128]{1,0:T(8,128)(2,1)S(1)}, u32[]{:S(2)}, u32[]{:S(2)}) collective-permute-start(bf16[192,128]{1,0:T(8,128)(2,1)S(1)} %get-tuple-element.61), channel_id=1, source_target_pairs={{0,2},{1,3},{2,0},{3,1},{4,6},{5,7},{6,4},{7,5},{8,10},{9,11},{10,... | collective-permute-start | bytes 147464 | tf_op jit(solution)/shard_map/ppermute | solution.py:508
  (23 other events, 173.4 us)

commit v7 on v6

--- a/solution.py
+++ b/solution.py
@@ -53,10 +53,10 @@
     return jnp.concatenate(tiles, axis=0)
 
 
-def start_kernel(place_ref, pattern_ref, weight_ref, features_ref, out_ref, cut_ref, sem):
+def start_kernel(pattern_ref, weight_ref, features_ref, out_ref, cut_ref, sem):
     cols = cut_ref.shape[0]
     ratio = features_ref.shape[0] // cols
-    at = pl.multiple_of(lax.rem(place_ref[1], ratio) * cols, cols)
+    at = pl.multiple_of(lax.rem(lax.axis_index("col"), ratio) * cols, cols)
     copy = pltpu.make_async_copy(features_ref.at[pl.ds(at, cols), :], cut_ref, sem)
     copy.start()
     for i in range(out_ref.shape[0] // BLK):
@@ -66,7 +66,7 @@
     copy.wait()
 
 
-def start(place, pattern, weight, features):
+def start(pattern, weight, features):
     rows, cols = weight.shape
     return pl.pallas_call(
         start_kernel,
@@ -74,13 +74,13 @@
             jax.ShapeDtypeStruct((rows, cols), BF16),
             jax.ShapeDtypeStruct((cols, features.shape[1]), BF16),
         ),
-        in_specs=[SMEM, SMEM, VMEM, HBM],
+        in_specs=[SMEM, VMEM, HBM],
         out_specs=(VMEM, VMEM),
         scratch_shapes=[pltpu.SemaphoreType.DMA],
         compiler_params=params(),
         cost_estimate=cost(rows * cols, 4 * rows * cols),
         name="start",
-    )(place, pattern, weight, features)
+    )(pattern, weight, features)
 
 
 def project_in_kernel(scale, place_ref, *refs):
@@ -538,7 +538,7 @@
             pairs.append((here * col_count + c, there * col_count + c))
         return lax.ppermute(value, ("row", "col"), pairs)
 
-    adjacency, features = start(place, pattern, edge_weight, node_features)
+    adjacency, features = start(pattern, edge_weight, node_features)
     blocks = spread({0: adjacency}, 1)
     near = [1, 2] if row_count == 4 else list(range(1, row_count))
     columns = {j: along_row(adjacency, j) for j in near}

time: 146 us -> 143 us (0.979)
  local copies, waits for them, and re-layouts: 6.56 us -> 3.5 us
    unnamed x36 -> x30, local copies, waits for them, and re-layouts: 4.57 us -> 1.51 us
  transfers between devices with their start and end apart: 29 -> 29, of which waited for: 12 -> 12; matrix products, arithmetic and copies ran while one was open for 3% -> 3% of each run, Pallas kernels for 25% -> 26%
where the time goes in v7:
time: 143 us
  waiting for transfers between devices  47.6 us (33%)
  starting transfers between devices  44.9 us (31%)
  Pallas kernels  42.9 us (30%)
  other arithmetic  3.83 us (3%)
  local copies, waits for them, and re-layouts  3.5 us (2%)
    ppermute x19, waiting for transfers between devices, along_col(): return lax.ppermute(value, 'col', xor_pairs(col_count, j))  36.1 us
    ppermute x7, starting transfers between devices, along_row(): return lax.ppermute(value, 'row', xor_pairs(row_count, j))  18.4 us
    ppermute x19, starting transfers between devices, along_col(): return lax.ppermute(value, 'col', xor_pairs(col_count, j))  17.6 us
    ppermute x7, waiting for transfers between devices, along_row(): return lax.ppermute(value, 'row', xor_pairs(row_count, j))  11.5 us
    pallas_call x3, Pallas kernels, sweep(): pl.pallas_call(functools.partial(sweep_kernel, first, ks, chips, [at for...  11.5 us
    pallas_call x3, Pallas kernels, weigh(): pl.pallas_call(functools.partial(weigh_kernel, root, ks, seg), out_shape=...  10.8 us
    ppermute x3, starting transfers between devices, feature_step(): return lax.ppermute(value, ('row', 'col'), pairs)  8.86 us
    pallas_call x1, Pallas kernels, exponentials(): pl.pallas_call(expo_kernel, out_shape=(jax.ShapeDtypeStruct((PAIRS, rows,...  8.34 us
  transfers between devices with their start and end apart: 29, of which 12 were waited for; matrix products, arithmetic and copies ran while one was open for 3% of the time, Pallas kernels for 26%

profile of v7, /device:TPU:0, one launch (start us, length us, event | category | flops | bytes accessed | tf_op | source)
XLA Modules:
  0.0 143.1 jit_solution(8752420738590331308)
XLA Ops:
  0.0 3.3 %start.1 = (bf16[768,384]{1,0:T(8,128)(2,1)}, bf16[384,1024]{1,0:T(8,128)(2,1)}) custom-call(s32[3,6]{1,0:T(4,128)} %bitcast.12, bf16[768,384]{1,0:T(8,128)(2,1)} %weight_ref.1, bf16[768,1024]{1,0:T(8,128)(2,1)} %features_ref.1), custom_call_target="tpu_custom_call" | custom-call | flops 294912 | bytes 1179648 | tf_op jit(solution)/shard_map/start/pallas_call | solution.py:71
  3.3 5.7 %collective-permute-start = (bf16[384,1024]{1,0:T(8,128)(2,1)}, bf16[384,1024]{1,0:T(8,128)(2,1)}, u32[]{:S(2)}, u32[]{:S(2)}) collective-permute-start(bf16[384,1024]{1,0:T(8,128)(2,1)} %get-tuple-element.34), channel_id=1, source_target_pairs={{0,8},{1,17},{10,26},{11,3},{20,4},{21,29},{30,22},{31,15}} | collective-permute-start | bytes 2359304 | tf_op jit(solution)/shard_map/ppermute | solution.py:539
  12.2 3.1 %collective-permute-start.1 = (bf16[768,384]{1,0:T(8,128)(2,1)}, bf16[768,384]{1,0:T(8,128)(2,1)}, u32[]{:S(2)}, u32[]{:S(2)}) collective-permute-start(bf16[768,384]{1,0:T(8,128)(2,1)} %get-tuple-element.41.refs_0_.refs_8_), channel_id=1, source_target_pairs={{0,8},{8,0},{16,24},{24,16},{1,9},{9,1},{17,25},{25,17},{2,10},{10... | collective-permute-start | bytes 1769480 | tf_op jit(solution)/shard_map/ppermute | solution.py:511
  15.3 3.6 %project_in.2.q_ref = bf16[768,512]{1,0:T(8,128)(2,1)} custom-call(s32[1]{0:T(128)} %bitcast.3.place_ref, bf16[768,1024]{1,0:T(8,128)(2,1)} %features_ref.1, bf16[1024,3072]{1,0:T(8,128)(2,1)} %refs_2_.1), custom_call_target="tpu_custom_call" | custom-call | flops 805306368 | bytes 2621440 | tf_op jit(solution)/shard_map/project_in/pallas_call | solution.py:106
  18.9 17.3 %collective-permute-done.4.refs_2_ = bf16[768,384]{1,0:T(8,128)(2,1)S(1)} collective-permute-done((bf16[768,384]{1,0:T(8,128)(2,1)}, bf16[768,384]{1,0:T(8,128)(2,1)S(1)}, u32[]{:S(2)}, u32[]{:S(2)}) %collective-permute-start.4) | collective-permute-done | bytes 589856 | tf_op jit(solution)/shard_map/ppermute | solution.py:508
  41.0 3.7 %collective-permute-start.6 = (bf16[384,384]{1,0:T(8,128)(2,1)S(1)}, bf16[384,384]{1,0:T(8,128)(2,1)S(1)}, u32[]{:S(2)}, u32[]{:S(2)}) collective-permute-start(bf16[384,384]{1,0:T(8,128)(2,1)S(1)} %slice.7), channel_id=1, source_target_pairs={{0,16},{8,24},{16,0},{24,8},{1,17},{9,25},{17,1},{25,9},{2,18},{10... | collective-permute-start | bytes 884744 | tf_op jit(solution)/shard_map/ppermute | solution.py:511
  44.6 3.5 %collective-permute-start.5 = (bf16[384,384]{1,0:T(8,128)(2,1)S(1)}, bf16[384,384]{1,0:T(8,128)(2,1)S(1)}, u32[]{:S(2)}, u32[]{:S(2)}) collective-permute-start(bf16[384,384]{1,0:T(8,128)(2,1)S(1)} %slice.6), channel_id=1, source_target_pairs={{0,8},{8,0},{16,24},{24,16},{1,9},{9,1},{17,25},{25,17},{2,10},{10... | collective-permute-start | bytes 884744 | tf_op jit(solution)/shard_map/ppermute | solution.py:511
  52.1 2.9 %collective-permute-done.5.refs_11_ = bf16[384,384]{1,0:T(8,128)(2,1)S(1)} collective-permute-done((bf16[384,384]{1,0:T(8,128)(2,1)S(1)}, bf16[384,384]{1,0:T(8,128)(2,1)S(1)}, u32[]{:S(2)}, u32[]{:S(2)}) %collective-permute-start.5) | collective-permute-done | bytes 294944 | tf_op jit(solution)/shard_map/ppermute | solution.py:511
  55.9 2.7 %select_select_fusion.refs_13_ = bf16[384,1024]{1,0:T(8,128)(2,1)} fusion(bf16[384,1024]{1,0:T(8,128)(2,1)} %collective-permute-done.10, bf16[384,1024]{1,0:T(8,128)(2,1)} %collective-permute-done, bf16[384,1024]{1,0:T(8,128)(2,1)} %get-tuple-element.34, pred[]{:T(512)S(6)} %eq.22, pred[]{:T(512)S(6)} %eq.21), kind=kLoop, calls=%fused_computation.1 | loop fusion | flops 786432 | bytes 3145730 | tf_op jit(solution)/shard_map/jit(_where)/select_n | solution.py:571
  58.7 5.0 %rank_sweep.3.refs_8_ = bf16[768,384]{1,0:T(8,128)(2,1)S(1)} custom-call(s32[2]{0:T(128)S(1)} %pad_add_fusion.place_ref, s32[3,6]{1,0:T(4,128)S(1)} %bitcast.13, bf16[768,384]{1,0:T(8,128)(2,1)S(1)} %copy-done.2, bf16[768,384]{1,0:T(8,128)(2,1)S(1)} %collective-permute-done.3.refs_1_, bf16[768,384]{1,0:T(8,128)(2,1)S(1)} %collective-permute-done.4.refs_2_, ...), custom_call_target="tpu_custom_call" | custom-call | flops 1811939328 | bytes 9437184 | tf_op jit(solution)/shard_map/rank_sweep/pallas_call | solution.py:212
  64.0 4.8 %collective-permute-start.13 = (bf16[768,384]{1,0:T(8,128)(2,1)S(1)}, bf16[768,384]{1,0:T(8,128)(2,1)S(1)}, u32[]{:S(2)}, u32[]{:S(2)}) collective-permute-start(bf16[768,384]{1,0:T(8,128)(2,1)S(1)} %rank_sweep.3.refs_8_), channel_id=1, source_target_pairs={{0,24},{8,16},{16,8},{24,0},{1,25},{9,17},{17,9},{25,1},{2,26},{10... | collective-permute-start | bytes 1769480 | tf_op jit(solution)/shard_map/ppermute | solution.py:511
  70.5 2.8 %project_in.3.k_ref.v_ref = bf16[768,1024]{1,0:T(8,128)(2,1)S(1)} custom-call(s32[1]{0:T(128)} %bitcast.3.place_ref, bf16[384,1024]{1,0:T(8,128)(2,1)S(1)} %broadcast_select_fusion.refs_0_, bf16[384,1024]{1,0:T(8,128)(2,1)S(1)} %collective-permute-done.15.refs_1_, bf16[1024,3072]{1,0:T(8,128)(2,1)S(1)} %bitcast.8), custom_call_target="tpu_custom_call" | custom-call | flops 1610612736 | bytes 3670016 | tf_op jit(solution)/shard_map/project_in/pallas_call | solution.py:106
  75.5 2.5 %collective-permute-start.16 = (bf16[1024,128]{1,0:T(8,128)(2,1)S(1)}, bf16[1024,128]{1,0:T(8,128)(2,1)S(1)}, u32[]{:S(2)}, u32[]{:S(2)}) collective-permute-start(bf16[1024,128]{1,0:T(8,128)(2,1)S(1)} %copy-done.8), channel_id=1, source_target_pairs={{0,2},{1,3},{2,0},{3,1},{4,6},{5,7},{6,4},{7,5},{8,10},{9,11},{10,... | collective-permute-start | bytes 786440 | tf_op jit(solution)/shard_map/ppermute | solution.py:508
  78.0 8.3 %expo.1 = (bf16[4,768,1536]{2,1,0:T(8,128)(2,1)S(1)}, f32[768,128]{1,0:T(8,128)S(1)}) custom-call(s32[3,6]{1,0:T(4,128)S(1)} %bitcast.15, s32[3,6]{1,0:T(4,128)S(1)} %collective-permute-done.18.other_ref, bf16[768,512]{1,0:T(8,128)(2,1)S(1)} %copy-done.3, bf16[768,1024]{1,0:T(8,128)(2,1)S(1)} %project_in.3.k_ref.v_ref), custom_call_target="tpu_custom_call" | custom-call | flops 2415919104 | bytes 9437184 | tf_op jit(solution)/shard_map/expo/pallas_call | solution.py:284
  86.4 2.3 %collective-permute-done.17.refs_14_.refs_2_ = bf16[1024,128]{1,0:T(8,128)(2,1)S(1)} collective-permute-done((bf16[1024,128]{1,0:T(8,128)(2,1)S(1)}, bf16[1024,128]{1,0:T(8,128)(2,1)S(1)}, u32[]{:S(2)}, u32[]{:S(2)}) %collective-permute-start.17) | collective-permute-done | bytes 262176 | tf_op jit(solution)/shard_map/ppermute | solution.py:508
  89.9 5.2 %collective-permute-done.12.refs_10_ = bf16[768,384]{1,0:T(8,128)(2,1)S(1)} collective-permute-done((bf16[768,384]{1,0:T(8,128)(2,1)S(1)}, bf16[768,384]{1,0:T(8,128)(2,1)S(1)}, u32[]{:S(2)}, u32[]{:S(2)}) %collective-permute-start.12) | collective-permute-done | bytes 589856 | tf_op jit(solution)/shard_map/ppermute | solution.py:511
  96.8 3.1 %rank_sweep.5.own_ref = bf16[384,384]{1,0:T(8,128)(2,1)S(1)} custom-call(s32[2]{0:T(128)S(1)} %pad_add_fusion.place_ref, s32[3,6]{1,0:T(4,128)S(1)} %bitcast.16, bf16[768,384]{1,0:T(8,128)(2,1)S(1)} %copy-done.2, bf16[768,384]{1,0:T(8,128)(2,1)S(1)} %collective-permute-done.3.refs_1_, bf16[768,384]{1,0:T(8,128)(2,1)S(1)} %collective-permute-done.4.refs_2_, ...), custom_call_target="tpu_custom_call" | custom-call | flops 905969664 | bytes 7077888 | tf_op jit(solution)/shard_map/rank_sweep/pallas_call | solution.py:212
  100.1 3.3 %rank_sweep.4.refs_0_.own_ref = bf16[384,384]{1,0:T(8,128)(2,1)S(1)} custom-call(s32[2]{0:T(128)S(1)} %pad_add_fusion.place_ref, s32[3,6]{1,0:T(4,128)S(1)} %bitcast.17, bf16[768,384]{1,0:T(8,128)(2,1)S(1)} %copy-done.2, bf16[768,384]{1,0:T(8,128)(2,1)S(1)} %collective-permute-done.3.refs_1_, bf16[768,384]{1,0:T(8,128)(2,1)S(1)} %collective-permute-done.4.refs_2_, ...), custom_call_target="tpu_custom_call" | custom-call | flops 905969664 | bytes 7077888 | tf_op jit(solution)/shard_map/rank_sweep/pallas_call | solution.py:212
  104.0 3.1 %weigh.3.refs_0_ = bf16[208,512]{1,0:T(8,128)(2,1)S(1)} custom-call(s32[2]{0:T(128)S(1)} %pad_add_fusion.place_ref, f32[16]{0:T(128)S(1)} %copy-done.10, f32[16]{0:T(128)S(1)} %copy-done.11, bf16[384,384]{1,0:T(8,128)(2,1)S(1)} %rank_sweep.5.own_ref, bf16[384,384]{1,0:T(8,128)(2,1)S(1)} %collective-permute-done.21.other_ref, ...), custom_call_target="tpu_custom_call" | custom-call | flops 603979776 | bytes 2359296 | tf_op jit(solution)/shard_map/weigh/pallas_call | solution.py:379
  109.2 3.1 %weigh.4.refs_0_ = bf16[208,512]{1,0:T(8,128)(2,1)S(1)} custom-call(s32[2]{0:T(128)S(1)} %pad_add_fusion.place_ref, f32[16]{0:T(128)S(1)} %copy-done.10, f32[16]{0:T(128)S(1)} %copy-done.11, bf16[384,384]{1,0:T(8,128)(2,1)S(1)} %rank_sweep.5.own_ref, bf16[384,384]{1,0:T(8,128)(2,1)S(1)} %collective-permute-done.21.other_ref, ...), custom_call_target="tpu_custom_call" | custom-call | flops 603979776 | bytes 2359296 | tf_op jit(solution)/shard_map/weigh/pallas_call | solution.py:379
  112.3 2.4 %collective-permute-start.23 = (bf16[208,512]{1,0:T(8,128)(2,1)S(1)}, bf16[208,512]{1,0:T(8,128)(2,1)S(1)}, u32[]{:S(2)}, u32[]{:S(2)}) collective-permute-start(bf16[208,512]{1,0:T(8,128)(2,1)S(1)} %weigh.4.refs_0_), channel_id=1, source_target_pairs={{0,4},{1,5},{2,6},{3,7},{4,0},{5,1},{6,2},{7,3},{8,12},{9,13},{10,... | collective-permute-start | bytes 638984 | tf_op jit(solution)/shard_map/ppermute | solution.py:508
  114.7 4.7 %weigh.5 = (bf16[208,512]{1,0:T(8,128)(2,1)S(1)}, bf16[208,512]{1,0:T(8,128)(2,1)S(1)}) custom-call(s32[2]{0:T(128)S(1)} %pad_add_fusion.place_ref, f32[16]{0:T(128)S(1)} %copy-done.10, f32[16]{0:T(128)S(1)} %copy-done.11, bf16[384,384]{1,0:T(8,128)(2,1)S(1)} %rank_sweep.4.refs_0_.own_ref, bf16[384,384]{1,0:T(8,128)(2,1)S(1)} %collective-permute-done.20.other_ref, ...), custom_call_target="tpu_custom_call" | custom-call | flops 1207959552 | bytes 4718592 | tf_op jit(solution)/shard_map/weigh/pallas_call | solution.py:379
  119.4 10.5 %collective-permute-done.23.refs_2_ = bf16[208,512]{1,0:T(8,128)(2,1)S(1)} collective-permute-done((bf16[208,512]{1,0:T(8,128)(2,1)S(1)}, bf16[208,512]{1,0:T(8,128)(2,1)S(1)}, u32[]{:S(2)}, u32[]{:S(2)}) %collective-permute-start.23) | collective-permute-done | bytes 213024 | tf_op jit(solution)/shard_map/ppermute | solution.py:508
  135.9 3.2 %collective-permute-start.28 = (bf16[192,128]{1,0:T(8,128)(2,1)S(1)}, bf16[192,128]{1,0:T(8,128)(2,1)S(1)}, u32[]{:S(2)}, u32[]{:S(2)}) collective-permute-start(bf16[192,128]{1,0:T(8,128)(2,1)S(1)} %get-tuple-element.61), channel_id=1, source_target_pairs={{0,2},{1,3},{2,0},{3,1},{4,6},{5,7},{6,4},{7,5},{8,10},{9,11},{10,... | collective-permute-start | bytes 147464 | tf_op jit(solution)/shard_map/ppermute | solution.py:508
  (85 shorter events, 32.7 us)
Async XLA Ops:
  3.3 33.4 %collective-permute-start = (bf16[384,1024]{1,0:T(8,128)(2,1)}, bf16[384,1024]{1,0:T(8,128)(2,1)}, u32[]{:S(2)}, u32[]{:S(2)}) collective-permute-start(bf16[384,1024]{1,0:T(8,128)(2,1)} %get-tuple-element.34), channel_id=1, source_target_pairs={{0,8},{1,17},{10,26},{11,3},{20,4},{21,29},{30,22},{31,15}} | collective-permute-start | bytes 2359304 | tf_op jit(solution)/shard_map/ppermute | solution.py:539
  9.0 27.1 %collective-permute-start.4 = (bf16[768,384]{1,0:T(8,128)(2,1)}, bf16[768,384]{1,0:T(8,128)(2,1)S(1)}, u32[]{:S(2)}, u32[]{:S(2)}) collective-permute-start(bf16[768,384]{1,0:T(8,128)(2,1)} %get-tuple-element.41.refs_0_.refs_8_), channel_id=1, source_target_pairs={{0,4},{1,5},{2,6},{3,7},{4,0},{5,1},{6,2},{7,3},{8,12},{9,13},{10,... | collective-permute-start | bytes 1769480 | tf_op jit(solution)/shard_map/ppermute | solution.py:508
  9.0 27.7 %collective-permute-start.3 = (bf16[768,384]{1,0:T(8,128)(2,1)}, bf16[768,384]{1,0:T(8,128)(2,1)S(1)}, u32[]{:S(2)}, u32[]{:S(2)}) collective-permute-start(bf16[768,384]{1,0:T(8,128)(2,1)} %get-tuple-element.41.refs_0_.refs_8_), channel_id=1, source_target_pairs={{0,2},{1,3},{2,0},{3,1},{4,6},{5,7},{6,4},{7,5},{8,10},{9,11},{10,... | collective-permute-start | bytes 1769480 | tf_op jit(solution)/shard_map/ppermute | solution.py:508
  10.5 26.2 %collective-permute-start.2 = (bf16[768,384]{1,0:T(8,128)(2,1)}, bf16[768,384]{1,0:T(8,128)(2,1)}, u32[]{:S(2)}, u32[]{:S(2)}) collective-permute-start(bf16[768,384]{1,0:T(8,128)(2,1)} %get-tuple-element.41.refs_0_.refs_8_), channel_id=1, source_target_pairs={{0,16},{8,24},{16,0},{24,8},{1,17},{9,25},{17,1},{25,9},{2,18},{10... | collective-permute-start | bytes 1769480 | tf_op jit(solution)/shard_map/ppermute | solution.py:511
  12.2 24.5 %collective-permute-start.1 = (bf16[768,384]{1,0:T(8,128)(2,1)}, bf16[768,384]{1,0:T(8,128)(2,1)}, u32[]{:S(2)}, u32[]{:S(2)}) collective-permute-start(bf16[768,384]{1,0:T(8,128)(2,1)} %get-tuple-element.41.refs_0_.refs_8_), channel_id=1, source_target_pairs={{0,8},{8,0},{16,24},{24,16},{1,9},{9,1},{17,25},{25,17},{2,10},{10... | collective-permute-start | bytes 1769480 | tf_op jit(solution)/shard_map/ppermute | solution.py:511
  37.0 18.7 %collective-permute-start.7 = (bf16[3,768,384]{2,1,0:T(8,128)(2,1)S(1)}, bf16[3,768,384]{2,1,0:T(8,128)(2,1)S(1)}, u32[]{:S(2)}, u32[]{:S(2)}) collective-permute-start(bf16[3,768,384]{2,1,0:T(8,128)(2,1)S(1)} %pad_maximum_fusion), channel_id=1, source_target_pairs={{0,1},{1,0},{2,3},{3,2},{4,5},{5,4},{6,7},{7,6},{8,9},{9,8},{10,11... | collective-permute-start | bytes 5308424 | tf_op jit(solution)/shard_map/ppermute | solution.py:508
  37.1 11.0 %collective-permute-start.10 = (bf16[384,1024]{1,0:T(8,128)(2,1)}, bf16[384,1024]{1,0:T(8,128)(2,1)}, u32[]{:S(2)}, u32[]{:S(2)}) collective-permute-start(bf16[384,1024]{1,0:T(8,128)(2,1)} %collective-permute-done), channel_id=1, source_target_pairs={{8,24},{17,25},{26,18},{3,19},{4,12},{29,13},{22,6},{15,7}} | collective-permute-start | bytes 2359304 | tf_op jit(solution)/shard_map/ppermute | solution.py:539
  38.6 17.1 %collective-permute-start.8 = (bf16[768,384]{1,0:T(8,128)(2,1)S(1)}, bf16[768,384]{1,0:T(8,128)(2,1)}, u32[]{:S(2)}, u32[]{:S(2)}) collective-permute-start(bf16[768,384]{1,0:T(8,128)(2,1)S(1)} %collective-permute-done.4.refs_2_), channel_id=1, source_target_pairs={{0,2},{1,3},{2,0},{3,1},{4,6},{5,7},{6,4},{7,5},{8,10},{9,11},{10,... | collective-permute-start | bytes 1769480 | tf_op jit(solution)/shard_map/ppermute | solution.py:508
  41.0 10.4 %collective-permute-start.6 = (bf16[384,384]{1,0:T(8,128)(2,1)S(1)}, bf16[384,384]{1,0:T(8,128)(2,1)S(1)}, u32[]{:S(2)}, u32[]{:S(2)}) collective-permute-start(bf16[384,384]{1,0:T(8,128)(2,1)S(1)} %slice.7), channel_id=1, source_target_pairs={{0,16},{8,24},{16,0},{24,8},{1,17},{9,25},{17,1},{25,9},{2,18},{10... | collective-permute-start | bytes 884744 | tf_op jit(solution)/shard_map/ppermute | solution.py:511
  44.6 10.4 %collective-permute-start.5 = (bf16[384,384]{1,0:T(8,128)(2,1)S(1)}, bf16[384,384]{1,0:T(8,128)(2,1)S(1)}, u32[]{:S(2)}, u32[]{:S(2)}) collective-permute-start(bf16[384,384]{1,0:T(8,128)(2,1)S(1)} %slice.6), channel_id=1, source_target_pairs={{0,8},{8,0},{16,24},{24,16},{1,9},{9,1},{17,25},{25,17},{2,10},{10... | collective-permute-start | bytes 884744 | tf_op jit(solution)/shard_map/ppermute | solution.py:511
  48.1 15.6 %collective-permute-start.14 = (bf16[384,1024]{1,0:T(8,128)(2,1)}, bf16[384,1024]{1,0:T(8,128)(2,1)}, u32[]{:S(2)}, u32[]{:S(2)}) collective-permute-start(bf16[384,1024]{1,0:T(8,128)(2,1)} %collective-permute-done.10), channel_id=1, source_target_pairs={{24,16},{25,9},{18,2},{19,27},{12,28},{13,5},{6,14},{7,23}} | collective-permute-start | bytes 2359304 | tf_op jit(solution)/shard_map/ppermute | solution.py:539
  63.9 6.6 %collective-permute-start.15 = (bf16[384,1024]{1,0:T(8,128)(2,1)S(1)}, bf16[384,1024]{1,0:T(8,128)(2,1)S(1)}, u32[]{:S(2)}, u32[]{:S(2)}) collective-permute-start(bf16[384,1024]{1,0:T(8,128)(2,1)S(1)} %broadcast_select_fusion.refs_0_), channel_id=1, source_target_pairs={{0,1},{1,0},{2,3},{3,2},{4,5},{5,4},{6,7},{7,6},{8,9},{9,8},{10,11... | collective-permute-start | bytes 2359304 | tf_op jit(solution)/shard_map/ppermute | solution.py:508
  64.0 25.9 %collective-permute-start.13 = (bf16[768,384]{1,0:T(8,128)(2,1)S(1)}, bf16[768,384]{1,0:T(8,128)(2,1)S(1)}, u32[]{:S(2)}, u32[]{:S(2)}) collective-permute-start(bf16[768,384]{1,0:T(8,128)(2,1)S(1)} %rank_sweep.3.refs_8_), channel_id=1, source_target_pairs={{0,24},{8,16},{16,8},{24,0},{1,25},{9,17},{17,9},{25,1},{2,26},{10... | collective-permute-start | bytes 1769480 | tf_op jit(solution)/shard_map/ppermute | solution.py:511
  68.8 26.3 %collective-permute-start.12 = (bf16[768,384]{1,0:T(8,128)(2,1)S(1)}, bf16[768,384]{1,0:T(8,128)(2,1)S(1)}, u32[]{:S(2)}, u32[]{:S(2)}) collective-permute-start(bf16[768,384]{1,0:T(8,128)(2,1)S(1)} %rank_sweep.3.refs_8_), channel_id=1, source_target_pairs={{0,16},{8,24},{16,0},{24,8},{1,17},{9,25},{17,1},{25,9},{2,18},{10... | collective-permute-start | bytes 1769480 | tf_op jit(solution)/shard_map/ppermute | solution.py:511
  69.8 27.0 %collective-permute-start.11 = (bf16[768,384]{1,0:T(8,128)(2,1)S(1)}, bf16[768,384]{1,0:T(8,128)(2,1)S(1)}, u32[]{:S(2)}, u32[]{:S(2)}) collective-permute-start(bf16[768,384]{1,0:T(8,128)(2,1)S(1)} %rank_sweep.3.refs_8_), channel_id=1, source_target_pairs={{0,8},{8,0},{16,24},{24,16},{1,9},{9,1},{17,25},{25,17},{2,10},{10... | collective-permute-start | bytes 1769480 | tf_op jit(solution)/shard_map/ppermute | solution.py:511
  73.4 15.3 %collective-permute-start.17 = (bf16[1024,128]{1,0:T(8,128)(2,1)S(1)}, bf16[1024,128]{1,0:T(8,128)(2,1)S(1)}, u32[]{:S(2)}, u32[]{:S(2)}) collective-permute-start(bf16[1024,128]{1,0:T(8,128)(2,1)S(1)} %copy-done.8), channel_id=1, source_target_pairs={{0,4},{1,5},{2,6},{3,7},{4,0},{5,1},{6,2},{7,3},{8,12},{9,13},{10,... | collective-permute-start | bytes 786440 | tf_op jit(solution)/shard_map/ppermute | solution.py:508
  75.5 13.2 %collective-permute-start.16 = (bf16[1024,128]{1,0:T(8,128)(2,1)S(1)}, bf16[1024,128]{1,0:T(8,128)(2,1)S(1)}, u32[]{:S(2)}, u32[]{:S(2)}) collective-permute-start(bf16[1024,128]{1,0:T(8,128)(2,1)S(1)} %copy-done.8), channel_id=1, source_target_pairs={{0,2},{1,3},{2,0},{3,1},{4,6},{5,7},{6,4},{7,5},{8,10},{9,11},{10,... | collective-permute-start | bytes 786440 | tf_op jit(solution)/shard_map/ppermute | solution.py:508
  88.7 11.4 %collective-permute-start.19 = (bf16[1024,128]{1,0:T(8,128)(2,1)S(1)}, bf16[1024,128]{1,0:T(8,128)(2,1)S(1)}, u32[]{:S(2)}, u32[]{:S(2)}) collective-permute-start(bf16[1024,128]{1,0:T(8,128)(2,1)S(1)} %collective-permute-done.17.refs_14_.refs_2_), channel_id=1, source_target_pairs={{0,2},{1,3},{2,0},{3,1},{4,6},{5,7},{6,4},{7,5},{8,10},{9,11},{10,... | collective-permute-start | bytes 786440 | tf_op jit(solution)/shard_map/ppermute | solution.py:508
  103.4 11.3 %collective-permute-start.20 = (bf16[384,384]{1,0:T(8,128)(2,1)S(1)}, bf16[384,384]{1,0:T(8,128)(2,1)S(1)}, u32[]{:S(2)}, u32[]{:S(2)}) collective-permute-start(bf16[384,384]{1,0:T(8,128)(2,1)S(1)} %rank_sweep.4.refs_0_.own_ref), channel_id=1, source_target_pairs={{0,1},{1,0},{2,3},{3,2},{4,5},{5,4},{6,7},{7,6},{8,9},{9,8},{10,11... | collective-permute-start | bytes 884744 | tf_op jit(solution)/shard_map/ppermute | solution.py:508
  107.0 22.9 %collective-permute-start.24 = (bf16[208,512]{1,0:T(8,128)(2,1)S(1)}, bf16[208,512]{1,0:T(8,128)(2,1)S(1)}, u32[]{:S(2)}, u32[]{:S(2)}) collective-permute-start(bf16[208,512]{1,0:T(8,128)(2,1)S(1)} %weigh.3.refs_0_), channel_id=1, source_target_pairs={{0,6},{1,7},{2,4},{3,5},{4,2},{5,3},{6,0},{7,1},{8,14},{9,15},{10,... | collective-permute-start | bytes 638984 | tf_op jit(solution)/shard_map/ppermute | solution.py:508
  112.3 17.6 %collective-permute-start.23 = (bf16[208,512]{1,0:T(8,128)(2,1)S(1)}, bf16[208,512]{1,0:T(8,128)(2,1)S(1)}, u32[]{:S(2)}, u32[]{:S(2)}) collective-permute-start(bf16[208,512]{1,0:T(8,128)(2,1)S(1)} %weigh.4.refs_0_), channel_id=1, source_target_pairs={{0,4},{1,5},{2,6},{3,7},{4,0},{5,1},{6,2},{7,3},{8,12},{9,13},{10,... | collective-permute-start | bytes 638984 | tf_op jit(solution)/shard_map/ppermute | solution.py:508
  119.3 11.3 %collective-permute-start.22 = (bf16[208,512]{1,0:T(8,128)(2,1)S(1)}, bf16[208,512]{1,0:T(8,128)(2,1)S(1)}, u32[]{:S(2)}, u32[]{:S(2)}) collective-permute-start(bf16[208,512]{1,0:T(8,128)(2,1)S(1)} %get-tuple-element.57), channel_id=1, source_target_pairs={{0,2},{1,3},{2,0},{3,1},{4,6},{5,7},{6,4},{7,5},{8,10},{9,11},{10,... | collective-permute-start | bytes 638984 | tf_op jit(solution)/shard_map/ppermute | solution.py:508
  134.7 6.5 %collective-permute-start.26 = (bf16[192,128]{1,0:T(8,128)(2,1)S(1)}, bf16[192,128]{1,0:T(8,128)(2,1)S(1)}, u32[]{:S(2)}, u32[]{:S(2)}) collective-permute-start(bf16[192,128]{1,0:T(8,128)(2,1)S(1)} %get-tuple-element.59), channel_id=1, source_target_pairs={{0,6},{1,7},{2,4},{3,5},{4,2},{5,3},{6,0},{7,1},{8,14},{9,15},{10,... | collective-permute-start | bytes 147464 | tf_op jit(solution)/shard_map/ppermute | solution.py:508
  135.9 6.5 %collective-permute-start.27 = (bf16[192,128]{1,0:T(8,128)(2,1)S(1)}, bf16[192,128]{1,0:T(8,128)(2,1)S(1)}, u32[]{:S(2)}, u32[]{:S(2)}) collective-permute-start(bf16[192,128]{1,0:T(8,128)(2,1)S(1)} %get-tuple-element.60), channel_id=1, source_target_pairs={{0,4},{1,5},{2,6},{3,7},{4,0},{5,1},{6,2},{7,3},{8,12},{9,13},{10,... | collective-permute-start | bytes 147464 | tf_op jit(solution)/shard_map/ppermute | solution.py:508
  (20 other events, 156.8 us)

commit v8 on v7

--- a/solution.py
+++ b/solution.py
@@ -53,30 +53,54 @@
     return jnp.concatenate(tiles, axis=0)
 
 
-def start_kernel(pattern_ref, weight_ref, features_ref, out_ref, cut_ref, sem):
+def start_kernel(pattern_ref, weight_ref, features_ref, out_ref, cut_ref, kept_ref, held_ref, sem):
     cols = cut_ref.shape[0]
+    rows = out_ref.shape[0] // 2
     ratio = features_ref.shape[0] // cols
     at = pl.multiple_of(lax.rem(lax.axis_index("col"), ratio) * cols, cols)
-    copy = pltpu.make_async_copy(features_ref.at[pl.ds(at, cols), :], cut_ref, sem)
-    copy.start()
-    for i in range(out_ref.shape[0] // BLK):
-        at = slice(i * BLK, (i + 1) * BLK)
-        keep = keep_tile(pattern_ref, i, 1)
-        out_ref[at, :] = jnp.where(keep > 0, weight_ref[at, :].astype(F32), 0.0).astype(BF16)
-    copy.wait()
+    halves = [slice(h * rows, (h + 1) * rows) for h in range(2)]
+    come = [
+        pltpu.make_async_copy(weight_ref.at[x, :], kept_ref.at[x, :], sem.at[h])
+        for h, x in enumerate(halves)
+    ]
+    go = [
+        pltpu.make_async_copy(kept_ref.at[x, :], out_ref.at[x, :], sem.at[2 + h])
+        for h, x in enumerate(halves)
+    ]
+    cut_in = pltpu.make_async_copy(features_ref.at[pl.ds(at, cols), :], held_ref, sem.at[4])
+    cut_out = pltpu.make_async_copy(held_ref, cut_ref, sem.at[5])
+    for copy in (*come, cut_in):
+        copy.start()
+    for h in range(2):
+        come[h].wait()
+        for i in range(h * rows // BLK, (h + 1) * rows // BLK):
+            x = slice(i * BLK, (i + 1) * BLK)
+            keep = keep_tile(pattern_ref, i, 1)
+            kept_ref[x, :] = jnp.where(keep > 0, kept_ref[x, :].astype(F32), 0.0).astype(BF16)
+        go[h].start()
+        if h == 0:
+            cut_in.wait()
+            cut_out.start()
+    for copy in (*go, cut_out):
+        copy.wait()
 
 
 def start(pattern, weight, features):
     rows, cols = weight.shape
+    depth = features.shape[1]
     return pl.pallas_call(
         start_kernel,
         out_shape=(
             jax.ShapeDtypeStruct((rows, cols), BF16),
-            jax.ShapeDtypeStruct((cols, features.shape[1]), BF16),
+            jax.ShapeDtypeStruct((cols, depth), BF16),
         ),
-        in_specs=[SMEM, VMEM, HBM],
-        out_specs=(VMEM, VMEM),
-        scratch_shapes=[pltpu.SemaphoreType.DMA],
+        in_specs=[SMEM, HBM, HBM],
+        out_specs=(HBM, HBM),
+        scratch_shapes=[
+            pltpu.VMEM((rows, cols), BF16),
+            pltpu.VMEM((cols, depth), BF16),
+            pltpu.SemaphoreType.DMA((6,)),
+        ],
         compiler_params=params(),
         cost_estimate=cost(rows * cols, 4 * rows * cols),
         name="start",

time: 143 us -> 143 us (level)
  no operation moved by 1% of the time
where the time goes in v8:
time: 143 us
  waiting for transfers between devices  47.6 us (33%)
  starting transfers between devices  44.9 us (31%)
  Pallas kernels  42.6 us (30%)
  other arithmetic  3.83 us (3%)
  local copies, waits for them, and re-layouts  3.5 us (2%)
    ppermute x19, waiting for transfers between devices, along_col(): return lax.ppermute(value, 'col', xor_pairs(col_count, j))  36.1 us
    ppermute x7, starting transfers between devices, along_row(): return lax.ppermute(value, 'row', xor_pairs(row_count, j))  18.4 us
    ppermute x19, starting transfers between devices, along_col(): return lax.ppermute(value, 'col', xor_pairs(col_count, j))  17.6 us
    ppermute x7, waiting for transfers between devices, along_row(): return lax.ppermute(value, 'row', xor_pairs(row_count, j))  11.5 us
    pallas_call x3, Pallas kernels, sweep(): pl.pallas_call(functools.partial(sweep_kernel, first, ks, chips, [at for...  11.5 us
    pallas_call x3, Pallas kernels, weigh(): pl.pallas_call(functools.partial(weigh_kernel, root, ks, seg), out_shape=...  10.8 us
    ppermute x3, starting transfers between devices, feature_step(): return lax.ppermute(value, ('row', 'col'), pairs)  8.86 us
    pallas_call x1, Pallas kernels, exponentials(): pl.pallas_call(expo_kernel, out_shape=(jax.ShapeDtypeStruct((PAIRS, rows,...  8.34 us
  transfers between devices with their start and end apart: 29, of which 12 were waited for; matrix products, arithmetic and copies ran while one was open for 3% of the time, Pallas kernels for 26%

profile of v8, /device:TPU:0, one launch (start us, length us, event | category | flops | bytes accessed | tf_op | source)
XLA Modules:
  0.0 142.9 jit_solution(16112189358000912287)
XLA Ops:
  0.0 3.0 %start.1 = (bf16[768,384]{1,0:T(8,128)(2,1)}, bf16[384,1024]{1,0:T(8,128)(2,1)}) custom-call(s32[3,6]{1,0:T(4,128)} %bitcast.12, bf16[768,384]{1,0:T(8,128)(2,1)} %weight_ref.1, bf16[768,1024]{1,0:T(8,128)(2,1)} %features_ref.1), custom_call_target="tpu_custom_call" | custom-call | flops 294912 | bytes 1179648 | tf_op jit(solution)/shard_map/start/pallas_call | solution.py:91
  3.1 5.7 %collective-permute-start = (bf16[384,1024]{1,0:T(8,128)(2,1)}, bf16[384,1024]{1,0:T(8,128)(2,1)}, u32[]{:S(2)}, u32[]{:S(2)}) collective-permute-start(bf16[384,1024]{1,0:T(8,128)(2,1)} %get-tuple-element.34), channel_id=1, source_target_pairs={{0,8},{1,17},{10,26},{11,3},{20,4},{21,29},{30,22},{31,15}} | collective-permute-start | bytes 2359304 | tf_op jit(solution)/shard_map/ppermute | solution.py:563
  11.9 3.1 %collective-permute-start.1 = (bf16[768,384]{1,0:T(8,128)(2,1)}, bf16[768,384]{1,0:T(8,128)(2,1)}, u32[]{:S(2)}, u32[]{:S(2)}) collective-permute-start(bf16[768,384]{1,0:T(8,128)(2,1)} %get-tuple-element.41.refs_0_.refs_8_), channel_id=1, source_target_pairs={{0,8},{8,0},{16,24},{24,16},{1,9},{9,1},{17,25},{25,17},{2,10},{10... | collective-permute-start | bytes 1769480 | tf_op jit(solution)/shard_map/ppermute | solution.py:535
  15.0 3.6 %project_in.2.q_ref = bf16[768,512]{1,0:T(8,128)(2,1)} custom-call(s32[1]{0:T(128)} %bitcast.3.place_ref, bf16[768,1024]{1,0:T(8,128)(2,1)} %features_ref.1, bf16[1024,3072]{1,0:T(8,128)(2,1)} %refs_2_.1), custom_call_target="tpu_custom_call" | custom-call | flops 805306368 | bytes 2621440 | tf_op jit(solution)/shard_map/project_in/pallas_call | solution.py:130
  18.6 17.3 %collective-permute-done.4.refs_2_ = bf16[768,384]{1,0:T(8,128)(2,1)S(1)} collective-permute-done((bf16[768,384]{1,0:T(8,128)(2,1)}, bf16[768,384]{1,0:T(8,128)(2,1)S(1)}, u32[]{:S(2)}, u32[]{:S(2)}) %collective-permute-start.4) | collective-permute-done | bytes 589856 | tf_op jit(solution)/shard_map/ppermute | solution.py:532
  40.7 3.7 %collective-permute-start.6 = (bf16[384,384]{1,0:T(8,128)(2,1)S(1)}, bf16[384,384]{1,0:T(8,128)(2,1)S(1)}, u32[]{:S(2)}, u32[]{:S(2)}) collective-permute-start(bf16[384,384]{1,0:T(8,128)(2,1)S(1)} %slice.7), channel_id=1, source_target_pairs={{0,16},{8,24},{16,0},{24,8},{1,17},{9,25},{17,1},{25,9},{2,18},{10... | collective-permute-start | bytes 884744 | tf_op jit(solution)/shard_map/ppermute | solution.py:535
  44.4 3.5 %collective-permute-start.5 = (bf16[384,384]{1,0:T(8,128)(2,1)S(1)}, bf16[384,384]{1,0:T(8,128)(2,1)S(1)}, u32[]{:S(2)}, u32[]{:S(2)}) collective-permute-start(bf16[384,384]{1,0:T(8,128)(2,1)S(1)} %slice.6), channel_id=1, source_target_pairs={{0,8},{8,0},{16,24},{24,16},{1,9},{9,1},{17,25},{25,17},{2,10},{10... | collective-permute-start | bytes 884744 | tf_op jit(solution)/shard_map/ppermute | solution.py:535
  51.8 2.9 %collective-permute-done.5.refs_11_ = bf16[384,384]{1,0:T(8,128)(2,1)S(1)} collective-permute-done((bf16[384,384]{1,0:T(8,128)(2,1)S(1)}, bf16[384,384]{1,0:T(8,128)(2,1)S(1)}, u32[]{:S(2)}, u32[]{:S(2)}) %collective-permute-start.5) | collective-permute-done | bytes 294944 | tf_op jit(solution)/shard_map/ppermute | solution.py:535
  55.7 2.7 %select_select_fusion.refs_13_ = bf16[384,1024]{1,0:T(8,128)(2,1)} fusion(bf16[384,1024]{1,0:T(8,128)(2,1)} %collective-permute-done.10, bf16[384,1024]{1,0:T(8,128)(2,1)} %collective-permute-done, bf16[384,1024]{1,0:T(8,128)(2,1)} %get-tuple-element.34, pred[]{:T(512)S(6)} %eq.22, pred[]{:T(512)S(6)} %eq.21), kind=kLoop, calls=%fused_computation.1 | loop fusion | flops 786432 | bytes 3145730 | tf_op jit(solution)/shard_map/jit(_where)/select_n | solution.py:595
  58.5 5.0 %rank_sweep.3.refs_8_ = bf16[768,384]{1,0:T(8,128)(2,1)S(1)} custom-call(s32[2]{0:T(128)S(1)} %pad_add_fusion.place_ref, s32[3,6]{1,0:T(4,128)S(1)} %bitcast.13, bf16[768,384]{1,0:T(8,128)(2,1)S(1)} %copy-done.2, bf16[768,384]{1,0:T(8,128)(2,1)S(1)} %collective-permute-done.3.refs_1_, bf16[768,384]{1,0:T(8,128)(2,1)S(1)} %collective-permute-done.4.refs_2_, ...), custom_call_target="tpu_custom_call" | custom-call | flops 1811939328 | bytes 9437184 | tf_op jit(solution)/shard_map/rank_sweep/pallas_call | solution.py:236
  63.7 4.8 %collective-permute-start.13 = (bf16[768,384]{1,0:T(8,128)(2,1)S(1)}, bf16[768,384]{1,0:T(8,128)(2,1)S(1)}, u32[]{:S(2)}, u32[]{:S(2)}) collective-permute-start(bf16[768,384]{1,0:T(8,128)(2,1)S(1)} %rank_sweep.3.refs_8_), channel_id=1, source_target_pairs={{0,24},{8,16},{16,8},{24,0},{1,25},{9,17},{17,9},{25,1},{2,26},{10... | collective-permute-start | bytes 1769480 | tf_op jit(solution)/shard_map/ppermute | solution.py:535
  70.2 2.8 %project_in.3.k_ref.v_ref = bf16[768,1024]{1,0:T(8,128)(2,1)S(1)} custom-call(s32[1]{0:T(128)} %bitcast.3.place_ref, bf16[384,1024]{1,0:T(8,128)(2,1)S(1)} %broadcast_select_fusion.refs_0_, bf16[384,1024]{1,0:T(8,128)(2,1)S(1)} %collective-permute-done.15.refs_1_, bf16[1024,3072]{1,0:T(8,128)(2,1)S(1)} %bitcast.8), custom_call_target="tpu_custom_call" | custom-call | flops 1610612736 | bytes 3670016 | tf_op jit(solution)/shard_map/project_in/pallas_call | solution.py:130
  75.3 2.5 %collective-permute-start.16 = (bf16[1024,128]{1,0:T(8,128)(2,1)S(1)}, bf16[1024,128]{1,0:T(8,128)(2,1)S(1)}, u32[]{:S(2)}, u32[]{:S(2)}) collective-permute-start(bf16[1024,128]{1,0:T(8,128)(2,1)S(1)} %copy-done.8), channel_id=1, source_target_pairs={{0,2},{1,3},{2,0},{3,1},{4,6},{5,7},{6,4},{7,5},{8,10},{9,11},{10,... | collective-permute-start | bytes 786440 | tf_op jit(solution)/shard_map/ppermute | solution.py:532
  77.8 8.3 %expo.1 = (bf16[4,768,1536]{2,1,0:T(8,128)(2,1)S(1)}, f32[768,128]{1,0:T(8,128)S(1)}) custom-call(s32[3,6]{1,0:T(4,128)S(1)} %bitcast.15, s32[3,6]{1,0:T(4,128)S(1)} %collective-permute-done.18.other_ref, bf16[768,512]{1,0:T(8,128)(2,1)S(1)} %copy-done.3, bf16[768,1024]{1,0:T(8,128)(2,1)S(1)} %project_in.3.k_ref.v_ref), custom_call_target="tpu_custom_call" | custom-call | flops 2415919104 | bytes 9437184 | tf_op jit(solution)/shard_map/expo/pallas_call | solution.py:308
  86.1 2.3 %collective-permute-done.17.refs_14_.refs_2_ = bf16[1024,128]{1,0:T(8,128)(2,1)S(1)} collective-permute-done((bf16[1024,128]{1,0:T(8,128)(2,1)S(1)}, bf16[1024,128]{1,0:T(8,128)(2,1)S(1)}, u32[]{:S(2)}, u32[]{:S(2)}) %collective-permute-start.17) | collective-permute-done | bytes 262176 | tf_op jit(solution)/shard_map/ppermute | solution.py:532
  89.6 5.2 %collective-permute-done.12.refs_10_ = bf16[768,384]{1,0:T(8,128)(2,1)S(1)} collective-permute-done((bf16[768,384]{1,0:T(8,128)(2,1)S(1)}, bf16[768,384]{1,0:T(8,128)(2,1)S(1)}, u32[]{:S(2)}, u32[]{:S(2)}) %collective-permute-start.12) | collective-permute-done | bytes 589856 | tf_op jit(solution)/shard_map/ppermute | solution.py:535
  96.6 3.1 %rank_sweep.5.own_ref = bf16[384,384]{1,0:T(8,128)(2,1)S(1)} custom-call(s32[2]{0:T(128)S(1)} %pad_add_fusion.place_ref, s32[3,6]{1,0:T(4,128)S(1)} %bitcast.16, bf16[768,384]{1,0:T(8,128)(2,1)S(1)} %copy-done.2, bf16[768,384]{1,0:T(8,128)(2,1)S(1)} %collective-permute-done.3.refs_1_, bf16[768,384]{1,0:T(8,128)(2,1)S(1)} %collective-permute-done.4.refs_2_, ...), custom_call_target="tpu_custom_call" | custom-call | flops 905969664 | bytes 7077888 | tf_op jit(solution)/shard_map/rank_sweep/pallas_call | solution.py:236
  99.8 3.3 %rank_sweep.4.refs_0_.own_ref = bf16[384,384]{1,0:T(8,128)(2,1)S(1)} custom-call(s32[2]{0:T(128)S(1)} %pad_add_fusion.place_ref, s32[3,6]{1,0:T(4,128)S(1)} %bitcast.17, bf16[768,384]{1,0:T(8,128)(2,1)S(1)} %copy-done.2, bf16[768,384]{1,0:T(8,128)(2,1)S(1)} %collective-permute-done.3.refs_1_, bf16[768,384]{1,0:T(8,128)(2,1)S(1)} %collective-permute-done.4.refs_2_, ...), custom_call_target="tpu_custom_call" | custom-call | flops 905969664 | bytes 7077888 | tf_op jit(solution)/shard_map/rank_sweep/pallas_call | solution.py:236
  103.7 3.1 %weigh.3.refs_0_ = bf16[208,512]{1,0:T(8,128)(2,1)S(1)} custom-call(s32[2]{0:T(128)S(1)} %pad_add_fusion.place_ref, f32[16]{0:T(128)S(1)} %copy-done.10, f32[16]{0:T(128)S(1)} %copy-done.11, bf16[384,384]{1,0:T(8,128)(2,1)S(1)} %rank_sweep.5.own_ref, bf16[384,384]{1,0:T(8,128)(2,1)S(1)} %collective-permute-done.21.other_ref, ...), custom_call_target="tpu_custom_call" | custom-call | flops 603979776 | bytes 2359296 | tf_op jit(solution)/shard_map/weigh/pallas_call | solution.py:403
  109.0 3.1 %weigh.4.refs_0_ = bf16[208,512]{1,0:T(8,128)(2,1)S(1)} custom-call(s32[2]{0:T(128)S(1)} %pad_add_fusion.place_ref, f32[16]{0:T(128)S(1)} %copy-done.10, f32[16]{0:T(128)S(1)} %copy-done.11, bf16[384,384]{1,0:T(8,128)(2,1)S(1)} %rank_sweep.5.own_ref, bf16[384,384]{1,0:T(8,128)(2,1)S(1)} %collective-permute-done.21.other_ref, ...), custom_call_target="tpu_custom_call" | custom-call | flops 603979776 | bytes 2359296 | tf_op jit(solution)/shard_map/weigh/pallas_call | solution.py:403
  112.0 2.4 %collective-permute-start.23 = (bf16[208,512]{1,0:T(8,128)(2,1)S(1)}, bf16[208,512]{1,0:T(8,128)(2,1)S(1)}, u32[]{:S(2)}, u32[]{:S(2)}) collective-permute-start(bf16[208,512]{1,0:T(8,128)(2,1)S(1)} %weigh.4.refs_0_), channel_id=1, source_target_pairs={{0,4},{1,5},{2,6},{3,7},{4,0},{5,1},{6,2},{7,3},{8,12},{9,13},{10,... | collective-permute-start | bytes 638984 | tf_op jit(solution)/shard_map/ppermute | solution.py:532
  114.4 4.7 %weigh.5 = (bf16[208,512]{1,0:T(8,128)(2,1)S(1)}, bf16[208,512]{1,0:T(8,128)(2,1)S(1)}) custom-call(s32[2]{0:T(128)S(1)} %pad_add_fusion.place_ref, f32[16]{0:T(128)S(1)} %copy-done.10, f32[16]{0:T(128)S(1)} %copy-done.11, bf16[384,384]{1,0:T(8,128)(2,1)S(1)} %rank_sweep.4.refs_0_.own_ref, bf16[384,384]{1,0:T(8,128)(2,1)S(1)} %collective-permute-done.20.other_ref, ...), custom_call_target="tpu_custom_call" | custom-call | flops 1207959552 | bytes 4718592 | tf_op jit(solution)/shard_map/weigh/pallas_call | solution.py:403
  119.2 10.5 %collective-permute-done.23.refs_2_ = bf16[208,512]{1,0:T(8,128)(2,1)S(1)} collective-permute-done((bf16[208,512]{1,0:T(8,128)(2,1)S(1)}, bf16[208,512]{1,0:T(8,128)(2,1)S(1)}, u32[]{:S(2)}, u32[]{:S(2)}) %collective-permute-start.23) | collective-permute-done | bytes 213024 | tf_op jit(solution)/shard_map/ppermute | solution.py:532
  135.7 3.2 %collective-permute-start.28 = (bf16[192,128]{1,0:T(8,128)(2,1)S(1)}, bf16[192,128]{1,0:T(8,128)(2,1)S(1)}, u32[]{:S(2)}, u32[]{:S(2)}) collective-permute-start(bf16[192,128]{1,0:T(8,128)(2,1)S(1)} %get-tuple-element.61), channel_id=1, source_target_pairs={{0,2},{1,3},{2,0},{3,1},{4,6},{5,7},{6,4},{7,5},{8,10},{9,11},{10,... | collective-permute-start | bytes 147464 | tf_op jit(solution)/shard_map/ppermute | solution.py:532
  (85 shorter events, 32.7 us)
Async XLA Ops:
  3.1 33.4 %collective-permute-start = (bf16[384,1024]{1,0:T(8,128)(2,1)}, bf16[384,1024]{1,0:T(8,128)(2,1)}, u32[]{:S(2)}, u32[]{:S(2)}) collective-permute-start(bf16[384,1024]{1,0:T(8,128)(2,1)} %get-tuple-element.34), channel_id=1, source_target_pairs={{0,8},{1,17},{10,26},{11,3},{20,4},{21,29},{30,22},{31,15}} | collective-permute-start | bytes 2359304 | tf_op jit(solution)/shard_map/ppermute | solution.py:563
  8.8 27.1 %collective-permute-start.4 = (bf16[768,384]{1,0:T(8,128)(2,1)}, bf16[768,384]{1,0:T(8,128)(2,1)S(1)}, u32[]{:S(2)}, u32[]{:S(2)}) collective-permute-start(bf16[768,384]{1,0:T(8,128)(2,1)} %get-tuple-element.41.refs_0_.refs_8_), channel_id=1, source_target_pairs={{0,4},{1,5},{2,6},{3,7},{4,0},{5,1},{6,2},{7,3},{8,12},{9,13},{10,... | collective-permute-start | bytes 1769480 | tf_op jit(solution)/shard_map/ppermute | solution.py:532
  8.8 27.7 %collective-permute-start.3 = (bf16[768,384]{1,0:T(8,128)(2,1)}, bf16[768,384]{1,0:T(8,128)(2,1)S(1)}, u32[]{:S(2)}, u32[]{:S(2)}) collective-permute-start(bf16[768,384]{1,0:T(8,128)(2,1)} %get-tuple-element.41.refs_0_.refs_8_), channel_id=1, source_target_pairs={{0,2},{1,3},{2,0},{3,1},{4,6},{5,7},{6,4},{7,5},{8,10},{9,11},{10,... | collective-permute-start | bytes 1769480 | tf_op jit(solution)/shard_map/ppermute | solution.py:532
  10.2 26.2 %collective-permute-start.2 = (bf16[768,384]{1,0:T(8,128)(2,1)}, bf16[768,384]{1,0:T(8,128)(2,1)}, u32[]{:S(2)}, u32[]{:S(2)}) collective-permute-start(bf16[768,384]{1,0:T(8,128)(2,1)} %get-tuple-element.41.refs_0_.refs_8_), channel_id=1, source_target_pairs={{0,16},{8,24},{16,0},{24,8},{1,17},{9,25},{17,1},{25,9},{2,18},{10... | collective-permute-start | bytes 1769480 | tf_op jit(solution)/shard_map/ppermute | solution.py:535
  11.9 24.5 %collective-permute-start.1 = (bf16[768,384]{1,0:T(8,128)(2,1)}, bf16[768,384]{1,0:T(8,128)(2,1)}, u32[]{:S(2)}, u32[]{:S(2)}) collective-permute-start(bf16[768,384]{1,0:T(8,128)(2,1)} %get-tuple-element.41.refs_0_.refs_8_), channel_id=1, source_target_pairs={{0,8},{8,0},{16,24},{24,16},{1,9},{9,1},{17,25},{25,17},{2,10},{10... | collective-permute-start | bytes 1769480 | tf_op jit(solution)/shard_map/ppermute | solution.py:535
  36.7 18.7 %collective-permute-start.7 = (bf16[3,768,384]{2,1,0:T(8,128)(2,1)S(1)}, bf16[3,768,384]{2,1,0:T(8,128)(2,1)S(1)}, u32[]{:S(2)}, u32[]{:S(2)}) collective-permute-start(bf16[3,768,384]{2,1,0:T(8,128)(2,1)S(1)} %pad_maximum_fusion), channel_id=1, source_target_pairs={{0,1},{1,0},{2,3},{3,2},{4,5},{5,4},{6,7},{7,6},{8,9},{9,8},{10,11... | collective-permute-start | bytes 5308424 | tf_op jit(solution)/shard_map/ppermute | solution.py:532
  36.8 11.0 %collective-permute-start.10 = (bf16[384,1024]{1,0:T(8,128)(2,1)}, bf16[384,1024]{1,0:T(8,128)(2,1)}, u32[]{:S(2)}, u32[]{:S(2)}) collective-permute-start(bf16[384,1024]{1,0:T(8,128)(2,1)} %collective-permute-done), channel_id=1, source_target_pairs={{8,24},{17,25},{26,18},{3,19},{4,12},{29,13},{22,6},{15,7}} | collective-permute-start | bytes 2359304 | tf_op jit(solution)/shard_map/ppermute | solution.py:563
  38.4 17.1 %collective-permute-start.8 = (bf16[768,384]{1,0:T(8,128)(2,1)S(1)}, bf16[768,384]{1,0:T(8,128)(2,1)}, u32[]{:S(2)}, u32[]{:S(2)}) collective-permute-start(bf16[768,384]{1,0:T(8,128)(2,1)S(1)} %collective-permute-done.4.refs_2_), channel_id=1, source_target_pairs={{0,2},{1,3},{2,0},{3,1},{4,6},{5,7},{6,4},{7,5},{8,10},{9,11},{10,... | collective-permute-start | bytes 1769480 | tf_op jit(solution)/shard_map/ppermute | solution.py:532
  40.7 10.4 %collective-permute-start.6 = (bf16[384,384]{1,0:T(8,128)(2,1)S(1)}, bf16[384,384]{1,0:T(8,128)(2,1)S(1)}, u32[]{:S(2)}, u32[]{:S(2)}) collective-permute-start(bf16[384,384]{1,0:T(8,128)(2,1)S(1)} %slice.7), channel_id=1, source_target_pairs={{0,16},{8,24},{16,0},{24,8},{1,17},{9,25},{17,1},{25,9},{2,18},{10... | collective-permute-start | bytes 884744 | tf_op jit(solution)/shard_map/ppermute | solution.py:535
  44.4 10.4 %collective-permute-start.5 = (bf16[384,384]{1,0:T(8,128)(2,1)S(1)}, bf16[384,384]{1,0:T(8,128)(2,1)S(1)}, u32[]{:S(2)}, u32[]{:S(2)}) collective-permute-start(bf16[384,384]{1,0:T(8,128)(2,1)S(1)} %slice.6), channel_id=1, source_target_pairs={{0,8},{8,0},{16,24},{24,16},{1,9},{9,1},{17,25},{25,17},{2,10},{10... | collective-permute-start | bytes 884744 | tf_op jit(solution)/shard_map/ppermute | solution.py:535
  47.9 15.6 %collective-permute-start.14 = (bf16[384,1024]{1,0:T(8,128)(2,1)}, bf16[384,1024]{1,0:T(8,128)(2,1)}, u32[]{:S(2)}, u32[]{:S(2)}) collective-permute-start(bf16[384,1024]{1,0:T(8,128)(2,1)} %collective-permute-done.10), channel_id=1, source_target_pairs={{24,16},{25,9},{18,2},{19,27},{12,28},{13,5},{6,14},{7,23}} | collective-permute-start | bytes 2359304 | tf_op jit(solution)/shard_map/ppermute | solution.py:563
  63.6 6.6 %collective-permute-start.15 = (bf16[384,1024]{1,0:T(8,128)(2,1)S(1)}, bf16[384,1024]{1,0:T(8,128)(2,1)S(1)}, u32[]{:S(2)}, u32[]{:S(2)}) collective-permute-start(bf16[384,1024]{1,0:T(8,128)(2,1)S(1)} %broadcast_select_fusion.refs_0_), channel_id=1, source_target_pairs={{0,1},{1,0},{2,3},{3,2},{4,5},{5,4},{6,7},{7,6},{8,9},{9,8},{10,11... | collective-permute-start | bytes 2359304 | tf_op jit(solution)/shard_map/ppermute | solution.py:532
  63.7 25.9 %collective-permute-start.13 = (bf16[768,384]{1,0:T(8,128)(2,1)S(1)}, bf16[768,384]{1,0:T(8,128)(2,1)S(1)}, u32[]{:S(2)}, u32[]{:S(2)}) collective-permute-start(bf16[768,384]{1,0:T(8,128)(2,1)S(1)} %rank_sweep.3.refs_8_), channel_id=1, source_target_pairs={{0,24},{8,16},{16,8},{24,0},{1,25},{9,17},{17,9},{25,1},{2,26},{10... | collective-permute-start | bytes 1769480 | tf_op jit(solution)/shard_map/ppermute | solution.py:535
  68.5 26.3 %collective-permute-start.12 = (bf16[768,384]{1,0:T(8,128)(2,1)S(1)}, bf16[768,384]{1,0:T(8,128)(2,1)S(1)}, u32[]{:S(2)}, u32[]{:S(2)}) collective-permute-start(bf16[768,384]{1,0:T(8,128)(2,1)S(1)} %rank_sweep.3.refs_8_), channel_id=1, source_target_pairs={{0,16},{8,24},{16,0},{24,8},{1,17},{9,25},{17,1},{25,9},{2,18},{10... | collective-permute-start | bytes 1769480 | tf_op jit(solution)/shard_map/ppermute | solution.py:535
  69.6 27.0 %collective-permute-start.11 = (bf16[768,384]{1,0:T(8,128)(2,1)S(1)}, bf16[768,384]{1,0:T(8,128)(2,1)S(1)}, u32[]{:S(2)}, u32[]{:S(2)}) collective-permute-start(bf16[768,384]{1,0:T(8,128)(2,1)S(1)} %rank_sweep.3.refs_8_), channel_id=1, source_target_pairs={{0,8},{8,0},{16,24},{24,16},{1,9},{9,1},{17,25},{25,17},{2,10},{10... | collective-permute-start | bytes 1769480 | tf_op jit(solution)/shard_map/ppermute | solution.py:535
  73.1 15.3 %collective-permute-start.17 = (bf16[1024,128]{1,0:T(8,128)(2,1)S(1)}, bf16[1024,128]{1,0:T(8,128)(2,1)S(1)}, u32[]{:S(2)}, u32[]{:S(2)}) collective-permute-start(bf16[1024,128]{1,0:T(8,128)(2,1)S(1)} %copy-done.8), channel_id=1, source_target_pairs={{0,4},{1,5},{2,6},{3,7},{4,0},{5,1},{6,2},{7,3},{8,12},{9,13},{10,... | collective-permute-start | bytes 786440 | tf_op jit(solution)/shard_map/ppermute | solution.py:532
  75.3 13.2 %collective-permute-start.16 = (bf16[1024,128]{1,0:T(8,128)(2,1)S(1)}, bf16[1024,128]{1,0:T(8,128)(2,1)S(1)}, u32[]{:S(2)}, u32[]{:S(2)}) collective-permute-start(bf16[1024,128]{1,0:T(8,128)(2,1)S(1)} %copy-done.8), channel_id=1, source_target_pairs={{0,2},{1,3},{2,0},{3,1},{4,6},{5,7},{6,4},{7,5},{8,10},{9,11},{10,... | collective-permute-start | bytes 786440 | tf_op jit(solution)/shard_map/ppermute | solution.py:532
  88.4 11.4 %collective-permute-start.19 = (bf16[1024,128]{1,0:T(8,128)(2,1)S(1)}, bf16[1024,128]{1,0:T(8,128)(2,1)S(1)}, u32[]{:S(2)}, u32[]{:S(2)}) collective-permute-start(bf16[1024,128]{1,0:T(8,128)(2,1)S(1)} %collective-permute-done.17.refs_14_.refs_2_), channel_id=1, source_target_pairs={{0,2},{1,3},{2,0},{3,1},{4,6},{5,7},{6,4},{7,5},{8,10},{9,11},{10,... | collective-permute-start | bytes 786440 | tf_op jit(solution)/shard_map/ppermute | solution.py:532
  103.2 11.3 %collective-permute-start.20 = (bf16[384,384]{1,0:T(8,128)(2,1)S(1)}, bf16[384,384]{1,0:T(8,128)(2,1)S(1)}, u32[]{:S(2)}, u32[]{:S(2)}) collective-permute-start(bf16[384,384]{1,0:T(8,128)(2,1)S(1)} %rank_sweep.4.refs_0_.own_ref), channel_id=1, source_target_pairs={{0,1},{1,0},{2,3},{3,2},{4,5},{5,4},{6,7},{7,6},{8,9},{9,8},{10,11... | collective-permute-start | bytes 884744 | tf_op jit(solution)/shard_map/ppermute | solution.py:532
  106.8 22.9 %collective-permute-start.24 = (bf16[208,512]{1,0:T(8,128)(2,1)S(1)}, bf16[208,512]{1,0:T(8,128)(2,1)S(1)}, u32[]{:S(2)}, u32[]{:S(2)}) collective-permute-start(bf16[208,512]{1,0:T(8,128)(2,1)S(1)} %weigh.3.refs_0_), channel_id=1, source_target_pairs={{0,6},{1,7},{2,4},{3,5},{4,2},{5,3},{6,0},{7,1},{8,14},{9,15},{10,... | collective-permute-start | bytes 638984 | tf_op jit(solution)/shard_map/ppermute | solution.py:532
  112.0 17.6 %collective-permute-start.23 = (bf16[208,512]{1,0:T(8,128)(2,1)S(1)}, bf16[208,512]{1,0:T(8,128)(2,1)S(1)}, u32[]{:S(2)}, u32[]{:S(2)}) collective-permute-start(bf16[208,512]{1,0:T(8,128)(2,1)S(1)} %weigh.4.refs_0_), channel_id=1, source_target_pairs={{0,4},{1,5},{2,6},{3,7},{4,0},{5,1},{6,2},{7,3},{8,12},{9,13},{10,... | collective-permute-start | bytes 638984 | tf_op jit(solution)/shard_map/ppermute | solution.py:532
  119.1 11.3 %collective-permute-start.22 = (bf16[208,512]{1,0:T(8,128)(2,1)S(1)}, bf16[208,512]{1,0:T(8,128)(2,1)S(1)}, u32[]{:S(2)}, u32[]{:S(2)}) collective-permute-start(bf16[208,512]{1,0:T(8,128)(2,1)S(1)} %get-tuple-element.57), channel_id=1, source_target_pairs={{0,2},{1,3},{2,0},{3,1},{4,6},{5,7},{6,4},{7,5},{8,10},{9,11},{10,... | collective-permute-start | bytes 638984 | tf_op jit(solution)/shard_map/ppermute | solution.py:532
  134.4 6.5 %collective-permute-start.26 = (bf16[192,128]{1,0:T(8,128)(2,1)S(1)}, bf16[192,128]{1,0:T(8,128)(2,1)S(1)}, u32[]{:S(2)}, u32[]{:S(2)}) collective-permute-start(bf16[192,128]{1,0:T(8,128)(2,1)S(1)} %get-tuple-element.59), channel_id=1, source_target_pairs={{0,6},{1,7},{2,4},{3,5},{4,2},{5,3},{6,0},{7,1},{8,14},{9,15},{10,... | collective-permute-start | bytes 147464 | tf_op jit(solution)/shard_map/ppermute | solution.py:532
  135.7 6.5 %collective-permute-start.27 = (bf16[192,128]{1,0:T(8,128)(2,1)S(1)}, bf16[192,128]{1,0:T(8,128)(2,1)S(1)}, u32[]{:S(2)}, u32[]{:S(2)}) collective-permute-start(bf16[192,128]{1,0:T(8,128)(2,1)S(1)} %get-tuple-element.60), channel_id=1, source_target_pairs={{0,4},{1,5},{2,6},{3,7},{4,0},{5,1},{6,2},{7,3},{8,12},{9,13},{10,... | collective-permute-start | bytes 147464 | tf_op jit(solution)/shard_map/ppermute | solution.py:532
  (20 other events, 156.8 us)

commit v9 on v8

--- a/solution.py
+++ b/solution.py
@@ -105,6 +105,36 @@
         cost_estimate=cost(rows * cols, 4 * rows * cols),
         name="start",
     )(pattern, weight, features)
+
+
+def choose_kernel(which_ref, *refs):
+    values, (out_ref, held_ref, sem) = refs[:-3], refs[-3:]
+    which = jnp.where(which_ref[0] < len(values), which_ref[0], 0)
+    for i, value in enumerate(values):
+
+        @pl.when(which == i)
+        def _():
+            copy = pltpu.make_async_copy(value, held_ref, sem)
+            copy.start()
+            copy.wait()
+
+    copy = pltpu.make_async_copy(held_ref, out_ref, sem)
+    copy.start()
+    copy.wait()
+
+
+def choose(which, values):
+    one = jax.ShapeDtypeStruct(values[0].shape, values[0].dtype)
+    return pl.pallas_call(
+        choose_kernel,
+        out_shape=one,
+        in_specs=[SMEM] + [HBM] * len(values),
+        out_specs=HBM,
+        scratch_shapes=[pltpu.VMEM(one.shape, one.dtype), pltpu.SemaphoreType.DMA],
+        compiler_params=params(),
+        cost_estimate=cost(0, 4 * values[0].size),
+        name="choose",
+    )(which.astype(jnp.int32).reshape(1), *values)
 
 
 def project_in_kernel(scale, place_ref, *refs):
@@ -590,9 +620,7 @@
     panel += [(along_col(x, 1), CORES * k + 1, None) for k, x in blocks.items() if k not in order]
     columns = [(0, 0, adjacency)] + [(j, 0, x) for j, x in raw_columns.items()]
     columns += [(3, i * x.shape[0], x) for i, x in enumerate(raw_far)]
-    key_rows = features
-    for s in range(1, row_count - 1):
-        key_rows = jnp.where(steps_away == s, moved[s], key_rows)
+    key_rows = choose(steps_away, moved[: row_count - 1])
     ranks = sweep(True, range(chips), place, pattern, panel, columns, [key_rows], 50 * 2**20)
     columns = [(j, 0, x) for j, x in enumerate(from_rows(ranks))]
 

time: 143 us -> 143 us (level)
  other arithmetic: 3.83 us -> 1.14 us
  Pallas kernels: 42.6 us -> 45.1 us
    select_n x1 -> x0, other arithmetic: 2.71 us -> none  [shards(): key_rows = jnp.where(steps_away == s, moved[s], key_rows)]
    pallas_call x0 -> x1, Pallas kernels: none -> 2.57 us  [choose(): pl.pallas_call(choose_kernel, out_shape=one, in_specs=[SMEM] + [HBM] * le...]
  transfers between devices with their start and end apart: 29 -> 29, of which waited for: 12 -> 12; matrix products, arithmetic and copies ran while one was open for 3% -> 1% of each run, Pallas kernels for 26% -> 28%
where the time goes in v9:
time: 143 us
  waiting for transfers between devices  47.5 us (33%)
  Pallas kernels  45.1 us (32%)
  starting transfers between devices  44.2 us (31%)
  local copies, waits for them, and re-layouts  4.6 us (3%)
    ppermute x19, waiting for transfers between devices, along_col(): return lax.ppermute(value, 'col', xor_pairs(col_count, j))  36.1 us
    ppermute x19, starting transfers between devices, along_col(): return lax.ppermute(value, 'col', xor_pairs(col_count, j))  17.7 us
    ppermute x7, starting transfers between devices, along_row(): return lax.ppermute(value, 'row', xor_pairs(row_count, j))  17.6 us
    ppermute x7, waiting for transfers between devices, along_row(): return lax.ppermute(value, 'row', xor_pairs(row_count, j))  11.4 us
    pallas_call x3, Pallas kernels, sweep(): pl.pallas_call(functools.partial(sweep_kernel, first, ks, chips, [at for...  11.3 us
    pallas_call x3, Pallas kernels, weigh(): pl.pallas_call(functools.partial(weigh_kernel, root, ks, seg), out_shape=...  10.8 us
    ppermute x3, starting transfers between devices, feature_step(): return lax.ppermute(value, ('row', 'col'), pairs)  8.86 us
    pallas_call x1, Pallas kernels, exponentials(): pl.pallas_call(expo_kernel, out_shape=(jax.ShapeDtypeStruct((PAIRS, rows,...  8.35 us
  transfers between devices with their start and end apart: 29, of which 12 were waited for; matrix products, arithmetic and copies ran while one was open for 1% of the time, Pallas kernels for 28%

profile of v9, /device:TPU:0, one launch (start us, length us, event | category | flops | bytes accessed | tf_op | source)
XLA Modules:
  0.0 142.9 jit_solution(5134541567574876284)
XLA Ops:
  0.0 3.0 %start.1 = (bf16[768,384]{1,0:T(8,128)(2,1)}, bf16[384,1024]{1,0:T(8,128)(2,1)}) custom-call(s32[3,6]{1,0:T(4,128)} %bitcast.13, bf16[768,384]{1,0:T(8,128)(2,1)} %weight_ref.1, bf16[768,1024]{1,0:T(8,128)(2,1)} %features_ref.1), custom_call_target="tpu_custom_call" | custom-call | flops 294912 | bytes 1179648 | tf_op jit(solution)/shard_map/start/pallas_call | solution.py:91
  3.1 5.7 %collective-permute-start = (bf16[384,1024]{1,0:T(8,128)(2,1)}, bf16[384,1024]{1,0:T(8,128)(2,1)}, u32[]{:S(2)}, u32[]{:S(2)}) collective-permute-start(bf16[384,1024]{1,0:T(8,128)(2,1)} %get-tuple-element.47.refs_0_), channel_id=1, source_target_pairs={{0,8},{1,17},{10,26},{11,3},{20,4},{21,29},{30,22},{31,15}} | collective-permute-start | bytes 2359304 | tf_op jit(solution)/shard_map/ppermute | solution.py:593
  11.9 3.1 %collective-permute-start.1 = (bf16[768,384]{1,0:T(8,128)(2,1)}, bf16[768,384]{1,0:T(8,128)(2,1)}, u32[]{:S(2)}, u32[]{:S(2)}) collective-permute-start(bf16[768,384]{1,0:T(8,128)(2,1)} %get-tuple-element.42.refs_0_.refs_8_), channel_id=1, source_target_pairs={{0,8},{8,0},{16,24},{24,16},{1,9},{9,1},{17,25},{25,17},{2,10},{10... | collective-permute-start | bytes 1769480 | tf_op jit(solution)/shard_map/ppermute | solution.py:565
  15.0 3.6 %project_in.2.q_ref = bf16[768,512]{1,0:T(8,128)(2,1)} custom-call(s32[1]{0:T(128)} %bitcast.3.place_ref, bf16[768,1024]{1,0:T(8,128)(2,1)} %features_ref.1, bf16[1024,3072]{1,0:T(8,128)(2,1)} %refs_2_.1), custom_call_target="tpu_custom_call" | custom-call | flops 805306368 | bytes 2621440 | tf_op jit(solution)/shard_map/project_in/pallas_call | solution.py:160
  18.6 17.3 %collective-permute-done.4.refs_2_ = bf16[768,384]{1,0:T(8,128)(2,1)S(1)} collective-permute-done((bf16[768,384]{1,0:T(8,128)(2,1)}, bf16[768,384]{1,0:T(8,128)(2,1)S(1)}, u32[]{:S(2)}, u32[]{:S(2)}) %collective-permute-start.4) | collective-permute-done | bytes 589856 | tf_op jit(solution)/shard_map/ppermute | solution.py:562
  40.7 3.7 %collective-permute-start.6 = (bf16[384,384]{1,0:T(8,128)(2,1)S(1)}, bf16[384,384]{1,0:T(8,128)(2,1)S(1)}, u32[]{:S(2)}, u32[]{:S(2)}) collective-permute-start(bf16[384,384]{1,0:T(8,128)(2,1)S(1)} %slice.7), channel_id=1, source_target_pairs={{0,16},{8,24},{16,0},{24,8},{1,17},{9,25},{17,1},{25,9},{2,18},{10... | collective-permute-start | bytes 884744 | tf_op jit(solution)/shard_map/ppermute | solution.py:565
  44.4 3.5 %collective-permute-start.5 = (bf16[384,384]{1,0:T(8,128)(2,1)S(1)}, bf16[384,384]{1,0:T(8,128)(2,1)S(1)}, u32[]{:S(2)}, u32[]{:S(2)}) collective-permute-start(bf16[384,384]{1,0:T(8,128)(2,1)S(1)} %slice.6), channel_id=1, source_target_pairs={{0,8},{8,0},{16,24},{24,16},{1,9},{9,1},{17,25},{25,17},{2,10},{10... | collective-permute-start | bytes 884744 | tf_op jit(solution)/shard_map/ppermute | solution.py:565
  51.8 2.9 %collective-permute-done.5.refs_11_ = bf16[384,384]{1,0:T(8,128)(2,1)S(1)} collective-permute-done((bf16[384,384]{1,0:T(8,128)(2,1)S(1)}, bf16[384,384]{1,0:T(8,128)(2,1)S(1)}, u32[]{:S(2)}, u32[]{:S(2)}) %collective-permute-start.5) | collective-permute-done | bytes 294944 | tf_op jit(solution)/shard_map/ppermute | solution.py:565
  55.7 2.6 %choose.1.refs_13_ = bf16[384,1024]{1,0:T(8,128)(2,1)} custom-call(s32[1]{0:T(128)} %bitcast.7.which_ref, bf16[384,1024]{1,0:T(8,128)(2,1)} %get-tuple-element.47.refs_0_, bf16[384,1024]{1,0:T(8,128)(2,1)} %collective-permute-done.refs_1_, bf16[384,1024]{1,0:T(8,128)(2,1)} %collective-permute-done.10.refs_2_), custom_call_target="tpu_custom_call" | custom-call | bytes 1572864 | tf_op jit(solution)/shard_map/choose/pallas_call | solution.py:128
  59.4 4.9 %rank_sweep.3.refs_8_ = bf16[768,384]{1,0:T(8,128)(2,1)S(1)} custom-call(s32[2]{0:T(128)S(1)} %pad_add_fusion.place_ref, s32[3,6]{1,0:T(4,128)S(1)} %bitcast.14, bf16[768,384]{1,0:T(8,128)(2,1)S(1)} %copy-done.2, bf16[768,384]{1,0:T(8,128)(2,1)S(1)} %collective-permute-done.3.refs_1_, bf16[768,384]{1,0:T(8,128)(2,1)S(1)} %collective-permute-done.4.refs_2_, ...), custom_call_target="tpu_custom_call" | custom-call | flops 1811939328 | bytes 9437184 | tf_op jit(solution)/shard_map/rank_sweep/pallas_call | solution.py:266
  64.6 4.5 %collective-permute-start.13 = (bf16[768,384]{1,0:T(8,128)(2,1)S(1)}, bf16[768,384]{1,0:T(8,128)(2,1)S(1)}, u32[]{:S(2)}, u32[]{:S(2)}) collective-permute-start(bf16[768,384]{1,0:T(8,128)(2,1)S(1)} %rank_sweep.3.refs_8_), channel_id=1, source_target_pairs={{0,24},{8,16},{16,8},{24,0},{1,25},{9,17},{17,9},{25,1},{2,26},{10... | collective-permute-start | bytes 1769480 | tf_op jit(solution)/shard_map/ppermute | solution.py:565
  70.3 2.8 %project_in.3.k_ref.v_ref = bf16[768,1024]{1,0:T(8,128)(2,1)S(1)} custom-call(s32[1]{0:T(128)} %bitcast.3.place_ref, bf16[384,1024]{1,0:T(8,128)(2,1)S(1)} %broadcast_select_fusion.refs_0_, bf16[384,1024]{1,0:T(8,128)(2,1)S(1)} %collective-permute-done.15.refs_1_, bf16[1024,3072]{1,0:T(8,128)(2,1)S(1)} %bitcast.9), custom_call_target="tpu_custom_call" | custom-call | flops 1610612736 | bytes 3670016 | tf_op jit(solution)/shard_map/project_in/pallas_call | solution.py:160
  75.4 2.4 %collective-permute-start.16 = (bf16[1024,128]{1,0:T(8,128)(2,1)S(1)}, bf16[1024,128]{1,0:T(8,128)(2,1)S(1)}, u32[]{:S(2)}, u32[]{:S(2)}) collective-permute-start(bf16[1024,128]{1,0:T(8,128)(2,1)S(1)} %copy-done.8), channel_id=1, source_target_pairs={{0,2},{1,3},{2,0},{3,1},{4,6},{5,7},{6,4},{7,5},{8,10},{9,11},{10,... | collective-permute-start | bytes 786440 | tf_op jit(solution)/shard_map/ppermute | solution.py:562
  77.8 8.3 %expo.1 = (bf16[4,768,1536]{2,1,0:T(8,128)(2,1)S(1)}, f32[768,128]{1,0:T(8,128)S(1)}) custom-call(s32[3,6]{1,0:T(4,128)S(1)} %bitcast.16, s32[3,6]{1,0:T(4,128)S(1)} %collective-permute-done.18.other_ref, bf16[768,512]{1,0:T(8,128)(2,1)S(1)} %copy-done.3, bf16[768,1024]{1,0:T(8,128)(2,1)S(1)} %project_in.3.k_ref.v_ref), custom_call_target="tpu_custom_call" | custom-call | flops 2415919104 | bytes 9437184 | tf_op jit(solution)/shard_map/expo/pallas_call | solution.py:338
  86.1 2.3 %collective-permute-done.17.refs_14_.refs_2_ = bf16[1024,128]{1,0:T(8,128)(2,1)S(1)} collective-permute-done((bf16[1024,128]{1,0:T(8,128)(2,1)S(1)}, bf16[1024,128]{1,0:T(8,128)(2,1)S(1)}, u32[]{:S(2)}, u32[]{:S(2)}) %collective-permute-start.17) | collective-permute-done | bytes 262176 | tf_op jit(solution)/shard_map/ppermute | solution.py:562
  89.7 5.7 %collective-permute-done.12.refs_10_ = bf16[768,384]{1,0:T(8,128)(2,1)S(1)} collective-permute-done((bf16[768,384]{1,0:T(8,128)(2,1)S(1)}, bf16[768,384]{1,0:T(8,128)(2,1)S(1)}, u32[]{:S(2)}, u32[]{:S(2)}) %collective-permute-start.12) | collective-permute-done | bytes 589856 | tf_op jit(solution)/shard_map/ppermute | solution.py:565
  96.6 3.1 %rank_sweep.5.own_ref = bf16[384,384]{1,0:T(8,128)(2,1)S(1)} custom-call(s32[2]{0:T(128)S(1)} %pad_add_fusion.place_ref, s32[3,6]{1,0:T(4,128)S(1)} %bitcast.17, bf16[768,384]{1,0:T(8,128)(2,1)S(1)} %copy-done.2, bf16[768,384]{1,0:T(8,128)(2,1)S(1)} %collective-permute-done.3.refs_1_, bf16[768,384]{1,0:T(8,128)(2,1)S(1)} %collective-permute-done.4.refs_2_, ...), custom_call_target="tpu_custom_call" | custom-call | flops 905969664 | bytes 7077888 | tf_op jit(solution)/shard_map/rank_sweep/pallas_call | solution.py:266
  99.8 3.3 %rank_sweep.4.refs_0_.own_ref = bf16[384,384]{1,0:T(8,128)(2,1)S(1)} custom-call(s32[2]{0:T(128)S(1)} %pad_add_fusion.place_ref, s32[3,6]{1,0:T(4,128)S(1)} %bitcast.18, bf16[768,384]{1,0:T(8,128)(2,1)S(1)} %copy-done.2, bf16[768,384]{1,0:T(8,128)(2,1)S(1)} %collective-permute-done.3.refs_1_, bf16[768,384]{1,0:T(8,128)(2,1)S(1)} %collective-permute-done.4.refs_2_, ...), custom_call_target="tpu_custom_call" | custom-call | flops 905969664 | bytes 7077888 | tf_op jit(solution)/shard_map/rank_sweep/pallas_call | solution.py:266
  103.7 3.1 %weigh.3.refs_0_ = bf16[208,512]{1,0:T(8,128)(2,1)S(1)} custom-call(s32[2]{0:T(128)S(1)} %pad_add_fusion.place_ref, f32[16]{0:T(128)S(1)} %copy-done.10, f32[16]{0:T(128)S(1)} %copy-done.11, bf16[384,384]{1,0:T(8,128)(2,1)S(1)} %rank_sweep.5.own_ref, bf16[384,384]{1,0:T(8,128)(2,1)S(1)} %collective-permute-done.21.other_ref, ...), custom_call_target="tpu_custom_call" | custom-call | flops 603979776 | bytes 2359296 | tf_op jit(solution)/shard_map/weigh/pallas_call | solution.py:433
  106.8 2.6 %collective-permute-start.24 = (bf16[208,512]{1,0:T(8,128)(2,1)S(1)}, bf16[208,512]{1,0:T(8,128)(2,1)S(1)}, u32[]{:S(2)}, u32[]{:S(2)}) collective-permute-start(bf16[208,512]{1,0:T(8,128)(2,1)S(1)} %weigh.3.refs_0_), channel_id=1, source_target_pairs={{0,6},{1,7},{2,4},{3,5},{4,2},{5,3},{6,0},{7,1},{8,14},{9,15},{10,... | collective-permute-start | bytes 638984 | tf_op jit(solution)/shard_map/ppermute | solution.py:562
  109.4 3.1 %weigh.4.refs_0_ = bf16[208,512]{1,0:T(8,128)(2,1)S(1)} custom-call(s32[2]{0:T(128)S(1)} %pad_add_fusion.place_ref, f32[16]{0:T(128)S(1)} %copy-done.10, f32[16]{0:T(128)S(1)} %copy-done.11, bf16[384,384]{1,0:T(8,128)(2,1)S(1)} %rank_sweep.5.own_ref, bf16[384,384]{1,0:T(8,128)(2,1)S(1)} %collective-permute-done.21.other_ref, ...), custom_call_target="tpu_custom_call" | custom-call | flops 603979776 | bytes 2359296 | tf_op jit(solution)/shard_map/weigh/pallas_call | solution.py:433
  114.4 4.7 %weigh.5 = (bf16[208,512]{1,0:T(8,128)(2,1)S(1)}, bf16[208,512]{1,0:T(8,128)(2,1)S(1)}) custom-call(s32[2]{0:T(128)S(1)} %pad_add_fusion.place_ref, f32[16]{0:T(128)S(1)} %copy-done.10, f32[16]{0:T(128)S(1)} %copy-done.11, bf16[384,384]{1,0:T(8,128)(2,1)S(1)} %rank_sweep.4.refs_0_.own_ref, bf16[384,384]{1,0:T(8,128)(2,1)S(1)} %collective-permute-done.20.other_ref, ...), custom_call_target="tpu_custom_call" | custom-call | flops 1207959552 | bytes 4718592 | tf_op jit(solution)/shard_map/weigh/pallas_call | solution.py:433
  119.2 10.5 %collective-permute-done.23.refs_2_ = bf16[208,512]{1,0:T(8,128)(2,1)S(1)} collective-permute-done((bf16[208,512]{1,0:T(8,128)(2,1)S(1)}, bf16[208,512]{1,0:T(8,128)(2,1)S(1)}, u32[]{:S(2)}, u32[]{:S(2)}) %collective-permute-start.23) | collective-permute-done | bytes 213024 | tf_op jit(solution)/shard_map/ppermute | solution.py:562
  135.7 3.2 %collective-permute-start.28 = (bf16[192,128]{1,0:T(8,128)(2,1)S(1)}, bf16[192,128]{1,0:T(8,128)(2,1)S(1)}, u32[]{:S(2)}, u32[]{:S(2)}) collective-permute-start(bf16[192,128]{1,0:T(8,128)(2,1)S(1)} %get-tuple-element.63), channel_id=1, source_target_pairs={{0,2},{1,3},{2,0},{3,1},{4,6},{5,7},{6,4},{7,5},{8,10},{9,11},{10,... | collective-permute-start | bytes 147464 | tf_op jit(solution)/shard_map/ppermute | solution.py:562
  (85 shorter events, 32.6 us)
Async XLA Ops:
  3.1 33.4 %collective-permute-start = (bf16[384,1024]{1,0:T(8,128)(2,1)}, bf16[384,1024]{1,0:T(8,128)(2,1)}, u32[]{:S(2)}, u32[]{:S(2)}) collective-permute-start(bf16[384,1024]{1,0:T(8,128)(2,1)} %get-tuple-element.47.refs_0_), channel_id=1, source_target_pairs={{0,8},{1,17},{10,26},{11,3},{20,4},{21,29},{30,22},{31,15}} | collective-permute-start | bytes 2359304 | tf_op jit(solution)/shard_map/ppermute | solution.py:593
  8.8 27.1 %collective-permute-start.4 = (bf16[768,384]{1,0:T(8,128)(2,1)}, bf16[768,384]{1,0:T(8,128)(2,1)S(1)}, u32[]{:S(2)}, u32[]{:S(2)}) collective-permute-start(bf16[768,384]{1,0:T(8,128)(2,1)} %get-tuple-element.42.refs_0_.refs_8_), channel_id=1, source_target_pairs={{0,4},{1,5},{2,6},{3,7},{4,0},{5,1},{6,2},{7,3},{8,12},{9,13},{10,... | collective-permute-start | bytes 1769480 | tf_op jit(solution)/shard_map/ppermute | solution.py:562
  8.8 27.7 %collective-permute-start.3 = (bf16[768,384]{1,0:T(8,128)(2,1)}, bf16[768,384]{1,0:T(8,128)(2,1)S(1)}, u32[]{:S(2)}, u32[]{:S(2)}) collective-permute-start(bf16[768,384]{1,0:T(8,128)(2,1)} %get-tuple-element.42.refs_0_.refs_8_), channel_id=1, source_target_pairs={{0,2},{1,3},{2,0},{3,1},{4,6},{5,7},{6,4},{7,5},{8,10},{9,11},{10,... | collective-permute-start | bytes 1769480 | tf_op jit(solution)/shard_map/ppermute | solution.py:562
  10.2 26.2 %collective-permute-start.2 = (bf16[768,384]{1,0:T(8,128)(2,1)}, bf16[768,384]{1,0:T(8,128)(2,1)}, u32[]{:S(2)}, u32[]{:S(2)}) collective-permute-start(bf16[768,384]{1,0:T(8,128)(2,1)} %get-tuple-element.42.refs_0_.refs_8_), channel_id=1, source_target_pairs={{0,16},{8,24},{16,0},{24,8},{1,17},{9,25},{17,1},{25,9},{2,18},{10... | collective-permute-start | bytes 1769480 | tf_op jit(solution)/shard_map/ppermute | solution.py:565
  11.9 24.5 %collective-permute-start.1 = (bf16[768,384]{1,0:T(8,128)(2,1)}, bf16[768,384]{1,0:T(8,128)(2,1)}, u32[]{:S(2)}, u32[]{:S(2)}) collective-permute-start(bf16[768,384]{1,0:T(8,128)(2,1)} %get-tuple-element.42.refs_0_.refs_8_), channel_id=1, source_target_pairs={{0,8},{8,0},{16,24},{24,16},{1,9},{9,1},{17,25},{25,17},{2,10},{10... | collective-permute-start | bytes 1769480 | tf_op jit(solution)/shard_map/ppermute | solution.py:565
  36.7 18.7 %collective-permute-start.7 = (bf16[3,768,384]{2,1,0:T(8,128)(2,1)S(1)}, bf16[3,768,384]{2,1,0:T(8,128)(2,1)S(1)}, u32[]{:S(2)}, u32[]{:S(2)}) collective-permute-start(bf16[3,768,384]{2,1,0:T(8,128)(2,1)S(1)} %pad_maximum_fusion), channel_id=1, source_target_pairs={{0,1},{1,0},{2,3},{3,2},{4,5},{5,4},{6,7},{7,6},{8,9},{9,8},{10,11... | collective-permute-start | bytes 5308424 | tf_op jit(solution)/shard_map/ppermute | solution.py:562
  36.8 11.0 %collective-permute-start.10 = (bf16[384,1024]{1,0:T(8,128)(2,1)}, bf16[384,1024]{1,0:T(8,128)(2,1)}, u32[]{:S(2)}, u32[]{:S(2)}) collective-permute-start(bf16[384,1024]{1,0:T(8,128)(2,1)} %collective-permute-done.refs_1_), channel_id=1, source_target_pairs={{8,24},{17,25},{26,18},{3,19},{4,12},{29,13},{22,6},{15,7}} | collective-permute-start | bytes 2359304 | tf_op jit(solution)/shard_map/ppermute | solution.py:593
  38.4 17.1 %collective-permute-start.8 = (bf16[768,384]{1,0:T(8,128)(2,1)S(1)}, bf16[768,384]{1,0:T(8,128)(2,1)}, u32[]{:S(2)}, u32[]{:S(2)}) collective-permute-start(bf16[768,384]{1,0:T(8,128)(2,1)S(1)} %collective-permute-done.4.refs_2_), channel_id=1, source_target_pairs={{0,2},{1,3},{2,0},{3,1},{4,6},{5,7},{6,4},{7,5},{8,10},{9,11},{10,... | collective-permute-start | bytes 1769480 | tf_op jit(solution)/shard_map/ppermute | solution.py:562
  40.7 10.4 %collective-permute-start.6 = (bf16[384,384]{1,0:T(8,128)(2,1)S(1)}, bf16[384,384]{1,0:T(8,128)(2,1)S(1)}, u32[]{:S(2)}, u32[]{:S(2)}) collective-permute-start(bf16[384,384]{1,0:T(8,128)(2,1)S(1)} %slice.7), channel_id=1, source_target_pairs={{0,16},{8,24},{16,0},{24,8},{1,17},{9,25},{17,1},{25,9},{2,18},{10... | collective-permute-start | bytes 884744 | tf_op jit(solution)/shard_map/ppermute | solution.py:565
  44.4 10.4 %collective-permute-start.5 = (bf16[384,384]{1,0:T(8,128)(2,1)S(1)}, bf16[384,384]{1,0:T(8,128)(2,1)S(1)}, u32[]{:S(2)}, u32[]{:S(2)}) collective-permute-start(bf16[384,384]{1,0:T(8,128)(2,1)S(1)} %slice.6), channel_id=1, source_target_pairs={{0,8},{8,0},{16,24},{24,16},{1,9},{9,1},{17,25},{25,17},{2,10},{10... | collective-permute-start | bytes 884744 | tf_op jit(solution)/shard_map/ppermute | solution.py:565
  47.9 16.4 %collective-permute-start.14 = (bf16[384,1024]{1,0:T(8,128)(2,1)}, bf16[384,1024]{1,0:T(8,128)(2,1)}, u32[]{:S(2)}, u32[]{:S(2)}) collective-permute-start(bf16[384,1024]{1,0:T(8,128)(2,1)} %collective-permute-done.10.refs_2_), channel_id=1, source_target_pairs={{24,16},{25,9},{18,2},{19,27},{12,28},{13,5},{6,14},{7,23}} | collective-permute-start | bytes 2359304 | tf_op jit(solution)/shard_map/ppermute | solution.py:593
  64.6 25.1 %collective-permute-start.13 = (bf16[768,384]{1,0:T(8,128)(2,1)S(1)}, bf16[768,384]{1,0:T(8,128)(2,1)S(1)}, u32[]{:S(2)}, u32[]{:S(2)}) collective-permute-start(bf16[768,384]{1,0:T(8,128)(2,1)S(1)} %rank_sweep.3.refs_8_), channel_id=1, source_target_pairs={{0,24},{8,16},{16,8},{24,0},{1,25},{9,17},{17,9},{25,1},{2,26},{10... | collective-permute-start | bytes 1769480 | tf_op jit(solution)/shard_map/ppermute | solution.py:565
  69.1 26.3 %collective-permute-start.12 = (bf16[768,384]{1,0:T(8,128)(2,1)S(1)}, bf16[768,384]{1,0:T(8,128)(2,1)S(1)}, u32[]{:S(2)}, u32[]{:S(2)}) collective-permute-start(bf16[768,384]{1,0:T(8,128)(2,1)S(1)} %rank_sweep.3.refs_8_), channel_id=1, source_target_pairs={{0,16},{8,24},{16,0},{24,8},{1,17},{9,25},{17,1},{25,9},{2,18},{10... | collective-permute-start | bytes 1769480 | tf_op jit(solution)/shard_map/ppermute | solution.py:565
  69.7 26.8 %collective-permute-start.11 = (bf16[768,384]{1,0:T(8,128)(2,1)S(1)}, bf16[768,384]{1,0:T(8,128)(2,1)S(1)}, u32[]{:S(2)}, u32[]{:S(2)}) collective-permute-start(bf16[768,384]{1,0:T(8,128)(2,1)S(1)} %rank_sweep.3.refs_8_), channel_id=1, source_target_pairs={{0,8},{8,0},{16,24},{24,16},{1,9},{9,1},{17,25},{25,17},{2,10},{10... | collective-permute-start | bytes 1769480 | tf_op jit(solution)/shard_map/ppermute | solution.py:565
  73.1 15.3 %collective-permute-start.17 = (bf16[1024,128]{1,0:T(8,128)(2,1)S(1)}, bf16[1024,128]{1,0:T(8,128)(2,1)S(1)}, u32[]{:S(2)}, u32[]{:S(2)}) collective-permute-start(bf16[1024,128]{1,0:T(8,128)(2,1)S(1)} %copy-done.8), channel_id=1, source_target_pairs={{0,4},{1,5},{2,6},{3,7},{4,0},{5,1},{6,2},{7,3},{8,12},{9,13},{10,... | collective-permute-start | bytes 786440 | tf_op jit(solution)/shard_map/ppermute | solution.py:562
  75.4 13.1 %collective-permute-start.16 = (bf16[1024,128]{1,0:T(8,128)(2,1)S(1)}, bf16[1024,128]{1,0:T(8,128)(2,1)S(1)}, u32[]{:S(2)}, u32[]{:S(2)}) collective-permute-start(bf16[1024,128]{1,0:T(8,128)(2,1)S(1)} %copy-done.8), channel_id=1, source_target_pairs={{0,2},{1,3},{2,0},{3,1},{4,6},{5,7},{6,4},{7,5},{8,10},{9,11},{10,... | collective-permute-start | bytes 786440 | tf_op jit(solution)/shard_map/ppermute | solution.py:562
  88.5 11.4 %collective-permute-start.19 = (bf16[1024,128]{1,0:T(8,128)(2,1)S(1)}, bf16[1024,128]{1,0:T(8,128)(2,1)S(1)}, u32[]{:S(2)}, u32[]{:S(2)}) collective-permute-start(bf16[1024,128]{1,0:T(8,128)(2,1)S(1)} %collective-permute-done.17.refs_14_.refs_2_), channel_id=1, source_target_pairs={{0,2},{1,3},{2,0},{3,1},{4,6},{5,7},{6,4},{7,5},{8,10},{9,11},{10,... | collective-permute-start | bytes 786440 | tf_op jit(solution)/shard_map/ppermute | solution.py:562
  103.2 11.3 %collective-permute-start.20 = (bf16[384,384]{1,0:T(8,128)(2,1)S(1)}, bf16[384,384]{1,0:T(8,128)(2,1)S(1)}, u32[]{:S(2)}, u32[]{:S(2)}) collective-permute-start(bf16[384,384]{1,0:T(8,128)(2,1)S(1)} %rank_sweep.4.refs_0_.own_ref), channel_id=1, source_target_pairs={{0,1},{1,0},{2,3},{3,2},{4,5},{5,4},{6,7},{7,6},{8,9},{9,8},{10,11... | collective-permute-start | bytes 884744 | tf_op jit(solution)/shard_map/ppermute | solution.py:562
  106.8 22.9 %collective-permute-start.24 = (bf16[208,512]{1,0:T(8,128)(2,1)S(1)}, bf16[208,512]{1,0:T(8,128)(2,1)S(1)}, u32[]{:S(2)}, u32[]{:S(2)}) collective-permute-start(bf16[208,512]{1,0:T(8,128)(2,1)S(1)} %weigh.3.refs_0_), channel_id=1, source_target_pairs={{0,6},{1,7},{2,4},{3,5},{4,2},{5,3},{6,0},{7,1},{8,14},{9,15},{10,... | collective-permute-start | bytes 638984 | tf_op jit(solution)/shard_map/ppermute | solution.py:562
  112.5 17.2 %collective-permute-start.23 = (bf16[208,512]{1,0:T(8,128)(2,1)S(1)}, bf16[208,512]{1,0:T(8,128)(2,1)S(1)}, u32[]{:S(2)}, u32[]{:S(2)}) collective-permute-start(bf16[208,512]{1,0:T(8,128)(2,1)S(1)} %weigh.4.refs_0_), channel_id=1, source_target_pairs={{0,4},{1,5},{2,6},{3,7},{4,0},{5,1},{6,2},{7,3},{8,12},{9,13},{10,... | collective-permute-start | bytes 638984 | tf_op jit(solution)/shard_map/ppermute | solution.py:562
  119.1 11.3 %collective-permute-start.22 = (bf16[208,512]{1,0:T(8,128)(2,1)S(1)}, bf16[208,512]{1,0:T(8,128)(2,1)S(1)}, u32[]{:S(2)}, u32[]{:S(2)}) collective-permute-start(bf16[208,512]{1,0:T(8,128)(2,1)S(1)} %get-tuple-element.59), channel_id=1, source_target_pairs={{0,2},{1,3},{2,0},{3,1},{4,6},{5,7},{6,4},{7,5},{8,10},{9,11},{10,... | collective-permute-start | bytes 638984 | tf_op jit(solution)/shard_map/ppermute | solution.py:562
  134.4 6.5 %collective-permute-start.26 = (bf16[192,128]{1,0:T(8,128)(2,1)S(1)}, bf16[192,128]{1,0:T(8,128)(2,1)S(1)}, u32[]{:S(2)}, u32[]{:S(2)}) collective-permute-start(bf16[192,128]{1,0:T(8,128)(2,1)S(1)} %get-tuple-element.61), channel_id=1, source_target_pairs={{0,6},{1,7},{2,4},{3,5},{4,2},{5,3},{6,0},{7,1},{8,14},{9,15},{10,... | collective-permute-start | bytes 147464 | tf_op jit(solution)/shard_map/ppermute | solution.py:562
  135.7 6.5 %collective-permute-start.27 = (bf16[192,128]{1,0:T(8,128)(2,1)S(1)}, bf16[192,128]{1,0:T(8,128)(2,1)S(1)}, u32[]{:S(2)}, u32[]{:S(2)}) collective-permute-start(bf16[192,128]{1,0:T(8,128)(2,1)S(1)} %get-tuple-element.62), channel_id=1, source_target_pairs={{0,4},{1,5},{2,6},{3,7},{4,0},{5,1},{6,2},{7,3},{8,12},{9,13},{10,... | collective-permute-start | bytes 147464 | tf_op jit(solution)/shard_map/ppermute | solution.py:562
  135.7 6.5 %collective-permute-start.28 = (bf16[192,128]{1,0:T(8,128)(2,1)S(1)}, bf16[192,128]{1,0:T(8,128)(2,1)S(1)}, u32[]{:S(2)}, u32[]{:S(2)}) collective-permute-start(bf16[192,128]{1,0:T(8,128)(2,1)S(1)} %get-tuple-element.63), channel_id=1, source_target_pairs={{0,2},{1,3},{2,0},{3,1},{4,6},{5,7},{6,4},{7,5},{8,10},{9,11},{10,... | collective-permute-start | bytes 147464 | tf_op jit(solution)/shard_map/ppermute | solution.py:562
  (20 other events, 152.3 us)
